TPU v7x, 32 devices: a whole 2x2x4 slice. The times are simulated.
32 devices in a mesh: gx: 4 (over z), gy: 4 (over y, core), gz: 2 (over x).
Axes of the slice: x: 2, y: 2, z: 4, core: 2. Of those that a mesh axis runs over, the one named last changes fastest.
Arguments:
- block: float32 [128, 64, 16, 128], P('gx', 'gy', 'gz'), may hold values from -30 to 30
- conductivity: float32 [128, 64, 16], P('gx', 'gy', 'gz'), may hold values from 0.3 to 3
Outputs:
- basis: float32 [128, 64, 16, 128], P('gx', 'gy', 'gz')
- projected: float32 [128, 128], replicated
All inputs are finite; a program needn't handle non-finite values.
Results may differ from a plain program's by a relative error of at most 0.00028.
Values sent between devices are 32-bit elements; how exact they have to be, the bound alone decides.
No kernel may reach another device: no remote copies, remote signals or barrier semaphores. Data moves between devices by JAX's collectives and lax.ppermute only.
A program may use at most 64 MiB of HBM per device.

v0:
```python
import jax
import jax.numpy as jnp
from jax import lax
from jax.sharding import PartitionSpec as P

DEG = 4


HIGH = lax.Precision.HIGHEST
center_value = 3.25
half_value = 2.75


def extended(block, sides, width):
    for axis, dim in sides:
        count = lax.axis_size(axis)
        forward = [(i, i + 1) for i in range(count - 1)]
        backward = [(target, source) for source, target in forward]
        low = lax.ppermute(
            lax.slice_in_dim(block, block.shape[dim] - width, None, axis=dim), axis, forward
        )
        high = lax.ppermute(lax.slice_in_dim(block, 0, width, axis=dim), axis, backward)
        block = jnp.concatenate([low, block, high], axis=dim)
    return block


def neighbours(padded):
    total = padded[2:, 1:-1, 1:-1] + padded[:-2, 1:-1, 1:-1]
    total = total + padded[1:-1, 2:, 1:-1] + padded[1:-1, :-2, 1:-1]
    total = total + padded[1:-1, 1:-1, 2:] + padded[1:-1, 1:-1, :-2]
    return total


def inner(left, right):
    width = left.shape[-1]
    return jnp.einsum(
        "ck,cl->kl", left.reshape(-1, width), right.reshape(-1, width), precision=HIGH
    )


def operator(vectors, sroot):
    scaled = sroot * vectors
    padded = extended(scaled, (("gx", 0), ("gy", 1), ("gz", 2)), 1)
    return sroot * (6.0 * scaled - neighbours(padded)) / 6.0


def quadratic(vectors, sroot):
    scaled = sroot * vectors
    padded = extended(scaled, (("gx", 0), ("gy", 1), ("gz", 2)), 1)
    image = sroot * (6.0 * scaled - neighbours(padded)) / 6.0
    return inner(vectors, image)


def lower_inverse(gram):
    lower = jnp.linalg.cholesky(gram)
    return lax.linalg.triangular_solve(
        lower, jnp.eye(gram.shape[0], dtype=gram.dtype), left_side=True, lower=True
    )


def on_device(block, conductivity):
    sroot = jnp.sqrt(conductivity)[..., None]
    cells = float(
        block.shape[0]
        * block.shape[1]
        * block.shape[2]
        * lax.axis_size("gx")
        * lax.axis_size("gy")
        * lax.axis_size("gz")
    )
    previous = block
    current = (operator(block, sroot) - center_value * block) / half_value
    for step in range(DEG - 1):
        following = (
            2.0 * (operator(current, sroot) - center_value * current) / half_value - previous
        )
        previous, current = (current, following)
    width = current.shape[-1]
    flat = current.reshape(-1, width)
    gram = lax.psum(inner(current, current) / cells, ("gx", "gy", "gz"))
    inverse = lower_inverse(gram)
    basis = jnp.dot(flat, inverse.T, precision=HIGH).reshape(current.shape)
    projected = lax.psum(quadratic(basis, sroot) / cells, ("gx", "gy", "gz"))
    return (basis, projected)


def solution(mesh):
    return jax.shard_map(
        on_device,
        mesh=mesh,
        in_specs=(P("gx", "gy", "gz", None), P("gx", "gy", "gz")),
        out_specs=(P("gx", "gy", "gz", None), P()),
        check_vma=False,
    )
```

profile of v0, /device:TPU:0, one launch (start us, length us, event | category | flops | bytes accessed | tf_op | source)
XLA Modules:
  0.0 462.9 jit_solution(13953084254091732854)
XLA Ops:
  10.5 4.9 %collective-permute-start.1 = (f32[1,16,8,128]{3,2,1,0:T(8,128)S(1)}, f32[1,16,8,128]{3,2,1,0:T(8,128)S(1)}, u32[]{:S(2)}, u32[]{:S(2)}) collective-permute-start(f32[1,16,8,128]{3,2,1,0:T(8,128)S(1)} %get-tuple-element.38), channel_id=1, source_target_pairs={{0,8},{8,16},{16,24},{1,9},{9,17},{17,25},{2,10},{10,18},{18,26},{... | collective-permute-start | bytes 196616 | tf_op jit(solution)/shard_map/ppermute | solution.py:19
  17.3 4.3 collective-permute-done
  24.2 3.7 collective-permute-done.2
  30.6 5.3 %collective-permute-start.5 = (f32[34,18,1,128]{3,2,1,0:T(1,128)}, f32[34,18,1,128]{3,2,1,0:T(1,128)}, u32[]{:S(2)}, u32[]{:S(2)}) collective-permute-start(f32[34,18,1,128]{3,2,1,0:T(1,128)} %get-tuple-element.19), channel_id=1, source_target_pairs={{0,1},{2,3},{4,5},{6,7},{8,9},{10,11},{12,13},{14,15},{16,17},{18,... | collective-permute-start | bytes 940040 | tf_op jit(solution)/shard_map/ppermute | solution.py:19
  40.9 6.3 %broadcast_multiply_fusion = (f32[32,16,8,128]{3,2,1,0:T(8,128)S(1)}, f32[32,16,8,128]{3,2,1,0:T(8,128)S(1)}) fusion(f32[32,16,8]{2,1,0:T(8,128)S(1)} %copy.5, f32[32,16,8,128]{3,2,1,0:T(8,128)} %param.2, f32[34,1,8,128]{3,2,1,0:T(8,128)S(1)} %collective-permute-done.2, f32[1,16,8,128]{3,2,1,0:T(8,128)S(1)} %collective-permute-done, ...), kind=kLoop, calls=%fused_computation.143 | loop fusion | flops 15728640 | bytes 9457664 | tf_op jit(solution)/shard_map/mul | solution.py:42
  47.2 3.5 collective-permute-start.7
  52.6 4.3 collective-permute-done.6
  56.9 3.2 collective-permute-start.9
  66.3 4.6 collective-permute-start.11
  70.9 3.4 collective-permute-done.10
  76.1 5.4 %broadcast_multiply_fusion.3 = (f32[32,16,8,128]{3,2,1,0:T(8,128)S(1)}, f32[32,16,8,128]{3,2,1,0:T(8,128)S(1)}) fusion(f32[32,16,8]{2,1,0:T(8,128)S(1)} %copy.4, f32[32,16,8,128]{3,2,1,0:T(8,128)S(1)} %copy-done.1, f32[32,16,8,128]{3,2,1,0:T(8,128)S(1)} %get-tuple-element.9, f32[34,1,8,128]{3,2,1,0:T(8,128)S(1)} %collective-permute-done.8, ...), kind=kLoop, calls=%fused_computation.146 | loop fusion | flops 16777216 | bytes 11538432 | tf_op jit(solution)/shard_map/mul | solution.py:42
  81.5 3.5 collective-permute-start.13
  86.8 4.3 collective-permute-done.12
  100.6 4.6 collective-permute-start.17
  105.1 3.4 collective-permute-done.16
  110.3 5.3 %broadcast_multiply_fusion.2 = (f32[32,16,8,128]{3,2,1,0:T(8,128)S(1)}, f32[32,16,8,128]{3,2,1,0:T(8,128)S(1)}) fusion(f32[32,16,8]{2,1,0:T(8,128)S(1)} %copy.4, f32[32,16,8,128]{3,2,1,0:T(8,128)S(1)} %get-tuple-element.9, f32[32,16,8,128]{3,2,1,0:T(8,128)S(1)} %get-tuple-element.7, f32[34,1,8,128]{3,2,1,0:T(8,128)S(1)} %collective-permute-done.14, ...), kind=kLoop, calls=%fused_computation.145 | loop fusion | flops 17301504 | bytes 11538432 | tf_op jit(solution)/shard_map/mul | solution.py:42
  119.5 4.3 collective-permute-done.18
  133.2 4.8 %collective-permute-start.23 = (f32[34,18,1,128]{3,2,1,0:T(1,128)S(1)}, f32[34,18,1,128]{3,2,1,0:T(1,128)S(1)}, u32[]{:S(2)}, u32[]{:S(2)}) collective-permute-start(f32[34,18,1,128]{3,2,1,0:T(1,128)S(1)} %get-tuple-element.13), channel_id=1, source_target_pairs={{0,1},{2,3},{4,5},{6,7},{8,9},{10,11},{12,13},{14,15},{16,17},{18,... | collective-permute-start | bytes 940040 | tf_op jit(solution)/shard_map/ppermute | solution.py:19
  138.0 3.3 collective-permute-done.22
  143.0 5.3 %fusion.14 = f32[32,16,8,128]{3,2,1,0:T(8,128)S(1)} fusion(f32[32,16,8,128]{3,2,1,0:T(8,128)S(1)} %get-tuple-element.7, f32[34,18,1,128]{3,2,1,0:T(1,128)S(1)} %collective-permute-done.23, f32[34,1,8,128]{3,2,1,0:T(8,128)S(1)} %collective-permute-done.20, f32[34,1,8,128]{3,2,1,0:T(8,128)S(1)} %collective-permute-done.21, ...), kind=kLoop, calls=%fused_computation.33 | loop fusion | flops 16252928 | bytes 9441280 | tf_op jit(solution)/shard_map/sub | solution.py:75
  148.3 4.1 fusion.50
  152.5 118.0 %all-reduce.3.cloned.1.call-done = f32[128,128]{0,1:T(8,128)} async-done(((f32[128,128]{0,1:T(8,128)}), f32[128,128]{0,1:T(8,128)}) %all-reduce.3.cloned.1.call-update) | async-done | bytes 65552 | tf_op jit(solution)/shard_map/psum | solution.py:80
  272.2 11.7 %cholesky.17 = f32[128,128]{1,0:T(8,128)S(1)} custom-call(f32[128,128]{1,0:T(8,128)S(1)} %fusion.54), custom_call_target="Cholesky" | custom-call | tf_op jit(solution)/shard_map/jit(cholesky)/cholesky | solution.py:55
  285.3 9.8 %custom-call.6 = f32[1,128,128]{1,2,0:T(8,128)S(1)} custom-call(f32[1,128,128]{2,1,0:T(8,128)S(1)} %fusion.51), custom_call_target="InvertDiagBlocksLowerTriangular" | custom-call | tf_op jit(solution)/shard_map/triangular_solve | solution.py:56
  298.0 4.7 %collective-permute-start.25 = (f32[1,16,8,128]{3,2,1,0:T(8,128)S(1)}, f32[1,16,8,128]{3,2,1,0:T(8,128)S(1)}, u32[]{:S(2)}, u32[]{:S(2)}) collective-permute-start(f32[1,16,8,128]{3,2,1,0:T(8,128)S(1)} %get-tuple-element.30), channel_id=1, source_target_pairs={{0,8},{8,16},{16,24},{1,9},{9,17},{17,25},{2,10},{10,18},{18,26},{... | collective-permute-start | bytes 196616 | tf_op jit(solution)/shard_map/ppermute | solution.py:19
  304.5 4.3 collective-permute-done.24
  311.4 3.6 collective-permute-done.26
  317.1 4.8 %collective-permute-start.29 = (f32[34,18,1,128]{3,2,1,0:T(1,128)S(1)}, f32[34,18,1,128]{3,2,1,0:T(1,128)S(1)}, u32[]{:S(2)}, u32[]{:S(2)}) collective-permute-start(f32[34,18,1,128]{3,2,1,0:T(1,128)S(1)} %get-tuple-element.11), channel_id=1, source_target_pairs={{0,1},{2,3},{4,5},{6,7},{8,9},{10,11},{12,13},{14,15},{16,17},{18,... | collective-permute-start | bytes 940040 | tf_op jit(solution)/shard_map/ppermute | solution.py:19
  321.9 3.3 collective-permute-done.28
  327.0 4.9 %fusion.3 = f32[32,16,8,128]{3,2,1,0:T(8,128)S(1)} fusion(f32[34,18,1,128]{3,2,1,0:T(1,128)S(1)} %collective-permute-done.29, f32[34,1,8,128]{3,2,1,0:T(8,128)S(1)} %collective-permute-done.26, f32[34,1,8,128]{3,2,1,0:T(8,128)S(1)} %collective-permute-done.27, f32[1,16,8,128]{3,2,1,0:T(8,128)S(1)} %collective-permute-done.24, ...), kind=kLoop, calls=%fused_computation.4 | loop fusion | flops 14155776 | bytes 5246976 | tf_op jit(solution)/shard_map/div | solution.py:50
  332.0 4.2 convolution_multiply_fusion
  336.2 118.3 %all-reduce.5.cloned.1.call-done = f32[128,128]{0,1:T(8,128)} async-done(((f32[128,128]{0,1:T(8,128)}), f32[128,128]{0,1:T(8,128)}) %all-reduce.5.cloned.1.call-update) | async-done | bytes 65552 | tf_op jit(solution)/shard_map/psum | solution.py:83
  (75 shorter events, 69.2 us)
Async XLA Ops:
  7.2 263.3 %all-reduce.3.cloned.1.call-start = ((), (), s32[]{:S(2)}) async-start(), calls=%async_computation | async-start | bytes 131072 | tf_op jit(solution)/shard_map/psum | solution.py:80
  10.5 6.8 %collective-permute-start.1 = (f32[1,16,8,128]{3,2,1,0:T(8,128)S(1)}, f32[1,16,8,128]{3,2,1,0:T(8,128)S(1)}, u32[]{:S(2)}, u32[]{:S(2)}) collective-permute-start(f32[1,16,8,128]{3,2,1,0:T(8,128)S(1)} %get-tuple-element.38), channel_id=1, source_target_pairs={{0,8},{8,16},{16,24},{1,9},{9,17},{17,25},{2,10},{10,18},{18,26},{... | collective-permute-start | bytes 196616 | tf_op jit(solution)/shard_map/ppermute | solution.py:19
  15.4 6.2 %collective-permute-start = (f32[1,16,8,128]{3,2,1,0:T(8,128)S(1)}, f32[1,16,8,128]{3,2,1,0:T(8,128)S(1)}, u32[]{:S(2)}, u32[]{:S(2)}) collective-permute-start(f32[1,16,8,128]{3,2,1,0:T(8,128)S(1)} %get-tuple-element.39), channel_id=1, source_target_pairs={{8,0},{16,8},{24,16},{9,1},{17,9},{25,17},{10,2},{18,10},{26,18},{... | collective-permute-start | bytes 196616 | tf_op jit(solution)/shard_map/ppermute | solution.py:22
  21.6 2.6 collective-permute-start.3
  22.9 5.0 %collective-permute-start.2 = (f32[34,1,8,128]{3,2,1,0:T(8,128)S(1)}, f32[34,1,8,128]{3,2,1,0:T(8,128)S(1)}, u32[]{:S(2)}, u32[]{:S(2)}) collective-permute-start(f32[34,1,8,128]{3,2,1,0:T(8,128)S(1)} %get-tuple-element.29), channel_id=1, source_target_pairs={{2,0},{4,2},{6,4},{3,1},{5,3},{7,5},{10,8},{12,10},{14,12},{11,9},... | collective-permute-start | bytes 417800 | tf_op jit(solution)/shard_map/ppermute | solution.py:22
  29.4 9.7 %collective-permute-start.4 = (f32[34,18,1,128]{3,2,1,0:T(1,128)}, f32[34,18,1,128]{3,2,1,0:T(1,128)S(1)}, u32[]{:S(2)}, u32[]{:S(2)}) collective-permute-start(f32[34,18,1,128]{3,2,1,0:T(1,128)} %get-tuple-element.18), channel_id=1, source_target_pairs={{1,0},{3,2},{5,4},{7,6},{9,8},{11,10},{13,12},{15,14},{17,16},{19,... | collective-permute-start | bytes 940040 | tf_op jit(solution)/shard_map/ppermute | solution.py:22
  30.6 10.2 %collective-permute-start.5 = (f32[34,18,1,128]{3,2,1,0:T(1,128)}, f32[34,18,1,128]{3,2,1,0:T(1,128)}, u32[]{:S(2)}, u32[]{:S(2)}) collective-permute-start(f32[34,18,1,128]{3,2,1,0:T(1,128)} %get-tuple-element.19), channel_id=1, source_target_pairs={{0,1},{2,3},{4,5},{6,7},{8,9},{10,11},{12,13},{14,15},{16,17},{18,... | collective-permute-start | bytes 940040 | tf_op jit(solution)/shard_map/ppermute | solution.py:19
  47.2 5.4 %collective-permute-start.7 = (f32[1,16,8,128]{3,2,1,0:T(8,128)S(1)}, f32[1,16,8,128]{3,2,1,0:T(8,128)S(1)}, u32[]{:S(2)}, u32[]{:S(2)}) collective-permute-start(f32[1,16,8,128]{3,2,1,0:T(8,128)S(1)} %get-tuple-element.36), channel_id=1, source_target_pairs={{0,8},{8,16},{16,24},{1,9},{9,17},{17,25},{2,10},{10,18},{18,26},{... | collective-permute-start | bytes 196616 | tf_op jit(solution)/shard_map/ppermute | solution.py:19
  50.7 6.2 %collective-permute-start.6 = (f32[1,16,8,128]{3,2,1,0:T(8,128)S(1)}, f32[1,16,8,128]{3,2,1,0:T(8,128)S(1)}, u32[]{:S(2)}, u32[]{:S(2)}) collective-permute-start(f32[1,16,8,128]{3,2,1,0:T(8,128)S(1)} %get-tuple-element.37), channel_id=1, source_target_pairs={{8,0},{16,8},{24,16},{9,1},{17,9},{25,17},{10,2},{18,10},{26,18},{... | collective-permute-start | bytes 196616 | tf_op jit(solution)/shard_map/ppermute | solution.py:22
  56.9 4.5 collective-permute-start.9
  60.0 4.2 collective-permute-start.8
  65.0 9.3 %collective-permute-start.10 = (f32[34,18,1,128]{3,2,1,0:T(1,128)S(1)}, f32[34,18,1,128]{3,2,1,0:T(1,128)S(1)}, u32[]{:S(2)}, u32[]{:S(2)}) collective-permute-start(f32[34,18,1,128]{3,2,1,0:T(1,128)S(1)} %get-tuple-element.16), channel_id=1, source_target_pairs={{1,0},{3,2},{5,4},{7,6},{9,8},{11,10},{13,12},{15,14},{17,16},{19,... | collective-permute-start | bytes 940040 | tf_op jit(solution)/shard_map/ppermute | solution.py:22
  66.3 9.8 %collective-permute-start.11 = (f32[34,18,1,128]{3,2,1,0:T(1,128)S(1)}, f32[34,18,1,128]{3,2,1,0:T(1,128)S(1)}, u32[]{:S(2)}, u32[]{:S(2)}) collective-permute-start(f32[34,18,1,128]{3,2,1,0:T(1,128)S(1)} %get-tuple-element.17), channel_id=1, source_target_pairs={{0,1},{2,3},{4,5},{6,7},{8,9},{10,11},{12,13},{14,15},{16,17},{18,... | collective-permute-start | bytes 940040 | tf_op jit(solution)/shard_map/ppermute | solution.py:19
  81.5 5.4 %collective-permute-start.13 = (f32[1,16,8,128]{3,2,1,0:T(8,128)S(1)}, f32[1,16,8,128]{3,2,1,0:T(8,128)S(1)}, u32[]{:S(2)}, u32[]{:S(2)}) collective-permute-start(f32[1,16,8,128]{3,2,1,0:T(8,128)S(1)} %get-tuple-element.34), channel_id=1, source_target_pairs={{0,8},{8,16},{16,24},{1,9},{9,17},{17,25},{2,10},{10,18},{18,26},{... | collective-permute-start | bytes 196616 | tf_op jit(solution)/shard_map/ppermute | solution.py:19
  85.0 6.2 %collective-permute-start.12 = (f32[1,16,8,128]{3,2,1,0:T(8,128)S(1)}, f32[1,16,8,128]{3,2,1,0:T(8,128)S(1)}, u32[]{:S(2)}, u32[]{:S(2)}) collective-permute-start(f32[1,16,8,128]{3,2,1,0:T(8,128)S(1)} %get-tuple-element.35), channel_id=1, source_target_pairs={{8,0},{16,8},{24,16},{9,1},{17,9},{25,17},{10,2},{18,10},{26,18},{... | collective-permute-start | bytes 196616 | tf_op jit(solution)/shard_map/ppermute | solution.py:22
  91.1 4.5 collective-permute-start.15
  94.3 4.2 collective-permute-start.14
  99.3 9.3 %collective-permute-start.16 = (f32[34,18,1,128]{3,2,1,0:T(1,128)S(1)}, f32[34,18,1,128]{3,2,1,0:T(1,128)S(1)}, u32[]{:S(2)}, u32[]{:S(2)}) collective-permute-start(f32[34,18,1,128]{3,2,1,0:T(1,128)S(1)} %get-tuple-element.14), channel_id=1, source_target_pairs={{1,0},{3,2},{5,4},{7,6},{9,8},{11,10},{13,12},{15,14},{17,16},{19,... | collective-permute-start | bytes 940040 | tf_op jit(solution)/shard_map/ppermute | solution.py:22
  100.6 9.8 %collective-permute-start.17 = (f32[34,18,1,128]{3,2,1,0:T(1,128)S(1)}, f32[34,18,1,128]{3,2,1,0:T(1,128)S(1)}, u32[]{:S(2)}, u32[]{:S(2)}) collective-permute-start(f32[34,18,1,128]{3,2,1,0:T(1,128)S(1)} %get-tuple-element.15), channel_id=1, source_target_pairs={{0,1},{2,3},{4,5},{6,7},{8,9},{10,11},{12,13},{14,15},{16,17},{18,... | collective-permute-start | bytes 940040 | tf_op jit(solution)/shard_map/ppermute | solution.py:19
  115.7 3.8 collective-permute-start.19
  117.6 6.2 %collective-permute-start.18 = (f32[1,16,8,128]{3,2,1,0:T(8,128)S(1)}, f32[1,16,8,128]{3,2,1,0:T(8,128)S(1)}, u32[]{:S(2)}, u32[]{:S(2)}) collective-permute-start(f32[1,16,8,128]{3,2,1,0:T(8,128)S(1)} %get-tuple-element.33), channel_id=1, source_target_pairs={{8,0},{16,8},{24,16},{9,1},{17,9},{25,17},{10,2},{18,10},{26,18},{... | collective-permute-start | bytes 196616 | tf_op jit(solution)/shard_map/ppermute | solution.py:22
  123.8 4.5 collective-permute-start.21
  127.0 4.2 collective-permute-start.20
  131.9 9.3 %collective-permute-start.22 = (f32[34,18,1,128]{3,2,1,0:T(1,128)S(1)}, f32[34,18,1,128]{3,2,1,0:T(1,128)S(1)}, u32[]{:S(2)}, u32[]{:S(2)}) collective-permute-start(f32[34,18,1,128]{3,2,1,0:T(1,128)S(1)} %get-tuple-element.12), channel_id=1, source_target_pairs={{1,0},{3,2},{5,4},{7,6},{9,8},{11,10},{13,12},{15,14},{17,16},{19,... | collective-permute-start | bytes 940040 | tf_op jit(solution)/shard_map/ppermute | solution.py:22
  133.2 9.8 %collective-permute-start.23 = (f32[34,18,1,128]{3,2,1,0:T(1,128)S(1)}, f32[34,18,1,128]{3,2,1,0:T(1,128)S(1)}, u32[]{:S(2)}, u32[]{:S(2)}) collective-permute-start(f32[34,18,1,128]{3,2,1,0:T(1,128)S(1)} %get-tuple-element.13), channel_id=1, source_target_pairs={{0,1},{2,3},{4,5},{6,7},{8,9},{10,11},{12,13},{14,15},{16,17},{18,... | collective-permute-start | bytes 940040 | tf_op jit(solution)/shard_map/ppermute | solution.py:19
  152.4 302.0 %all-reduce.5.cloned.1.call-start = ((), (), s32[]{:S(2)}) async-start(), calls=%async_computation.1 | async-start | bytes 131072 | tf_op jit(solution)/shard_map/psum | solution.py:83
  298.0 6.6 %collective-permute-start.25 = (f32[1,16,8,128]{3,2,1,0:T(8,128)S(1)}, f32[1,16,8,128]{3,2,1,0:T(8,128)S(1)}, u32[]{:S(2)}, u32[]{:S(2)}) collective-permute-start(f32[1,16,8,128]{3,2,1,0:T(8,128)S(1)} %get-tuple-element.30), channel_id=1, source_target_pairs={{0,8},{8,16},{16,24},{1,9},{9,17},{17,25},{2,10},{10,18},{18,26},{... | collective-permute-start | bytes 196616 | tf_op jit(solution)/shard_map/ppermute | solution.py:19
  302.6 6.2 %collective-permute-start.24 = (f32[1,16,8,128]{3,2,1,0:T(8,128)S(1)}, f32[1,16,8,128]{3,2,1,0:T(8,128)S(1)}, u32[]{:S(2)}, u32[]{:S(2)}) collective-permute-start(f32[1,16,8,128]{3,2,1,0:T(8,128)S(1)} %get-tuple-element.31), channel_id=1, source_target_pairs={{8,0},{16,8},{24,16},{9,1},{17,9},{25,17},{10,2},{18,10},{26,18},{... | collective-permute-start | bytes 196616 | tf_op jit(solution)/shard_map/ppermute | solution.py:22
  308.8 2.6 collective-permute-start.27
  310.1 4.9 %collective-permute-start.26 = (f32[34,1,8,128]{3,2,1,0:T(8,128)S(1)}, f32[34,1,8,128]{3,2,1,0:T(8,128)S(1)}, u32[]{:S(2)}, u32[]{:S(2)}) collective-permute-start(f32[34,1,8,128]{3,2,1,0:T(8,128)S(1)} %get-tuple-element.21), channel_id=1, source_target_pairs={{2,0},{4,2},{6,4},{3,1},{5,3},{7,5},{10,8},{12,10},{14,12},{11,9},... | collective-permute-start | bytes 417800 | tf_op jit(solution)/shard_map/ppermute | solution.py:22
  315.8 9.5 %collective-permute-start.28 = (f32[34,18,1,128]{3,2,1,0:T(1,128)S(1)}, f32[34,18,1,128]{3,2,1,0:T(1,128)S(1)}, u32[]{:S(2)}, u32[]{:S(2)}) collective-permute-start(f32[34,18,1,128]{3,2,1,0:T(1,128)S(1)} %get-tuple-element.10), channel_id=1, source_target_pairs={{1,0},{3,2},{5,4},{7,6},{9,8},{11,10},{13,12},{15,14},{17,16},{19,... | collective-permute-start | bytes 940040 | tf_op jit(solution)/shard_map/ppermute | solution.py:22
  317.1 9.9 %collective-permute-start.29 = (f32[34,18,1,128]{3,2,1,0:T(1,128)S(1)}, f32[34,18,1,128]{3,2,1,0:T(1,128)S(1)}, u32[]{:S(2)}, u32[]{:S(2)}) collective-permute-start(f32[34,18,1,128]{3,2,1,0:T(1,128)S(1)} %get-tuple-element.11), channel_id=1, source_target_pairs={{0,1},{2,3},{4,5},{6,7},{8,9},{10,11},{12,13},{14,15},{16,17},{18,... | collective-permute-start | bytes 940040 | tf_op jit(solution)/shard_map/ppermute | solution.py:19
  (2 other events, 53.9 us)
Sparse Core Ops, SparseCore 0:
  152.5 117.8 all-reduce.2
  336.3 118.1 all-reduce.4
where the time goes:
time: 465 us; the launch traced here: 463 us
  waiting for transfers between devices  302 us (65%)
  starting transfers between devices  74 us (16%)
  other arithmetic  59.1 us (13%)
  between operations  14.5 us (3%)
  matrix products  10.4 us (2%)
    psum x1, waiting for transfers between devices, on_device(): projected = lax.psum(quadratic(basis, sroot) / cells, ('gx', 'gy', 'gz'))  118 us
    psum x1, waiting for transfers between devices, on_device(): gram = lax.psum(inner(current, current) / cells, ('gx', 'gy', 'gz'))  118 us
    ppermute x15, starting transfers between devices, extended(): lax.ppermute(lax.slice_in_dim(block, block.shape[dim] - width, None, axis...  54.6 us
    ppermute x15, waiting for transfers between devices, extended(): lax.ppermute(lax.slice_in_dim(block, 0, width, axis=dim), axis, backward)  53.7 us
    mul x5, other arithmetic, operator(): scaled = sroot * vectors  20 us
    ppermute x15, starting transfers between devices, extended(): lax.ppermute(lax.slice_in_dim(block, 0, width, axis=dim), axis, backward)  19.4 us
    another operation x3, other arithmetic, lower_inverse(): lower = jnp.linalg.cholesky(gram)  12.4 us
    ppermute x15, waiting for transfers between devices, extended(): lax.ppermute(lax.slice_in_dim(block, block.shape[dim] - width, None, axis...  11.8 us
  transfers between devices with their start and end apart: 32, of which 27 were waited for; matrix products, arithmetic and copies ran while one was open for 0% of the time, Pallas kernels for 0%

commit v1 on v0

--- a/solution.py
+++ b/solution.py
@@ -44,11 +44,14 @@
     return sroot * (6.0 * scaled - neighbours(padded)) / 6.0
 
 
-def quadratic(vectors, sroot):
-    scaled = sroot * vectors
-    padded = extended(scaled, (("gx", 0), ("gy", 1), ("gz", 2)), 1)
-    image = sroot * (6.0 * scaled - neighbours(padded)) / 6.0
-    return inner(vectors, image)
+def total(value, axes):
+    for axis in axes:
+        count = lax.axis_size(axis)
+        bit = 1
+        while bit < count:
+            value = value + lax.ppermute(value, axis, [(i, i ^ bit) for i in range(count)])
+            bit *= 2
+    return value
 
 
 def lower_inverse(gram):
@@ -77,10 +80,13 @@
         previous, current = (current, following)
     width = current.shape[-1]
     flat = current.reshape(-1, width)
-    gram = lax.psum(inner(current, current) / cells, ("gx", "gy", "gz"))
+    image = operator(current, sroot)
+    local = jnp.concatenate([inner(current, current), inner(current, image)], axis=0)
+    summed = total(local, ("gy", "gz", "gx")) / cells
+    gram, raw = summed[:width], summed[width:]
     inverse = lower_inverse(gram)
     basis = jnp.dot(flat, inverse.T, precision=HIGH).reshape(current.shape)
-    projected = lax.psum(quadratic(basis, sroot) / cells, ("gx", "gy", "gz"))
+    projected = jnp.dot(jnp.dot(inverse, raw, precision=HIGH), inverse.T, precision=HIGH)
     return (basis, projected)
 
 

time: 465 us -> 225 us (0.48)
  waiting for transfers between devices: 302 us -> 87 us
  other arithmetic: 59.1 us -> 42.7 us
  between operations: 14.5 us -> 1.14 us
    psum x2 -> x0, waiting for transfers between devices: 236 us -> none  [the longest x1 118 us: on_device(): projected = lax.psum(quadratic(basis, sroot) / cells, ('gx', 'gy', 'gz'))]
    ppermute x0 -> x5, waiting for transfers between devices: none -> 21.6 us  [total(): lax.ppermute(value, axis, [(i, i ^ bit) for i in range(count)])]
    ppermute x0 -> x5, starting transfers between devices: none -> 5.44 us  [total(): lax.ppermute(value, axis, [(i, i ^ bit) for i in range(count)])]
    sub x1 -> x0, other arithmetic: 5.26 us -> none  [on_device(): 2.0 * (operator(current, sroot) - center_value * current) / half_value]
    div x1, other arithmetic: 4.9 us -> 0.02 us  [on_device(): summed = total(local, ('gy', 'gz', 'gx')) / cells]
    mul x5 -> x6, other arithmetic: 20 us -> 19 us  [operator(): scaled = sroot * vectors]
  transfers between devices with their start and end apart: 32 -> 35, of which waited for: 27 -> 30; matrix products, arithmetic and copies ran while one was open for 0% -> 2% of each run, Pallas kernels for 0% -> 0%
where the time goes in v1:
time: 225 us; the launch traced here: 224 us
  waiting for transfers between devices  87 us (39%)
  starting transfers between devices  78.5 us (35%)
  other arithmetic  42.7 us (19%)
  matrix products  14.4 us (6%)
    ppermute x15, starting transfers between devices, extended(): lax.ppermute(lax.slice_in_dim(block, block.shape[dim] - width, None, axis...  53.7 us
    ppermute x15, waiting for transfers between devices, extended(): lax.ppermute(lax.slice_in_dim(block, 0, width, axis=dim), axis, backward)  53.7 us
    ppermute x5, waiting for transfers between devices, total(): lax.ppermute(value, axis, [(i, i ^ bit) for i in range(count)])  21.6 us
    ppermute x15, starting transfers between devices, extended(): lax.ppermute(lax.slice_in_dim(block, 0, width, axis=dim), axis, backward)  19.4 us
    mul x6, other arithmetic, operator(): scaled = sroot * vectors  19 us
    another operation x3, other arithmetic, lower_inverse(): lower = jnp.linalg.cholesky(gram)  12.6 us
    ppermute x15, waiting for transfers between devices, extended(): lax.ppermute(lax.slice_in_dim(block, block.shape[dim] - width, None, axis...  11.7 us
    another operation x2, other arithmetic, lower_inverse(): lax.linalg.triangular_solve(lower, jnp.eye(gram.shape[0], dtype=gram.dtyp...  10.5 us
  transfers between devices with their start and end apart: 35, of which 30 were waited for; matrix products, arithmetic and copies ran while one was open for 2% of the time, Pallas kernels for 0%

profile of v1, /device:TPU:0, one launch (start us, length us, event | category | flops | bytes accessed | tf_op | source)
XLA Modules:
  0.0 224.3 jit_solution(4409650163214813970)
XLA Ops:
  4.6 4.9 %collective-permute-start.1 = (f32[1,16,8,128]{3,0,2,1:T(1,128)S(1)}, f32[1,16,8,128]{3,0,2,1:T(1,128)S(1)}, u32[]{:S(2)}, u32[]{:S(2)}) collective-permute-start(f32[1,16,8,128]{3,0,2,1:T(1,128)S(1)} %get-tuple-element.38), channel_id=1, source_target_pairs={{0,8},{8,16},{16,24},{1,9},{9,17},{17,25},{2,10},{10,18},{18,26},{... | collective-permute-start | bytes 196616 | tf_op jit(solution)/shard_map/ppermute | solution.py:19
  11.4 4.3 %collective-permute-done = f32[1,16,8,128]{3,0,2,1:T(1,128)S(1)} collective-permute-done((f32[1,16,8,128]{3,0,2,1:T(1,128)S(1)}, f32[1,16,8,128]{3,0,2,1:T(1,128)S(1)}, u32[]{:S(2)}, u32[]{:S(2)}) %collective-permute-start) | collective-permute-done | bytes 65568 | tf_op jit(solution)/shard_map/ppermute | solution.py:22
  18.5 3.7 %collective-permute-done.2 = f32[34,1,8,128]{3,0,2,1:T(8,128)S(1)} collective-permute-done((f32[34,1,8,128]{3,0,2,1:T(8,128)S(1)}, f32[34,1,8,128]{3,0,2,1:T(8,128)S(1)}, u32[]{:S(2)}, u32[]{:S(2)}) %collective-permute-start.2) | collective-permute-done | bytes 139296 | tf_op jit(solution)/shard_map/ppermute | solution.py:22
  23.6 4.6 %collective-permute-start.5 = (f32[34,18,1,128]{3,0,2,1:T(8,128)S(1)}, f32[34,18,1,128]{3,0,2,1:T(8,128)S(1)}, u32[]{:S(2)}, u32[]{:S(2)}) collective-permute-start(f32[34,18,1,128]{3,0,2,1:T(8,128)S(1)} %get-tuple-element.19), channel_id=1, source_target_pairs={{0,1},{2,3},{4,5},{6,7},{8,9},{10,11},{12,13},{14,15},{16,17},{18,... | collective-permute-start | bytes 940040 | tf_op jit(solution)/shard_map/ppermute | solution.py:19
  28.2 4.5 %collective-permute-done.4 = f32[34,18,1,128]{3,0,2,1:T(8,128)S(1)} collective-permute-done((f32[34,18,1,128]{3,0,2,1:T(8,128)S(1)}, f32[34,18,1,128]{3,0,2,1:T(8,128)S(1)}, u32[]{:S(2)}, u32[]{:S(2)}) %collective-permute-start.4) | collective-permute-done | bytes 313376 | tf_op jit(solution)/shard_map/ppermute | solution.py:22
  34.5 4.1 %broadcast_multiply_fusion = (f32[32,16,8,128]{3,0,2,1:T(8,128)S(1)}, f32[32,16,8,128]{3,0,2,1:T(8,128)S(1)}) fusion(f32[32,16,8]{0,2,1:T(8,128)S(1)} %get-tuple-element.40, f32[32,16,8,128]{3,2,1,0:T(8,128)S(1)} %copy-done, f32[34,1,8,128]{3,0,2,1:T(8,128)S(1)} %collective-permute-done.2, f32[1,16,8,128]{3,0,2,1:T(1,128)S(1)} %collective-permute-done, ...), kind=kLoop, calls=%fused_computation.153 | loop fusion | flops 15728640 | bytes 9457664 | tf_op jit(solution)/shard_map/mul | solution.py:42
  38.7 3.5 %collective-permute-start.7 = (f32[1,16,8,128]{3,0,2,1:T(1,128)S(1)}, f32[1,16,8,128]{3,0,2,1:T(1,128)S(1)}, u32[]{:S(2)}, u32[]{:S(2)}) collective-permute-start(f32[1,16,8,128]{3,0,2,1:T(1,128)S(1)} %get-tuple-element.36), channel_id=1, source_target_pairs={{0,8},{8,16},{16,24},{1,9},{9,17},{17,25},{2,10},{10,18},{18,26},{... | collective-permute-start | bytes 196616 | tf_op jit(solution)/shard_map/ppermute | solution.py:19
  44.1 4.3 %collective-permute-done.6 = f32[1,16,8,128]{3,0,2,1:T(1,128)S(1)} collective-permute-done((f32[1,16,8,128]{3,0,2,1:T(1,128)S(1)}, f32[1,16,8,128]{3,0,2,1:T(1,128)S(1)}, u32[]{:S(2)}, u32[]{:S(2)}) %collective-permute-start.6) | collective-permute-done | bytes 65568 | tf_op jit(solution)/shard_map/ppermute | solution.py:22
  56.9 4.6 %collective-permute-start.11 = (f32[34,18,1,128]{3,0,2,1:T(8,128)S(1)}, f32[34,18,1,128]{3,0,2,1:T(8,128)S(1)}, u32[]{:S(2)}, u32[]{:S(2)}) collective-permute-start(f32[34,18,1,128]{3,0,2,1:T(8,128)S(1)} %get-tuple-element.17), channel_id=1, source_target_pairs={{0,1},{2,3},{4,5},{6,7},{8,9},{10,11},{12,13},{14,15},{16,17},{18,... | collective-permute-start | bytes 940040 | tf_op jit(solution)/shard_map/ppermute | solution.py:19
  61.5 4.4 %collective-permute-done.10 = f32[34,18,1,128]{3,0,2,1:T(8,128)S(1)} collective-permute-done((f32[34,18,1,128]{3,0,2,1:T(8,128)S(1)}, f32[34,18,1,128]{3,0,2,1:T(8,128)S(1)}, u32[]{:S(2)}, u32[]{:S(2)}) %collective-permute-start.10) | collective-permute-done | bytes 313376 | tf_op jit(solution)/shard_map/ppermute | solution.py:22
  67.6 4.1 %broadcast_multiply_fusion.3 = (f32[32,16,8,128]{3,0,2,1:T(8,128)S(1)}, f32[32,16,8,128]{3,0,2,1:T(8,128)S(1)}) fusion(f32[32,16,8]{0,2,1:T(8,128)S(1)} %get-tuple-element.41, f32[32,16,8,128]{3,2,1,0:T(8,128)S(1)} %copy-done, f32[32,16,8,128]{3,0,2,1:T(8,128)S(1)} %get-tuple-element.9, f32[34,1,8,128]{3,0,2,1:T(8,128)S(1)} %collective-permute-done.8, ...), kind=kLoop, calls=%fused_computation.159 | loop fusion | flops 16777216 | bytes 11538432 | tf_op jit(solution)/shard_map/mul | solution.py:42
  71.9 3.5 %collective-permute-start.13 = (f32[1,16,8,128]{3,0,2,1:T(1,128)S(1)}, f32[1,16,8,128]{3,0,2,1:T(1,128)S(1)}, u32[]{:S(2)}, u32[]{:S(2)}) collective-permute-start(f32[1,16,8,128]{3,0,2,1:T(1,128)S(1)} %get-tuple-element.34), channel_id=1, source_target_pairs={{0,8},{8,16},{16,24},{1,9},{9,17},{17,25},{2,10},{10,18},{18,26},{... | collective-permute-start | bytes 196616 | tf_op jit(solution)/shard_map/ppermute | solution.py:19
  77.2 4.3 %collective-permute-done.12 = f32[1,16,8,128]{3,0,2,1:T(1,128)S(1)} collective-permute-done((f32[1,16,8,128]{3,0,2,1:T(1,128)S(1)}, f32[1,16,8,128]{3,0,2,1:T(1,128)S(1)}, u32[]{:S(2)}, u32[]{:S(2)}) %collective-permute-start.12) | collective-permute-done | bytes 65568 | tf_op jit(solution)/shard_map/ppermute | solution.py:22
  81.5 3.4 %collective-permute-start.15 = (f32[34,1,8,128]{3,0,2,1:T(8,128)S(1)}, f32[34,1,8,128]{3,0,2,1:T(8,128)S(1)}, u32[]{:S(2)}, u32[]{:S(2)}) collective-permute-start(f32[34,1,8,128]{3,0,2,1:T(8,128)S(1)} %get-tuple-element.24), channel_id=1, source_target_pairs={{0,2},{2,4},{4,6},{1,3},{3,5},{5,7},{8,10},{10,12},{12,14},{9,11},... | collective-permute-start | bytes 417800 | tf_op jit(solution)/shard_map/ppermute | solution.py:19
  90.2 4.6 %collective-permute-start.17 = (f32[34,18,1,128]{3,0,2,1:T(8,128)S(1)}, f32[34,18,1,128]{3,0,2,1:T(8,128)S(1)}, u32[]{:S(2)}, u32[]{:S(2)}) collective-permute-start(f32[34,18,1,128]{3,0,2,1:T(8,128)S(1)} %get-tuple-element.15), channel_id=1, source_target_pairs={{0,1},{2,3},{4,5},{6,7},{8,9},{10,11},{12,13},{14,15},{16,17},{18,... | collective-permute-start | bytes 940040 | tf_op jit(solution)/shard_map/ppermute | solution.py:19
  94.8 4.4 %collective-permute-done.16 = f32[34,18,1,128]{3,0,2,1:T(8,128)S(1)} collective-permute-done((f32[34,18,1,128]{3,0,2,1:T(8,128)S(1)}, f32[34,18,1,128]{3,0,2,1:T(8,128)S(1)}, u32[]{:S(2)}, u32[]{:S(2)}) %collective-permute-start.16) | collective-permute-done | bytes 313376 | tf_op jit(solution)/shard_map/ppermute | solution.py:22
  100.9 3.5 %broadcast_multiply_fusion.2 = (f32[32,16,8,128]{3,0,2,1:T(8,128)S(1)}, f32[32,16,8,128]{3,0,2,1:T(8,128)S(1)}) fusion(f32[32,16,8]{0,2,1:T(8,128)S(1)} %get-tuple-element.41, f32[32,16,8,128]{3,0,2,1:T(8,128)S(1)} %get-tuple-element.9, f32[32,16,8,128]{3,0,2,1:T(8,128)S(1)} %get-tuple-element.7, f32[34,1,8,128]{3,0,2,1:T(8,128)S(1)} %collective-permute-done.14, ...), kind=kLoop, calls=%fused_computation.158 | loop fusion | flops 17301504 | bytes 11538432 | tf_op jit(solution)/shard_map/mul | solution.py:42
  108.3 4.3 %collective-permute-done.18 = f32[1,16,8,128]{3,0,2,1:T(1,128)S(1)} collective-permute-done((f32[1,16,8,128]{3,0,2,1:T(1,128)S(1)}, f32[1,16,8,128]{3,0,2,1:T(1,128)S(1)}, u32[]{:S(2)}, u32[]{:S(2)}) %collective-permute-start.18) | collective-permute-done | bytes 65568 | tf_op jit(solution)/shard_map/ppermute | solution.py:22
  112.6 3.4 %collective-permute-start.21 = (f32[34,1,8,128]{3,0,2,1:T(8,128)S(1)}, f32[34,1,8,128]{3,0,2,1:T(8,128)S(1)}, u32[]{:S(2)}, u32[]{:S(2)}) collective-permute-start(f32[34,1,8,128]{3,0,2,1:T(8,128)S(1)} %get-tuple-element.22), channel_id=1, source_target_pairs={{0,2},{2,4},{4,6},{1,3},{3,5},{5,7},{8,10},{10,12},{12,14},{9,11},... | collective-permute-start | bytes 417800 | tf_op jit(solution)/shard_map/ppermute | solution.py:19
  121.2 4.6 %collective-permute-start.23 = (f32[34,18,1,128]{3,0,2,1:T(8,128)S(1)}, f32[34,18,1,128]{3,0,2,1:T(8,128)S(1)}, u32[]{:S(2)}, u32[]{:S(2)}) collective-permute-start(f32[34,18,1,128]{3,0,2,1:T(8,128)S(1)} %get-tuple-element.13), channel_id=1, source_target_pairs={{0,1},{2,3},{4,5},{6,7},{8,9},{10,11},{12,13},{14,15},{16,17},{18,... | collective-permute-start | bytes 940040 | tf_op jit(solution)/shard_map/ppermute | solution.py:19
  125.8 4.4 %collective-permute-done.22 = f32[34,18,1,128]{3,0,2,1:T(8,128)S(1)} collective-permute-done((f32[34,18,1,128]{3,0,2,1:T(8,128)S(1)}, f32[34,18,1,128]{3,0,2,1:T(8,128)S(1)}, u32[]{:S(2)}, u32[]{:S(2)}) %collective-permute-start.22) | collective-permute-done | bytes 313376 | tf_op jit(solution)/shard_map/ppermute | solution.py:22
  132.0 3.4 %broadcast_multiply_fusion.1 = (f32[32,16,8,128]{3,0,2,1:T(8,128)S(1)}, f32[32,16,8,128]{3,0,2,1:T(8,128)S(1)}) fusion(f32[32,16,8]{0,2,1:T(8,128)S(1)} %get-tuple-element.41, f32[32,16,8,128]{3,0,2,1:T(8,128)S(1)} %get-tuple-element.7, f32[32,16,8,128]{3,0,2,1:T(8,128)S(1)} %get-tuple-element.5, f32[34,1,8,128]{3,0,2,1:T(8,128)S(1)} %collective-permute-done.20, ...), kind=kLoop, calls=%fused_computation.157 | loop fusion | flops 16777216 | bytes 11538432 | tf_op jit(solution)/shard_map/mul | solution.py:42
  139.3 4.3 %collective-permute-done.24 = f32[1,16,8,128]{3,0,2,1:T(1,128)S(1)} collective-permute-done((f32[1,16,8,128]{3,0,2,1:T(1,128)S(1)}, f32[1,16,8,128]{3,0,2,1:T(1,128)S(1)}, u32[]{:S(2)}, u32[]{:S(2)}) %collective-permute-start.24) | collective-permute-done | bytes 65568 | tf_op jit(solution)/shard_map/ppermute | solution.py:22
  152.3 4.8 %collective-permute-start.29 = (f32[34,18,1,128]{3,0,2,1:T(8,128)S(1)}, f32[34,18,1,128]{3,0,2,1:T(8,128)S(1)}, u32[]{:S(2)}, u32[]{:S(2)}) collective-permute-start(f32[34,18,1,128]{3,0,2,1:T(8,128)S(1)} %get-tuple-element.11), channel_id=1, source_target_pairs={{0,1},{2,3},{4,5},{6,7},{8,9},{10,11},{12,13},{14,15},{16,17},{18,... | collective-permute-start | bytes 940040 | tf_op jit(solution)/shard_map/ppermute | solution.py:19
  157.1 3.5 %convolution_bitcast_fusion = f32[128,128]{0,1:T(8,128)S(1)} fusion(f32[32,16,8,128]{3,0,2,1:T(8,128)S(1)} %get-tuple-element.3), kind=kOutput, calls=%fused_computation.152 | convolution fusion | flops 805306368 | bytes 2162688 | tf_op jit(solution)/shard_map/ck,cl->kl/dot_general | solution.py:36
  163.0 4.9 %fusion.65 = f32[128,128]{0,1:T(8,128)S(1)} fusion(f32[32,16,8,128]{3,0,2,1:T(8,128)S(1)} %get-tuple-element.3, f32[34,18,1,128]{3,0,2,1:T(8,128)S(1)} %collective-permute-done.29, f32[34,1,8,128]{3,0,2,1:T(8,128)S(1)} %collective-permute-done.26, f32[34,1,8,128]{3,0,2,1:T(8,128)S(1)} %collective-permute-done.27, ...), kind=kOutput, calls=%fused_computation.151 | convolution fusion | flops 819462144 | bytes 5312512 | tf_op jit(solution)/shard_map/ck,cl->kl/dot_general | solution.py:36
  172.0 5.8 %collective-permute-done.31 = f32[256,128]{0,1:T(8,128)S(1)} collective-permute-done((f32[256,128]{0,1:T(8,128)S(1)}, f32[256,128]{0,1:T(8,128)S(1)}, u32[]{:S(2)}, u32[]{:S(2)}) %collective-permute-start.31) | collective-permute-done | bytes 131104 | tf_op jit(solution)/shard_map/ppermute | solution.py:52
  183.3 5.0 %collective-permute-done.33 = f32[256,128]{0,1:T(8,128)S(1)} collective-permute-done((f32[256,128]{0,1:T(8,128)S(1)}, f32[256,128]{0,1:T(8,128)S(1)}, u32[]{:S(2)}, u32[]{:S(2)}) %collective-permute-start.33) | collective-permute-done | bytes 131104 | tf_op jit(solution)/shard_map/ppermute | solution.py:52
  188.4 6.7 %collective-permute-done.34 = f32[256,128]{0,1:T(8,128)S(1)} collective-permute-done((f32[256,128]{0,1:T(8,128)S(1)}, f32[256,128]{0,1:T(8,128)S(1)}, u32[]{:S(2)}, u32[]{:S(2)}) %collective-permute-start.34) | collective-permute-done | bytes 131104 | tf_op jit(solution)/shard_map/ppermute | solution.py:52
  195.2 11.9 %cholesky.17 = f32[128,128]{1,0:T(8,128)S(1)} custom-call(f32[128,128]{1,0:T(8,128)S(1)} %fusion.77), custom_call_target="Cholesky" | custom-call | tf_op jit(solution)/shard_map/jit(cholesky)/cholesky | solution.py:58
  208.5 9.8 %custom-call.6 = f32[1,128,128]{1,2,0:T(8,128)S(1)} custom-call(f32[1,128,128]{2,1,0:T(8,128)S(1)} %fusion.71), custom_call_target="InvertDiagBlocksLowerTriangular" | custom-call | tf_op jit(solution)/shard_map/triangular_solve | solution.py:59
  218.8 4.6 %fusion.62 = f32[32,16,8,128]{3,2,1,0:T(8,128)} fusion(f32[32,16,8,128]{3,0,2,1:T(8,128)S(1)} %get-tuple-element.3, f32[128,128]{1,0:T(8,128)S(1)} %fusion.75), kind=kOutput, calls=%fused_computation.147 | convolution fusion | flops 805306368 | bytes 4259840 | tf_op jit(solution)/shard_map/dot_general | solution.py:88
  (81 shorter events, 71.4 us)
Async XLA Ops:
  4.6 6.8 %collective-permute-start.1 = (f32[1,16,8,128]{3,0,2,1:T(1,128)S(1)}, f32[1,16,8,128]{3,0,2,1:T(1,128)S(1)}, u32[]{:S(2)}, u32[]{:S(2)}) collective-permute-start(f32[1,16,8,128]{3,0,2,1:T(1,128)S(1)} %get-tuple-element.38), channel_id=1, source_target_pairs={{0,8},{8,16},{16,24},{1,9},{9,17},{17,25},{2,10},{10,18},{18,26},{... | collective-permute-start | bytes 196616 | tf_op jit(solution)/shard_map/ppermute | solution.py:19
  9.5 6.2 %collective-permute-start = (f32[1,16,8,128]{3,0,2,1:T(1,128)S(1)}, f32[1,16,8,128]{3,0,2,1:T(1,128)S(1)}, u32[]{:S(2)}, u32[]{:S(2)}) collective-permute-start(f32[1,16,8,128]{3,0,2,1:T(1,128)S(1)} %get-tuple-element.39), channel_id=1, source_target_pairs={{8,0},{16,8},{24,16},{9,1},{17,9},{25,17},{10,2},{18,10},{26,18},{... | collective-permute-start | bytes 196616 | tf_op jit(solution)/shard_map/ppermute | solution.py:22
  17.2 5.0 %collective-permute-start.2 = (f32[34,1,8,128]{3,0,2,1:T(8,128)S(1)}, f32[34,1,8,128]{3,0,2,1:T(8,128)S(1)}, u32[]{:S(2)}, u32[]{:S(2)}) collective-permute-start(f32[34,1,8,128]{3,0,2,1:T(8,128)S(1)} %get-tuple-element.29), channel_id=1, source_target_pairs={{2,0},{4,2},{6,4},{3,1},{5,3},{7,5},{10,8},{12,10},{14,12},{11,9},... | collective-permute-start | bytes 417800 | tf_op jit(solution)/shard_map/ppermute | solution.py:22
  22.3 10.4 %collective-permute-start.4 = (f32[34,18,1,128]{3,0,2,1:T(8,128)S(1)}, f32[34,18,1,128]{3,0,2,1:T(8,128)S(1)}, u32[]{:S(2)}, u32[]{:S(2)}) collective-permute-start(f32[34,18,1,128]{3,0,2,1:T(8,128)S(1)} %get-tuple-element.18), channel_id=1, source_target_pairs={{1,0},{3,2},{5,4},{7,6},{9,8},{11,10},{13,12},{15,14},{17,16},{19,... | collective-permute-start | bytes 940040 | tf_op jit(solution)/shard_map/ppermute | solution.py:22
  23.6 10.9 %collective-permute-start.5 = (f32[34,18,1,128]{3,0,2,1:T(8,128)S(1)}, f32[34,18,1,128]{3,0,2,1:T(8,128)S(1)}, u32[]{:S(2)}, u32[]{:S(2)}) collective-permute-start(f32[34,18,1,128]{3,0,2,1:T(8,128)S(1)} %get-tuple-element.19), channel_id=1, source_target_pairs={{0,1},{2,3},{4,5},{6,7},{8,9},{10,11},{12,13},{14,15},{16,17},{18,... | collective-permute-start | bytes 940040 | tf_op jit(solution)/shard_map/ppermute | solution.py:19
  38.7 5.4 %collective-permute-start.7 = (f32[1,16,8,128]{3,0,2,1:T(1,128)S(1)}, f32[1,16,8,128]{3,0,2,1:T(1,128)S(1)}, u32[]{:S(2)}, u32[]{:S(2)}) collective-permute-start(f32[1,16,8,128]{3,0,2,1:T(1,128)S(1)} %get-tuple-element.36), channel_id=1, source_target_pairs={{0,8},{8,16},{16,24},{1,9},{9,17},{17,25},{2,10},{10,18},{18,26},{... | collective-permute-start | bytes 196616 | tf_op jit(solution)/shard_map/ppermute | solution.py:19
  42.2 6.2 %collective-permute-start.6 = (f32[1,16,8,128]{3,0,2,1:T(1,128)S(1)}, f32[1,16,8,128]{3,0,2,1:T(1,128)S(1)}, u32[]{:S(2)}, u32[]{:S(2)}) collective-permute-start(f32[1,16,8,128]{3,0,2,1:T(1,128)S(1)} %get-tuple-element.37), channel_id=1, source_target_pairs={{8,0},{16,8},{24,16},{9,1},{17,9},{25,17},{10,2},{18,10},{26,18},{... | collective-permute-start | bytes 196616 | tf_op jit(solution)/shard_map/ppermute | solution.py:22
  48.4 4.6 %collective-permute-start.9 = (f32[34,1,8,128]{3,0,2,1:T(8,128)S(1)}, f32[34,1,8,128]{3,0,2,1:T(8,128)S(1)}, u32[]{:S(2)}, u32[]{:S(2)}) collective-permute-start(f32[34,1,8,128]{3,0,2,1:T(8,128)S(1)} %get-tuple-element.26), channel_id=1, source_target_pairs={{0,2},{2,4},{4,6},{1,3},{3,5},{5,7},{8,10},{10,12},{12,14},{9,11},... | collective-permute-start | bytes 417800 | tf_op jit(solution)/shard_map/ppermute | solution.py:19
  51.7 3.8 %collective-permute-start.8 = (f32[34,1,8,128]{3,0,2,1:T(8,128)S(1)}, f32[34,1,8,128]{3,0,2,1:T(8,128)S(1)}, u32[]{:S(2)}, u32[]{:S(2)}) collective-permute-start(f32[34,1,8,128]{3,0,2,1:T(8,128)S(1)} %get-tuple-element.27), channel_id=1, source_target_pairs={{2,0},{4,2},{6,4},{3,1},{5,3},{7,5},{10,8},{12,10},{14,12},{11,9},... | collective-permute-start | bytes 417800 | tf_op jit(solution)/shard_map/ppermute | solution.py:22
  55.6 10.3 %collective-permute-start.10 = (f32[34,18,1,128]{3,0,2,1:T(8,128)S(1)}, f32[34,18,1,128]{3,0,2,1:T(8,128)S(1)}, u32[]{:S(2)}, u32[]{:S(2)}) collective-permute-start(f32[34,18,1,128]{3,0,2,1:T(8,128)S(1)} %get-tuple-element.16), channel_id=1, source_target_pairs={{1,0},{3,2},{5,4},{7,6},{9,8},{11,10},{13,12},{15,14},{17,16},{19,... | collective-permute-start | bytes 940040 | tf_op jit(solution)/shard_map/ppermute | solution.py:22
  56.9 10.7 %collective-permute-start.11 = (f32[34,18,1,128]{3,0,2,1:T(8,128)S(1)}, f32[34,18,1,128]{3,0,2,1:T(8,128)S(1)}, u32[]{:S(2)}, u32[]{:S(2)}) collective-permute-start(f32[34,18,1,128]{3,0,2,1:T(8,128)S(1)} %get-tuple-element.17), channel_id=1, source_target_pairs={{0,1},{2,3},{4,5},{6,7},{8,9},{10,11},{12,13},{14,15},{16,17},{18,... | collective-permute-start | bytes 940040 | tf_op jit(solution)/shard_map/ppermute | solution.py:19
  71.9 5.4 %collective-permute-start.13 = (f32[1,16,8,128]{3,0,2,1:T(1,128)S(1)}, f32[1,16,8,128]{3,0,2,1:T(1,128)S(1)}, u32[]{:S(2)}, u32[]{:S(2)}) collective-permute-start(f32[1,16,8,128]{3,0,2,1:T(1,128)S(1)} %get-tuple-element.34), channel_id=1, source_target_pairs={{0,8},{8,16},{16,24},{1,9},{9,17},{17,25},{2,10},{10,18},{18,26},{... | collective-permute-start | bytes 196616 | tf_op jit(solution)/shard_map/ppermute | solution.py:19
  75.3 6.2 %collective-permute-start.12 = (f32[1,16,8,128]{3,0,2,1:T(1,128)S(1)}, f32[1,16,8,128]{3,0,2,1:T(1,128)S(1)}, u32[]{:S(2)}, u32[]{:S(2)}) collective-permute-start(f32[1,16,8,128]{3,0,2,1:T(1,128)S(1)} %get-tuple-element.35), channel_id=1, source_target_pairs={{8,0},{16,8},{24,16},{9,1},{17,9},{25,17},{10,2},{18,10},{26,18},{... | collective-permute-start | bytes 196616 | tf_op jit(solution)/shard_map/ppermute | solution.py:22
  81.5 4.7 %collective-permute-start.15 = (f32[34,1,8,128]{3,0,2,1:T(8,128)S(1)}, f32[34,1,8,128]{3,0,2,1:T(8,128)S(1)}, u32[]{:S(2)}, u32[]{:S(2)}) collective-permute-start(f32[34,1,8,128]{3,0,2,1:T(8,128)S(1)} %get-tuple-element.24), channel_id=1, source_target_pairs={{0,2},{2,4},{4,6},{1,3},{3,5},{5,7},{8,10},{10,12},{12,14},{9,11},... | collective-permute-start | bytes 417800 | tf_op jit(solution)/shard_map/ppermute | solution.py:19
  84.9 3.8 %collective-permute-start.14 = (f32[34,1,8,128]{3,0,2,1:T(8,128)S(1)}, f32[34,1,8,128]{3,0,2,1:T(8,128)S(1)}, u32[]{:S(2)}, u32[]{:S(2)}) collective-permute-start(f32[34,1,8,128]{3,0,2,1:T(8,128)S(1)} %get-tuple-element.25), channel_id=1, source_target_pairs={{2,0},{4,2},{6,4},{3,1},{5,3},{7,5},{10,8},{12,10},{14,12},{11,9},... | collective-permute-start | bytes 417800 | tf_op jit(solution)/shard_map/ppermute | solution.py:22
  88.9 10.3 %collective-permute-start.16 = (f32[34,18,1,128]{3,0,2,1:T(8,128)S(1)}, f32[34,18,1,128]{3,0,2,1:T(8,128)S(1)}, u32[]{:S(2)}, u32[]{:S(2)}) collective-permute-start(f32[34,18,1,128]{3,0,2,1:T(8,128)S(1)} %get-tuple-element.14), channel_id=1, source_target_pairs={{1,0},{3,2},{5,4},{7,6},{9,8},{11,10},{13,12},{15,14},{17,16},{19,... | collective-permute-start | bytes 940040 | tf_op jit(solution)/shard_map/ppermute | solution.py:22
  90.2 10.7 %collective-permute-start.17 = (f32[34,18,1,128]{3,0,2,1:T(8,128)S(1)}, f32[34,18,1,128]{3,0,2,1:T(8,128)S(1)}, u32[]{:S(2)}, u32[]{:S(2)}) collective-permute-start(f32[34,18,1,128]{3,0,2,1:T(8,128)S(1)} %get-tuple-element.15), channel_id=1, source_target_pairs={{0,1},{2,3},{4,5},{6,7},{8,9},{10,11},{12,13},{14,15},{16,17},{18,... | collective-permute-start | bytes 940040 | tf_op jit(solution)/shard_map/ppermute | solution.py:19
  106.4 6.2 %collective-permute-start.18 = (f32[1,16,8,128]{3,0,2,1:T(1,128)S(1)}, f32[1,16,8,128]{3,0,2,1:T(1,128)S(1)}, u32[]{:S(2)}, u32[]{:S(2)}) collective-permute-start(f32[1,16,8,128]{3,0,2,1:T(1,128)S(1)} %get-tuple-element.33), channel_id=1, source_target_pairs={{8,0},{16,8},{24,16},{9,1},{17,9},{25,17},{10,2},{18,10},{26,18},{... | collective-permute-start | bytes 196616 | tf_op jit(solution)/shard_map/ppermute | solution.py:22
  112.6 4.7 %collective-permute-start.21 = (f32[34,1,8,128]{3,0,2,1:T(8,128)S(1)}, f32[34,1,8,128]{3,0,2,1:T(8,128)S(1)}, u32[]{:S(2)}, u32[]{:S(2)}) collective-permute-start(f32[34,1,8,128]{3,0,2,1:T(8,128)S(1)} %get-tuple-element.22), channel_id=1, source_target_pairs={{0,2},{2,4},{4,6},{1,3},{3,5},{5,7},{8,10},{10,12},{12,14},{9,11},... | collective-permute-start | bytes 417800 | tf_op jit(solution)/shard_map/ppermute | solution.py:19
  116.0 3.8 %collective-permute-start.20 = (f32[34,1,8,128]{3,0,2,1:T(8,128)S(1)}, f32[34,1,8,128]{3,0,2,1:T(8,128)S(1)}, u32[]{:S(2)}, u32[]{:S(2)}) collective-permute-start(f32[34,1,8,128]{3,0,2,1:T(8,128)S(1)} %get-tuple-element.23), channel_id=1, source_target_pairs={{2,0},{4,2},{6,4},{3,1},{5,3},{7,5},{10,8},{12,10},{14,12},{11,9},... | collective-permute-start | bytes 417800 | tf_op jit(solution)/shard_map/ppermute | solution.py:22
  119.9 10.3 %collective-permute-start.22 = (f32[34,18,1,128]{3,0,2,1:T(8,128)S(1)}, f32[34,18,1,128]{3,0,2,1:T(8,128)S(1)}, u32[]{:S(2)}, u32[]{:S(2)}) collective-permute-start(f32[34,18,1,128]{3,0,2,1:T(8,128)S(1)} %get-tuple-element.12), channel_id=1, source_target_pairs={{1,0},{3,2},{5,4},{7,6},{9,8},{11,10},{13,12},{15,14},{17,16},{19,... | collective-permute-start | bytes 940040 | tf_op jit(solution)/shard_map/ppermute | solution.py:22
  121.2 10.7 %collective-permute-start.23 = (f32[34,18,1,128]{3,0,2,1:T(8,128)S(1)}, f32[34,18,1,128]{3,0,2,1:T(8,128)S(1)}, u32[]{:S(2)}, u32[]{:S(2)}) collective-permute-start(f32[34,18,1,128]{3,0,2,1:T(8,128)S(1)} %get-tuple-element.13), channel_id=1, source_target_pairs={{0,1},{2,3},{4,5},{6,7},{8,9},{10,11},{12,13},{14,15},{16,17},{18,... | collective-permute-start | bytes 940040 | tf_op jit(solution)/shard_map/ppermute | solution.py:19
  137.5 6.2 %collective-permute-start.24 = (f32[1,16,8,128]{3,0,2,1:T(1,128)S(1)}, f32[1,16,8,128]{3,0,2,1:T(1,128)S(1)}, u32[]{:S(2)}, u32[]{:S(2)}) collective-permute-start(f32[1,16,8,128]{3,0,2,1:T(1,128)S(1)} %get-tuple-element.31), channel_id=1, source_target_pairs={{8,0},{16,8},{24,16},{9,1},{17,9},{25,17},{10,2},{18,10},{26,18},{... | collective-permute-start | bytes 196616 | tf_op jit(solution)/shard_map/ppermute | solution.py:22
  143.7 4.7 %collective-permute-start.27 = (f32[34,1,8,128]{3,0,2,1:T(8,128)S(1)}, f32[34,1,8,128]{3,0,2,1:T(8,128)S(1)}, u32[]{:S(2)}, u32[]{:S(2)}) collective-permute-start(f32[34,1,8,128]{3,0,2,1:T(8,128)S(1)} %get-tuple-element.20), channel_id=1, source_target_pairs={{0,2},{2,4},{4,6},{1,3},{3,5},{5,7},{8,10},{10,12},{12,14},{9,11},... | collective-permute-start | bytes 417800 | tf_op jit(solution)/shard_map/ppermute | solution.py:19
  147.1 3.8 %collective-permute-start.26 = (f32[34,1,8,128]{3,0,2,1:T(8,128)S(1)}, f32[34,1,8,128]{3,0,2,1:T(8,128)S(1)}, u32[]{:S(2)}, u32[]{:S(2)}) collective-permute-start(f32[34,1,8,128]{3,0,2,1:T(8,128)S(1)} %get-tuple-element.21), channel_id=1, source_target_pairs={{2,0},{4,2},{6,4},{3,1},{5,3},{7,5},{10,8},{12,10},{14,12},{11,9},... | collective-permute-start | bytes 417800 | tf_op jit(solution)/shard_map/ppermute | solution.py:22
  151.0 10.3 %collective-permute-start.28 = (f32[34,18,1,128]{3,0,2,1:T(8,128)S(1)}, f32[34,18,1,128]{3,0,2,1:T(8,128)S(1)}, u32[]{:S(2)}, u32[]{:S(2)}) collective-permute-start(f32[34,18,1,128]{3,0,2,1:T(8,128)S(1)} %get-tuple-element.10), channel_id=1, source_target_pairs={{1,0},{3,2},{5,4},{7,6},{9,8},{11,10},{13,12},{15,14},{17,16},{19,... | collective-permute-start | bytes 940040 | tf_op jit(solution)/shard_map/ppermute | solution.py:22
  152.3 10.7 %collective-permute-start.29 = (f32[34,18,1,128]{3,0,2,1:T(8,128)S(1)}, f32[34,18,1,128]{3,0,2,1:T(8,128)S(1)}, u32[]{:S(2)}, u32[]{:S(2)}) collective-permute-start(f32[34,18,1,128]{3,0,2,1:T(8,128)S(1)} %get-tuple-element.11), channel_id=1, source_target_pairs={{0,1},{2,3},{4,5},{6,7},{8,9},{10,11},{12,13},{14,15},{16,17},{18,... | collective-permute-start | bytes 940040 | tf_op jit(solution)/shard_map/ppermute | solution.py:19
  167.9 4.0 %collective-permute-start.30 = (f32[256,128]{0,1:T(8,128)S(1)}, f32[256,128]{0,1:T(8,128)S(1)}, u32[]{:S(2)}, u32[]{:S(2)}) collective-permute-start(f32[256,128]{0,1:T(8,128)S(1)} %pad_maximum_fusion.143), channel_id=1, source_target_pairs={{0,2},{2,0},{4,6},{6,4},{1,3},{3,1},{5,7},{7,5},{8,10},{10,8},{12,... | collective-permute-start | bytes 393224 | tf_op jit(solution)/shard_map/ppermute | solution.py:52
  171.9 5.8 %collective-permute-start.31 = (f32[256,128]{0,1:T(8,128)S(1)}, f32[256,128]{0,1:T(8,128)S(1)}, u32[]{:S(2)}, u32[]{:S(2)}) collective-permute-start(f32[256,128]{0,1:T(8,128)S(1)} %fusion.81), channel_id=1, source_target_pairs={{0,4},{2,6},{4,0},{6,2},{1,5},{3,7},{5,1},{7,3},{8,12},{10,14},{12... | collective-permute-start | bytes 393224 | tf_op jit(solution)/shard_map/ppermute | solution.py:52
  177.7 5.5 %collective-permute-start.32 = (f32[256,128]{0,1:T(8,128)S(1)}, f32[256,128]{0,1:T(8,128)S(1)}, u32[]{:S(2)}, u32[]{:S(2)}) collective-permute-start(f32[256,128]{0,1:T(8,128)S(1)} %add.127), channel_id=1, source_target_pairs={{0,1},{1,0},{2,3},{3,2},{4,5},{5,4},{6,7},{7,6},{8,9},{9,8},{10,11... | collective-permute-start | bytes 393224 | tf_op jit(solution)/shard_map/ppermute | solution.py:52
  183.2 5.0 %collective-permute-start.33 = (f32[256,128]{0,1:T(8,128)S(1)}, f32[256,128]{0,1:T(8,128)S(1)}, u32[]{:S(2)}, u32[]{:S(2)}) collective-permute-start(f32[256,128]{0,1:T(8,128)S(1)} %add.128), channel_id=1, source_target_pairs={{0,8},{8,0},{16,24},{24,16},{1,9},{9,1},{17,25},{25,17},{2,10},{10... | collective-permute-start | bytes 393224 | tf_op jit(solution)/shard_map/ppermute | solution.py:52
  188.3 6.8 %collective-permute-start.34 = (f32[256,128]{0,1:T(8,128)S(1)}, f32[256,128]{0,1:T(8,128)S(1)}, u32[]{:S(2)}, u32[]{:S(2)}) collective-permute-start(f32[256,128]{0,1:T(8,128)S(1)} %add.129), channel_id=1, source_target_pairs={{0,16},{8,24},{16,0},{24,8},{1,17},{9,25},{17,1},{25,9},{2,18},{10... | collective-permute-start | bytes 393224 | tf_op jit(solution)/shard_map/ppermute | solution.py:52
  (4 other events, 29.1 us)

commit v2 on v1

v2 whole, which is shorter than its diff:
```python
import functools
import jax
import jax.numpy as jnp
from jax import lax
from jax.experimental import pallas as pl
from jax.experimental.pallas import tpu as pltpu
from jax.sharding import PartitionSpec as P

DEG = 4

HIGH = lax.Precision.HIGHEST
center_value = 3.25
half_value = 2.75
VMEM = pl.BlockSpec(memory_space=pltpu.VMEM)
SMEM = pl.BlockSpec(memory_space=pltpu.SMEM)
BF = jnp.bfloat16


def call(body, outs, ins, flops, aliases=None):
    moved = sum(4 * a.size for a in list(outs) + list(ins))
    return pl.pallas_call(
        body,
        out_shape=outs,
        in_specs=[SMEM] + [VMEM] * (len(ins) - 1),
        out_specs=tuple(VMEM for _ in outs),
        input_output_aliases=aliases or {},
        compiler_params=pltpu.CompilerParams(vmem_limit_bytes=32 * 1024 * 1024),
        cost_estimate=pl.CostEstimate(flops=flops, bytes_accessed=moved, transcendentals=0),
    )(*ins)


def f32(rows, width):
    return jax.ShapeDtypeStruct((rows, width), jnp.float32)


class Shape:
    def __init__(self, shape):
        self.x, self.y, self.z, self.k = shape
        self.row = self.y * self.z
        self.cells = self.x * self.row


def faces_of(s, at, w_ref, out, x):
    for i in range(out["nz"]):
        out["z"][i][pl.ds(x * s.y, s.y), :] = w_ref[
            pl.ds(x * s.row + at[4 + i], s.y, stride=s.z), :
        ]
    for i in range(2):
        out["y"][i][pl.ds(x * s.z, s.z), :] = w_ref[pl.ds(x * s.row + at[2 + i] * s.z, s.z), :]


def x_faces(s, at, w_ref, out):
    for i in range(2):
        out["x"][i][...] = w_ref[pl.ds(at[i] * s.row, s.row), :]


def face_shapes(s, nz):
    return (
        [f32(s.row, s.k)] * 2 + [f32(s.x * s.z, s.k)] * 2 + [f32(s.x * s.y, s.k)] * nz
    )


def split_faces(refs, nz):
    return {"x": refs[0:2], "y": refs[2:4], "z": refs[4 : 4 + nz], "nz": nz}


def prepare(block, wide, at, s, nz):
    def body(at_ref, b_ref, k_ref, w_ref, *faces):
        out = split_faces(faces, nz)

        def step(x, _):
            here = pl.ds(pl.multiple_of(x * s.row, s.row), s.row)
            w_ref[here, :] = jnp.sqrt(k_ref[here, :]) * b_ref[here, :]
            faces_of(s, at_ref, w_ref, out, x)
            return 0

        lax.fori_loop(0, s.x, step, 0)
        x_faces(s, at_ref, w_ref, out)

    outs = [f32(s.cells, s.k)] + face_shapes(s, nz)
    return call(body, outs, [at, block, wide], 4 * s.cells * s.k)


def around(s, w_ref, x, low, high, emit):
    base = pl.multiple_of(x * s.row, s.row)
    place = lax.broadcasted_iota(jnp.int32, (s.z, s.k), 0)
    tiles = [w_ref[pl.ds(base + y * s.z, s.z), :] for y in range(s.y)]
    for y in range(s.y):
        c = tiles[y]
        up = jnp.where(place == s.z - 1, 0.0, pltpu.roll(c, s.z - 1, 0))
        down = jnp.where(place == 0, 0.0, pltpu.roll(c, 1, 0))
        near = up + down
        if y > 0:
            near = near + tiles[y - 1]
        if y < s.y - 1:
            near = near + tiles[y + 1]
        if low:
            near = near + w_ref[pl.ds(base - s.row + y * s.z, s.z), :]
        if high:
            near = near + w_ref[pl.ds(base + s.row + y * s.z, s.z), :]
        emit(pl.ds(base + y * s.z, s.z), c, near)


def sweep(s, w_ref, emit):
    around(s, w_ref, 0, False, True, emit)

    def step(x, _):
        around(s, w_ref, x, True, True, emit)
        return 0

    lax.fori_loop(1, s.x - 1, step, 0)
    around(s, w_ref, s.x - 1, True, False, emit)


def interior(w, before, wide, at, s):
    scale = (1.0 if before is None else 2.0) / half_value

    def body(at_ref, w_ref, k_ref, *rest):
        o_ref = rest[-1]

        def emit(here, c, near):
            new = k_ref[here, :] * ((c - near * (1.0 / 6.0)) * scale) - (scale * center_value) * c
            if before is not None:
                new = new - rest[0][here, :]
            o_ref[here, :] = new

        sweep(s, w_ref, emit)

    ins = [at, w, wide] + ([] if before is None else [before])
    return call(body, [f32(s.cells, s.k)], ins, 12 * s.cells * s.k)[0]


def finish(part, wide, ghosts, at, s, nz, scale):
    def body(at_ref, p_ref, k_ref, *refs):
        ghost = split_faces(refs[: 4 + nz], nz)
        w_ref = refs[4 + nz]
        out = split_faces(refs[5 + nz :], nz)
        factor = scale / 6.0
        for i in range(2):
            here = pl.ds(at_ref[i] * s.row, s.row)
            p_ref[here, :] = p_ref[here, :] - (k_ref[here, :] * factor) * ghost["x"][i][...]
        place = lax.broadcasted_iota(jnp.int32, (s.z, s.k), 0)

        def step(x, _):
            base = pl.multiple_of(x * s.row, s.row)
            for i in range(2):
                here = pl.ds(base + at_ref[2 + i] * s.z, s.z)
                g = ghost["y"][i][pl.ds(x * s.z, s.z), :]
                p_ref[here, :] = p_ref[here, :] - (k_ref[here, :] * factor) * g
            for y in range(s.y):
                here = pl.ds(base + y * s.z, s.z)
                add = 0.0
                for i in range(nz):
                    g = ghost["z"][i][pl.ds(x * s.y + y, 1), :]
                    add = jnp.where(place == at_ref[4 + i], jnp.broadcast_to(g, (s.z, s.k)), add)
                w_ref[here, :] = p_ref[here, :] - (k_ref[here, :] * factor) * add
            faces_of(s, at_ref, w_ref, out, x)
            return 0

        lax.fori_loop(0, s.x, step, 0)
        x_faces(s, at_ref, w_ref, out)

    outs = [f32(s.cells, s.k)] + face_shapes(s, nz)
    return call(body, outs, [at, part, wide] + list(ghosts), 4 * s.cells * s.k, {1: 0})


def exchange(faces, axes):
    got = []
    for face, (axis, first) in zip(faces, axes):
        count = lax.axis_size(axis)
        pairs = []
        for i in range(first, count - 1, 2):
            pairs += [(i, i + 1), (i + 1, i)]
        got.append(lax.ppermute(face, axis, pairs))
    return got


def transposed_dot(left, right):
    return lax.dot_general(
        left, right, (((0,), (0,)), ((), ())), preferred_element_type=jnp.float32
    )


def two(value):
    high = value.astype(BF)
    low = (value - high.astype(jnp.float32)).astype(BF)
    return jnp.concatenate([high, low], axis=1)


def both(left, right):
    k = left.shape[1] // 2
    full = transposed_dot(left, right)
    return full[:k, :k] + (full[:k, k:] + full[k:, :k]) + full[k:, k:]


def gather_terms(w, wide, at, s):
    rows = 4 * s.row

    def body(at_ref, w_ref, k_ref, f_ref, g_ref, m_ref, q_ref):
        def emit(here, c, near):
            q_ref[here, :] = c - near * (1.0 / 6.0)

        sweep(s, w_ref, emit)
        g_ref[...] = jnp.zeros_like(g_ref)
        m_ref[...] = jnp.zeros_like(m_ref)

        def step(i, _):
            here = pl.ds(pl.multiple_of(i * rows, rows), rows)
            w = w_ref[here, :]
            f = w * lax.rsqrt(k_ref[here, :])
            f_ref[here, :] = f
            pair = two(f)
            g_ref[...] += both(pair, pair)
            m_ref[...] += both(two(w), two(q_ref[here, :]))
            return 0

        lax.fori_loop(0, s.cells // rows, step, 0)

    outs = [f32(s.cells, s.k), f32(s.k, s.k), f32(s.k, s.k)]
    moved = 4 * 4 * s.cells * s.k
    return pl.pallas_call(
        body,
        out_shape=outs,
        in_specs=[SMEM, VMEM, VMEM],
        out_specs=(VMEM, VMEM, VMEM),
        scratch_shapes=[pltpu.VMEM((s.cells, s.k), jnp.float32)],
        compiler_params=pltpu.CompilerParams(vmem_limit_bytes=32 * 1024 * 1024),
        cost_estimate=pl.CostEstimate(
            flops=16 * s.cells * s.k * s.k, bytes_accessed=moved, transcendentals=0
        ),
    )(at, w, wide)


def pack_terms(gram, own, faces, ghosts, at, s, cells):
    k = s.k

    def body(at_ref, g_ref, m_ref, *refs):
        n = len(faces)
        m = jnp.zeros((k, k), jnp.float32)
        for left, right in zip(refs[:n], refs[n : 2 * n]):
            m += both(two(left[...]), two(right[...]))
        m = m_ref[...] - m * (1.0 / 6.0)
        raw = (m + m.T) * (0.5 / cells)
        below = lax.broadcasted_iota(jnp.int32, (k, k), 0)
        along = lax.broadcasted_iota(jnp.int32, (k, k), 1)
        refs[-1][:k, :] = jnp.where(below >= along, g_ref[...] * (1.0 / cells), raw)
        diagonal = jnp.sum(jnp.where(below == along, raw, 0.0), axis=0, keepdims=True)
        refs[-1][k:, :] = jnp.broadcast_to(diagonal, (8, k))

    ins = [at, gram, own] + list(faces) + list(ghosts)
    return call(body, [f32(k + 8, k)], ins, 6 * s.cells * k)[0]


def total(value, axes):
    for axis in axes:
        count = lax.axis_size(axis)
        bit = 1
        while bit < count:
            value = value + lax.ppermute(value, axis, [(i, i ^ bit) for i in range(count)])
            bit *= 2
    return value


def lower_inverse(gram):
    lower = jnp.linalg.cholesky(gram)
    return lax.linalg.triangular_solve(
        lower, jnp.eye(gram.shape[0], dtype=gram.dtype), left_side=True, lower=True
    )


def on_device(block, conductivity):
    s = Shape(block.shape)
    sizes = [lax.axis_size(a) for a in ("gx", "gy", "gz")]
    nz = 1 if sizes[2] == 2 else 2
    cells = float(s.cells * sizes[0] * sizes[1] * sizes[2])
    odd = [lax.rem(lax.axis_index(a), 2) for a in ("gx", "gy", "gz")]
    tops = (s.x - 1, s.y - 1, s.z - 1)
    at = jnp.stack(
        [jnp.where(odd[d] == first, tops[d], 0) for d in range(3) for first in range(2)]
    ).astype(jnp.int32)
    axes = [("gx", 0), ("gx", 1), ("gy", 0), ("gy", 1), ("gz", 0), ("gz", 1)][: 4 + nz]

    flat = block.reshape(s.cells, s.k)
    wide = jnp.broadcast_to(conductivity[..., None], block.shape).reshape(s.cells, s.k)
    w, *faces = prepare(flat, wide, at, s, nz)
    before = None
    for step in range(DEG):
        ghosts = exchange(faces, axes)
        part = interior(w, before, wide, at, s)
        scale = (1.0 if before is None else 2.0) / half_value
        before = w
        w, *faces = finish(part, wide, ghosts, at, s, nz, scale)
    ghosts = exchange(faces, axes)
    filtered, gram, own = gather_terms(w, wide, at, s)
    packed = total(pack_terms(gram, own, faces, ghosts, at, s, cells), ("gy", "gz", "gx"))
    upper, diagonal = packed[: s.k], packed[s.k]
    keep = jnp.tril(jnp.ones((s.k, s.k), bool))
    strict = jnp.tril(jnp.ones((s.k, s.k), bool), -1)
    gram = jnp.where(keep, upper, upper.T)
    raw = jnp.where(strict, upper.T, upper)
    raw = jnp.where(jnp.eye(s.k, dtype=bool), diagonal[None, :], raw)
    inverse = lower_inverse(gram)
    basis = jnp.dot(filtered, inverse.T, precision=HIGH).reshape(block.shape)
    projected = jnp.dot(jnp.dot(inverse, raw, precision=HIGH), inverse.T, precision=HIGH)
    return (basis, projected)


def solution(mesh):
    return jax.shard_map(
        on_device,
        mesh=mesh,
        in_specs=(P("gx", "gy", "gz", None), P("gx", "gy", "gz")),
        out_specs=(P("gx", "gy", "gz", None), P()),
        check_vma=False,
    )
```

time: 225 us -> 116 us (0.52)
  waiting for transfers between devices: 87 us -> 16.1 us
  starting transfers between devices: 78.5 us -> 44.8 us
  Pallas kernels: 0 us -> 24.2 us
  other arithmetic: 42.7 us -> 22.9 us
  matrix products: 14.4 us -> 4.55 us
    ppermute x30 -> x25, waiting for transfers between devices: 65.4 us -> 2.17 us  [exchange(): got.append(lax.ppermute(face, axis, pairs))]
    ppermute x30 -> x25, starting transfers between devices: 73.1 us -> 36 us  [exchange(): got.append(lax.ppermute(face, axis, pairs))]
    pallas_call x0 -> x11, Pallas kernels: none -> 24.2 us  [the longest x10 19.7 us: call(): pl.pallas_call(body, out_shape=outs, in_specs=[SMEM] + [VMEM] * (len(ins)...]
    mul x6 -> x0, other arithmetic: 19 us -> none  [operator(): scaled = sroot * vectors]
    dot_general x3 -> x1, matrix products: 13 us -> 3.12 us  [on_device(): basis = jnp.dot(filtered, inverse.T, precision=HIGH).reshape(block.shape)]
    ppermute x5, waiting for transfers between devices: 21.6 us -> 13.9 us  [total(): lax.ppermute(value, axis, [(i, i ^ bit) for i in range(count)])]
    ppermute x5, starting transfers between devices: 5.44 us -> 8.83 us  [total(): lax.ppermute(value, axis, [(i, i ^ bit) for i in range(count)])]
  transfers between devices with their start and end apart: 35 -> 30, of which waited for: 30 -> 8; matrix products, arithmetic and copies ran while one was open for 2% -> 0% of each run, Pallas kernels for 0% -> 10%
where the time goes in v2:
time: 116 us
  starting transfers between devices  44.8 us (39%)
  Pallas kernels  24.2 us (21%)
  other arithmetic  22.9 us (20%)
  waiting for transfers between devices  16.1 us (14%)
  matrix products  4.55 us (4%)
  local copies, waits for them, and re-layouts  2.17 us (2%)
    ppermute x25, starting transfers between devices, exchange(): got.append(lax.ppermute(face, axis, pairs))  36 us
    pallas_call x10, Pallas kernels, call(): pl.pallas_call(body, out_shape=outs, in_specs=[SMEM] + [VMEM] * (len(ins)...  19.7 us
    ppermute x5, waiting for transfers between devices, total(): lax.ppermute(value, axis, [(i, i ^ bit) for i in range(count)])  13.9 us
    another operation x3, other arithmetic, lower_inverse(): lower = jnp.linalg.cholesky(gram)  12.4 us
    another operation x2, other arithmetic, lower_inverse(): lax.linalg.triangular_solve(lower, jnp.eye(gram.shape[0], dtype=gram.dtyp...  10.5 us
    ppermute x5, starting transfers between devices, total(): lax.ppermute(value, axis, [(i, i ^ bit) for i in range(count)])  8.83 us
    pallas_call x1, Pallas kernels, gather_terms(): pl.pallas_call(body, out_shape=outs, in_specs=[SMEM, VMEM, VMEM], out_spe...  4.49 us
    dot_general x1, matrix products, on_device(): basis = jnp.dot(filtered, inverse.T, precision=HIGH).reshape(block.shape)  3.12 us
  transfers between devices with their start and end apart: 30, of which 8 were waited for; matrix products, arithmetic and copies ran while one was open for 0% of the time, Pallas kernels for 10%

profile of v2, /device:TPU:0, one launch (start us, length us, event | category | flops | bytes accessed | tf_op | source)
XLA Modules:
  0.0 115.8 jit_solution(13983846551026818853)
XLA Ops:
  2.7 1.5 %shard_map.41 = (f32[4096,128]{1,0:T(8,128)S(1)}, f32[128,128]{1,0:T(8,128)S(1)}, f32[128,128]{1,0:T(8,128)S(1)}, f32[256,128]{1,0:T(8,128)S(1)}, f32[256,128]{1,0:T(8,128)S(1)}, /*index=5*/f32[512,128]{1,0:T(8,128)S(1)}) custom-call(s32[6]{0:T(128)S(1)} %stack.27.at_ref, f32[4096,128]{1,0:T(8,128)S(1)} %bitcast.30, f32[4096,128]{1,0:T(8,128)S(1)} %broadcast_in_dim.25.k_ref), custom_call_target="tpu_custom_call" | custom-call | flops 2097152 | bytes 6946840 | tf_op jit(solution)/shard_map/pallas_call | solution.py:21
  4.1 3.0 %collective-permute-start.4 = (f32[512,128]{1,0:T(8,128)S(1)}, f32[512,128]{1,0:T(8,128)S(1)}, u32[]{:S(2)}, u32[]{:S(2)}) collective-permute-start(f32[512,128]{1,0:T(8,128)S(1)} %get-tuple-element.40), channel_id=1, source_target_pairs={{0,1},{1,0},{2,3},{3,2},{4,5},{5,4},{6,7},{7,6},{8,9},{9,8},{10,11... | collective-permute-start | bytes 786440 | tf_op jit(solution)/shard_map/ppermute | solution.py:174
  7.8 1.6 %collective-permute-start = (f32[128,128]{1,0:T(8,128)S(1)}, f32[128,128]{1,0:T(8,128)S(1)}, u32[]{:S(2)}, u32[]{:S(2)}) collective-permute-start(f32[128,128]{1,0:T(8,128)S(1)} %get-tuple-element.36), channel_id=1, source_target_pairs={{0,8},{8,0},{16,24},{24,16},{1,9},{9,1},{17,25},{25,17},{2,10},{10... | collective-permute-start | bytes 196616 | tf_op jit(solution)/shard_map/ppermute | solution.py:174
  10.1 1.8 %shard_map.42.p_ref = f32[4096,128]{1,0:T(8,128)S(1)} custom-call(s32[6]{0:T(128)S(1)} %stack.27.at_ref, f32[4096,128]{1,0:T(8,128)S(1)} %get-tuple-element.35.w_ref.rest_0_, f32[4096,128]{1,0:T(8,128)S(1)} %broadcast_in_dim.25.k_ref), custom_call_target="tpu_custom_call" | custom-call | flops 6291456 | bytes 6291480 | tf_op jit(solution)/shard_map/pallas_call | solution.py:21
  12.2 1.3 %collective-permute-done.4.refs_4_ = f32[512,128]{1,0:T(8,128)S(1)} collective-permute-done((f32[512,128]{1,0:T(8,128)S(1)}, f32[512,128]{1,0:T(8,128)S(1)}, u32[]{:S(2)}, u32[]{:S(2)}) %collective-permute-start.4) | collective-permute-done | bytes 262176 | tf_op jit(solution)/shard_map/ppermute | solution.py:174
  13.4 2.5 %shard_map.43 = (f32[4096,128]{1,0:T(8,128)S(1)}, f32[128,128]{1,0:T(8,128)S(1)}, f32[128,128]{1,0:T(8,128)S(1)}, f32[256,128]{1,0:T(8,128)S(1)}, f32[256,128]{1,0:T(8,128)S(1)}, /*index=5*/f32[512,128]{1,0:T(8,128)S(1)}) custom-call(s32[6]{0:T(128)S(1)} %stack.27.at_ref, f32[4096,128]{1,0:T(8,128)S(1)} %shard_map.42.p_ref, ...), custom_call_target="tpu_custom_call", output_to_operand_aliasing={{0}: (1, {})} | custom-call | flops 2097152 | bytes 7602200 | tf_op jit(solution)/shard_map/pallas_call | solution.py:21
  15.9 1.8 %collective-permute-start.9 = (f32[512,128]{1,0:T(8,128)S(1)}, f32[512,128]{1,0:T(8,128)S(1)}, u32[]{:S(2)}, u32[]{:S(2)}) collective-permute-start(f32[512,128]{1,0:T(8,128)S(1)} %get-tuple-element.46), channel_id=1, source_target_pairs={{0,1},{1,0},{2,3},{3,2},{4,5},{5,4},{6,7},{7,6},{8,9},{9,8},{10,11... | collective-permute-start | bytes 786440 | tf_op jit(solution)/shard_map/ppermute | solution.py:174
  18.4 3.6 %collective-permute-start.5 = (f32[128,128]{1,0:T(8,128)S(1)}, f32[128,128]{1,0:T(8,128)S(1)}, u32[]{:S(2)}, u32[]{:S(2)}) collective-permute-start(f32[128,128]{1,0:T(8,128)S(1)} %get-tuple-element.42), channel_id=1, source_target_pairs={{0,8},{8,0},{16,24},{24,16},{1,9},{9,1},{17,25},{25,17},{2,10},{10... | collective-permute-start | bytes 196616 | tf_op jit(solution)/shard_map/ppermute | solution.py:174
  22.7 1.8 %shard_map.44.p_ref = f32[4096,128]{1,0:T(8,128)S(1)} custom-call(s32[6]{0:T(128)S(1)} %stack.27.at_ref, f32[4096,128]{1,0:T(8,128)S(1)} %get-tuple-element.41.w_ref.rest_0_, f32[4096,128]{1,0:T(8,128)S(1)} %broadcast_in_dim.25.k_ref, f32[4096,128]{1,0:T(8,128)S(1)} %get-tuple-element.35.w_ref.rest_0_), custom_call_target="tpu_custom_call" | custom-call | flops 6291456 | bytes 8388632 | tf_op jit(solution)/shard_map/pallas_call | solution.py:21
  25.2 2.5 %shard_map.45 = (f32[4096,128]{1,0:T(8,128)S(1)}, f32[128,128]{1,0:T(8,128)S(1)}, f32[128,128]{1,0:T(8,128)S(1)}, f32[256,128]{1,0:T(8,128)S(1)}, f32[256,128]{1,0:T(8,128)S(1)}, /*index=5*/f32[512,128]{1,0:T(8,128)S(1)}) custom-call(s32[6]{0:T(128)S(1)} %stack.27.at_ref, f32[4096,128]{1,0:T(8,128)S(1)} %shard_map.44.p_ref, ...), custom_call_target="tpu_custom_call", output_to_operand_aliasing={{0}: (1, {})} | custom-call | flops 2097152 | bytes 7602200 | tf_op jit(solution)/shard_map/pallas_call | solution.py:21
  28.6 2.6 %collective-permute-start.12 = (f32[256,128]{1,0:T(8,128)S(1)}, f32[256,128]{1,0:T(8,128)S(1)}, u32[]{:S(2)}, u32[]{:S(2)}) collective-permute-start(f32[256,128]{1,0:T(8,128)S(1)} %get-tuple-element.50), channel_id=1, source_target_pairs={{0,2},{2,0},{4,6},{6,4},{1,3},{3,1},{5,7},{7,5},{8,10},{10,8},{12,... | collective-permute-start | bytes 393224 | tf_op jit(solution)/shard_map/ppermute | solution.py:174
  31.9 3.3 %collective-permute-start.10 = (f32[128,128]{1,0:T(8,128)S(1)}, f32[128,128]{1,0:T(8,128)S(1)}, u32[]{:S(2)}, u32[]{:S(2)}) collective-permute-start(f32[128,128]{1,0:T(8,128)S(1)} %get-tuple-element.48), channel_id=1, source_target_pairs={{0,8},{8,0},{16,24},{24,16},{1,9},{9,1},{17,25},{25,17},{2,10},{10... | collective-permute-start | bytes 196616 | tf_op jit(solution)/shard_map/ppermute | solution.py:174
  35.9 1.8 %shard_map.46.p_ref = f32[4096,128]{1,0:T(8,128)S(1)} custom-call(s32[6]{0:T(128)S(1)} %stack.27.at_ref, f32[4096,128]{1,0:T(8,128)S(1)} %get-tuple-element.47.w_ref.rest_0_, f32[4096,128]{1,0:T(8,128)S(1)} %broadcast_in_dim.25.k_ref, f32[4096,128]{1,0:T(8,128)S(1)} %get-tuple-element.41.w_ref.rest_0_), custom_call_target="tpu_custom_call" | custom-call | flops 6291456 | bytes 8388632 | tf_op jit(solution)/shard_map/pallas_call | solution.py:21
  37.8 2.5 %shard_map.47 = (f32[4096,128]{1,0:T(8,128)S(1)}, f32[128,128]{1,0:T(8,128)S(1)}, f32[128,128]{1,0:T(8,128)S(1)}, f32[256,128]{1,0:T(8,128)S(1)}, f32[256,128]{1,0:T(8,128)S(1)}, /*index=5*/f32[512,128]{1,0:T(8,128)S(1)}) custom-call(s32[6]{0:T(128)S(1)} %stack.27.at_ref, f32[4096,128]{1,0:T(8,128)S(1)} %shard_map.46.p_ref, ...), custom_call_target="tpu_custom_call", output_to_operand_aliasing={{0}: (1, {})} | custom-call | flops 2097152 | bytes 7602200 | tf_op jit(solution)/shard_map/pallas_call | solution.py:21
  40.9 1.6 %collective-permute-start.17 = (f32[256,128]{1,0:T(8,128)S(1)}, f32[256,128]{1,0:T(8,128)S(1)}, u32[]{:S(2)}, u32[]{:S(2)}) collective-permute-start(f32[256,128]{1,0:T(8,128)S(1)} %get-tuple-element.56), channel_id=1, source_target_pairs={{0,2},{2,0},{4,6},{6,4},{1,3},{3,1},{5,7},{7,5},{8,10},{10,8},{12,... | collective-permute-start | bytes 393224 | tf_op jit(solution)/shard_map/ppermute | solution.py:174
  43.1 3.3 %collective-permute-start.15 = (f32[128,128]{1,0:T(8,128)S(1)}, f32[128,128]{1,0:T(8,128)S(1)}, u32[]{:S(2)}, u32[]{:S(2)}) collective-permute-start(f32[128,128]{1,0:T(8,128)S(1)} %get-tuple-element.54), channel_id=1, source_target_pairs={{0,8},{8,0},{16,24},{24,16},{1,9},{9,1},{17,25},{25,17},{2,10},{10... | collective-permute-start | bytes 196616 | tf_op jit(solution)/shard_map/ppermute | solution.py:174
  47.1 1.8 %shard_map.48.p_ref = f32[4096,128]{1,0:T(8,128)S(1)} custom-call(s32[6]{0:T(128)S(1)} %stack.27.at_ref, f32[4096,128]{1,0:T(8,128)S(1)} %get-tuple-element.53.w_ref, f32[4096,128]{1,0:T(8,128)S(1)} %broadcast_in_dim.25.k_ref, f32[4096,128]{1,0:T(8,128)S(1)} %get-tuple-element.47.w_ref.rest_0_), custom_call_target="tpu_custom_call" | custom-call | flops 6291456 | bytes 8388632 | tf_op jit(solution)/shard_map/pallas_call | solution.py:21
  49.0 2.5 %shard_map.49 = (f32[4096,128]{1,0:T(8,128)S(1)}, f32[128,128]{1,0:T(8,128)S(1)}, f32[128,128]{1,0:T(8,128)S(1)}, f32[256,128]{1,0:T(8,128)S(1)}, f32[256,128]{1,0:T(8,128)S(1)}, /*index=5*/f32[512,128]{1,0:T(8,128)S(1)}) custom-call(s32[6]{0:T(128)S(1)} %stack.27.at_ref, f32[4096,128]{1,0:T(8,128)S(1)} %shard_map.48.p_ref, ...), custom_call_target="tpu_custom_call", output_to_operand_aliasing={{0}: (1, {})} | custom-call | flops 2097152 | bytes 7602200 | tf_op jit(solution)/shard_map/pallas_call | solution.py:21
  51.5 1.6 %collective-permute-start.24 = (f32[512,128]{1,0:T(8,128)S(1)}, f32[512,128]{1,0:T(8,128)S(1)}, u32[]{:S(2)}, u32[]{:S(2)}) collective-permute-start(f32[512,128]{1,0:T(8,128)S(1)} %get-tuple-element.67.refs_4_), channel_id=1, source_target_pairs={{0,1},{1,0},{2,3},{3,2},{4,5},{5,4},{6,7},{7,6},{8,9},{9,8},{10,11... | collective-permute-start | bytes 786440 | tf_op jit(solution)/shard_map/ppermute | solution.py:174
  53.1 2.3 %collective-permute-start.22 = (f32[256,128]{1,0:T(8,128)S(1)}, f32[256,128]{1,0:T(8,128)S(1)}, u32[]{:S(2)}, u32[]{:S(2)}) collective-permute-start(f32[256,128]{1,0:T(8,128)S(1)} %get-tuple-element.65.refs_2_), channel_id=1, source_target_pairs={{0,2},{2,0},{4,6},{6,4},{1,3},{3,1},{5,7},{7,5},{8,10},{10,8},{12,... | collective-permute-start | bytes 393224 | tf_op jit(solution)/shard_map/ppermute | solution.py:174
  56.0 2.8 %collective-permute-start.20 = (f32[128,128]{1,0:T(8,128)S(1)}, f32[128,128]{1,0:T(8,128)S(1)}, u32[]{:S(2)}, u32[]{:S(2)}) collective-permute-start(f32[128,128]{1,0:T(8,128)S(1)} %get-tuple-element.63.refs_0_), channel_id=1, source_target_pairs={{0,8},{8,0},{16,24},{24,16},{1,9},{9,1},{17,25},{25,17},{2,10},{10... | collective-permute-start | bytes 196616 | tf_op jit(solution)/shard_map/ppermute | solution.py:174
  59.7 4.5 %shard_map.50 = (f32[4096,128]{1,0:T(8,128)S(1)}, f32[128,128]{1,0:T(8,128)S(1)}, f32[128,128]{1,0:T(8,128)S(1)}) custom-call(s32[6]{0:T(128)S(1)} %stack.27.at_ref, f32[4096,128]{1,0:T(8,128)S(1)} %get-tuple-element.59.w_ref, f32[4096,128]{1,0:T(8,128)S(1)} %broadcast_in_dim.25.k_ref), custom_call_target="tpu_custom_call" | custom-call | flops 1073741824 | bytes 8388608 | tf_op jit(solution)/shard_map/pallas_call | solution.py:221
  65.3 2.6 %collective-permute-start.25 = (f32[136,128]{1,0:T(8,128)S(1)}, f32[136,128]{1,0:T(8,128)S(1)}, u32[]{:S(2)}, u32[]{:S(2)}) collective-permute-start(f32[136,128]{1,0:T(8,128)S(1)} %shard_map.51), channel_id=1, source_target_pairs={{0,2},{2,0},{4,6},{6,4},{1,3},{3,1},{5,7},{7,5},{8,10},{10,8},{12,... | collective-permute-start | bytes 208904 | tf_op jit(solution)/shard_map/ppermute | solution.py:259
  69.5 3.8 %collective-permute-done.26 = f32[136,128]{1,0:T(8,128)S(1)} collective-permute-done((f32[136,128]{1,0:T(8,128)S(1)}, f32[136,128]{1,0:T(8,128)S(1)}, u32[]{:S(2)}, u32[]{:S(2)}) %collective-permute-start.26) | collective-permute-done | bytes 69664 | tf_op jit(solution)/shard_map/ppermute | solution.py:259
  73.9 3.8 %collective-permute-done.27 = f32[136,128]{1,0:T(8,128)S(1)} collective-permute-done((f32[136,128]{1,0:T(8,128)S(1)}, f32[136,128]{1,0:T(8,128)S(1)}, u32[]{:S(2)}, u32[]{:S(2)}) %collective-permute-start.27) | collective-permute-done | bytes 69664 | tf_op jit(solution)/shard_map/ppermute | solution.py:259
  77.7 2.8 %collective-permute-start.28 = (f32[136,128]{1,0:T(8,128)S(1)}, f32[136,128]{1,0:T(8,128)S(1)}, u32[]{:S(2)}, u32[]{:S(2)}) collective-permute-start(f32[136,128]{1,0:T(8,128)S(1)} %add.37), channel_id=1, source_target_pairs={{0,8},{8,0},{16,24},{24,16},{1,9},{9,1},{17,25},{25,17},{2,10},{10... | collective-permute-start | bytes 208904 | tf_op jit(solution)/shard_map/ppermute | solution.py:259
  80.5 2.3 %collective-permute-done.28 = f32[136,128]{1,0:T(8,128)S(1)} collective-permute-done((f32[136,128]{1,0:T(8,128)S(1)}, f32[136,128]{1,0:T(8,128)S(1)}, u32[]{:S(2)}, u32[]{:S(2)}) %collective-permute-start.28) | collective-permute-done | bytes 69664 | tf_op jit(solution)/shard_map/ppermute | solution.py:259
  82.8 2.1 %collective-permute-start.29 = (f32[136,128]{1,0:T(8,128)S(1)}, f32[136,128]{1,0:T(8,128)S(1)}, u32[]{:S(2)}, u32[]{:S(2)}) collective-permute-start(f32[136,128]{1,0:T(8,128)S(1)} %add.38), channel_id=1, source_target_pairs={{0,16},{8,24},{16,0},{24,8},{1,17},{9,25},{17,1},{25,9},{2,18},{10... | collective-permute-start | bytes 208904 | tf_op jit(solution)/shard_map/ppermute | solution.py:259
  84.9 3.2 %collective-permute-done.29 = f32[136,128]{1,0:T(8,128)S(1)} collective-permute-done((f32[136,128]{1,0:T(8,128)S(1)}, f32[136,128]{1,0:T(8,128)S(1)}, u32[]{:S(2)}, u32[]{:S(2)}) %collective-permute-start.29) | collective-permute-done | bytes 69664 | tf_op jit(solution)/shard_map/ppermute | solution.py:259
  88.4 11.7 %cholesky.18 = f32[128,128]{1,0:T(8,128)S(1)} custom-call(f32[128,128]{1,0:T(8,128)S(1)} %fusion.3), custom_call_target="Cholesky" | custom-call | tf_op jit(solution)/shard_map/jit(cholesky)/cholesky | solution.py:265
  101.4 9.8 %custom-call.6 = f32[1,128,128]{1,2,0:T(8,128)S(1)} custom-call(f32[1,128,128]{2,1,0:T(8,128)S(1)} %fusion), custom_call_target="InvertDiagBlocksLowerTriangular" | custom-call | tf_op jit(solution)/shard_map/triangular_solve | solution.py:266
  112.7 3.1 %fusion.10 = f32[4096,128]{1,0:T(8,128)} fusion(f32[4096,128]{1,0:T(8,128)S(1)} %get-tuple-element.60, f32[128,128]{1,0:T(8,128)S(1)} %fusion.1), kind=kOutput, calls=%fused_computation.20 | convolution fusion | flops 805306368 | bytes 4259840 | tf_op jit(solution)/shard_map/dot_general | solution.py:303
  (66 shorter events, 17.5 us)
Async XLA Ops:
  0.6 2.0 %copy-start = (f32[32,16,8,128]{3,2,1,0:T(8,128)S(1)}, f32[32,16,8,128]{3,2,1,0:T(8,128)}, u32[]{:S(2)}) copy-start(f32[32,16,8,128]{3,2,1,0:T(8,128)} %param.2) | copy-start | bytes 6291460
  4.1 9.3 %collective-permute-start.4 = (f32[512,128]{1,0:T(8,128)S(1)}, f32[512,128]{1,0:T(8,128)S(1)}, u32[]{:S(2)}, u32[]{:S(2)}) collective-permute-start(f32[512,128]{1,0:T(8,128)S(1)} %get-tuple-element.40), channel_id=1, source_target_pairs={{0,1},{1,0},{2,3},{3,2},{4,5},{5,4},{6,7},{7,6},{8,9},{9,8},{10,11... | collective-permute-start | bytes 786440 | tf_op jit(solution)/shard_map/ppermute | solution.py:174
  7.1 5.0 %collective-permute-start.2 = (f32[256,128]{1,0:T(8,128)S(1)}, f32[256,128]{1,0:T(8,128)S(1)}, u32[]{:S(2)}, u32[]{:S(2)}) collective-permute-start(f32[256,128]{1,0:T(8,128)S(1)} %get-tuple-element.38), channel_id=1, source_target_pairs={{0,2},{2,0},{4,6},{6,4},{1,3},{3,1},{5,7},{7,5},{8,10},{10,8},{12,... | collective-permute-start | bytes 393224 | tf_op jit(solution)/shard_map/ppermute | solution.py:174
  7.1 5.0 %collective-permute-start.3 = (f32[256,128]{1,0:T(8,128)S(1)}, f32[256,128]{1,0:T(8,128)S(1)}, u32[]{:S(2)}, u32[]{:S(2)}) collective-permute-start(f32[256,128]{1,0:T(8,128)S(1)} %get-tuple-element.39), channel_id=1, source_target_pairs={{2,4},{4,2},{3,5},{5,3},{10,12},{12,10},{11,13},{13,11},{18,20},{2... | collective-permute-start | bytes 393224 | tf_op jit(solution)/shard_map/ppermute | solution.py:174
  7.8 4.3 %collective-permute-start = (f32[128,128]{1,0:T(8,128)S(1)}, f32[128,128]{1,0:T(8,128)S(1)}, u32[]{:S(2)}, u32[]{:S(2)}) collective-permute-start(f32[128,128]{1,0:T(8,128)S(1)} %get-tuple-element.36), channel_id=1, source_target_pairs={{0,8},{8,0},{16,24},{24,16},{1,9},{9,1},{17,25},{25,17},{2,10},{10... | collective-permute-start | bytes 196616 | tf_op jit(solution)/shard_map/ppermute | solution.py:174
  9.5 2.7 %collective-permute-start.1 = (f32[128,128]{1,0:T(8,128)S(1)}, f32[128,128]{1,0:T(8,128)S(1)}, u32[]{:S(2)}, u32[]{:S(2)}) collective-permute-start(f32[128,128]{1,0:T(8,128)S(1)} %get-tuple-element.37), channel_id=1, source_target_pairs={{8,16},{16,8},{9,17},{17,9},{10,18},{18,10},{11,19},{19,11},{12,20... | collective-permute-start | bytes 196616 | tf_op jit(solution)/shard_map/ppermute | solution.py:174
  15.9 9.2 %collective-permute-start.9 = (f32[512,128]{1,0:T(8,128)S(1)}, f32[512,128]{1,0:T(8,128)S(1)}, u32[]{:S(2)}, u32[]{:S(2)}) collective-permute-start(f32[512,128]{1,0:T(8,128)S(1)} %get-tuple-element.46), channel_id=1, source_target_pairs={{0,1},{1,0},{2,3},{3,2},{4,5},{5,4},{6,7},{7,6},{8,9},{9,8},{10,11... | collective-permute-start | bytes 786440 | tf_op jit(solution)/shard_map/ppermute | solution.py:174
  17.7 6.8 %collective-permute-start.7 = (f32[256,128]{1,0:T(8,128)S(1)}, f32[256,128]{1,0:T(8,128)S(1)}, u32[]{:S(2)}, u32[]{:S(2)}) collective-permute-start(f32[256,128]{1,0:T(8,128)S(1)} %get-tuple-element.44), channel_id=1, source_target_pairs={{0,2},{2,0},{4,6},{6,4},{1,3},{3,1},{5,7},{7,5},{8,10},{10,8},{12,... | collective-permute-start | bytes 393224 | tf_op jit(solution)/shard_map/ppermute | solution.py:174
  17.7 6.9 %collective-permute-start.8 = (f32[256,128]{1,0:T(8,128)S(1)}, f32[256,128]{1,0:T(8,128)S(1)}, u32[]{:S(2)}, u32[]{:S(2)}) collective-permute-start(f32[256,128]{1,0:T(8,128)S(1)} %get-tuple-element.45), channel_id=1, source_target_pairs={{2,4},{4,2},{3,5},{5,3},{10,12},{12,10},{11,13},{13,11},{18,20},{2... | collective-permute-start | bytes 393224 | tf_op jit(solution)/shard_map/ppermute | solution.py:174
  18.4 6.2 %collective-permute-start.5 = (f32[128,128]{1,0:T(8,128)S(1)}, f32[128,128]{1,0:T(8,128)S(1)}, u32[]{:S(2)}, u32[]{:S(2)}) collective-permute-start(f32[128,128]{1,0:T(8,128)S(1)} %get-tuple-element.42), channel_id=1, source_target_pairs={{0,8},{8,0},{16,24},{24,16},{1,9},{9,1},{17,25},{25,17},{2,10},{10... | collective-permute-start | bytes 196616 | tf_op jit(solution)/shard_map/ppermute | solution.py:174
  22.0 2.5 %collective-permute-start.6 = (f32[128,128]{1,0:T(8,128)S(1)}, f32[128,128]{1,0:T(8,128)S(1)}, u32[]{:S(2)}, u32[]{:S(2)}) collective-permute-start(f32[128,128]{1,0:T(8,128)S(1)} %get-tuple-element.43), channel_id=1, source_target_pairs={{8,16},{16,8},{9,17},{17,9},{10,18},{18,10},{11,19},{19,11},{12,20... | collective-permute-start | bytes 196616 | tf_op jit(solution)/shard_map/ppermute | solution.py:174
  27.6 10.1 %collective-permute-start.14 = (f32[512,128]{1,0:T(8,128)S(1)}, f32[512,128]{1,0:T(8,128)S(1)}, u32[]{:S(2)}, u32[]{:S(2)}) collective-permute-start(f32[512,128]{1,0:T(8,128)S(1)} %get-tuple-element.52), channel_id=1, source_target_pairs={{0,1},{1,0},{2,3},{3,2},{4,5},{5,4},{6,7},{7,6},{8,9},{9,8},{10,11... | collective-permute-start | bytes 786440 | tf_op jit(solution)/shard_map/ppermute | solution.py:174
  28.6 9.1 %collective-permute-start.12 = (f32[256,128]{1,0:T(8,128)S(1)}, f32[256,128]{1,0:T(8,128)S(1)}, u32[]{:S(2)}, u32[]{:S(2)}) collective-permute-start(f32[256,128]{1,0:T(8,128)S(1)} %get-tuple-element.50), channel_id=1, source_target_pairs={{0,2},{2,0},{4,6},{6,4},{1,3},{3,1},{5,7},{7,5},{8,10},{10,8},{12,... | collective-permute-start | bytes 393224 | tf_op jit(solution)/shard_map/ppermute | solution.py:174
  31.2 6.6 %collective-permute-start.13 = (f32[256,128]{1,0:T(8,128)S(1)}, f32[256,128]{1,0:T(8,128)S(1)}, u32[]{:S(2)}, u32[]{:S(2)}) collective-permute-start(f32[256,128]{1,0:T(8,128)S(1)} %get-tuple-element.51), channel_id=1, source_target_pairs={{2,4},{4,2},{3,5},{5,3},{10,12},{12,10},{11,13},{13,11},{18,20},{2... | collective-permute-start | bytes 393224 | tf_op jit(solution)/shard_map/ppermute | solution.py:174
  31.9 5.9 %collective-permute-start.10 = (f32[128,128]{1,0:T(8,128)S(1)}, f32[128,128]{1,0:T(8,128)S(1)}, u32[]{:S(2)}, u32[]{:S(2)}) collective-permute-start(f32[128,128]{1,0:T(8,128)S(1)} %get-tuple-element.48), channel_id=1, source_target_pairs={{0,8},{8,0},{16,24},{24,16},{1,9},{9,1},{17,25},{25,17},{2,10},{10... | collective-permute-start | bytes 196616 | tf_op jit(solution)/shard_map/ppermute | solution.py:174
  35.2 2.5 %collective-permute-start.11 = (f32[128,128]{1,0:T(8,128)S(1)}, f32[128,128]{1,0:T(8,128)S(1)}, u32[]{:S(2)}, u32[]{:S(2)}) collective-permute-start(f32[128,128]{1,0:T(8,128)S(1)} %get-tuple-element.49), channel_id=1, source_target_pairs={{8,16},{16,8},{9,17},{17,9},{10,18},{18,10},{11,19},{19,11},{12,20... | collective-permute-start | bytes 196616 | tf_op jit(solution)/shard_map/ppermute | solution.py:174
  40.3 8.8 %collective-permute-start.19 = (f32[512,128]{1,0:T(8,128)S(1)}, f32[512,128]{1,0:T(8,128)S(1)}, u32[]{:S(2)}, u32[]{:S(2)}) collective-permute-start(f32[512,128]{1,0:T(8,128)S(1)} %get-tuple-element.58), channel_id=1, source_target_pairs={{0,1},{1,0},{2,3},{3,2},{4,5},{5,4},{6,7},{7,6},{8,9},{9,8},{10,11... | collective-permute-start | bytes 786440 | tf_op jit(solution)/shard_map/ppermute | solution.py:174
  40.9 8.1 %collective-permute-start.17 = (f32[256,128]{1,0:T(8,128)S(1)}, f32[256,128]{1,0:T(8,128)S(1)}, u32[]{:S(2)}, u32[]{:S(2)}) collective-permute-start(f32[256,128]{1,0:T(8,128)S(1)} %get-tuple-element.56), channel_id=1, source_target_pairs={{0,2},{2,0},{4,6},{6,4},{1,3},{3,1},{5,7},{7,5},{8,10},{10,8},{12,... | collective-permute-start | bytes 393224 | tf_op jit(solution)/shard_map/ppermute | solution.py:174
  42.5 6.6 %collective-permute-start.18 = (f32[256,128]{1,0:T(8,128)S(1)}, f32[256,128]{1,0:T(8,128)S(1)}, u32[]{:S(2)}, u32[]{:S(2)}) collective-permute-start(f32[256,128]{1,0:T(8,128)S(1)} %get-tuple-element.57), channel_id=1, source_target_pairs={{2,4},{4,2},{3,5},{5,3},{10,12},{12,10},{11,13},{13,11},{18,20},{2... | collective-permute-start | bytes 393224 | tf_op jit(solution)/shard_map/ppermute | solution.py:174
  43.1 5.9 %collective-permute-start.15 = (f32[128,128]{1,0:T(8,128)S(1)}, f32[128,128]{1,0:T(8,128)S(1)}, u32[]{:S(2)}, u32[]{:S(2)}) collective-permute-start(f32[128,128]{1,0:T(8,128)S(1)} %get-tuple-element.54), channel_id=1, source_target_pairs={{0,8},{8,0},{16,24},{24,16},{1,9},{9,1},{17,25},{25,17},{2,10},{10... | collective-permute-start | bytes 196616 | tf_op jit(solution)/shard_map/ppermute | solution.py:174
  46.5 2.5 %collective-permute-start.16 = (f32[128,128]{1,0:T(8,128)S(1)}, f32[128,128]{1,0:T(8,128)S(1)}, u32[]{:S(2)}, u32[]{:S(2)}) collective-permute-start(f32[128,128]{1,0:T(8,128)S(1)} %get-tuple-element.55), channel_id=1, source_target_pairs={{8,16},{16,8},{9,17},{17,9},{10,18},{18,10},{11,19},{19,11},{12,20... | collective-permute-start | bytes 196616 | tf_op jit(solution)/shard_map/ppermute | solution.py:174
  51.5 12.7 %collective-permute-start.24 = (f32[512,128]{1,0:T(8,128)S(1)}, f32[512,128]{1,0:T(8,128)S(1)}, u32[]{:S(2)}, u32[]{:S(2)}) collective-permute-start(f32[512,128]{1,0:T(8,128)S(1)} %get-tuple-element.67.refs_4_), channel_id=1, source_target_pairs={{0,1},{1,0},{2,3},{3,2},{4,5},{5,4},{6,7},{7,6},{8,9},{9,8},{10,11... | collective-permute-start | bytes 786440 | tf_op jit(solution)/shard_map/ppermute | solution.py:174
  53.1 11.1 %collective-permute-start.22 = (f32[256,128]{1,0:T(8,128)S(1)}, f32[256,128]{1,0:T(8,128)S(1)}, u32[]{:S(2)}, u32[]{:S(2)}) collective-permute-start(f32[256,128]{1,0:T(8,128)S(1)} %get-tuple-element.65.refs_2_), channel_id=1, source_target_pairs={{0,2},{2,0},{4,6},{6,4},{1,3},{3,1},{5,7},{7,5},{8,10},{10,8},{12,... | collective-permute-start | bytes 393224 | tf_op jit(solution)/shard_map/ppermute | solution.py:174
  55.4 8.9 %collective-permute-start.23 = (f32[256,128]{1,0:T(8,128)S(1)}, f32[256,128]{1,0:T(8,128)S(1)}, u32[]{:S(2)}, u32[]{:S(2)}) collective-permute-start(f32[256,128]{1,0:T(8,128)S(1)} %get-tuple-element.66.refs_3_), channel_id=1, source_target_pairs={{2,4},{4,2},{3,5},{5,3},{10,12},{12,10},{11,13},{13,11},{18,20},{2... | collective-permute-start | bytes 393224 | tf_op jit(solution)/shard_map/ppermute | solution.py:174
  56.0 8.2 %collective-permute-start.20 = (f32[128,128]{1,0:T(8,128)S(1)}, f32[128,128]{1,0:T(8,128)S(1)}, u32[]{:S(2)}, u32[]{:S(2)}) collective-permute-start(f32[128,128]{1,0:T(8,128)S(1)} %get-tuple-element.63.refs_0_), channel_id=1, source_target_pairs={{0,8},{8,0},{16,24},{24,16},{1,9},{9,1},{17,25},{25,17},{2,10},{10... | collective-permute-start | bytes 196616 | tf_op jit(solution)/shard_map/ppermute | solution.py:174
  58.8 5.3 %collective-permute-start.21 = (f32[128,128]{1,0:T(8,128)S(1)}, f32[128,128]{1,0:T(8,128)S(1)}, u32[]{:S(2)}, u32[]{:S(2)}) collective-permute-start(f32[128,128]{1,0:T(8,128)S(1)} %get-tuple-element.64.refs_1_), channel_id=1, source_target_pairs={{8,16},{16,8},{9,17},{17,9},{10,18},{18,10},{11,19},{19,11},{12,20... | collective-permute-start | bytes 196616 | tf_op jit(solution)/shard_map/ppermute | solution.py:174
  65.3 3.5 %collective-permute-start.25 = (f32[136,128]{1,0:T(8,128)S(1)}, f32[136,128]{1,0:T(8,128)S(1)}, u32[]{:S(2)}, u32[]{:S(2)}) collective-permute-start(f32[136,128]{1,0:T(8,128)S(1)} %shard_map.51), channel_id=1, source_target_pairs={{0,2},{2,0},{4,6},{6,4},{1,3},{3,1},{5,7},{7,5},{8,10},{10,8},{12,... | collective-permute-start | bytes 208904 | tf_op jit(solution)/shard_map/ppermute | solution.py:259
  68.8 4.5 %collective-permute-start.26 = (f32[136,128]{1,0:T(8,128)S(1)}, f32[136,128]{1,0:T(8,128)S(1)}, u32[]{:S(2)}, u32[]{:S(2)}) collective-permute-start(f32[136,128]{1,0:T(8,128)S(1)} %add.35), channel_id=1, source_target_pairs={{0,4},{2,6},{4,0},{6,2},{1,5},{3,7},{5,1},{7,3},{8,12},{10,14},{12... | collective-permute-start | bytes 208904 | tf_op jit(solution)/shard_map/ppermute | solution.py:259
  73.3 4.4 %collective-permute-start.27 = (f32[136,128]{1,0:T(8,128)S(1)}, f32[136,128]{1,0:T(8,128)S(1)}, u32[]{:S(2)}, u32[]{:S(2)}) collective-permute-start(f32[136,128]{1,0:T(8,128)S(1)} %add.36), channel_id=1, source_target_pairs={{0,1},{1,0},{2,3},{3,2},{4,5},{5,4},{6,7},{7,6},{8,9},{9,8},{10,11... | collective-permute-start | bytes 208904 | tf_op jit(solution)/shard_map/ppermute | solution.py:259
  77.7 5.1 %collective-permute-start.28 = (f32[136,128]{1,0:T(8,128)S(1)}, f32[136,128]{1,0:T(8,128)S(1)}, u32[]{:S(2)}, u32[]{:S(2)}) collective-permute-start(f32[136,128]{1,0:T(8,128)S(1)} %add.37), channel_id=1, source_target_pairs={{0,8},{8,0},{16,24},{24,16},{1,9},{9,1},{17,25},{25,17},{2,10},{10... | collective-permute-start | bytes 208904 | tf_op jit(solution)/shard_map/ppermute | solution.py:259
  82.8 5.3 %collective-permute-start.29 = (f32[136,128]{1,0:T(8,128)S(1)}, f32[136,128]{1,0:T(8,128)S(1)}, u32[]{:S(2)}, u32[]{:S(2)}) collective-permute-start(f32[136,128]{1,0:T(8,128)S(1)} %add.38), channel_id=1, source_target_pairs={{0,16},{8,24},{16,0},{24,8},{1,17},{9,25},{17,1},{25,9},{2,18},{10... | collective-permute-start | bytes 208904 | tf_op jit(solution)/shard_map/ppermute | solution.py:259

commit v3 on v2

--- a/solution.py
+++ b/solution.py
@@ -261,11 +261,87 @@
     return value
 
 
-def lower_inverse(gram):
-    lower = jnp.linalg.cholesky(gram)
-    return lax.linalg.triangular_solve(
-        lower, jnp.eye(gram.shape[0], dtype=gram.dtype), left_side=True, lower=True
-    )
+PANEL = 32
+GROUP = 8
+
+
+def eliminate(m_ref, n):
+    place = lax.broadcasted_iota(jnp.int32, (PANEL, n), 0)
+    for top in range(0, n, PANEL):
+        left, right = m_ref[top : top + PANEL, :n], m_ref[top : top + PANEL, n:]
+        for first in range(0, PANEL, GROUP):
+            columns = [
+                jnp.broadcast_to(left[:, top + k : top + k + 1], (PANEL, n))
+                for k in range(first, first + GROUP)
+            ]
+            for i in range(GROUP):
+                k = first + i
+                pivot = columns[i][k : k + 1, :]
+                inverse = 1.0 / pivot
+                root = lax.rsqrt(pivot)
+                below = jnp.where(place > k, columns[i], 0.0)
+                for t in range(i + 1, GROUP):
+                    columns[t] = columns[t] - below * (columns[t][k : k + 1, :] * inverse)
+                here = place == k
+                one, two_ = left[k : k + 1, :], right[k : k + 1, :]
+                left = jnp.where(here, one * root, left - below * (one * inverse))
+                right = jnp.where(here, two_ * root, right - below * (two_ * inverse))
+        m_ref[top : top + PANEL, :n] = left
+        m_ref[top : top + PANEL, n:] = right
+        if top + PANEL < n:
+            both_sides = jnp.concatenate([left, right], axis=1)
+            update = lax.dot_general(
+                left, both_sides, (((0,), (0,)), ((), ())),
+                precision=HIGH, preferred_element_type=jnp.float32,
+            )
+            m_ref[top + PANEL :, :] = m_ref[top + PANEL :, :] - update[top + PANEL :, :]
+
+
+def orthonormal(packed, filtered, s):
+    k = s.k
+    rows = s.cells // 8
+
+    def body(p_ref, f_ref, b_ref, o_ref, m_ref, t_ref):
+        @pl.when(pl.program_id(0) == 0)
+        def _():
+            upper = p_ref[:k, :]
+            turned = upper.T
+            below = lax.broadcasted_iota(jnp.int32, (k, k), 0)
+            along = lax.broadcasted_iota(jnp.int32, (k, k), 1)
+            m_ref[:, :k] = jnp.where(below >= along, upper, turned)
+            m_ref[:, k:] = jnp.where(below == along, 1.0, 0.0)
+            raw = jnp.where(below < along, upper, turned)
+            raw = jnp.where(below == along, p_ref[k : k + 1, :], raw)
+            eliminate(m_ref, k)
+            inverse = m_ref[:, k:]
+            half = jnp.dot(inverse, raw, precision=HIGH, preferred_element_type=jnp.float32)
+            o_ref[...] = lax.dot_general(
+                half, inverse, (((1,), (1,)), ((), ())),
+                precision=HIGH, preferred_element_type=jnp.float32,
+            )
+            pair = two(inverse.T)
+            t_ref[:k, :] = pair
+            t_ref[k:, :] = pair
+
+        f = f_ref[pl.ds(pl.multiple_of(pl.program_id(0) * rows, rows), rows), :]
+        out = jnp.dot(two(f), t_ref[...], preferred_element_type=jnp.float32)
+        b_ref[...] = out[:, :k] + out[:, k:]
+
+    return pl.pallas_call(
+        body,
+        grid=(8,),
+        out_shape=[f32(s.cells, k), f32(k, k)],
+        in_specs=[VMEM, VMEM],
+        out_specs=(
+            pl.BlockSpec((rows, k), lambda i: (i, 0)),
+            pl.BlockSpec((k, k), lambda i: (0, 0)),
+        ),
+        scratch_shapes=[pltpu.VMEM((k, 2 * k), jnp.float32), pltpu.VMEM((2 * k, 2 * k), BF)],
+        compiler_params=pltpu.CompilerParams(vmem_limit_bytes=32 * 1024 * 1024),
+        cost_estimate=pl.CostEstimate(
+            flops=8 * s.cells * k * k, bytes_accessed=8 * s.cells * k, transcendentals=0
+        ),
+    )(packed, filtered)
 
 
 def on_device(block, conductivity):
@@ -293,16 +369,8 @@
     ghosts = exchange(faces, axes)
     filtered, gram, own = gather_terms(w, wide, at, s)
     packed = total(pack_terms(gram, own, faces, ghosts, at, s, cells), ("gy", "gz", "gx"))
-    upper, diagonal = packed[: s.k], packed[s.k]
-    keep = jnp.tril(jnp.ones((s.k, s.k), bool))
-    strict = jnp.tril(jnp.ones((s.k, s.k), bool), -1)
-    gram = jnp.where(keep, upper, upper.T)
-    raw = jnp.where(strict, upper.T, upper)
-    raw = jnp.where(jnp.eye(s.k, dtype=bool), diagonal[None, :], raw)
-    inverse = lower_inverse(gram)
-    basis = jnp.dot(filtered, inverse.T, precision=HIGH).reshape(block.shape)
-    projected = jnp.dot(jnp.dot(inverse, raw, precision=HIGH), inverse.T, precision=HIGH)
-    return (basis, projected)
+    basis, projected = orthonormal(packed, filtered, s)
+    return (basis.reshape(block.shape), projected)
 
 
 def solution(mesh):

time: 116 us -> 96.7 us (0.83)
  other arithmetic: 22.9 us -> 0.05 us
  Pallas kernels: 24.2 us -> 32.6 us
  matrix products: 4.55 us -> 0 us
    another operation x5 -> x0, other arithmetic: 22.9 us -> none  [the longest x3 12.4 us: lower_inverse(): lower = jnp.linalg.cholesky(gram)]
    pallas_call x0 -> x1, Pallas kernels: none -> 8.43 us  [orthonormal(): pl.pallas_call(body, grid=(8,), out_shape=[f32(s.cells, k), f32(k, k)], i...]
    dot_general x3 -> x0, matrix products: 4.3 us -> none  [the longest x1 3.12 us: on_device(): basis = jnp.dot(filtered, inverse.T, precision=HIGH).reshape(block.shape)]
  transfers between devices with their start and end apart: 30 -> 30, of which waited for: 8 -> 8; matrix products, arithmetic and copies ran while one was open for 0% -> 0% of each run, Pallas kernels for 10% -> 12%
where the time goes in v3:
time: 96.7 us; the launch traced here: 96.4 us
  starting transfers between devices  44.6 us (46%)
  Pallas kernels  32.6 us (34%)
  waiting for transfers between devices  16.1 us (17%)
  local copies, waits for them, and re-layouts  1.98 us (2%)
  between operations  1.01 us (1%)
    ppermute x25, starting transfers between devices, exchange(): got.append(lax.ppermute(face, axis, pairs))  35.8 us
    pallas_call x10, Pallas kernels, call(): pl.pallas_call(body, out_shape=outs, in_specs=[SMEM] + [VMEM] * (len(ins)...  19.7 us
    ppermute x5, waiting for transfers between devices, total(): lax.ppermute(value, axis, [(i, i ^ bit) for i in range(count)])  13.9 us
    ppermute x5, starting transfers between devices, total(): lax.ppermute(value, axis, [(i, i ^ bit) for i in range(count)])  8.84 us
    pallas_call x1, Pallas kernels, orthonormal(): pl.pallas_call(body, grid=(8,), out_shape=[f32(s.cells, k), f32(k, k)], i...  8.43 us
    pallas_call x1, Pallas kernels, gather_terms(): pl.pallas_call(body, out_shape=outs, in_specs=[SMEM, VMEM, VMEM], out_spe...  4.49 us
    ppermute x25, waiting for transfers between devices, exchange(): got.append(lax.ppermute(face, axis, pairs))  2.17 us
  transfers between devices with their start and end apart: 30, of which 8 were waited for; matrix products, arithmetic and copies ran while one was open for 0% of the time, Pallas kernels for 12%

profile of v3, /device:TPU:0, one launch (start us, length us, event | category | flops | bytes accessed | tf_op | source)
XLA Modules:
  0.0 96.4 jit_solution(14338091446474695719)
XLA Ops:
  0.7 1.1 %copy.8 = f32[32,16,8]{2,1,0:T(8,128)S(1)} copy(f32[32,16,8]{0,2,1:T(8,128)} %param.3) | data formatting | bytes 32768 | tf_op args[1]
  2.7 1.5 %shard_map.41 = (f32[4096,128]{1,0:T(8,128)S(1)}, f32[128,128]{1,0:T(8,128)S(1)}, f32[128,128]{1,0:T(8,128)S(1)}, f32[256,128]{1,0:T(8,128)S(1)}, f32[256,128]{1,0:T(8,128)S(1)}, /*index=5*/f32[512,128]{1,0:T(8,128)S(1)}) custom-call(s32[6]{0:T(128)S(1)} %stack.27.at_ref, f32[4096,128]{1,0:T(8,128)S(1)} %bitcast.8, f32[4096,128]{1,0:T(8,128)S(1)} %broadcast_in_dim.9.k_ref), custom_call_target="tpu_custom_call" | custom-call | flops 2097152 | bytes 6946840 | tf_op jit(solution)/shard_map/pallas_call | solution.py:21
  4.1 3.0 %collective-permute-start.4 = (f32[512,128]{1,0:T(8,128)S(1)}, f32[512,128]{1,0:T(8,128)S(1)}, u32[]{:S(2)}, u32[]{:S(2)}) collective-permute-start(f32[512,128]{1,0:T(8,128)S(1)} %get-tuple-element.42), channel_id=1, source_target_pairs={{0,1},{1,0},{2,3},{3,2},{4,5},{5,4},{6,7},{7,6},{8,9},{9,8},{10,11... | collective-permute-start | bytes 786440 | tf_op jit(solution)/shard_map/ppermute | solution.py:174
  7.8 1.6 %collective-permute-start = (f32[128,128]{1,0:T(8,128)S(1)}, f32[128,128]{1,0:T(8,128)S(1)}, u32[]{:S(2)}, u32[]{:S(2)}) collective-permute-start(f32[128,128]{1,0:T(8,128)S(1)} %get-tuple-element.38), channel_id=1, source_target_pairs={{0,8},{8,0},{16,24},{24,16},{1,9},{9,1},{17,25},{25,17},{2,10},{10... | collective-permute-start | bytes 196616 | tf_op jit(solution)/shard_map/ppermute | solution.py:174
  10.1 1.8 %shard_map.42.p_ref = f32[4096,128]{1,0:T(8,128)S(1)} custom-call(s32[6]{0:T(128)S(1)} %stack.27.at_ref, f32[4096,128]{1,0:T(8,128)S(1)} %get-tuple-element.37.w_ref.rest_0_, f32[4096,128]{1,0:T(8,128)S(1)} %broadcast_in_dim.9.k_ref), custom_call_target="tpu_custom_call" | custom-call | flops 6291456 | bytes 6291480 | tf_op jit(solution)/shard_map/pallas_call | solution.py:21
  12.2 1.3 %collective-permute-done.4.refs_4_ = f32[512,128]{1,0:T(8,128)S(1)} collective-permute-done((f32[512,128]{1,0:T(8,128)S(1)}, f32[512,128]{1,0:T(8,128)S(1)}, u32[]{:S(2)}, u32[]{:S(2)}) %collective-permute-start.4) | collective-permute-done | bytes 262176 | tf_op jit(solution)/shard_map/ppermute | solution.py:174
  13.4 2.5 %shard_map.43 = (f32[4096,128]{1,0:T(8,128)S(1)}, f32[128,128]{1,0:T(8,128)S(1)}, f32[128,128]{1,0:T(8,128)S(1)}, f32[256,128]{1,0:T(8,128)S(1)}, f32[256,128]{1,0:T(8,128)S(1)}, /*index=5*/f32[512,128]{1,0:T(8,128)S(1)}) custom-call(s32[6]{0:T(128)S(1)} %stack.27.at_ref, f32[4096,128]{1,0:T(8,128)S(1)} %shard_map.42.p_ref, ...), custom_call_target="tpu_custom_call", output_to_operand_aliasing={{0}: (1, {})} | custom-call | flops 2097152 | bytes 7602200 | tf_op jit(solution)/shard_map/pallas_call | solution.py:21
  15.9 1.8 %collective-permute-start.9 = (f32[512,128]{1,0:T(8,128)S(1)}, f32[512,128]{1,0:T(8,128)S(1)}, u32[]{:S(2)}, u32[]{:S(2)}) collective-permute-start(f32[512,128]{1,0:T(8,128)S(1)} %get-tuple-element.48), channel_id=1, source_target_pairs={{0,1},{1,0},{2,3},{3,2},{4,5},{5,4},{6,7},{7,6},{8,9},{9,8},{10,11... | collective-permute-start | bytes 786440 | tf_op jit(solution)/shard_map/ppermute | solution.py:174
  18.4 3.6 %collective-permute-start.5 = (f32[128,128]{1,0:T(8,128)S(1)}, f32[128,128]{1,0:T(8,128)S(1)}, u32[]{:S(2)}, u32[]{:S(2)}) collective-permute-start(f32[128,128]{1,0:T(8,128)S(1)} %get-tuple-element.44), channel_id=1, source_target_pairs={{0,8},{8,0},{16,24},{24,16},{1,9},{9,1},{17,25},{25,17},{2,10},{10... | collective-permute-start | bytes 196616 | tf_op jit(solution)/shard_map/ppermute | solution.py:174
  22.7 1.8 %shard_map.44.p_ref = f32[4096,128]{1,0:T(8,128)S(1)} custom-call(s32[6]{0:T(128)S(1)} %stack.27.at_ref, f32[4096,128]{1,0:T(8,128)S(1)} %get-tuple-element.43.w_ref.rest_0_, f32[4096,128]{1,0:T(8,128)S(1)} %broadcast_in_dim.9.k_ref, f32[4096,128]{1,0:T(8,128)S(1)} %get-tuple-element.37.w_ref.rest_0_), custom_call_target="tpu_custom_call" | custom-call | flops 6291456 | bytes 8388632 | tf_op jit(solution)/shard_map/pallas_call | solution.py:21
  25.2 2.5 %shard_map.45 = (f32[4096,128]{1,0:T(8,128)S(1)}, f32[128,128]{1,0:T(8,128)S(1)}, f32[128,128]{1,0:T(8,128)S(1)}, f32[256,128]{1,0:T(8,128)S(1)}, f32[256,128]{1,0:T(8,128)S(1)}, /*index=5*/f32[512,128]{1,0:T(8,128)S(1)}) custom-call(s32[6]{0:T(128)S(1)} %stack.27.at_ref, f32[4096,128]{1,0:T(8,128)S(1)} %shard_map.44.p_ref, ...), custom_call_target="tpu_custom_call", output_to_operand_aliasing={{0}: (1, {})} | custom-call | flops 2097152 | bytes 7602200 | tf_op jit(solution)/shard_map/pallas_call | solution.py:21
  28.6 2.6 %collective-permute-start.12 = (f32[256,128]{1,0:T(8,128)S(1)}, f32[256,128]{1,0:T(8,128)S(1)}, u32[]{:S(2)}, u32[]{:S(2)}) collective-permute-start(f32[256,128]{1,0:T(8,128)S(1)} %get-tuple-element.52), channel_id=1, source_target_pairs={{0,2},{2,0},{4,6},{6,4},{1,3},{3,1},{5,7},{7,5},{8,10},{10,8},{12,... | collective-permute-start | bytes 393224 | tf_op jit(solution)/shard_map/ppermute | solution.py:174
  31.9 3.3 %collective-permute-start.10 = (f32[128,128]{1,0:T(8,128)S(1)}, f32[128,128]{1,0:T(8,128)S(1)}, u32[]{:S(2)}, u32[]{:S(2)}) collective-permute-start(f32[128,128]{1,0:T(8,128)S(1)} %get-tuple-element.50), channel_id=1, source_target_pairs={{0,8},{8,0},{16,24},{24,16},{1,9},{9,1},{17,25},{25,17},{2,10},{10... | collective-permute-start | bytes 196616 | tf_op jit(solution)/shard_map/ppermute | solution.py:174
  35.9 1.8 %shard_map.46.p_ref = f32[4096,128]{1,0:T(8,128)S(1)} custom-call(s32[6]{0:T(128)S(1)} %stack.27.at_ref, f32[4096,128]{1,0:T(8,128)S(1)} %get-tuple-element.49.w_ref.rest_0_, f32[4096,128]{1,0:T(8,128)S(1)} %broadcast_in_dim.9.k_ref, f32[4096,128]{1,0:T(8,128)S(1)} %get-tuple-element.43.w_ref.rest_0_), custom_call_target="tpu_custom_call" | custom-call | flops 6291456 | bytes 8388632 | tf_op jit(solution)/shard_map/pallas_call | solution.py:21
  37.8 2.5 %shard_map.47 = (f32[4096,128]{1,0:T(8,128)S(1)}, f32[128,128]{1,0:T(8,128)S(1)}, f32[128,128]{1,0:T(8,128)S(1)}, f32[256,128]{1,0:T(8,128)S(1)}, f32[256,128]{1,0:T(8,128)S(1)}, /*index=5*/f32[512,128]{1,0:T(8,128)S(1)}) custom-call(s32[6]{0:T(128)S(1)} %stack.27.at_ref, f32[4096,128]{1,0:T(8,128)S(1)} %shard_map.46.p_ref, ...), custom_call_target="tpu_custom_call", output_to_operand_aliasing={{0}: (1, {})} | custom-call | flops 2097152 | bytes 7602200 | tf_op jit(solution)/shard_map/pallas_call | solution.py:21
  40.9 1.6 %collective-permute-start.17 = (f32[256,128]{1,0:T(8,128)S(1)}, f32[256,128]{1,0:T(8,128)S(1)}, u32[]{:S(2)}, u32[]{:S(2)}) collective-permute-start(f32[256,128]{1,0:T(8,128)S(1)} %get-tuple-element.58), channel_id=1, source_target_pairs={{0,2},{2,0},{4,6},{6,4},{1,3},{3,1},{5,7},{7,5},{8,10},{10,8},{12,... | collective-permute-start | bytes 393224 | tf_op jit(solution)/shard_map/ppermute | solution.py:174
  43.1 3.3 %collective-permute-start.15 = (f32[128,128]{1,0:T(8,128)S(1)}, f32[128,128]{1,0:T(8,128)S(1)}, u32[]{:S(2)}, u32[]{:S(2)}) collective-permute-start(f32[128,128]{1,0:T(8,128)S(1)} %get-tuple-element.56), channel_id=1, source_target_pairs={{0,8},{8,0},{16,24},{24,16},{1,9},{9,1},{17,25},{25,17},{2,10},{10... | collective-permute-start | bytes 196616 | tf_op jit(solution)/shard_map/ppermute | solution.py:174
  47.1 1.8 %shard_map.48.p_ref = f32[4096,128]{1,0:T(8,128)S(1)} custom-call(s32[6]{0:T(128)S(1)} %stack.27.at_ref, f32[4096,128]{1,0:T(8,128)S(1)} %get-tuple-element.55.w_ref, f32[4096,128]{1,0:T(8,128)S(1)} %broadcast_in_dim.9.k_ref, f32[4096,128]{1,0:T(8,128)S(1)} %get-tuple-element.49.w_ref.rest_0_), custom_call_target="tpu_custom_call" | custom-call | flops 6291456 | bytes 8388632 | tf_op jit(solution)/shard_map/pallas_call | solution.py:21
  49.0 2.5 %shard_map.49 = (f32[4096,128]{1,0:T(8,128)S(1)}, f32[128,128]{1,0:T(8,128)S(1)}, f32[128,128]{1,0:T(8,128)S(1)}, f32[256,128]{1,0:T(8,128)S(1)}, f32[256,128]{1,0:T(8,128)S(1)}, /*index=5*/f32[512,128]{1,0:T(8,128)S(1)}) custom-call(s32[6]{0:T(128)S(1)} %stack.27.at_ref, f32[4096,128]{1,0:T(8,128)S(1)} %shard_map.48.p_ref, ...), custom_call_target="tpu_custom_call", output_to_operand_aliasing={{0}: (1, {})} | custom-call | flops 2097152 | bytes 7602200 | tf_op jit(solution)/shard_map/pallas_call | solution.py:21
  51.5 1.6 %collective-permute-start.24 = (f32[512,128]{1,0:T(8,128)S(1)}, f32[512,128]{1,0:T(8,128)S(1)}, u32[]{:S(2)}, u32[]{:S(2)}) collective-permute-start(f32[512,128]{1,0:T(8,128)S(1)} %get-tuple-element.68.refs_4_), channel_id=1, source_target_pairs={{0,1},{1,0},{2,3},{3,2},{4,5},{5,4},{6,7},{7,6},{8,9},{9,8},{10,11... | collective-permute-start | bytes 786440 | tf_op jit(solution)/shard_map/ppermute | solution.py:174
  53.1 2.3 %collective-permute-start.22 = (f32[256,128]{1,0:T(8,128)S(1)}, f32[256,128]{1,0:T(8,128)S(1)}, u32[]{:S(2)}, u32[]{:S(2)}) collective-permute-start(f32[256,128]{1,0:T(8,128)S(1)} %get-tuple-element.66.refs_2_), channel_id=1, source_target_pairs={{0,2},{2,0},{4,6},{6,4},{1,3},{3,1},{5,7},{7,5},{8,10},{10,8},{12,... | collective-permute-start | bytes 393224 | tf_op jit(solution)/shard_map/ppermute | solution.py:174
  56.0 2.8 %collective-permute-start.20 = (f32[128,128]{1,0:T(8,128)S(1)}, f32[128,128]{1,0:T(8,128)S(1)}, u32[]{:S(2)}, u32[]{:S(2)}) collective-permute-start(f32[128,128]{1,0:T(8,128)S(1)} %get-tuple-element.64.refs_0_), channel_id=1, source_target_pairs={{0,8},{8,0},{16,24},{24,16},{1,9},{9,1},{17,25},{25,17},{2,10},{10... | collective-permute-start | bytes 196616 | tf_op jit(solution)/shard_map/ppermute | solution.py:174
  59.5 4.5 %shard_map.50 = (f32[4096,128]{1,0:T(8,128)S(1)}, f32[128,128]{1,0:T(8,128)S(1)}, f32[128,128]{1,0:T(8,128)S(1)}) custom-call(s32[6]{0:T(128)S(1)} %stack.27.at_ref, f32[4096,128]{1,0:T(8,128)S(1)} %get-tuple-element.61.w_ref, f32[4096,128]{1,0:T(8,128)S(1)} %broadcast_in_dim.9.k_ref), custom_call_target="tpu_custom_call" | custom-call | flops 1073741824 | bytes 8388608 | tf_op jit(solution)/shard_map/pallas_call | solution.py:221
  64.1 1.0 %shard_map.51 = f32[136,128]{1,0:T(8,128)S(1)} custom-call(s32[6]{0:T(128)S(1)} %stack.27.at_ref, f32[128,128]{1,0:T(8,128)S(1)} %get-tuple-element.62.g_ref, f32[128,128]{1,0:T(8,128)S(1)} %get-tuple-element.63.m_ref, f32[128,128]{1,0:T(8,128)S(1)} %get-tuple-element.64.refs_0_, f32[128,128]{1,0:T(8,128)S(1)} %get-tuple-element.65.refs_1_, ...), custom_call_target="tpu_custom_call" | custom-call | flops 3145728 | bytes 1511448 | tf_op jit(solution)/shard_map/pallas_call | solution.py:21
  65.1 2.6 %collective-permute-start.25 = (f32[136,128]{1,0:T(8,128)S(1)}, f32[136,128]{1,0:T(8,128)S(1)}, u32[]{:S(2)}, u32[]{:S(2)}) collective-permute-start(f32[136,128]{1,0:T(8,128)S(1)} %shard_map.51), channel_id=1, source_target_pairs={{0,2},{2,0},{4,6},{6,4},{1,3},{3,1},{5,7},{7,5},{8,10},{10,8},{12,... | collective-permute-start | bytes 208904 | tf_op jit(solution)/shard_map/ppermute | solution.py:259
  69.4 3.7 %collective-permute-done.26 = f32[136,128]{1,0:T(8,128)S(1)} collective-permute-done((f32[136,128]{1,0:T(8,128)S(1)}, f32[136,128]{1,0:T(8,128)S(1)}, u32[]{:S(2)}, u32[]{:S(2)}) %collective-permute-start.26) | collective-permute-done | bytes 69664 | tf_op jit(solution)/shard_map/ppermute | solution.py:259
  73.7 3.8 %collective-permute-done.27 = f32[136,128]{1,0:T(8,128)S(1)} collective-permute-done((f32[136,128]{1,0:T(8,128)S(1)}, f32[136,128]{1,0:T(8,128)S(1)}, u32[]{:S(2)}, u32[]{:S(2)}) %collective-permute-start.27) | collective-permute-done | bytes 69664 | tf_op jit(solution)/shard_map/ppermute | solution.py:259
  77.5 2.8 %collective-permute-start.28 = (f32[136,128]{1,0:T(8,128)S(1)}, f32[136,128]{1,0:T(8,128)S(1)}, u32[]{:S(2)}, u32[]{:S(2)}) collective-permute-start(f32[136,128]{1,0:T(8,128)S(1)} %add.17), channel_id=1, source_target_pairs={{0,8},{8,0},{16,24},{24,16},{1,9},{9,1},{17,25},{25,17},{2,10},{10... | collective-permute-start | bytes 208904 | tf_op jit(solution)/shard_map/ppermute | solution.py:259
  80.3 2.3 %collective-permute-done.28 = f32[136,128]{1,0:T(8,128)S(1)} collective-permute-done((f32[136,128]{1,0:T(8,128)S(1)}, f32[136,128]{1,0:T(8,128)S(1)}, u32[]{:S(2)}, u32[]{:S(2)}) %collective-permute-start.28) | collective-permute-done | bytes 69664 | tf_op jit(solution)/shard_map/ppermute | solution.py:259
  82.6 2.1 %collective-permute-start.29 = (f32[136,128]{1,0:T(8,128)S(1)}, f32[136,128]{1,0:T(8,128)S(1)}, u32[]{:S(2)}, u32[]{:S(2)}) collective-permute-start(f32[136,128]{1,0:T(8,128)S(1)} %add.18), channel_id=1, source_target_pairs={{0,16},{8,24},{16,0},{24,8},{1,17},{9,25},{17,1},{25,9},{2,18},{10... | collective-permute-start | bytes 208904 | tf_op jit(solution)/shard_map/ppermute | solution.py:259
  84.7 3.2 %collective-permute-done.29 = f32[136,128]{1,0:T(8,128)S(1)} collective-permute-done((f32[136,128]{1,0:T(8,128)S(1)}, f32[136,128]{1,0:T(8,128)S(1)}, u32[]{:S(2)}, u32[]{:S(2)}) %collective-permute-start.29) | collective-permute-done | bytes 69664 | tf_op jit(solution)/shard_map/ppermute | solution.py:259
  87.9 8.4 %shard_map.52 = (f32[4096,128]{1,0:T(8,128)}, f32[128,128]{1,0:T(8,128)}) custom-call(f32[136,128]{1,0:T(8,128)S(1)} %add.19.p_ref, f32[4096,128]{1,0:T(8,128)S(1)} %get-tuple-element.69.f_ref), custom_call_target="tpu_custom_call" | custom-call | flops 536870912 | bytes 4194304 | tf_op jit(solution)/shard_map/pallas_call | solution.py:330
  (51 shorter events, 12.2 us)
Async XLA Ops:
  0.6 2.0 %copy-start = (f32[32,16,8,128]{3,2,1,0:T(8,128)S(1)}, f32[32,16,8,128]{3,2,1,0:T(8,128)}, u32[]{:S(2)}) copy-start(f32[32,16,8,128]{3,2,1,0:T(8,128)} %param.2) | copy-start | bytes 6291460
  4.1 9.3 %collective-permute-start.4 = (f32[512,128]{1,0:T(8,128)S(1)}, f32[512,128]{1,0:T(8,128)S(1)}, u32[]{:S(2)}, u32[]{:S(2)}) collective-permute-start(f32[512,128]{1,0:T(8,128)S(1)} %get-tuple-element.42), channel_id=1, source_target_pairs={{0,1},{1,0},{2,3},{3,2},{4,5},{5,4},{6,7},{7,6},{8,9},{9,8},{10,11... | collective-permute-start | bytes 786440 | tf_op jit(solution)/shard_map/ppermute | solution.py:174
  7.1 5.0 %collective-permute-start.2 = (f32[256,128]{1,0:T(8,128)S(1)}, f32[256,128]{1,0:T(8,128)S(1)}, u32[]{:S(2)}, u32[]{:S(2)}) collective-permute-start(f32[256,128]{1,0:T(8,128)S(1)} %get-tuple-element.40), channel_id=1, source_target_pairs={{0,2},{2,0},{4,6},{6,4},{1,3},{3,1},{5,7},{7,5},{8,10},{10,8},{12,... | collective-permute-start | bytes 393224 | tf_op jit(solution)/shard_map/ppermute | solution.py:174
  7.1 5.0 %collective-permute-start.3 = (f32[256,128]{1,0:T(8,128)S(1)}, f32[256,128]{1,0:T(8,128)S(1)}, u32[]{:S(2)}, u32[]{:S(2)}) collective-permute-start(f32[256,128]{1,0:T(8,128)S(1)} %get-tuple-element.41), channel_id=1, source_target_pairs={{2,4},{4,2},{3,5},{5,3},{10,12},{12,10},{11,13},{13,11},{18,20},{2... | collective-permute-start | bytes 393224 | tf_op jit(solution)/shard_map/ppermute | solution.py:174
  7.8 4.3 %collective-permute-start = (f32[128,128]{1,0:T(8,128)S(1)}, f32[128,128]{1,0:T(8,128)S(1)}, u32[]{:S(2)}, u32[]{:S(2)}) collective-permute-start(f32[128,128]{1,0:T(8,128)S(1)} %get-tuple-element.38), channel_id=1, source_target_pairs={{0,8},{8,0},{16,24},{24,16},{1,9},{9,1},{17,25},{25,17},{2,10},{10... | collective-permute-start | bytes 196616 | tf_op jit(solution)/shard_map/ppermute | solution.py:174
  9.5 2.7 %collective-permute-start.1 = (f32[128,128]{1,0:T(8,128)S(1)}, f32[128,128]{1,0:T(8,128)S(1)}, u32[]{:S(2)}, u32[]{:S(2)}) collective-permute-start(f32[128,128]{1,0:T(8,128)S(1)} %get-tuple-element.39), channel_id=1, source_target_pairs={{8,16},{16,8},{9,17},{17,9},{10,18},{18,10},{11,19},{19,11},{12,20... | collective-permute-start | bytes 196616 | tf_op jit(solution)/shard_map/ppermute | solution.py:174
  15.9 9.2 %collective-permute-start.9 = (f32[512,128]{1,0:T(8,128)S(1)}, f32[512,128]{1,0:T(8,128)S(1)}, u32[]{:S(2)}, u32[]{:S(2)}) collective-permute-start(f32[512,128]{1,0:T(8,128)S(1)} %get-tuple-element.48), channel_id=1, source_target_pairs={{0,1},{1,0},{2,3},{3,2},{4,5},{5,4},{6,7},{7,6},{8,9},{9,8},{10,11... | collective-permute-start | bytes 786440 | tf_op jit(solution)/shard_map/ppermute | solution.py:174
  17.7 6.8 %collective-permute-start.7 = (f32[256,128]{1,0:T(8,128)S(1)}, f32[256,128]{1,0:T(8,128)S(1)}, u32[]{:S(2)}, u32[]{:S(2)}) collective-permute-start(f32[256,128]{1,0:T(8,128)S(1)} %get-tuple-element.46), channel_id=1, source_target_pairs={{0,2},{2,0},{4,6},{6,4},{1,3},{3,1},{5,7},{7,5},{8,10},{10,8},{12,... | collective-permute-start | bytes 393224 | tf_op jit(solution)/shard_map/ppermute | solution.py:174
  17.7 6.9 %collective-permute-start.8 = (f32[256,128]{1,0:T(8,128)S(1)}, f32[256,128]{1,0:T(8,128)S(1)}, u32[]{:S(2)}, u32[]{:S(2)}) collective-permute-start(f32[256,128]{1,0:T(8,128)S(1)} %get-tuple-element.47), channel_id=1, source_target_pairs={{2,4},{4,2},{3,5},{5,3},{10,12},{12,10},{11,13},{13,11},{18,20},{2... | collective-permute-start | bytes 393224 | tf_op jit(solution)/shard_map/ppermute | solution.py:174
  18.4 6.2 %collective-permute-start.5 = (f32[128,128]{1,0:T(8,128)S(1)}, f32[128,128]{1,0:T(8,128)S(1)}, u32[]{:S(2)}, u32[]{:S(2)}) collective-permute-start(f32[128,128]{1,0:T(8,128)S(1)} %get-tuple-element.44), channel_id=1, source_target_pairs={{0,8},{8,0},{16,24},{24,16},{1,9},{9,1},{17,25},{25,17},{2,10},{10... | collective-permute-start | bytes 196616 | tf_op jit(solution)/shard_map/ppermute | solution.py:174
  22.0 2.5 %collective-permute-start.6 = (f32[128,128]{1,0:T(8,128)S(1)}, f32[128,128]{1,0:T(8,128)S(1)}, u32[]{:S(2)}, u32[]{:S(2)}) collective-permute-start(f32[128,128]{1,0:T(8,128)S(1)} %get-tuple-element.45), channel_id=1, source_target_pairs={{8,16},{16,8},{9,17},{17,9},{10,18},{18,10},{11,19},{19,11},{12,20... | collective-permute-start | bytes 196616 | tf_op jit(solution)/shard_map/ppermute | solution.py:174
  27.6 10.1 %collective-permute-start.14 = (f32[512,128]{1,0:T(8,128)S(1)}, f32[512,128]{1,0:T(8,128)S(1)}, u32[]{:S(2)}, u32[]{:S(2)}) collective-permute-start(f32[512,128]{1,0:T(8,128)S(1)} %get-tuple-element.54), channel_id=1, source_target_pairs={{0,1},{1,0},{2,3},{3,2},{4,5},{5,4},{6,7},{7,6},{8,9},{9,8},{10,11... | collective-permute-start | bytes 786440 | tf_op jit(solution)/shard_map/ppermute | solution.py:174
  28.6 9.1 %collective-permute-start.12 = (f32[256,128]{1,0:T(8,128)S(1)}, f32[256,128]{1,0:T(8,128)S(1)}, u32[]{:S(2)}, u32[]{:S(2)}) collective-permute-start(f32[256,128]{1,0:T(8,128)S(1)} %get-tuple-element.52), channel_id=1, source_target_pairs={{0,2},{2,0},{4,6},{6,4},{1,3},{3,1},{5,7},{7,5},{8,10},{10,8},{12,... | collective-permute-start | bytes 393224 | tf_op jit(solution)/shard_map/ppermute | solution.py:174
  31.2 6.6 %collective-permute-start.13 = (f32[256,128]{1,0:T(8,128)S(1)}, f32[256,128]{1,0:T(8,128)S(1)}, u32[]{:S(2)}, u32[]{:S(2)}) collective-permute-start(f32[256,128]{1,0:T(8,128)S(1)} %get-tuple-element.53), channel_id=1, source_target_pairs={{2,4},{4,2},{3,5},{5,3},{10,12},{12,10},{11,13},{13,11},{18,20},{2... | collective-permute-start | bytes 393224 | tf_op jit(solution)/shard_map/ppermute | solution.py:174
  31.9 5.9 %collective-permute-start.10 = (f32[128,128]{1,0:T(8,128)S(1)}, f32[128,128]{1,0:T(8,128)S(1)}, u32[]{:S(2)}, u32[]{:S(2)}) collective-permute-start(f32[128,128]{1,0:T(8,128)S(1)} %get-tuple-element.50), channel_id=1, source_target_pairs={{0,8},{8,0},{16,24},{24,16},{1,9},{9,1},{17,25},{25,17},{2,10},{10... | collective-permute-start | bytes 196616 | tf_op jit(solution)/shard_map/ppermute | solution.py:174
  35.2 2.5 %collective-permute-start.11 = (f32[128,128]{1,0:T(8,128)S(1)}, f32[128,128]{1,0:T(8,128)S(1)}, u32[]{:S(2)}, u32[]{:S(2)}) collective-permute-start(f32[128,128]{1,0:T(8,128)S(1)} %get-tuple-element.51), channel_id=1, source_target_pairs={{8,16},{16,8},{9,17},{17,9},{10,18},{18,10},{11,19},{19,11},{12,20... | collective-permute-start | bytes 196616 | tf_op jit(solution)/shard_map/ppermute | solution.py:174
  40.3 8.8 %collective-permute-start.19 = (f32[512,128]{1,0:T(8,128)S(1)}, f32[512,128]{1,0:T(8,128)S(1)}, u32[]{:S(2)}, u32[]{:S(2)}) collective-permute-start(f32[512,128]{1,0:T(8,128)S(1)} %get-tuple-element.60), channel_id=1, source_target_pairs={{0,1},{1,0},{2,3},{3,2},{4,5},{5,4},{6,7},{7,6},{8,9},{9,8},{10,11... | collective-permute-start | bytes 786440 | tf_op jit(solution)/shard_map/ppermute | solution.py:174
  40.9 8.1 %collective-permute-start.17 = (f32[256,128]{1,0:T(8,128)S(1)}, f32[256,128]{1,0:T(8,128)S(1)}, u32[]{:S(2)}, u32[]{:S(2)}) collective-permute-start(f32[256,128]{1,0:T(8,128)S(1)} %get-tuple-element.58), channel_id=1, source_target_pairs={{0,2},{2,0},{4,6},{6,4},{1,3},{3,1},{5,7},{7,5},{8,10},{10,8},{12,... | collective-permute-start | bytes 393224 | tf_op jit(solution)/shard_map/ppermute | solution.py:174
  42.5 6.6 %collective-permute-start.18 = (f32[256,128]{1,0:T(8,128)S(1)}, f32[256,128]{1,0:T(8,128)S(1)}, u32[]{:S(2)}, u32[]{:S(2)}) collective-permute-start(f32[256,128]{1,0:T(8,128)S(1)} %get-tuple-element.59), channel_id=1, source_target_pairs={{2,4},{4,2},{3,5},{5,3},{10,12},{12,10},{11,13},{13,11},{18,20},{2... | collective-permute-start | bytes 393224 | tf_op jit(solution)/shard_map/ppermute | solution.py:174
  43.1 5.9 %collective-permute-start.15 = (f32[128,128]{1,0:T(8,128)S(1)}, f32[128,128]{1,0:T(8,128)S(1)}, u32[]{:S(2)}, u32[]{:S(2)}) collective-permute-start(f32[128,128]{1,0:T(8,128)S(1)} %get-tuple-element.56), channel_id=1, source_target_pairs={{0,8},{8,0},{16,24},{24,16},{1,9},{9,1},{17,25},{25,17},{2,10},{10... | collective-permute-start | bytes 196616 | tf_op jit(solution)/shard_map/ppermute | solution.py:174
  46.5 2.5 %collective-permute-start.16 = (f32[128,128]{1,0:T(8,128)S(1)}, f32[128,128]{1,0:T(8,128)S(1)}, u32[]{:S(2)}, u32[]{:S(2)}) collective-permute-start(f32[128,128]{1,0:T(8,128)S(1)} %get-tuple-element.57), channel_id=1, source_target_pairs={{8,16},{16,8},{9,17},{17,9},{10,18},{18,10},{11,19},{19,11},{12,20... | collective-permute-start | bytes 196616 | tf_op jit(solution)/shard_map/ppermute | solution.py:174
  51.5 12.5 %collective-permute-start.24 = (f32[512,128]{1,0:T(8,128)S(1)}, f32[512,128]{1,0:T(8,128)S(1)}, u32[]{:S(2)}, u32[]{:S(2)}) collective-permute-start(f32[512,128]{1,0:T(8,128)S(1)} %get-tuple-element.68.refs_4_), channel_id=1, source_target_pairs={{0,1},{1,0},{2,3},{3,2},{4,5},{5,4},{6,7},{7,6},{8,9},{9,8},{10,11... | collective-permute-start | bytes 786440 | tf_op jit(solution)/shard_map/ppermute | solution.py:174
  53.1 10.9 %collective-permute-start.22 = (f32[256,128]{1,0:T(8,128)S(1)}, f32[256,128]{1,0:T(8,128)S(1)}, u32[]{:S(2)}, u32[]{:S(2)}) collective-permute-start(f32[256,128]{1,0:T(8,128)S(1)} %get-tuple-element.66.refs_2_), channel_id=1, source_target_pairs={{0,2},{2,0},{4,6},{6,4},{1,3},{3,1},{5,7},{7,5},{8,10},{10,8},{12,... | collective-permute-start | bytes 393224 | tf_op jit(solution)/shard_map/ppermute | solution.py:174
  55.4 8.7 %collective-permute-start.23 = (f32[256,128]{1,0:T(8,128)S(1)}, f32[256,128]{1,0:T(8,128)S(1)}, u32[]{:S(2)}, u32[]{:S(2)}) collective-permute-start(f32[256,128]{1,0:T(8,128)S(1)} %get-tuple-element.67.refs_3_), channel_id=1, source_target_pairs={{2,4},{4,2},{3,5},{5,3},{10,12},{12,10},{11,13},{13,11},{18,20},{2... | collective-permute-start | bytes 393224 | tf_op jit(solution)/shard_map/ppermute | solution.py:174
  56.0 8.0 %collective-permute-start.20 = (f32[128,128]{1,0:T(8,128)S(1)}, f32[128,128]{1,0:T(8,128)S(1)}, u32[]{:S(2)}, u32[]{:S(2)}) collective-permute-start(f32[128,128]{1,0:T(8,128)S(1)} %get-tuple-element.64.refs_0_), channel_id=1, source_target_pairs={{0,8},{8,0},{16,24},{24,16},{1,9},{9,1},{17,25},{25,17},{2,10},{10... | collective-permute-start | bytes 196616 | tf_op jit(solution)/shard_map/ppermute | solution.py:174
  58.8 5.2 %collective-permute-start.21 = (f32[128,128]{1,0:T(8,128)S(1)}, f32[128,128]{1,0:T(8,128)S(1)}, u32[]{:S(2)}, u32[]{:S(2)}) collective-permute-start(f32[128,128]{1,0:T(8,128)S(1)} %get-tuple-element.65.refs_1_), channel_id=1, source_target_pairs={{8,16},{16,8},{9,17},{17,9},{10,18},{18,10},{11,19},{19,11},{12,20... | collective-permute-start | bytes 196616 | tf_op jit(solution)/shard_map/ppermute | solution.py:174
  65.1 3.5 %collective-permute-start.25 = (f32[136,128]{1,0:T(8,128)S(1)}, f32[136,128]{1,0:T(8,128)S(1)}, u32[]{:S(2)}, u32[]{:S(2)}) collective-permute-start(f32[136,128]{1,0:T(8,128)S(1)} %shard_map.51), channel_id=1, source_target_pairs={{0,2},{2,0},{4,6},{6,4},{1,3},{3,1},{5,7},{7,5},{8,10},{10,8},{12,... | collective-permute-start | bytes 208904 | tf_op jit(solution)/shard_map/ppermute | solution.py:259
  68.6 4.5 %collective-permute-start.26 = (f32[136,128]{1,0:T(8,128)S(1)}, f32[136,128]{1,0:T(8,128)S(1)}, u32[]{:S(2)}, u32[]{:S(2)}) collective-permute-start(f32[136,128]{1,0:T(8,128)S(1)} %add.15), channel_id=1, source_target_pairs={{0,4},{2,6},{4,0},{6,2},{1,5},{3,7},{5,1},{7,3},{8,12},{10,14},{12... | collective-permute-start | bytes 208904 | tf_op jit(solution)/shard_map/ppermute | solution.py:259
  73.1 4.4 %collective-permute-start.27 = (f32[136,128]{1,0:T(8,128)S(1)}, f32[136,128]{1,0:T(8,128)S(1)}, u32[]{:S(2)}, u32[]{:S(2)}) collective-permute-start(f32[136,128]{1,0:T(8,128)S(1)} %add.16), channel_id=1, source_target_pairs={{0,1},{1,0},{2,3},{3,2},{4,5},{5,4},{6,7},{7,6},{8,9},{9,8},{10,11... | collective-permute-start | bytes 208904 | tf_op jit(solution)/shard_map/ppermute | solution.py:259
  77.5 5.1 %collective-permute-start.28 = (f32[136,128]{1,0:T(8,128)S(1)}, f32[136,128]{1,0:T(8,128)S(1)}, u32[]{:S(2)}, u32[]{:S(2)}) collective-permute-start(f32[136,128]{1,0:T(8,128)S(1)} %add.17), channel_id=1, source_target_pairs={{0,8},{8,0},{16,24},{24,16},{1,9},{9,1},{17,25},{25,17},{2,10},{10... | collective-permute-start | bytes 208904 | tf_op jit(solution)/shard_map/ppermute | solution.py:259
  82.6 5.3 %collective-permute-start.29 = (f32[136,128]{1,0:T(8,128)S(1)}, f32[136,128]{1,0:T(8,128)S(1)}, u32[]{:S(2)}, u32[]{:S(2)}) collective-permute-start(f32[136,128]{1,0:T(8,128)S(1)} %add.18), channel_id=1, source_target_pairs={{0,16},{8,24},{16,0},{24,8},{1,17},{9,25},{17,1},{25,9},{2,18},{10... | collective-permute-start | bytes 208904 | tf_op jit(solution)/shard_map/ppermute | solution.py:259

commit v4 on v3

--- a/solution.py
+++ b/solution.py
@@ -40,18 +40,16 @@
         self.cells = self.x * self.row
 
 
-def faces_of(s, at, w_ref, out, x):
-    for i in range(out["nz"]):
-        out["z"][i][pl.ds(x * s.y, s.y), :] = w_ref[
-            pl.ds(x * s.row + at[4 + i], s.y, stride=s.z), :
-        ]
-    for i in range(2):
-        out["y"][i][pl.ds(x * s.z, s.z), :] = w_ref[pl.ds(x * s.row + at[2 + i] * s.z, s.z), :]
-
-
-def x_faces(s, at, w_ref, out):
+def faces_of(s, at, w_ref, out, with_z=True):
+    if with_z:
+        for i in range(out["nz"]):
+            out["z"][i][...] = w_ref[pl.ds(at[4 + i], s.x * s.y, stride=s.z), :]
     for i in range(2):
         out["x"][i][...] = w_ref[pl.ds(at[i] * s.row, s.row), :]
+        for x in range(s.x):
+            out["y"][i][pl.ds(x * s.z, s.z), :] = w_ref[
+                pl.ds(x * s.row + at[2 + i] * s.z, s.z), :
+            ]
 
 
 def face_shapes(s, nz):
@@ -64,21 +62,53 @@
     return {"x": refs[0:2], "y": refs[2:4], "z": refs[4 : 4 + nz], "nz": nz}
 
 
-def prepare(block, wide, at, s, nz):
-    def body(at_ref, b_ref, k_ref, w_ref, *faces):
-        out = split_faces(faces, nz)
-
-        def step(x, _):
-            here = pl.ds(pl.multiple_of(x * s.row, s.row), s.row)
-            w_ref[here, :] = jnp.sqrt(k_ref[here, :]) * b_ref[here, :]
-            faces_of(s, at_ref, w_ref, out, x)
-            return 0
-
-        lax.fori_loop(0, s.x, step, 0)
-        x_faces(s, at_ref, w_ref, out)
-
-    outs = [f32(s.cells, s.k)] + face_shapes(s, nz)
-    return call(body, outs, [at, block, wide], 4 * s.cells * s.k)
+def prepare(block, turned, at, s, nz):
+    parts = 4
+    rows = s.cells // parts
+
+    def body(at_ref, b_hbm, k_ref, w_ref, wide_ref, *refs):
+        out = split_faces(refs[: 4 + nz], nz)
+        edge = refs[4 + nz : 4 + 2 * nz]
+        b_ref, sems = refs[-2:]
+        copies = []
+        for i in range(parts):
+            here = pl.ds(i * rows, rows)
+            copies.append(pltpu.make_async_copy(b_hbm.at[here], b_ref.at[here], sems.at[i]))
+            copies[-1].start()
+        tiles = [k_ref[y] for y in range(s.y)]
+        for x in range(s.x):
+            for y in range(s.y):
+                wide_ref[pl.ds(x * s.row + y * s.z, s.z), :] = jnp.broadcast_to(
+                    tiles[y][:, x : x + 1], (s.z, s.k)
+                )
+        for i in range(parts):
+            copies[i].wait()
+
+            def step(x, _):
+                here = pl.ds(pl.multiple_of(x * s.row, s.row), s.row)
+                w_ref[here, :] = jnp.sqrt(wide_ref[here, :]) * b_ref[here, :]
+                return 0
+
+            lax.fori_loop(i * s.x // parts, (i + 1) * s.x // parts, step, 0, unroll=2)
+        for i in range(nz):
+            edge[i][...] = wide_ref[pl.ds(at_ref[4 + i], s.x * s.y, stride=s.z), :]
+        faces_of(s, at_ref, w_ref, out)
+
+    outs = [f32(s.cells, s.k)] * 2 + face_shapes(s, nz) + [f32(s.x * s.y, s.k)] * nz
+    return pl.pallas_call(
+        body,
+        out_shape=outs,
+        in_specs=[SMEM, pl.BlockSpec(memory_space=pl.ANY), VMEM],
+        out_specs=tuple(VMEM for _ in outs),
+        scratch_shapes=[
+            pltpu.VMEM((s.cells, s.k), jnp.float32),
+            pltpu.SemaphoreType.DMA((parts,)),
+        ],
+        compiler_params=pltpu.CompilerParams(vmem_limit_bytes=32 * 1024 * 1024),
+        cost_estimate=pl.CostEstimate(
+            flops=4 * s.cells * s.k, bytes_accessed=16 * s.cells * s.k, transcendentals=0
+        ),
+    )(at, block, turned)
 
 
 def around(s, w_ref, x, low, high, emit):
@@ -130,38 +160,33 @@
     return call(body, [f32(s.cells, s.k)], ins, 12 * s.cells * s.k)[0]
 
 
-def finish(part, wide, ghosts, at, s, nz, scale):
+def finish(part, wide, edge, ghosts, at, s, nz, scale):
     def body(at_ref, p_ref, k_ref, *refs):
-        ghost = split_faces(refs[: 4 + nz], nz)
-        w_ref = refs[4 + nz]
-        out = split_faces(refs[5 + nz :], nz)
+        del p_ref
+        edges = refs[:nz]
+        ghost = split_faces(refs[nz : 4 + 2 * nz], nz)
+        w_ref = refs[4 + 2 * nz]
+        out = split_faces(refs[5 + 2 * nz :], nz)
         factor = scale / 6.0
         for i in range(2):
             here = pl.ds(at_ref[i] * s.row, s.row)
-            p_ref[here, :] = p_ref[here, :] - (k_ref[here, :] * factor) * ghost["x"][i][...]
-        place = lax.broadcasted_iota(jnp.int32, (s.z, s.k), 0)
-
-        def step(x, _):
-            base = pl.multiple_of(x * s.row, s.row)
-            for i in range(2):
-                here = pl.ds(base + at_ref[2 + i] * s.z, s.z)
+            w_ref[here, :] = w_ref[here, :] - (k_ref[here, :] * factor) * ghost["x"][i][...]
+            for x in range(s.x):
+                here = pl.ds(x * s.row + at_ref[2 + i] * s.z, s.z)
                 g = ghost["y"][i][pl.ds(x * s.z, s.z), :]
-                p_ref[here, :] = p_ref[here, :] - (k_ref[here, :] * factor) * g
-            for y in range(s.y):
-                here = pl.ds(base + y * s.z, s.z)
-                add = 0.0
-                for i in range(nz):
-                    g = ghost["z"][i][pl.ds(x * s.y + y, 1), :]
-                    add = jnp.where(place == at_ref[4 + i], jnp.broadcast_to(g, (s.z, s.k)), add)
-                w_ref[here, :] = p_ref[here, :] - (k_ref[here, :] * factor) * add
-            faces_of(s, at_ref, w_ref, out, x)
-            return 0
-
-        lax.fori_loop(0, s.x, step, 0)
-        x_faces(s, at_ref, w_ref, out)
+                w_ref[here, :] = w_ref[here, :] - (k_ref[here, :] * factor) * g
+        for i in range(nz):
+            for x in range(s.x):
+                here = pl.ds(x * s.row + at_ref[4 + i], s.y, stride=s.z)
+                flat = pl.ds(x * s.y, s.y)
+                new = w_ref[here, :] - (edges[i][flat, :] * factor) * ghost["z"][i][flat, :]
+                w_ref[here, :] = new
+                out["z"][i][flat, :] = new
+        faces_of(s, at_ref, w_ref, out, with_z=False)
 
     outs = [f32(s.cells, s.k)] + face_shapes(s, nz)
-    return call(body, outs, [at, part, wide] + list(ghosts), 4 * s.cells * s.k, {1: 0})
+    ins = [at, part, wide] + list(edge) + list(ghosts)
+    return call(body, outs, ins, 4 * s.x * s.y * s.k, {1: 0})
 
 
 def exchange(faces, axes):
@@ -187,34 +212,31 @@
     return jnp.concatenate([high, low], axis=1)
 
 
-def both(left, right):
-    k = left.shape[1] // 2
-    full = transposed_dot(left, right)
+def both(full):
+    k = full.shape[0] // 2
     return full[:k, :k] + (full[:k, k:] + full[k:, :k]) + full[k:, k:]
 
 
 def gather_terms(w, wide, at, s):
-    rows = 4 * s.row
+    rows = s.cells // 4
 
     def body(at_ref, w_ref, k_ref, f_ref, g_ref, m_ref, q_ref):
         def emit(here, c, near):
             q_ref[here, :] = c - near * (1.0 / 6.0)
 
         sweep(s, w_ref, emit)
-        g_ref[...] = jnp.zeros_like(g_ref)
-        m_ref[...] = jnp.zeros_like(m_ref)
-
-        def step(i, _):
-            here = pl.ds(pl.multiple_of(i * rows, rows), rows)
-            w = w_ref[here, :]
-            f = w * lax.rsqrt(k_ref[here, :])
+        sums = jnp.zeros((2 * s.k, 4 * s.k), jnp.float32)
+        for i in range(s.cells // rows):
+            here = pl.ds(i * rows, rows)
+            k = k_ref[here, :]
+            inverse = lax.rsqrt(k)
+            f = w_ref[here, :] * inverse
             f_ref[here, :] = f
             pair = two(f)
-            g_ref[...] += both(pair, pair)
-            m_ref[...] += both(two(w), two(q_ref[here, :]))
-            return 0
-
-        lax.fori_loop(0, s.cells // rows, step, 0)
+            image = two((k * inverse) * q_ref[here, :])
+            sums += transposed_dot(pair, jnp.concatenate([pair, image], axis=1))
+        g_ref[...] = both(sums[:, : 2 * s.k])
+        m_ref[...] = both(sums[:, 2 * s.k :])
 
     outs = [f32(s.cells, s.k), f32(s.k, s.k), f32(s.k, s.k)]
     moved = 4 * 4 * s.cells * s.k
@@ -238,7 +260,7 @@
         n = len(faces)
         m = jnp.zeros((k, k), jnp.float32)
         for left, right in zip(refs[:n], refs[n : 2 * n]):
-            m += both(two(left[...]), two(right[...]))
+            m += both(transposed_dot(two(left[...]), two(right[...])))
         m = m_ref[...] - m * (1.0 / 6.0)
         raw = (m + m.T) * (0.5 / cells)
         below = lax.broadcasted_iota(jnp.int32, (k, k), 0)
@@ -357,15 +379,16 @@
     axes = [("gx", 0), ("gx", 1), ("gy", 0), ("gy", 1), ("gz", 0), ("gz", 1)][: 4 + nz]
 
     flat = block.reshape(s.cells, s.k)
-    wide = jnp.broadcast_to(conductivity[..., None], block.shape).reshape(s.cells, s.k)
-    w, *faces = prepare(flat, wide, at, s, nz)
+    turned = jnp.transpose(conductivity, (1, 2, 0))
+    w, wide, *rest = prepare(flat, turned, at, s, nz)
+    faces, edge = rest[: 4 + nz], rest[4 + nz :]
     before = None
     for step in range(DEG):
         ghosts = exchange(faces, axes)
         part = interior(w, before, wide, at, s)
         scale = (1.0 if before is None else 2.0) / half_value
         before = w
-        w, *faces = finish(part, wide, ghosts, at, s, nz, scale)
+        w, *faces = finish(part, wide, edge, ghosts, at, s, nz, scale)
     ghosts = exchange(faces, axes)
     filtered, gram, own = gather_terms(w, wide, at, s)
     packed = total(pack_terms(gram, own, faces, ghosts, at, s, cells), ("gy", "gz", "gx"))

time: 96.7 us -> 90 us (0.931)
  Pallas kernels: 32.6 us -> 25.1 us
    pallas_call x10 -> x9, Pallas kernels: 19.7 us -> 11.6 us  [call(): pl.pallas_call(body, out_shape=outs, in_specs=[SMEM] + [VMEM] * (len(ins)...]
    pallas_call x0 -> x1, Pallas kernels: none -> 2.24 us  [prepare(): pl.pallas_call(body, out_shape=outs, in_specs=[SMEM, pl.BlockSpec(memory_...]
    pallas_call x1, Pallas kernels: 4.49 us -> 2.83 us  [gather_terms(): pl.pallas_call(body, out_shape=outs, in_specs=[SMEM, VMEM, VMEM], out_spe...]
    unnamed x3 -> x4, local copies, waits for them, and re-layouts: 1.15 us -> 2.43 us
  transfers between devices with their start and end apart: 30 -> 30, of which waited for: 8 -> 8; matrix products, arithmetic and copies ran while one was open for 0% -> 0% of each run, Pallas kernels for 12% -> 11%
where the time goes in v4:
time: 90 us; the launch traced here: 89.5 us
  starting transfers between devices  45.1 us (50%)
  Pallas kernels  25.1 us (28%)
  waiting for transfers between devices  15.7 us (17%)
  local copies, waits for them, and re-layouts  2.52 us (3%)
  between operations  1 us (1%)
    ppermute x25, starting transfers between devices, exchange(): got.append(lax.ppermute(face, axis, pairs))  36.3 us
    ppermute x5, waiting for transfers between devices, total(): lax.ppermute(value, axis, [(i, i ^ bit) for i in range(count)])  13.8 us
    pallas_call x9, Pallas kernels, call(): pl.pallas_call(body, out_shape=outs, in_specs=[SMEM] + [VMEM] * (len(ins)...  11.6 us
    ppermute x5, starting transfers between devices, total(): lax.ppermute(value, axis, [(i, i ^ bit) for i in range(count)])  8.84 us
    pallas_call x1, Pallas kernels, orthonormal(): pl.pallas_call(body, grid=(8,), out_shape=[f32(s.cells, k), f32(k, k)], i...  8.43 us
    pallas_call x1, Pallas kernels, gather_terms(): pl.pallas_call(body, out_shape=outs, in_specs=[SMEM, VMEM, VMEM], out_spe...  2.83 us
    unnamed x4, local copies, waits for them, and re-layouts  2.43 us
    pallas_call x1, Pallas kernels, prepare(): pl.pallas_call(body, out_shape=outs, in_specs=[SMEM, pl.BlockSpec(memory_...  2.24 us
  transfers between devices with their start and end apart: 30, of which 8 were waited for; matrix products, arithmetic and copies ran while one was open for 0% of the time, Pallas kernels for 11%

profile of v4, /device:TPU:0, one launch (start us, length us, event | category | flops | bytes accessed | tf_op | source)
XLA Modules:
  0.0 89.5 jit_solution(14354896368026720482)
XLA Ops:
  0.7 1.6 %copy-done = f32[32,16,8,128]{3,2,1,0:T(8,128)S(1)} copy-done((f32[32,16,8,128]{3,2,1,0:T(8,128)S(1)}, f32[32,16,8,128]{3,2,1,0:T(8,128)}, u32[]{:S(2)}) %copy-start) | copy-done | bytes 2097176
  2.3 0.8 copy-done.1
  3.2 2.2 %shard_map.41 = (f32[4096,128]{1,0:T(8,128)S(1)}, f32[4096,128]{1,0:T(8,128)S(1)}, f32[128,128]{1,0:T(8,128)S(1)}, f32[128,128]{1,0:T(8,128)S(1)}, f32[256,128]{...) custom-call(s32[6]{0:T(128)S(1)} %stack.27.at_ref, ...), custom_call_target="tpu_custom_call" | custom-call | flops 2097152 | bytes 8388608 | tf_op jit(solution)/shard_map/pallas_call | solution.py:98
  5.4 3.0 %collective-permute-start.4 = (f32[512,128]{1,0:T(8,128)S(1)}, f32[512,128]{1,0:T(8,128)S(1)}, u32[]{:S(2)}, u32[]{:S(2)}) collective-permute-start(f32[512,128]{1,0:T(8,128)S(1)} %get-tuple-element.46), channel_id=1, source_target_pairs={{0,1},{1,0},{2,3},{3,2},{4,5},{5,4},{6,7},{7,6},{8,9},{9,8},{10,11... | collective-permute-start | bytes 786440 | tf_op jit(solution)/shard_map/ppermute | solution.py:199
  9.1 1.6 %collective-permute-start = (f32[128,128]{1,0:T(8,128)S(1)}, f32[128,128]{1,0:T(8,128)S(1)}, u32[]{:S(2)}, u32[]{:S(2)}) collective-permute-start(f32[128,128]{1,0:T(8,128)S(1)} %get-tuple-element.42), channel_id=1, source_target_pairs={{0,8},{8,0},{16,24},{24,16},{1,9},{9,1},{17,25},{25,17},{2,10},{10... | collective-permute-start | bytes 196616 | tf_op jit(solution)/shard_map/ppermute | solution.py:199
  11.4 1.8 %shard_map.42.p_ref = f32[4096,128]{1,0:T(8,128)S(1)} custom-call(s32[6]{0:T(128)S(1)} %stack.27.at_ref, f32[4096,128]{1,0:T(8,128)S(1)} %get-tuple-element.39.w_ref.rest_0_, f32[4096,128]{1,0:T(8,128)S(1)} %get-tuple-element.40.k_ref), custom_call_target="tpu_custom_call" | custom-call | flops 6291456 | bytes 6291480 | tf_op jit(solution)/shard_map/pallas_call | solution.py:21
  13.4 1.3 %collective-permute-done.4.refs_5_ = f32[512,128]{1,0:T(8,128)S(1)} collective-permute-done((f32[512,128]{1,0:T(8,128)S(1)}, f32[512,128]{1,0:T(8,128)S(1)}, u32[]{:S(2)}, u32[]{:S(2)}) %collective-permute-start.4) | collective-permute-done | bytes 262176 | tf_op jit(solution)/shard_map/ppermute | solution.py:199
  15.6 1.8 %collective-permute-start.9 = (f32[512,128]{1,0:T(8,128)S(1)}, f32[512,128]{1,0:T(8,128)S(1)}, u32[]{:S(2)}, u32[]{:S(2)}) collective-permute-start(f32[512,128]{1,0:T(8,128)S(1)} %get-tuple-element.52), channel_id=1, source_target_pairs={{0,1},{1,0},{2,3},{3,2},{4,5},{5,4},{6,7},{7,6},{8,9},{9,8},{10,11... | collective-permute-start | bytes 786440 | tf_op jit(solution)/shard_map/ppermute | solution.py:199
  18.0 3.8 %collective-permute-start.5 = (f32[128,128]{1,0:T(8,128)S(1)}, f32[128,128]{1,0:T(8,128)S(1)}, u32[]{:S(2)}, u32[]{:S(2)}) collective-permute-start(f32[128,128]{1,0:T(8,128)S(1)} %get-tuple-element.48), channel_id=1, source_target_pairs={{0,8},{8,0},{16,24},{24,16},{1,9},{9,1},{17,25},{25,17},{2,10},{10... | collective-permute-start | bytes 196616 | tf_op jit(solution)/shard_map/ppermute | solution.py:199
  22.5 1.8 %shard_map.44.p_ref = f32[4096,128]{1,0:T(8,128)S(1)} custom-call(s32[6]{0:T(128)S(1)} %stack.27.at_ref, f32[4096,128]{1,0:T(8,128)S(1)} %get-tuple-element.47.w_ref.rest_0_, f32[4096,128]{1,0:T(8,128)S(1)} %get-tuple-element.40.k_ref, f32[4096,128]{1,0:T(8,128)S(1)} %get-tuple-element.39.w_ref.rest_0_), custom_call_target="tpu_custom_call" | custom-call | flops 6291456 | bytes 8388632 | tf_op jit(solution)/shard_map/pallas_call | solution.py:21
  25.5 1.3 %collective-permute-start.14 = (f32[512,128]{1,0:T(8,128)S(1)}, f32[512,128]{1,0:T(8,128)S(1)}, u32[]{:S(2)}, u32[]{:S(2)}) collective-permute-start(f32[512,128]{1,0:T(8,128)S(1)} %get-tuple-element.58), channel_id=1, source_target_pairs={{0,1},{1,0},{2,3},{3,2},{4,5},{5,4},{6,7},{7,6},{8,9},{9,8},{10,11... | collective-permute-start | bytes 786440 | tf_op jit(solution)/shard_map/ppermute | solution.py:199
  26.8 2.6 %collective-permute-start.12 = (f32[256,128]{1,0:T(8,128)S(1)}, f32[256,128]{1,0:T(8,128)S(1)}, u32[]{:S(2)}, u32[]{:S(2)}) collective-permute-start(f32[256,128]{1,0:T(8,128)S(1)} %get-tuple-element.56), channel_id=1, source_target_pairs={{0,2},{2,0},{4,6},{6,4},{1,3},{3,1},{5,7},{7,5},{8,10},{10,8},{12,... | collective-permute-start | bytes 393224 | tf_op jit(solution)/shard_map/ppermute | solution.py:199
  30.0 3.3 %collective-permute-start.10 = (f32[128,128]{1,0:T(8,128)S(1)}, f32[128,128]{1,0:T(8,128)S(1)}, u32[]{:S(2)}, u32[]{:S(2)}) collective-permute-start(f32[128,128]{1,0:T(8,128)S(1)} %get-tuple-element.54), channel_id=1, source_target_pairs={{0,8},{8,0},{16,24},{24,16},{1,9},{9,1},{17,25},{25,17},{2,10},{10... | collective-permute-start | bytes 196616 | tf_op jit(solution)/shard_map/ppermute | solution.py:199
  34.0 1.8 %shard_map.46.p_ref = f32[4096,128]{1,0:T(8,128)S(1)} custom-call(s32[6]{0:T(128)S(1)} %stack.27.at_ref, f32[4096,128]{1,0:T(8,128)S(1)} %get-tuple-element.53.w_ref.rest_0_, f32[4096,128]{1,0:T(8,128)S(1)} %get-tuple-element.40.k_ref, f32[4096,128]{1,0:T(8,128)S(1)} %get-tuple-element.47.w_ref.rest_0_), custom_call_target="tpu_custom_call" | custom-call | flops 6291456 | bytes 8388632 | tf_op jit(solution)/shard_map/pallas_call | solution.py:21
  37.4 1.6 %collective-permute-start.17 = (f32[256,128]{1,0:T(8,128)S(1)}, f32[256,128]{1,0:T(8,128)S(1)}, u32[]{:S(2)}, u32[]{:S(2)}) collective-permute-start(f32[256,128]{1,0:T(8,128)S(1)} %get-tuple-element.62), channel_id=1, source_target_pairs={{0,2},{2,0},{4,6},{6,4},{1,3},{3,1},{5,7},{7,5},{8,10},{10,8},{12,... | collective-permute-start | bytes 393224 | tf_op jit(solution)/shard_map/ppermute | solution.py:199
  39.6 3.3 %collective-permute-start.15 = (f32[128,128]{1,0:T(8,128)S(1)}, f32[128,128]{1,0:T(8,128)S(1)}, u32[]{:S(2)}, u32[]{:S(2)}) collective-permute-start(f32[128,128]{1,0:T(8,128)S(1)} %get-tuple-element.60), channel_id=1, source_target_pairs={{0,8},{8,0},{16,24},{24,16},{1,9},{9,1},{17,25},{25,17},{2,10},{10... | collective-permute-start | bytes 196616 | tf_op jit(solution)/shard_map/ppermute | solution.py:199
  43.6 1.8 %shard_map.48.p_ref = f32[4096,128]{1,0:T(8,128)S(1)} custom-call(s32[6]{0:T(128)S(1)} %stack.27.at_ref, f32[4096,128]{1,0:T(8,128)S(1)} %get-tuple-element.59.w_ref, f32[4096,128]{1,0:T(8,128)S(1)} %get-tuple-element.40.k_ref, f32[4096,128]{1,0:T(8,128)S(1)} %get-tuple-element.53.w_ref.rest_0_), custom_call_target="tpu_custom_call" | custom-call | flops 6291456 | bytes 8388632 | tf_op jit(solution)/shard_map/pallas_call | solution.py:21
  46.4 1.6 %collective-permute-start.24 = (f32[512,128]{1,0:T(8,128)S(1)}, f32[512,128]{1,0:T(8,128)S(1)}, u32[]{:S(2)}, u32[]{:S(2)}) collective-permute-start(f32[512,128]{1,0:T(8,128)S(1)} %get-tuple-element.72.refs_4_), channel_id=1, source_target_pairs={{0,1},{1,0},{2,3},{3,2},{4,5},{5,4},{6,7},{7,6},{8,9},{9,8},{10,11... | collective-permute-start | bytes 786440 | tf_op jit(solution)/shard_map/ppermute | solution.py:199
  47.9 2.4 %collective-permute-start.22 = (f32[256,128]{1,0:T(8,128)S(1)}, f32[256,128]{1,0:T(8,128)S(1)}, u32[]{:S(2)}, u32[]{:S(2)}) collective-permute-start(f32[256,128]{1,0:T(8,128)S(1)} %get-tuple-element.70.refs_2_), channel_id=1, source_target_pairs={{0,2},{2,0},{4,6},{6,4},{1,3},{3,1},{5,7},{7,5},{8,10},{10,8},{12,... | collective-permute-start | bytes 393224 | tf_op jit(solution)/shard_map/ppermute | solution.py:199
  51.0 2.8 %collective-permute-start.20 = (f32[128,128]{1,0:T(8,128)S(1)}, f32[128,128]{1,0:T(8,128)S(1)}, u32[]{:S(2)}, u32[]{:S(2)}) collective-permute-start(f32[128,128]{1,0:T(8,128)S(1)} %get-tuple-element.68.refs_0_), channel_id=1, source_target_pairs={{0,8},{8,0},{16,24},{24,16},{1,9},{9,1},{17,25},{25,17},{2,10},{10... | collective-permute-start | bytes 196616 | tf_op jit(solution)/shard_map/ppermute | solution.py:199
  54.5 2.8 %shard_map.50 = (f32[4096,128]{1,0:T(8,128)S(1)}, f32[128,128]{1,0:T(8,128)S(1)}, f32[128,128]{1,0:T(8,128)S(1)}) custom-call(s32[6]{0:T(128)S(1)} %stack.27.at_ref, f32[4096,128]{1,0:T(8,128)S(1)} %get-tuple-element.65.w_ref, f32[4096,128]{1,0:T(8,128)S(1)} %get-tuple-element.40.k_ref), custom_call_target="tpu_custom_call" | custom-call | flops 1073741824 | bytes 8388608 | tf_op jit(solution)/shard_map/pallas_call | solution.py:243
  57.4 1.0 %shard_map.51 = f32[136,128]{1,0:T(8,128)S(1)} custom-call(s32[6]{0:T(128)S(1)} %stack.27.at_ref, f32[128,128]{1,0:T(8,128)S(1)} %get-tuple-element.66.g_ref, f32[128,128]{1,0:T(8,128)S(1)} %get-tuple-element.67.m_ref, f32[128,128]{1,0:T(8,128)S(1)} %get-tuple-element.68.refs_0_, f32[128,128]{1,0:T(8,128)S(1)} %get-tuple-element.69.refs_1_, ...), custom_call_target="tpu_custom_call" | custom-call | flops 3145728 | bytes 1511448 | tf_op jit(solution)/shard_map/pallas_call | solution.py:21
  58.4 2.5 %collective-permute-start.25 = (f32[136,128]{1,0:T(8,128)S(1)}, f32[136,128]{1,0:T(8,128)S(1)}, u32[]{:S(2)}, u32[]{:S(2)}) collective-permute-start(f32[136,128]{1,0:T(8,128)S(1)} %shard_map.51), channel_id=1, source_target_pairs={{0,2},{2,0},{4,6},{6,4},{1,3},{3,1},{5,7},{7,5},{8,10},{10,8},{12,... | collective-permute-start | bytes 208904 | tf_op jit(solution)/shard_map/ppermute | solution.py:281
  60.9 0.9 %collective-permute-done.25 = f32[136,128]{1,0:T(8,128)S(1)} collective-permute-done((f32[136,128]{1,0:T(8,128)S(1)}, f32[136,128]{1,0:T(8,128)S(1)}, u32[]{:S(2)}, u32[]{:S(2)}) %collective-permute-start.25) | collective-permute-done | bytes 69664 | tf_op jit(solution)/shard_map/ppermute | solution.py:281
  61.8 0.9 collective-permute-start.26
  62.7 3.6 %collective-permute-done.26 = f32[136,128]{1,0:T(8,128)S(1)} collective-permute-done((f32[136,128]{1,0:T(8,128)S(1)}, f32[136,128]{1,0:T(8,128)S(1)}, u32[]{:S(2)}, u32[]{:S(2)}) %collective-permute-start.26) | collective-permute-done | bytes 69664 | tf_op jit(solution)/shard_map/ppermute | solution.py:281
  66.9 3.8 %collective-permute-done.27 = f32[136,128]{1,0:T(8,128)S(1)} collective-permute-done((f32[136,128]{1,0:T(8,128)S(1)}, f32[136,128]{1,0:T(8,128)S(1)}, u32[]{:S(2)}, u32[]{:S(2)}) %collective-permute-start.27) | collective-permute-done | bytes 69664 | tf_op jit(solution)/shard_map/ppermute | solution.py:281
  70.7 2.8 %collective-permute-start.28 = (f32[136,128]{1,0:T(8,128)S(1)}, f32[136,128]{1,0:T(8,128)S(1)}, u32[]{:S(2)}, u32[]{:S(2)}) collective-permute-start(f32[136,128]{1,0:T(8,128)S(1)} %add.17), channel_id=1, source_target_pairs={{0,8},{8,0},{16,24},{24,16},{1,9},{9,1},{17,25},{25,17},{2,10},{10... | collective-permute-start | bytes 208904 | tf_op jit(solution)/shard_map/ppermute | solution.py:281
  73.5 2.3 %collective-permute-done.28 = f32[136,128]{1,0:T(8,128)S(1)} collective-permute-done((f32[136,128]{1,0:T(8,128)S(1)}, f32[136,128]{1,0:T(8,128)S(1)}, u32[]{:S(2)}, u32[]{:S(2)}) %collective-permute-start.28) | collective-permute-done | bytes 69664 | tf_op jit(solution)/shard_map/ppermute | solution.py:281
  75.8 2.1 %collective-permute-start.29 = (f32[136,128]{1,0:T(8,128)S(1)}, f32[136,128]{1,0:T(8,128)S(1)}, u32[]{:S(2)}, u32[]{:S(2)}) collective-permute-start(f32[136,128]{1,0:T(8,128)S(1)} %add.18), channel_id=1, source_target_pairs={{0,16},{8,24},{16,0},{24,8},{1,17},{9,25},{17,1},{25,9},{2,18},{10... | collective-permute-start | bytes 208904 | tf_op jit(solution)/shard_map/ppermute | solution.py:281
  77.9 3.2 %collective-permute-done.29 = f32[136,128]{1,0:T(8,128)S(1)} collective-permute-done((f32[136,128]{1,0:T(8,128)S(1)}, f32[136,128]{1,0:T(8,128)S(1)}, u32[]{:S(2)}, u32[]{:S(2)}) %collective-permute-start.29) | collective-permute-done | bytes 69664 | tf_op jit(solution)/shard_map/ppermute | solution.py:281
  81.1 8.4 %shard_map.52 = (f32[4096,128]{1,0:T(8,128)}, f32[128,128]{1,0:T(8,128)}) custom-call(f32[136,128]{1,0:T(8,128)S(1)} %add.19.p_ref, f32[4096,128]{1,0:T(8,128)S(1)} %get-tuple-element.73.f_ref), custom_call_target="tpu_custom_call" | custom-call | flops 536870912 | bytes 4194304 | tf_op jit(solution)/shard_map/pallas_call | solution.py:352
  (50 shorter events, 11.9 us)
Async XLA Ops:
  0.7 1.6 %copy-start = (f32[32,16,8,128]{3,2,1,0:T(8,128)S(1)}, f32[32,16,8,128]{3,2,1,0:T(8,128)}, u32[]{:S(2)}) copy-start(f32[32,16,8,128]{3,2,1,0:T(8,128)} %param.2) | copy-start | bytes 6291460
  2.3 0.8 copy-start.1
  5.4 9.3 %collective-permute-start.4 = (f32[512,128]{1,0:T(8,128)S(1)}, f32[512,128]{1,0:T(8,128)S(1)}, u32[]{:S(2)}, u32[]{:S(2)}) collective-permute-start(f32[512,128]{1,0:T(8,128)S(1)} %get-tuple-element.46), channel_id=1, source_target_pairs={{0,1},{1,0},{2,3},{3,2},{4,5},{5,4},{6,7},{7,6},{8,9},{9,8},{10,11... | collective-permute-start | bytes 786440 | tf_op jit(solution)/shard_map/ppermute | solution.py:199
  8.4 5.0 %collective-permute-start.2 = (f32[256,128]{1,0:T(8,128)S(1)}, f32[256,128]{1,0:T(8,128)S(1)}, u32[]{:S(2)}, u32[]{:S(2)}) collective-permute-start(f32[256,128]{1,0:T(8,128)S(1)} %get-tuple-element.44), channel_id=1, source_target_pairs={{0,2},{2,0},{4,6},{6,4},{1,3},{3,1},{5,7},{7,5},{8,10},{10,8},{12,... | collective-permute-start | bytes 393224 | tf_op jit(solution)/shard_map/ppermute | solution.py:199
  8.4 5.0 %collective-permute-start.3 = (f32[256,128]{1,0:T(8,128)S(1)}, f32[256,128]{1,0:T(8,128)S(1)}, u32[]{:S(2)}, u32[]{:S(2)}) collective-permute-start(f32[256,128]{1,0:T(8,128)S(1)} %get-tuple-element.45), channel_id=1, source_target_pairs={{2,4},{4,2},{3,5},{5,3},{10,12},{12,10},{11,13},{13,11},{18,20},{2... | collective-permute-start | bytes 393224 | tf_op jit(solution)/shard_map/ppermute | solution.py:199
  9.1 4.3 %collective-permute-start = (f32[128,128]{1,0:T(8,128)S(1)}, f32[128,128]{1,0:T(8,128)S(1)}, u32[]{:S(2)}, u32[]{:S(2)}) collective-permute-start(f32[128,128]{1,0:T(8,128)S(1)} %get-tuple-element.42), channel_id=1, source_target_pairs={{0,8},{8,0},{16,24},{24,16},{1,9},{9,1},{17,25},{25,17},{2,10},{10... | collective-permute-start | bytes 196616 | tf_op jit(solution)/shard_map/ppermute | solution.py:199
  10.7 2.7 %collective-permute-start.1 = (f32[128,128]{1,0:T(8,128)S(1)}, f32[128,128]{1,0:T(8,128)S(1)}, u32[]{:S(2)}, u32[]{:S(2)}) collective-permute-start(f32[128,128]{1,0:T(8,128)S(1)} %get-tuple-element.43), channel_id=1, source_target_pairs={{8,16},{16,8},{9,17},{17,9},{10,18},{18,10},{11,19},{19,11},{12,20... | collective-permute-start | bytes 196616 | tf_op jit(solution)/shard_map/ppermute | solution.py:199
  15.6 9.1 %collective-permute-start.9 = (f32[512,128]{1,0:T(8,128)S(1)}, f32[512,128]{1,0:T(8,128)S(1)}, u32[]{:S(2)}, u32[]{:S(2)}) collective-permute-start(f32[512,128]{1,0:T(8,128)S(1)} %get-tuple-element.52), channel_id=1, source_target_pairs={{0,1},{1,0},{2,3},{3,2},{4,5},{5,4},{6,7},{7,6},{8,9},{9,8},{10,11... | collective-permute-start | bytes 786440 | tf_op jit(solution)/shard_map/ppermute | solution.py:199
  17.4 7.0 %collective-permute-start.7 = (f32[256,128]{1,0:T(8,128)S(1)}, f32[256,128]{1,0:T(8,128)S(1)}, u32[]{:S(2)}, u32[]{:S(2)}) collective-permute-start(f32[256,128]{1,0:T(8,128)S(1)} %get-tuple-element.50), channel_id=1, source_target_pairs={{0,2},{2,0},{4,6},{6,4},{1,3},{3,1},{5,7},{7,5},{8,10},{10,8},{12,... | collective-permute-start | bytes 393224 | tf_op jit(solution)/shard_map/ppermute | solution.py:199
  17.4 7.0 %collective-permute-start.8 = (f32[256,128]{1,0:T(8,128)S(1)}, f32[256,128]{1,0:T(8,128)S(1)}, u32[]{:S(2)}, u32[]{:S(2)}) collective-permute-start(f32[256,128]{1,0:T(8,128)S(1)} %get-tuple-element.51), channel_id=1, source_target_pairs={{2,4},{4,2},{3,5},{5,3},{10,12},{12,10},{11,13},{13,11},{18,20},{2... | collective-permute-start | bytes 393224 | tf_op jit(solution)/shard_map/ppermute | solution.py:199
  18.0 6.3 %collective-permute-start.5 = (f32[128,128]{1,0:T(8,128)S(1)}, f32[128,128]{1,0:T(8,128)S(1)}, u32[]{:S(2)}, u32[]{:S(2)}) collective-permute-start(f32[128,128]{1,0:T(8,128)S(1)} %get-tuple-element.48), channel_id=1, source_target_pairs={{0,8},{8,0},{16,24},{24,16},{1,9},{9,1},{17,25},{25,17},{2,10},{10... | collective-permute-start | bytes 196616 | tf_op jit(solution)/shard_map/ppermute | solution.py:199
  21.8 2.5 %collective-permute-start.6 = (f32[128,128]{1,0:T(8,128)S(1)}, f32[128,128]{1,0:T(8,128)S(1)}, u32[]{:S(2)}, u32[]{:S(2)}) collective-permute-start(f32[128,128]{1,0:T(8,128)S(1)} %get-tuple-element.49), channel_id=1, source_target_pairs={{8,16},{16,8},{9,17},{17,9},{10,18},{18,10},{11,19},{19,11},{12,20... | collective-permute-start | bytes 196616 | tf_op jit(solution)/shard_map/ppermute | solution.py:199
  25.5 10.4 %collective-permute-start.14 = (f32[512,128]{1,0:T(8,128)S(1)}, f32[512,128]{1,0:T(8,128)S(1)}, u32[]{:S(2)}, u32[]{:S(2)}) collective-permute-start(f32[512,128]{1,0:T(8,128)S(1)} %get-tuple-element.58), channel_id=1, source_target_pairs={{0,1},{1,0},{2,3},{3,2},{4,5},{5,4},{6,7},{7,6},{8,9},{9,8},{10,11... | collective-permute-start | bytes 786440 | tf_op jit(solution)/shard_map/ppermute | solution.py:199
  26.8 9.1 %collective-permute-start.12 = (f32[256,128]{1,0:T(8,128)S(1)}, f32[256,128]{1,0:T(8,128)S(1)}, u32[]{:S(2)}, u32[]{:S(2)}) collective-permute-start(f32[256,128]{1,0:T(8,128)S(1)} %get-tuple-element.56), channel_id=1, source_target_pairs={{0,2},{2,0},{4,6},{6,4},{1,3},{3,1},{5,7},{7,5},{8,10},{10,8},{12,... | collective-permute-start | bytes 393224 | tf_op jit(solution)/shard_map/ppermute | solution.py:199
  29.3 6.6 %collective-permute-start.13 = (f32[256,128]{1,0:T(8,128)S(1)}, f32[256,128]{1,0:T(8,128)S(1)}, u32[]{:S(2)}, u32[]{:S(2)}) collective-permute-start(f32[256,128]{1,0:T(8,128)S(1)} %get-tuple-element.57), channel_id=1, source_target_pairs={{2,4},{4,2},{3,5},{5,3},{10,12},{12,10},{11,13},{13,11},{18,20},{2... | collective-permute-start | bytes 393224 | tf_op jit(solution)/shard_map/ppermute | solution.py:199
  30.0 5.9 %collective-permute-start.10 = (f32[128,128]{1,0:T(8,128)S(1)}, f32[128,128]{1,0:T(8,128)S(1)}, u32[]{:S(2)}, u32[]{:S(2)}) collective-permute-start(f32[128,128]{1,0:T(8,128)S(1)} %get-tuple-element.54), channel_id=1, source_target_pairs={{0,8},{8,0},{16,24},{24,16},{1,9},{9,1},{17,25},{25,17},{2,10},{10... | collective-permute-start | bytes 196616 | tf_op jit(solution)/shard_map/ppermute | solution.py:199
  33.4 2.5 %collective-permute-start.11 = (f32[128,128]{1,0:T(8,128)S(1)}, f32[128,128]{1,0:T(8,128)S(1)}, u32[]{:S(2)}, u32[]{:S(2)}) collective-permute-start(f32[128,128]{1,0:T(8,128)S(1)} %get-tuple-element.55), channel_id=1, source_target_pairs={{8,16},{16,8},{9,17},{17,9},{10,18},{18,10},{11,19},{19,11},{12,20... | collective-permute-start | bytes 196616 | tf_op jit(solution)/shard_map/ppermute | solution.py:199
  36.8 8.8 %collective-permute-start.19 = (f32[512,128]{1,0:T(8,128)S(1)}, f32[512,128]{1,0:T(8,128)S(1)}, u32[]{:S(2)}, u32[]{:S(2)}) collective-permute-start(f32[512,128]{1,0:T(8,128)S(1)} %get-tuple-element.64), channel_id=1, source_target_pairs={{0,1},{1,0},{2,3},{3,2},{4,5},{5,4},{6,7},{7,6},{8,9},{9,8},{10,11... | collective-permute-start | bytes 786440 | tf_op jit(solution)/shard_map/ppermute | solution.py:199
  37.4 8.1 %collective-permute-start.17 = (f32[256,128]{1,0:T(8,128)S(1)}, f32[256,128]{1,0:T(8,128)S(1)}, u32[]{:S(2)}, u32[]{:S(2)}) collective-permute-start(f32[256,128]{1,0:T(8,128)S(1)} %get-tuple-element.62), channel_id=1, source_target_pairs={{0,2},{2,0},{4,6},{6,4},{1,3},{3,1},{5,7},{7,5},{8,10},{10,8},{12,... | collective-permute-start | bytes 393224 | tf_op jit(solution)/shard_map/ppermute | solution.py:199
  39.0 6.6 %collective-permute-start.18 = (f32[256,128]{1,0:T(8,128)S(1)}, f32[256,128]{1,0:T(8,128)S(1)}, u32[]{:S(2)}, u32[]{:S(2)}) collective-permute-start(f32[256,128]{1,0:T(8,128)S(1)} %get-tuple-element.63), channel_id=1, source_target_pairs={{2,4},{4,2},{3,5},{5,3},{10,12},{12,10},{11,13},{13,11},{18,20},{2... | collective-permute-start | bytes 393224 | tf_op jit(solution)/shard_map/ppermute | solution.py:199
  39.6 5.9 %collective-permute-start.15 = (f32[128,128]{1,0:T(8,128)S(1)}, f32[128,128]{1,0:T(8,128)S(1)}, u32[]{:S(2)}, u32[]{:S(2)}) collective-permute-start(f32[128,128]{1,0:T(8,128)S(1)} %get-tuple-element.60), channel_id=1, source_target_pairs={{0,8},{8,0},{16,24},{24,16},{1,9},{9,1},{17,25},{25,17},{2,10},{10... | collective-permute-start | bytes 196616 | tf_op jit(solution)/shard_map/ppermute | solution.py:199
  43.0 2.5 %collective-permute-start.16 = (f32[128,128]{1,0:T(8,128)S(1)}, f32[128,128]{1,0:T(8,128)S(1)}, u32[]{:S(2)}, u32[]{:S(2)}) collective-permute-start(f32[128,128]{1,0:T(8,128)S(1)} %get-tuple-element.61), channel_id=1, source_target_pairs={{8,16},{16,8},{9,17},{17,9},{10,18},{18,10},{11,19},{19,11},{12,20... | collective-permute-start | bytes 196616 | tf_op jit(solution)/shard_map/ppermute | solution.py:199
  46.4 11.0 %collective-permute-start.24 = (f32[512,128]{1,0:T(8,128)S(1)}, f32[512,128]{1,0:T(8,128)S(1)}, u32[]{:S(2)}, u32[]{:S(2)}) collective-permute-start(f32[512,128]{1,0:T(8,128)S(1)} %get-tuple-element.72.refs_4_), channel_id=1, source_target_pairs={{0,1},{1,0},{2,3},{3,2},{4,5},{5,4},{6,7},{7,6},{8,9},{9,8},{10,11... | collective-permute-start | bytes 786440 | tf_op jit(solution)/shard_map/ppermute | solution.py:199
  47.9 9.4 %collective-permute-start.22 = (f32[256,128]{1,0:T(8,128)S(1)}, f32[256,128]{1,0:T(8,128)S(1)}, u32[]{:S(2)}, u32[]{:S(2)}) collective-permute-start(f32[256,128]{1,0:T(8,128)S(1)} %get-tuple-element.70.refs_2_), channel_id=1, source_target_pairs={{0,2},{2,0},{4,6},{6,4},{1,3},{3,1},{5,7},{7,5},{8,10},{10,8},{12,... | collective-permute-start | bytes 393224 | tf_op jit(solution)/shard_map/ppermute | solution.py:199
  50.3 7.0 %collective-permute-start.23 = (f32[256,128]{1,0:T(8,128)S(1)}, f32[256,128]{1,0:T(8,128)S(1)}, u32[]{:S(2)}, u32[]{:S(2)}) collective-permute-start(f32[256,128]{1,0:T(8,128)S(1)} %get-tuple-element.71.refs_3_), channel_id=1, source_target_pairs={{2,4},{4,2},{3,5},{5,3},{10,12},{12,10},{11,13},{13,11},{18,20},{2... | collective-permute-start | bytes 393224 | tf_op jit(solution)/shard_map/ppermute | solution.py:199
  51.0 6.3 %collective-permute-start.20 = (f32[128,128]{1,0:T(8,128)S(1)}, f32[128,128]{1,0:T(8,128)S(1)}, u32[]{:S(2)}, u32[]{:S(2)}) collective-permute-start(f32[128,128]{1,0:T(8,128)S(1)} %get-tuple-element.68.refs_0_), channel_id=1, source_target_pairs={{0,8},{8,0},{16,24},{24,16},{1,9},{9,1},{17,25},{25,17},{2,10},{10... | collective-permute-start | bytes 196616 | tf_op jit(solution)/shard_map/ppermute | solution.py:199
  53.8 3.5 %collective-permute-start.21 = (f32[128,128]{1,0:T(8,128)S(1)}, f32[128,128]{1,0:T(8,128)S(1)}, u32[]{:S(2)}, u32[]{:S(2)}) collective-permute-start(f32[128,128]{1,0:T(8,128)S(1)} %get-tuple-element.69.refs_1_), channel_id=1, source_target_pairs={{8,16},{16,8},{9,17},{17,9},{10,18},{18,10},{11,19},{19,11},{12,20... | collective-permute-start | bytes 196616 | tf_op jit(solution)/shard_map/ppermute | solution.py:199
  58.4 3.4 %collective-permute-start.25 = (f32[136,128]{1,0:T(8,128)S(1)}, f32[136,128]{1,0:T(8,128)S(1)}, u32[]{:S(2)}, u32[]{:S(2)}) collective-permute-start(f32[136,128]{1,0:T(8,128)S(1)} %shard_map.51), channel_id=1, source_target_pairs={{0,2},{2,0},{4,6},{6,4},{1,3},{3,1},{5,7},{7,5},{8,10},{10,8},{12,... | collective-permute-start | bytes 208904 | tf_op jit(solution)/shard_map/ppermute | solution.py:281
  61.8 4.5 %collective-permute-start.26 = (f32[136,128]{1,0:T(8,128)S(1)}, f32[136,128]{1,0:T(8,128)S(1)}, u32[]{:S(2)}, u32[]{:S(2)}) collective-permute-start(f32[136,128]{1,0:T(8,128)S(1)} %add.15), channel_id=1, source_target_pairs={{0,4},{2,6},{4,0},{6,2},{1,5},{3,7},{5,1},{7,3},{8,12},{10,14},{12... | collective-permute-start | bytes 208904 | tf_op jit(solution)/shard_map/ppermute | solution.py:281
  66.3 4.4 %collective-permute-start.27 = (f32[136,128]{1,0:T(8,128)S(1)}, f32[136,128]{1,0:T(8,128)S(1)}, u32[]{:S(2)}, u32[]{:S(2)}) collective-permute-start(f32[136,128]{1,0:T(8,128)S(1)} %add.16), channel_id=1, source_target_pairs={{0,1},{1,0},{2,3},{3,2},{4,5},{5,4},{6,7},{7,6},{8,9},{9,8},{10,11... | collective-permute-start | bytes 208904 | tf_op jit(solution)/shard_map/ppermute | solution.py:281
  70.7 5.1 %collective-permute-start.28 = (f32[136,128]{1,0:T(8,128)S(1)}, f32[136,128]{1,0:T(8,128)S(1)}, u32[]{:S(2)}, u32[]{:S(2)}) collective-permute-start(f32[136,128]{1,0:T(8,128)S(1)} %add.17), channel_id=1, source_target_pairs={{0,8},{8,0},{16,24},{24,16},{1,9},{9,1},{17,25},{25,17},{2,10},{10... | collective-permute-start | bytes 208904 | tf_op jit(solution)/shard_map/ppermute | solution.py:281
  75.8 5.3 %collective-permute-start.29 = (f32[136,128]{1,0:T(8,128)S(1)}, f32[136,128]{1,0:T(8,128)S(1)}, u32[]{:S(2)}, u32[]{:S(2)}) collective-permute-start(f32[136,128]{1,0:T(8,128)S(1)} %add.18), channel_id=1, source_target_pairs={{0,16},{8,24},{16,0},{24,8},{1,17},{9,25},{17,1},{25,9},{2,18},{10... | collective-permute-start | bytes 208904 | tf_op jit(solution)/shard_map/ppermute | solution.py:281

commit v5 on v4

--- a/solution.py
+++ b/solution.py
@@ -38,6 +38,7 @@
         self.x, self.y, self.z, self.k = shape
         self.row = self.y * self.z
         self.cells = self.x * self.row
+        self.room = self.cells + self.z
 
 
 def faces_of(s, at, w_ref, out, with_z=True):
@@ -69,13 +70,16 @@
     def body(at_ref, b_hbm, k_ref, w_ref, wide_ref, *refs):
         out = split_faces(refs[: 4 + nz], nz)
         edge = refs[4 + nz : 4 + 2 * nz]
-        b_ref, sems = refs[-2:]
+        b_ref, c_ref, sems = refs[-3:]
+        first = pltpu.make_async_copy(k_ref, c_ref, sems.at[parts])
+        first.start()
         copies = []
         for i in range(parts):
             here = pl.ds(i * rows, rows)
             copies.append(pltpu.make_async_copy(b_hbm.at[here], b_ref.at[here], sems.at[i]))
             copies[-1].start()
-        tiles = [k_ref[y] for y in range(s.y)]
+        first.wait()
+        tiles = [c_ref[y] for y in range(s.y)]
         for x in range(s.x):
             for y in range(s.y):
                 wide_ref[pl.ds(x * s.row + y * s.z, s.z), :] = jnp.broadcast_to(
@@ -94,15 +98,16 @@
             edge[i][...] = wide_ref[pl.ds(at_ref[4 + i], s.x * s.y, stride=s.z), :]
         faces_of(s, at_ref, w_ref, out)
 
-    outs = [f32(s.cells, s.k)] * 2 + face_shapes(s, nz) + [f32(s.x * s.y, s.k)] * nz
+    outs = [f32(s.room, s.k)] * 2 + face_shapes(s, nz) + [f32(s.x * s.y, s.k)] * nz
     return pl.pallas_call(
         body,
         out_shape=outs,
-        in_specs=[SMEM, pl.BlockSpec(memory_space=pl.ANY), VMEM],
+        in_specs=[SMEM] + [pl.BlockSpec(memory_space=pltpu.HBM)] * 2,
         out_specs=tuple(VMEM for _ in outs),
         scratch_shapes=[
             pltpu.VMEM((s.cells, s.k), jnp.float32),
-            pltpu.SemaphoreType.DMA((parts,)),
+            pltpu.VMEM(turned.shape, jnp.float32),
+            pltpu.SemaphoreType.DMA((parts + 1,)),
         ],
         compiler_params=pltpu.CompilerParams(vmem_limit_bytes=32 * 1024 * 1024),
         cost_estimate=pl.CostEstimate(
@@ -157,16 +162,19 @@
         sweep(s, w_ref, emit)
 
     ins = [at, w, wide] + ([] if before is None else [before])
-    return call(body, [f32(s.cells, s.k)], ins, 12 * s.cells * s.k)[0]
-
-
-def finish(part, wide, edge, ghosts, at, s, nz, scale):
+    return call(body, [f32(s.room, s.k)], ins, 12 * s.cells * s.k)[0]
+
+
+def finish(part, wide, edge, ghosts, at, s, nz, scale, last):
     def body(at_ref, p_ref, k_ref, *refs):
         del p_ref
         edges = refs[:nz]
         ghost = split_faces(refs[nz : 4 + 2 * nz], nz)
         w_ref = refs[4 + 2 * nz]
-        out = split_faces(refs[5 + 2 * nz :], nz)
+        if last:
+            out = refs[5 + 2 * nz :]
+        else:
+            out = split_faces(refs[5 + 2 * nz :], nz)
         factor = scale / 6.0
         for i in range(2):
             here = pl.ds(at_ref[i] * s.row, s.row)
@@ -181,12 +189,40 @@
                 flat = pl.ds(x * s.y, s.y)
                 new = w_ref[here, :] - (edges[i][flat, :] * factor) * ghost["z"][i][flat, :]
                 w_ref[here, :] = new
-                out["z"][i][flat, :] = new
-        faces_of(s, at_ref, w_ref, out, with_z=False)
-
-    outs = [f32(s.cells, s.k)] + face_shapes(s, nz)
+                if not last:
+                    out["z"][i][flat, :] = new
+        if last:
+            out[0][...] = w_ref[: s.row, :]
+            for x in range(s.x):
+                out[1][x * s.z : (x + 1) * s.z, :] = w_ref[x * s.row : x * s.row + s.z, :]
+            if halved(s, nz):
+                start = (1 - at_ref[6]) * (s.cells // 2) + at_ref[4]
+                out[2][...] = w_ref[pl.ds(start, s.x * s.y // 2, stride=s.z), :]
+            else:
+                out[2][...] = w_ref[pl.ds(0, s.x * s.y, stride=s.z), :]
+        else:
+            faces_of(s, at_ref, w_ref, out, with_z=False)
+
+    if last:
+        outs = [f32(s.room, s.k), f32(s.row, s.k), f32(s.x * s.z, s.k), f32(s.x * s.y // (2 if halved(s, nz) else 1), s.k)]
+    else:
+        outs = [f32(s.room, s.k)] + face_shapes(s, nz)
     ins = [at, part, wide] + list(edge) + list(ghosts)
     return call(body, outs, ins, 4 * s.x * s.y * s.k, {1: 0})
+
+
+def halved(s, nz):
+    return nz == 1 and s.x % 2 == 0
+
+
+def one_way(faces, s, nz):
+    got = []
+    for face, axis in zip(faces, ("gx", "gy", "gz")):
+        pairs = [(i, i - 1) for i in range(1, lax.axis_size(axis))]
+        if axis == "gz" and halved(s, nz):
+            pairs = [(0, 1), (1, 0)]
+        got.append(lax.ppermute(face, axis, pairs))
+    return got
 
 
 def exchange(faces, axes):
@@ -253,23 +289,29 @@
     )(at, w, wide)
 
 
-def pack_terms(gram, own, faces, ghosts, at, s, cells):
+def pack_terms(gram, own, w, ghosts, at, s, nz, cells):
     k = s.k
 
-    def body(at_ref, g_ref, m_ref, *refs):
-        n = len(faces)
-        m = jnp.zeros((k, k), jnp.float32)
-        for left, right in zip(refs[:n], refs[n : 2 * n]):
-            m += both(transposed_dot(two(left[...]), two(right[...])))
-        m = m_ref[...] - m * (1.0 / 6.0)
+    def body(at_ref, g_ref, m_ref, w_ref, x_ref, y_ref, z_ref, p_ref):
+        lefts = [w_ref[s.cells - s.row : s.cells, :]]
+        tops = [w_ref[(x + 1) * s.row - s.z : (x + 1) * s.row, :] for x in range(s.x)]
+        lefts.append(jnp.concatenate(tops, axis=0))
+        if halved(s, nz):
+            start = at_ref[6] * (s.cells // 2) + at_ref[4]
+            lefts.append(w_ref[pl.ds(start, s.x * s.y // 2, stride=s.z), :])
+        else:
+            lefts.append(w_ref[pl.ds(s.z - 1, s.x * s.y, stride=s.z), :])
+        left = jnp.concatenate(lefts, axis=0)
+        right = jnp.concatenate([x_ref[...], y_ref[...], z_ref[...]], axis=0)
+        m = m_ref[...] - both(transposed_dot(two(left), two(right))) * (2.0 / 6.0)
         raw = (m + m.T) * (0.5 / cells)
         below = lax.broadcasted_iota(jnp.int32, (k, k), 0)
         along = lax.broadcasted_iota(jnp.int32, (k, k), 1)
-        refs[-1][:k, :] = jnp.where(below >= along, g_ref[...] * (1.0 / cells), raw)
+        p_ref[:k, :] = jnp.where(below >= along, g_ref[...] * (1.0 / cells), raw)
         diagonal = jnp.sum(jnp.where(below == along, raw, 0.0), axis=0, keepdims=True)
-        refs[-1][k:, :] = jnp.broadcast_to(diagonal, (8, k))
-
-    ins = [at, gram, own] + list(faces) + list(ghosts)
+        p_ref[k:, :] = jnp.broadcast_to(diagonal, (8, k))
+
+    ins = [at, gram, own, w] + list(ghosts)
     return call(body, [f32(k + 8, k)], ins, 6 * s.cells * k)[0]
 
 
@@ -375,6 +417,7 @@
     tops = (s.x - 1, s.y - 1, s.z - 1)
     at = jnp.stack(
         [jnp.where(odd[d] == first, tops[d], 0) for d in range(3) for first in range(2)]
+        + [odd[2], odd[1]]
     ).astype(jnp.int32)
     axes = [("gx", 0), ("gx", 1), ("gy", 0), ("gy", 1), ("gz", 0), ("gz", 1)][: 4 + nz]
 
@@ -388,10 +431,10 @@
         part = interior(w, before, wide, at, s)
         scale = (1.0 if before is None else 2.0) / half_value
         before = w
-        w, *faces = finish(part, wide, edge, ghosts, at, s, nz, scale)
-    ghosts = exchange(faces, axes)
+        w, *faces = finish(part, wide, edge, ghosts, at, s, nz, scale, step == DEG - 1)
+    ghosts = one_way(faces, s, nz)
     filtered, gram, own = gather_terms(w, wide, at, s)
-    packed = total(pack_terms(gram, own, faces, ghosts, at, s, cells), ("gy", "gz", "gx"))
+    packed = total(pack_terms(gram, own, w, ghosts, at, s, nz, cells), ("gy", "gz", "gx"))
     basis, projected = orthonormal(packed, filtered, s)
     return (basis.reshape(block.shape), projected)
 

time: 90 us -> 89 us (0.989)
  starting transfers between devices: 45.1 us -> 42.5 us
  waiting for transfers between devices: 15.7 us -> 17.2 us
    ppermute x25 -> x20, starting transfers between devices: 36.3 us -> 28.2 us  [exchange(): got.append(lax.ppermute(face, axis, pairs))]
    ppermute x0 -> x3, starting transfers between devices: none -> 4.13 us  [one_way(): got.append(lax.ppermute(face, axis, pairs))]
    ppermute x0 -> x3, waiting for transfers between devices: none -> 3.61 us  [one_way(): got.append(lax.ppermute(face, axis, pairs))]
    ppermute x5, waiting for transfers between devices: 13.8 us -> 11.8 us  [total(): lax.ppermute(value, axis, [(i, i ^ bit) for i in range(count)])]
    ppermute x5, starting transfers between devices: 8.84 us -> 10.1 us  [total(): lax.ppermute(value, axis, [(i, i ^ bit) for i in range(count)])]
    ppermute x25 -> x20, waiting for transfers between devices: 1.93 us -> 1.75 us  [exchange(): got.append(lax.ppermute(face, axis, pairs))]
  transfers between devices with their start and end apart: 30 -> 28, of which waited for: 8 -> 9; matrix products, arithmetic and copies ran while one was open for 0% -> 0% of each run, Pallas kernels for 11% -> 12%
where the time goes in v5:
time: 89 us; the launch traced here: 88.6 us
  starting transfers between devices  42.5 us (48%)
  Pallas kernels  25.4 us (29%)
  waiting for transfers between devices  17.2 us (19%)
  local copies, waits for them, and re-layouts  2.52 us (3%)
  between operations  0.94 us (1%)
    ppermute x20, starting transfers between devices, exchange(): got.append(lax.ppermute(face, axis, pairs))  28.2 us
    ppermute x5, waiting for transfers between devices, total(): lax.ppermute(value, axis, [(i, i ^ bit) for i in range(count)])  11.8 us
    pallas_call x9, Pallas kernels, call(): pl.pallas_call(body, out_shape=outs, in_specs=[SMEM] + [VMEM] * (len(ins)...  11.8 us
    ppermute x5, starting transfers between devices, total(): lax.ppermute(value, axis, [(i, i ^ bit) for i in range(count)])  10.1 us
    pallas_call x1, Pallas kernels, orthonormal(): pl.pallas_call(body, grid=(8,), out_shape=[f32(s.cells, k), f32(k, k)], i...  8.43 us
    ppermute x3, starting transfers between devices, one_way(): got.append(lax.ppermute(face, axis, pairs))  4.13 us
    ppermute x3, waiting for transfers between devices, one_way(): got.append(lax.ppermute(face, axis, pairs))  3.61 us
    pallas_call x1, Pallas kernels, gather_terms(): pl.pallas_call(body, out_shape=outs, in_specs=[SMEM, VMEM, VMEM], out_spe...  2.86 us
  transfers between devices with their start and end apart: 28, of which 9 were waited for; matrix products, arithmetic and copies ran while one was open for 0% of the time, Pallas kernels for 12%

profile of v5, /device:TPU:0, one launch (start us, length us, event | category | flops | bytes accessed | tf_op | source)
XLA Modules:
  0.0 88.6 jit_solution(9179000327711884098)
XLA Ops:
  0.7 1.6 %copy-done = f32[32,16,8,128]{3,2,1,0:T(8,128)S(1)} copy-done((f32[32,16,8,128]{3,2,1,0:T(8,128)S(1)}, f32[32,16,8,128]{3,2,1,0:T(8,128)}, u32[]{:S(2)}) %copy-start) | copy-done | bytes 2097176
  3.2 2.3 %shard_map.41 = (f32[4104,128]{1,0:T(8,128)S(1)}, f32[4104,128]{1,0:T(8,128)S(1)}, f32[128,128]{1,0:T(8,128)S(1)}, f32[128,128]{1,0:T(8,128)S(1)}, f32[256,128]{...) custom-call(s32[8]{0:T(128)S(1)} %stack.35.at_ref, ...), custom_call_target="tpu_custom_call" | custom-call | flops 2097152 | bytes 8388608 | tf_op jit(solution)/shard_map/pallas_call | solution.py:102
  5.5 3.0 %collective-permute-start.4 = (f32[512,128]{1,0:T(8,128)S(1)}, f32[512,128]{1,0:T(8,128)S(1)}, u32[]{:S(2)}, u32[]{:S(2)}) collective-permute-start(f32[512,128]{1,0:T(8,128)S(1)} %get-tuple-element.44), channel_id=1, source_target_pairs={{0,1},{1,0},{2,3},{3,2},{4,5},{5,4},{6,7},{7,6},{8,9},{9,8},{10,11... | collective-permute-start | bytes 786440 | tf_op jit(solution)/shard_map/ppermute | solution.py:235
  9.2 1.6 %collective-permute-start = (f32[128,128]{1,0:T(8,128)S(1)}, f32[128,128]{1,0:T(8,128)S(1)}, u32[]{:S(2)}, u32[]{:S(2)}) collective-permute-start(f32[128,128]{1,0:T(8,128)S(1)} %get-tuple-element.40), channel_id=1, source_target_pairs={{0,8},{8,0},{16,24},{24,16},{1,9},{9,1},{17,25},{25,17},{2,10},{10... | collective-permute-start | bytes 196616 | tf_op jit(solution)/shard_map/ppermute | solution.py:235
  11.5 1.8 %shard_map.42.p_ref = f32[4104,128]{1,0:T(8,128)S(1)} custom-call(s32[8]{0:T(128)S(1)} %stack.35.at_ref, f32[4104,128]{1,0:T(8,128)S(1)} %get-tuple-element.37.w_ref.rest_0_, f32[4104,128]{1,0:T(8,128)S(1)} %get-tuple-element.38.k_ref), custom_call_target="tpu_custom_call" | custom-call | flops 6291456 | bytes 6303776 | tf_op jit(solution)/shard_map/pallas_call | solution.py:21
  13.5 1.3 %collective-permute-done.4.refs_5_ = f32[512,128]{1,0:T(8,128)S(1)} collective-permute-done((f32[512,128]{1,0:T(8,128)S(1)}, f32[512,128]{1,0:T(8,128)S(1)}, u32[]{:S(2)}, u32[]{:S(2)}) %collective-permute-start.4) | collective-permute-done | bytes 262176 | tf_op jit(solution)/shard_map/ppermute | solution.py:235
  15.7 1.8 %collective-permute-start.9 = (f32[512,128]{1,0:T(8,128)S(1)}, f32[512,128]{1,0:T(8,128)S(1)}, u32[]{:S(2)}, u32[]{:S(2)}) collective-permute-start(f32[512,128]{1,0:T(8,128)S(1)} %get-tuple-element.50), channel_id=1, source_target_pairs={{0,1},{1,0},{2,3},{3,2},{4,5},{5,4},{6,7},{7,6},{8,9},{9,8},{10,11... | collective-permute-start | bytes 786440 | tf_op jit(solution)/shard_map/ppermute | solution.py:235
  18.1 3.8 %collective-permute-start.5 = (f32[128,128]{1,0:T(8,128)S(1)}, f32[128,128]{1,0:T(8,128)S(1)}, u32[]{:S(2)}, u32[]{:S(2)}) collective-permute-start(f32[128,128]{1,0:T(8,128)S(1)} %get-tuple-element.46), channel_id=1, source_target_pairs={{0,8},{8,0},{16,24},{24,16},{1,9},{9,1},{17,25},{25,17},{2,10},{10... | collective-permute-start | bytes 196616 | tf_op jit(solution)/shard_map/ppermute | solution.py:235
  22.6 1.9 %shard_map.44.p_ref = f32[4104,128]{1,0:T(8,128)S(1)} custom-call(s32[8]{0:T(128)S(1)} %stack.35.at_ref, f32[4104,128]{1,0:T(8,128)S(1)} %get-tuple-element.45.w_ref.rest_0_, f32[4104,128]{1,0:T(8,128)S(1)} %get-tuple-element.38.k_ref, f32[4104,128]{1,0:T(8,128)S(1)} %get-tuple-element.37.w_ref.rest_0_), custom_call_target="tpu_custom_call" | custom-call | flops 6291456 | bytes 8405024 | tf_op jit(solution)/shard_map/pallas_call | solution.py:21
  25.6 1.4 %collective-permute-start.14 = (f32[512,128]{1,0:T(8,128)S(1)}, f32[512,128]{1,0:T(8,128)S(1)}, u32[]{:S(2)}, u32[]{:S(2)}) collective-permute-start(f32[512,128]{1,0:T(8,128)S(1)} %get-tuple-element.56), channel_id=1, source_target_pairs={{0,1},{1,0},{2,3},{3,2},{4,5},{5,4},{6,7},{7,6},{8,9},{9,8},{10,11... | collective-permute-start | bytes 786440 | tf_op jit(solution)/shard_map/ppermute | solution.py:235
  27.0 2.5 %collective-permute-start.12 = (f32[256,128]{1,0:T(8,128)S(1)}, f32[256,128]{1,0:T(8,128)S(1)}, u32[]{:S(2)}, u32[]{:S(2)}) collective-permute-start(f32[256,128]{1,0:T(8,128)S(1)} %get-tuple-element.54), channel_id=1, source_target_pairs={{0,2},{2,0},{4,6},{6,4},{1,3},{3,1},{5,7},{7,5},{8,10},{10,8},{12,... | collective-permute-start | bytes 393224 | tf_op jit(solution)/shard_map/ppermute | solution.py:235
  30.2 3.3 %collective-permute-start.10 = (f32[128,128]{1,0:T(8,128)S(1)}, f32[128,128]{1,0:T(8,128)S(1)}, u32[]{:S(2)}, u32[]{:S(2)}) collective-permute-start(f32[128,128]{1,0:T(8,128)S(1)} %get-tuple-element.52), channel_id=1, source_target_pairs={{0,8},{8,0},{16,24},{24,16},{1,9},{9,1},{17,25},{25,17},{2,10},{10... | collective-permute-start | bytes 196616 | tf_op jit(solution)/shard_map/ppermute | solution.py:235
  34.2 2.0 %shard_map.46.p_ref = f32[4104,128]{1,0:T(8,128)S(1)} custom-call(s32[8]{0:T(128)S(1)} %stack.35.at_ref, f32[4104,128]{1,0:T(8,128)S(1)} %get-tuple-element.51.w_ref.rest_0_, f32[4104,128]{1,0:T(8,128)S(1)} %get-tuple-element.38.k_ref, f32[4104,128]{1,0:T(8,128)S(1)} %get-tuple-element.45.w_ref.rest_0_), custom_call_target="tpu_custom_call" | custom-call | flops 6291456 | bytes 8405024 | tf_op jit(solution)/shard_map/pallas_call | solution.py:21
  37.6 1.5 %collective-permute-start.17 = (f32[256,128]{1,0:T(8,128)S(1)}, f32[256,128]{1,0:T(8,128)S(1)}, u32[]{:S(2)}, u32[]{:S(2)}) collective-permute-start(f32[256,128]{1,0:T(8,128)S(1)} %get-tuple-element.60), channel_id=1, source_target_pairs={{0,2},{2,0},{4,6},{6,4},{1,3},{3,1},{5,7},{7,5},{8,10},{10,8},{12,... | collective-permute-start | bytes 393224 | tf_op jit(solution)/shard_map/ppermute | solution.py:235
  39.8 3.3 %collective-permute-start.15 = (f32[128,128]{1,0:T(8,128)S(1)}, f32[128,128]{1,0:T(8,128)S(1)}, u32[]{:S(2)}, u32[]{:S(2)}) collective-permute-start(f32[128,128]{1,0:T(8,128)S(1)} %get-tuple-element.58), channel_id=1, source_target_pairs={{0,8},{8,0},{16,24},{24,16},{1,9},{9,1},{17,25},{25,17},{2,10},{10... | collective-permute-start | bytes 196616 | tf_op jit(solution)/shard_map/ppermute | solution.py:235
  43.8 1.8 %shard_map.48.p_ref = f32[4104,128]{1,0:T(8,128)S(1)} custom-call(s32[8]{0:T(128)S(1)} %stack.35.at_ref, f32[4104,128]{1,0:T(8,128)S(1)} %get-tuple-element.57.w_ref, f32[4104,128]{1,0:T(8,128)S(1)} %get-tuple-element.38.k_ref, f32[4104,128]{1,0:T(8,128)S(1)} %get-tuple-element.51.w_ref.rest_0_), custom_call_target="tpu_custom_call" | custom-call | flops 6291456 | bytes 8405024 | tf_op jit(solution)/shard_map/pallas_call | solution.py:21
  46.6 1.3 %collective-permute-start.21 = (f32[256,128]{1,0:T(8,128)S(1)}, f32[256,128]{1,0:T(8,128)S(1)}, u32[]{:S(2)}, u32[]{:S(2)}) collective-permute-start(f32[256,128]{1,0:T(8,128)S(1)} %get-tuple-element.67), channel_id=1, source_target_pairs={{2,0},{4,2},{6,4},{3,1},{5,3},{7,5},{10,8},{12,10},{14,12},{11,9},... | collective-permute-start | bytes 393224 | tf_op jit(solution)/shard_map/ppermute | solution.py:224
  47.9 1.6 %collective-permute-start.22 = (f32[256,128]{1,0:T(8,128)S(1)}, f32[256,128]{1,0:T(8,128)S(1)}, u32[]{:S(2)}, u32[]{:S(2)}) collective-permute-start(f32[256,128]{1,0:T(8,128)S(1)} %get-tuple-element.68), channel_id=1, source_target_pairs={{0,1},{1,0},{2,3},{3,2},{4,5},{5,4},{6,7},{7,6},{8,9},{9,8},{10,11... | collective-permute-start | bytes 393224 | tf_op jit(solution)/shard_map/ppermute | solution.py:224
  49.4 1.3 %collective-permute-start.20 = (f32[128,128]{1,0:T(8,128)S(1)}, f32[128,128]{1,0:T(8,128)S(1)}, u32[]{:S(2)}, u32[]{:S(2)}) collective-permute-start(f32[128,128]{1,0:T(8,128)S(1)} %get-tuple-element.66), channel_id=1, source_target_pairs={{8,0},{16,8},{24,16},{9,1},{17,9},{25,17},{10,2},{18,10},{26,18},{... | collective-permute-start | bytes 196616 | tf_op jit(solution)/shard_map/ppermute | solution.py:224
  50.7 2.9 %shard_map.50 = (f32[4096,128]{1,0:T(8,128)S(1)}, f32[128,128]{1,0:T(8,128)S(1)}, f32[128,128]{1,0:T(8,128)S(1)}) custom-call(s32[8]{0:T(128)S(1)} %stack.35.at_ref, f32[4104,128]{1,0:T(8,128)S(1)} %get-tuple-element.63.w_ref, f32[4104,128]{1,0:T(8,128)S(1)} %get-tuple-element.38.k_ref), custom_call_target="tpu_custom_call" | custom-call | flops 1073741824 | bytes 8388608 | tf_op jit(solution)/shard_map/pallas_call | solution.py:279
  53.6 3.6 %collective-permute-done.20.x_ref = f32[128,128]{1,0:T(8,128)S(1)} collective-permute-done((f32[128,128]{1,0:T(8,128)S(1)}, f32[128,128]{1,0:T(8,128)S(1)}, u32[]{:S(2)}, u32[]{:S(2)}) %collective-permute-start.20) | collective-permute-done | bytes 65568 | tf_op jit(solution)/shard_map/ppermute | solution.py:224
  57.2 1.0 %shard_map.51 = f32[136,128]{1,0:T(8,128)S(1)} custom-call(s32[8]{0:T(128)S(1)} %stack.35.at_ref, f32[128,128]{1,0:T(8,128)S(1)} %get-tuple-element.64.g_ref, f32[128,128]{1,0:T(8,128)S(1)} %get-tuple-element.65.m_ref, f32[4104,128]{1,0:T(8,128)S(1)} %get-tuple-element.63.w_ref, f32[128,128]{1,0:T(8,128)S(1)} %collective-permute-done.20.x_ref, ...), custom_call_target="tpu_custom_call" | custom-call | flops 3145728 | bytes 2629664 | tf_op jit(solution)/shard_map/pallas_call | solution.py:21
  58.2 1.3 %collective-permute-start.23 = (f32[136,128]{1,0:T(8,128)S(1)}, f32[136,128]{1,0:T(8,128)S(1)}, u32[]{:S(2)}, u32[]{:S(2)}) collective-permute-start(f32[136,128]{1,0:T(8,128)S(1)} %shard_map.51), channel_id=1, source_target_pairs={{0,2},{2,0},{4,6},{6,4},{1,3},{3,1},{5,7},{7,5},{8,10},{10,8},{12,... | collective-permute-start | bytes 208904 | tf_op jit(solution)/shard_map/ppermute | solution.py:323
  59.5 0.9 %collective-permute-done.23 = f32[136,128]{1,0:T(8,128)S(1)} collective-permute-done((f32[136,128]{1,0:T(8,128)S(1)}, f32[136,128]{1,0:T(8,128)S(1)}, u32[]{:S(2)}, u32[]{:S(2)}) %collective-permute-start.23) | collective-permute-done | bytes 69664 | tf_op jit(solution)/shard_map/ppermute | solution.py:323
  60.4 3.2 %collective-permute-start.24 = (f32[136,128]{1,0:T(8,128)S(1)}, f32[136,128]{1,0:T(8,128)S(1)}, u32[]{:S(2)}, u32[]{:S(2)}) collective-permute-start(f32[136,128]{1,0:T(8,128)S(1)} %add.15), channel_id=1, source_target_pairs={{0,4},{2,6},{4,0},{6,2},{1,5},{3,7},{5,1},{7,3},{8,12},{10,14},{12... | collective-permute-start | bytes 208904 | tf_op jit(solution)/shard_map/ppermute | solution.py:323
  63.6 2.5 %collective-permute-done.24 = f32[136,128]{1,0:T(8,128)S(1)} collective-permute-done((f32[136,128]{1,0:T(8,128)S(1)}, f32[136,128]{1,0:T(8,128)S(1)}, u32[]{:S(2)}, u32[]{:S(2)}) %collective-permute-start.24) | collective-permute-done | bytes 69664 | tf_op jit(solution)/shard_map/ppermute | solution.py:323
  66.7 3.8 %collective-permute-done.25 = f32[136,128]{1,0:T(8,128)S(1)} collective-permute-done((f32[136,128]{1,0:T(8,128)S(1)}, f32[136,128]{1,0:T(8,128)S(1)}, u32[]{:S(2)}, u32[]{:S(2)}) %collective-permute-start.25) | collective-permute-done | bytes 69664 | tf_op jit(solution)/shard_map/ppermute | solution.py:323
  70.5 2.1 %collective-permute-start.26 = (f32[136,128]{1,0:T(8,128)S(1)}, f32[136,128]{1,0:T(8,128)S(1)}, u32[]{:S(2)}, u32[]{:S(2)}) collective-permute-start(f32[136,128]{1,0:T(8,128)S(1)} %add.17), channel_id=1, source_target_pairs={{0,8},{8,0},{16,24},{24,16},{1,9},{9,1},{17,25},{25,17},{2,10},{10... | collective-permute-start | bytes 208904 | tf_op jit(solution)/shard_map/ppermute | solution.py:323
  72.6 2.3 %collective-permute-done.26 = f32[136,128]{1,0:T(8,128)S(1)} collective-permute-done((f32[136,128]{1,0:T(8,128)S(1)}, f32[136,128]{1,0:T(8,128)S(1)}, u32[]{:S(2)}, u32[]{:S(2)}) %collective-permute-start.26) | collective-permute-done | bytes 69664 | tf_op jit(solution)/shard_map/ppermute | solution.py:323
  74.9 2.9 %collective-permute-start.27 = (f32[136,128]{1,0:T(8,128)S(1)}, f32[136,128]{1,0:T(8,128)S(1)}, u32[]{:S(2)}, u32[]{:S(2)}) collective-permute-start(f32[136,128]{1,0:T(8,128)S(1)} %add.18), channel_id=1, source_target_pairs={{0,16},{8,24},{16,0},{24,8},{1,17},{9,25},{17,1},{25,9},{2,18},{10... | collective-permute-start | bytes 208904 | tf_op jit(solution)/shard_map/ppermute | solution.py:323
  77.8 2.3 %collective-permute-done.27 = f32[136,128]{1,0:T(8,128)S(1)} collective-permute-done((f32[136,128]{1,0:T(8,128)S(1)}, f32[136,128]{1,0:T(8,128)S(1)}, u32[]{:S(2)}, u32[]{:S(2)}) %collective-permute-start.27) | collective-permute-done | bytes 69664 | tf_op jit(solution)/shard_map/ppermute | solution.py:323
  80.2 8.4 %shard_map.52 = (f32[4096,128]{1,0:T(8,128)}, f32[128,128]{1,0:T(8,128)}) custom-call(f32[136,128]{1,0:T(8,128)S(1)} %add.19.p_ref, f32[4096,128]{1,0:T(8,128)S(1)} %get-tuple-element.69.f_ref), custom_call_target="tpu_custom_call" | custom-call | flops 536870912 | bytes 4194304 | tf_op jit(solution)/shard_map/pallas_call | solution.py:394
  (46 shorter events, 11.2 us)
Async XLA Ops:
  0.7 1.6 %copy-start = (f32[32,16,8,128]{3,2,1,0:T(8,128)S(1)}, f32[32,16,8,128]{3,2,1,0:T(8,128)}, u32[]{:S(2)}) copy-start(f32[32,16,8,128]{3,2,1,0:T(8,128)} %param.2) | copy-start | bytes 6291460
  2.3 0.8 copy-start.1
  5.5 9.3 %collective-permute-start.4 = (f32[512,128]{1,0:T(8,128)S(1)}, f32[512,128]{1,0:T(8,128)S(1)}, u32[]{:S(2)}, u32[]{:S(2)}) collective-permute-start(f32[512,128]{1,0:T(8,128)S(1)} %get-tuple-element.44), channel_id=1, source_target_pairs={{0,1},{1,0},{2,3},{3,2},{4,5},{5,4},{6,7},{7,6},{8,9},{9,8},{10,11... | collective-permute-start | bytes 786440 | tf_op jit(solution)/shard_map/ppermute | solution.py:235
  8.5 5.0 %collective-permute-start.2 = (f32[256,128]{1,0:T(8,128)S(1)}, f32[256,128]{1,0:T(8,128)S(1)}, u32[]{:S(2)}, u32[]{:S(2)}) collective-permute-start(f32[256,128]{1,0:T(8,128)S(1)} %get-tuple-element.42), channel_id=1, source_target_pairs={{0,2},{2,0},{4,6},{6,4},{1,3},{3,1},{5,7},{7,5},{8,10},{10,8},{12,... | collective-permute-start | bytes 393224 | tf_op jit(solution)/shard_map/ppermute | solution.py:235
  8.5 5.0 %collective-permute-start.3 = (f32[256,128]{1,0:T(8,128)S(1)}, f32[256,128]{1,0:T(8,128)S(1)}, u32[]{:S(2)}, u32[]{:S(2)}) collective-permute-start(f32[256,128]{1,0:T(8,128)S(1)} %get-tuple-element.43), channel_id=1, source_target_pairs={{2,4},{4,2},{3,5},{5,3},{10,12},{12,10},{11,13},{13,11},{18,20},{2... | collective-permute-start | bytes 393224 | tf_op jit(solution)/shard_map/ppermute | solution.py:235
  9.2 4.3 %collective-permute-start = (f32[128,128]{1,0:T(8,128)S(1)}, f32[128,128]{1,0:T(8,128)S(1)}, u32[]{:S(2)}, u32[]{:S(2)}) collective-permute-start(f32[128,128]{1,0:T(8,128)S(1)} %get-tuple-element.40), channel_id=1, source_target_pairs={{0,8},{8,0},{16,24},{24,16},{1,9},{9,1},{17,25},{25,17},{2,10},{10... | collective-permute-start | bytes 196616 | tf_op jit(solution)/shard_map/ppermute | solution.py:235
  10.8 2.7 %collective-permute-start.1 = (f32[128,128]{1,0:T(8,128)S(1)}, f32[128,128]{1,0:T(8,128)S(1)}, u32[]{:S(2)}, u32[]{:S(2)}) collective-permute-start(f32[128,128]{1,0:T(8,128)S(1)} %get-tuple-element.41), channel_id=1, source_target_pairs={{8,16},{16,8},{9,17},{17,9},{10,18},{18,10},{11,19},{19,11},{12,20... | collective-permute-start | bytes 196616 | tf_op jit(solution)/shard_map/ppermute | solution.py:235
  15.7 9.1 %collective-permute-start.9 = (f32[512,128]{1,0:T(8,128)S(1)}, f32[512,128]{1,0:T(8,128)S(1)}, u32[]{:S(2)}, u32[]{:S(2)}) collective-permute-start(f32[512,128]{1,0:T(8,128)S(1)} %get-tuple-element.50), channel_id=1, source_target_pairs={{0,1},{1,0},{2,3},{3,2},{4,5},{5,4},{6,7},{7,6},{8,9},{9,8},{10,11... | collective-permute-start | bytes 786440 | tf_op jit(solution)/shard_map/ppermute | solution.py:235
  17.5 7.1 %collective-permute-start.7 = (f32[256,128]{1,0:T(8,128)S(1)}, f32[256,128]{1,0:T(8,128)S(1)}, u32[]{:S(2)}, u32[]{:S(2)}) collective-permute-start(f32[256,128]{1,0:T(8,128)S(1)} %get-tuple-element.48), channel_id=1, source_target_pairs={{0,2},{2,0},{4,6},{6,4},{1,3},{3,1},{5,7},{7,5},{8,10},{10,8},{12,... | collective-permute-start | bytes 393224 | tf_op jit(solution)/shard_map/ppermute | solution.py:235
  17.5 7.1 %collective-permute-start.8 = (f32[256,128]{1,0:T(8,128)S(1)}, f32[256,128]{1,0:T(8,128)S(1)}, u32[]{:S(2)}, u32[]{:S(2)}) collective-permute-start(f32[256,128]{1,0:T(8,128)S(1)} %get-tuple-element.49), channel_id=1, source_target_pairs={{2,4},{4,2},{3,5},{5,3},{10,12},{12,10},{11,13},{13,11},{18,20},{2... | collective-permute-start | bytes 393224 | tf_op jit(solution)/shard_map/ppermute | solution.py:235
  18.1 6.4 %collective-permute-start.5 = (f32[128,128]{1,0:T(8,128)S(1)}, f32[128,128]{1,0:T(8,128)S(1)}, u32[]{:S(2)}, u32[]{:S(2)}) collective-permute-start(f32[128,128]{1,0:T(8,128)S(1)} %get-tuple-element.46), channel_id=1, source_target_pairs={{0,8},{8,0},{16,24},{24,16},{1,9},{9,1},{17,25},{25,17},{2,10},{10... | collective-permute-start | bytes 196616 | tf_op jit(solution)/shard_map/ppermute | solution.py:235
  21.9 2.6 %collective-permute-start.6 = (f32[128,128]{1,0:T(8,128)S(1)}, f32[128,128]{1,0:T(8,128)S(1)}, u32[]{:S(2)}, u32[]{:S(2)}) collective-permute-start(f32[128,128]{1,0:T(8,128)S(1)} %get-tuple-element.47), channel_id=1, source_target_pairs={{8,16},{16,8},{9,17},{17,9},{10,18},{18,10},{11,19},{19,11},{12,20... | collective-permute-start | bytes 196616 | tf_op jit(solution)/shard_map/ppermute | solution.py:235
  25.6 10.6 %collective-permute-start.14 = (f32[512,128]{1,0:T(8,128)S(1)}, f32[512,128]{1,0:T(8,128)S(1)}, u32[]{:S(2)}, u32[]{:S(2)}) collective-permute-start(f32[512,128]{1,0:T(8,128)S(1)} %get-tuple-element.56), channel_id=1, source_target_pairs={{0,1},{1,0},{2,3},{3,2},{4,5},{5,4},{6,7},{7,6},{8,9},{9,8},{10,11... | collective-permute-start | bytes 786440 | tf_op jit(solution)/shard_map/ppermute | solution.py:235
  27.0 9.2 %collective-permute-start.12 = (f32[256,128]{1,0:T(8,128)S(1)}, f32[256,128]{1,0:T(8,128)S(1)}, u32[]{:S(2)}, u32[]{:S(2)}) collective-permute-start(f32[256,128]{1,0:T(8,128)S(1)} %get-tuple-element.54), channel_id=1, source_target_pairs={{0,2},{2,0},{4,6},{6,4},{1,3},{3,1},{5,7},{7,5},{8,10},{10,8},{12,... | collective-permute-start | bytes 393224 | tf_op jit(solution)/shard_map/ppermute | solution.py:235
  29.5 6.7 %collective-permute-start.13 = (f32[256,128]{1,0:T(8,128)S(1)}, f32[256,128]{1,0:T(8,128)S(1)}, u32[]{:S(2)}, u32[]{:S(2)}) collective-permute-start(f32[256,128]{1,0:T(8,128)S(1)} %get-tuple-element.55), channel_id=1, source_target_pairs={{2,4},{4,2},{3,5},{5,3},{10,12},{12,10},{11,13},{13,11},{18,20},{2... | collective-permute-start | bytes 393224 | tf_op jit(solution)/shard_map/ppermute | solution.py:235
  30.2 6.0 %collective-permute-start.10 = (f32[128,128]{1,0:T(8,128)S(1)}, f32[128,128]{1,0:T(8,128)S(1)}, u32[]{:S(2)}, u32[]{:S(2)}) collective-permute-start(f32[128,128]{1,0:T(8,128)S(1)} %get-tuple-element.52), channel_id=1, source_target_pairs={{0,8},{8,0},{16,24},{24,16},{1,9},{9,1},{17,25},{25,17},{2,10},{10... | collective-permute-start | bytes 196616 | tf_op jit(solution)/shard_map/ppermute | solution.py:235
  33.5 2.6 %collective-permute-start.11 = (f32[128,128]{1,0:T(8,128)S(1)}, f32[128,128]{1,0:T(8,128)S(1)}, u32[]{:S(2)}, u32[]{:S(2)}) collective-permute-start(f32[128,128]{1,0:T(8,128)S(1)} %get-tuple-element.53), channel_id=1, source_target_pairs={{8,16},{16,8},{9,17},{17,9},{10,18},{18,10},{11,19},{19,11},{12,20... | collective-permute-start | bytes 196616 | tf_op jit(solution)/shard_map/ppermute | solution.py:235
  37.0 8.7 %collective-permute-start.19 = (f32[512,128]{1,0:T(8,128)S(1)}, f32[512,128]{1,0:T(8,128)S(1)}, u32[]{:S(2)}, u32[]{:S(2)}) collective-permute-start(f32[512,128]{1,0:T(8,128)S(1)} %get-tuple-element.62), channel_id=1, source_target_pairs={{0,1},{1,0},{2,3},{3,2},{4,5},{5,4},{6,7},{7,6},{8,9},{9,8},{10,11... | collective-permute-start | bytes 786440 | tf_op jit(solution)/shard_map/ppermute | solution.py:235
  37.6 8.1 %collective-permute-start.17 = (f32[256,128]{1,0:T(8,128)S(1)}, f32[256,128]{1,0:T(8,128)S(1)}, u32[]{:S(2)}, u32[]{:S(2)}) collective-permute-start(f32[256,128]{1,0:T(8,128)S(1)} %get-tuple-element.60), channel_id=1, source_target_pairs={{0,2},{2,0},{4,6},{6,4},{1,3},{3,1},{5,7},{7,5},{8,10},{10,8},{12,... | collective-permute-start | bytes 393224 | tf_op jit(solution)/shard_map/ppermute | solution.py:235
  39.2 6.6 %collective-permute-start.18 = (f32[256,128]{1,0:T(8,128)S(1)}, f32[256,128]{1,0:T(8,128)S(1)}, u32[]{:S(2)}, u32[]{:S(2)}) collective-permute-start(f32[256,128]{1,0:T(8,128)S(1)} %get-tuple-element.61), channel_id=1, source_target_pairs={{2,4},{4,2},{3,5},{5,3},{10,12},{12,10},{11,13},{13,11},{18,20},{2... | collective-permute-start | bytes 393224 | tf_op jit(solution)/shard_map/ppermute | solution.py:235
  39.8 5.9 %collective-permute-start.15 = (f32[128,128]{1,0:T(8,128)S(1)}, f32[128,128]{1,0:T(8,128)S(1)}, u32[]{:S(2)}, u32[]{:S(2)}) collective-permute-start(f32[128,128]{1,0:T(8,128)S(1)} %get-tuple-element.58), channel_id=1, source_target_pairs={{0,8},{8,0},{16,24},{24,16},{1,9},{9,1},{17,25},{25,17},{2,10},{10... | collective-permute-start | bytes 196616 | tf_op jit(solution)/shard_map/ppermute | solution.py:235
  43.2 2.5 %collective-permute-start.16 = (f32[128,128]{1,0:T(8,128)S(1)}, f32[128,128]{1,0:T(8,128)S(1)}, u32[]{:S(2)}, u32[]{:S(2)}) collective-permute-start(f32[128,128]{1,0:T(8,128)S(1)} %get-tuple-element.59), channel_id=1, source_target_pairs={{8,16},{16,8},{9,17},{17,9},{10,18},{18,10},{11,19},{19,11},{12,20... | collective-permute-start | bytes 196616 | tf_op jit(solution)/shard_map/ppermute | solution.py:235
  46.6 10.6 %collective-permute-start.21 = (f32[256,128]{1,0:T(8,128)S(1)}, f32[256,128]{1,0:T(8,128)S(1)}, u32[]{:S(2)}, u32[]{:S(2)}) collective-permute-start(f32[256,128]{1,0:T(8,128)S(1)} %get-tuple-element.67), channel_id=1, source_target_pairs={{2,0},{4,2},{6,4},{3,1},{5,3},{7,5},{10,8},{12,10},{14,12},{11,9},... | collective-permute-start | bytes 393224 | tf_op jit(solution)/shard_map/ppermute | solution.py:224
  47.9 9.3 %collective-permute-start.22 = (f32[256,128]{1,0:T(8,128)S(1)}, f32[256,128]{1,0:T(8,128)S(1)}, u32[]{:S(2)}, u32[]{:S(2)}) collective-permute-start(f32[256,128]{1,0:T(8,128)S(1)} %get-tuple-element.68), channel_id=1, source_target_pairs={{0,1},{1,0},{2,3},{3,2},{4,5},{5,4},{6,7},{7,6},{8,9},{9,8},{10,11... | collective-permute-start | bytes 393224 | tf_op jit(solution)/shard_map/ppermute | solution.py:224
  49.4 7.8 %collective-permute-start.20 = (f32[128,128]{1,0:T(8,128)S(1)}, f32[128,128]{1,0:T(8,128)S(1)}, u32[]{:S(2)}, u32[]{:S(2)}) collective-permute-start(f32[128,128]{1,0:T(8,128)S(1)} %get-tuple-element.66), channel_id=1, source_target_pairs={{8,0},{16,8},{24,16},{9,1},{17,9},{25,17},{10,2},{18,10},{26,18},{... | collective-permute-start | bytes 196616 | tf_op jit(solution)/shard_map/ppermute | solution.py:224
  58.2 2.2 %collective-permute-start.23 = (f32[136,128]{1,0:T(8,128)S(1)}, f32[136,128]{1,0:T(8,128)S(1)}, u32[]{:S(2)}, u32[]{:S(2)}) collective-permute-start(f32[136,128]{1,0:T(8,128)S(1)} %shard_map.51), channel_id=1, source_target_pairs={{0,2},{2,0},{4,6},{6,4},{1,3},{3,1},{5,7},{7,5},{8,10},{10,8},{12,... | collective-permute-start | bytes 208904 | tf_op jit(solution)/shard_map/ppermute | solution.py:323
  60.4 5.7 %collective-permute-start.24 = (f32[136,128]{1,0:T(8,128)S(1)}, f32[136,128]{1,0:T(8,128)S(1)}, u32[]{:S(2)}, u32[]{:S(2)}) collective-permute-start(f32[136,128]{1,0:T(8,128)S(1)} %add.15), channel_id=1, source_target_pairs={{0,4},{2,6},{4,0},{6,2},{1,5},{3,7},{5,1},{7,3},{8,12},{10,14},{12... | collective-permute-start | bytes 208904 | tf_op jit(solution)/shard_map/ppermute | solution.py:323
  66.1 4.4 %collective-permute-start.25 = (f32[136,128]{1,0:T(8,128)S(1)}, f32[136,128]{1,0:T(8,128)S(1)}, u32[]{:S(2)}, u32[]{:S(2)}) collective-permute-start(f32[136,128]{1,0:T(8,128)S(1)} %add.16), channel_id=1, source_target_pairs={{0,1},{1,0},{2,3},{3,2},{4,5},{5,4},{6,7},{7,6},{8,9},{9,8},{10,11... | collective-permute-start | bytes 208904 | tf_op jit(solution)/shard_map/ppermute | solution.py:323
  70.5 4.4 %collective-permute-start.26 = (f32[136,128]{1,0:T(8,128)S(1)}, f32[136,128]{1,0:T(8,128)S(1)}, u32[]{:S(2)}, u32[]{:S(2)}) collective-permute-start(f32[136,128]{1,0:T(8,128)S(1)} %add.17), channel_id=1, source_target_pairs={{0,8},{8,0},{16,24},{24,16},{1,9},{9,1},{17,25},{25,17},{2,10},{10... | collective-permute-start | bytes 208904 | tf_op jit(solution)/shard_map/ppermute | solution.py:323
  74.9 5.3 %collective-permute-start.27 = (f32[136,128]{1,0:T(8,128)S(1)}, f32[136,128]{1,0:T(8,128)S(1)}, u32[]{:S(2)}, u32[]{:S(2)}) collective-permute-start(f32[136,128]{1,0:T(8,128)S(1)} %add.18), channel_id=1, source_target_pairs={{0,16},{8,24},{16,0},{24,8},{1,17},{9,25},{17,1},{25,9},{2,18},{10... | collective-permute-start | bytes 208904 | tf_op jit(solution)/shard_map/ppermute | solution.py:323

commit v6 on v5

--- a/solution.py
+++ b/solution.py
@@ -63,57 +63,32 @@
     return {"x": refs[0:2], "y": refs[2:4], "z": refs[4 : 4 + nz], "nz": nz}
 
 
-def prepare(block, turned, at, s, nz):
-    parts = 4
-    rows = s.cells // parts
-
-    def body(at_ref, b_hbm, k_ref, w_ref, wide_ref, *refs):
-        out = split_faces(refs[: 4 + nz], nz)
-        edge = refs[4 + nz : 4 + 2 * nz]
-        b_ref, c_ref, sems = refs[-3:]
-        first = pltpu.make_async_copy(k_ref, c_ref, sems.at[parts])
-        first.start()
-        copies = []
-        for i in range(parts):
-            here = pl.ds(i * rows, rows)
-            copies.append(pltpu.make_async_copy(b_hbm.at[here], b_ref.at[here], sems.at[i]))
-            copies[-1].start()
-        first.wait()
-        tiles = [c_ref[y] for y in range(s.y)]
-        for x in range(s.x):
-            for y in range(s.y):
+def spread(turned, at, s, nz):
+    def body(at_ref, k_ref, wide_ref, *edge):
+        for y in range(s.y):
+            tile = k_ref[y]
+            for x in range(s.x):
                 wide_ref[pl.ds(x * s.row + y * s.z, s.z), :] = jnp.broadcast_to(
-                    tiles[y][:, x : x + 1], (s.z, s.k)
+                    tile[:, x : x + 1], (s.z, s.k)
                 )
-        for i in range(parts):
-            copies[i].wait()
-
-            def step(x, _):
-                here = pl.ds(pl.multiple_of(x * s.row, s.row), s.row)
-                w_ref[here, :] = jnp.sqrt(wide_ref[here, :]) * b_ref[here, :]
-                return 0
-
-            lax.fori_loop(i * s.x // parts, (i + 1) * s.x // parts, step, 0, unroll=2)
         for i in range(nz):
             edge[i][...] = wide_ref[pl.ds(at_ref[4 + i], s.x * s.y, stride=s.z), :]
-        faces_of(s, at_ref, w_ref, out)
-
-    outs = [f32(s.room, s.k)] * 2 + face_shapes(s, nz) + [f32(s.x * s.y, s.k)] * nz
-    return pl.pallas_call(
-        body,
-        out_shape=outs,
-        in_specs=[SMEM] + [pl.BlockSpec(memory_space=pltpu.HBM)] * 2,
-        out_specs=tuple(VMEM for _ in outs),
-        scratch_shapes=[
-            pltpu.VMEM((s.cells, s.k), jnp.float32),
-            pltpu.VMEM(turned.shape, jnp.float32),
-            pltpu.SemaphoreType.DMA((parts + 1,)),
-        ],
-        compiler_params=pltpu.CompilerParams(vmem_limit_bytes=32 * 1024 * 1024),
-        cost_estimate=pl.CostEstimate(
-            flops=4 * s.cells * s.k, bytes_accessed=16 * s.cells * s.k, transcendentals=0
-        ),
-    )(at, block, turned)
+
+    outs = [f32(s.room, s.k)] + [f32(s.x * s.y, s.k)] * nz
+    return call(body, outs, [at, turned], s.cells * s.k)
+
+
+def prepare(block, wide, at, s, nz):
+    def body(at_ref, b_ref, k_ref, w_ref, *faces):
+        def step(x, _):
+            here = pl.ds(pl.multiple_of(x * s.row, s.row), s.row)
+            w_ref[here, :] = jnp.sqrt(k_ref[here, :]) * b_ref[here, :]
+            return 0
+
+        lax.fori_loop(0, s.x, step, 0, unroll=2)
+        faces_of(s, at_ref, w_ref, split_faces(faces, nz))
+
+    return call(body, [f32(s.room, s.k)] + face_shapes(s, nz), [at, block, wide], 4 * s.cells * s.k)
 
 
 def around(s, w_ref, x, low, high, emit):
@@ -292,7 +267,7 @@
 def pack_terms(gram, own, w, ghosts, at, s, nz, cells):
     k = s.k
 
-    def body(at_ref, g_ref, m_ref, w_ref, x_ref, y_ref, z_ref, p_ref):
+    def body(at_ref, g_ref, m_ref, w_ref, x_ref, y_ref, z_ref, mine_ref, other_ref):
         lefts = [w_ref[s.cells - s.row : s.cells, :]]
         tops = [w_ref[(x + 1) * s.row - s.z : (x + 1) * s.row, :] for x in range(s.x)]
         lefts.append(jnp.concatenate(tops, axis=0))
@@ -307,22 +282,46 @@
         raw = (m + m.T) * (0.5 / cells)
         below = lax.broadcasted_iota(jnp.int32, (k, k), 0)
         along = lax.broadcasted_iota(jnp.int32, (k, k), 1)
-        p_ref[:k, :] = jnp.where(below >= along, g_ref[...] * (1.0 / cells), raw)
+        full = jnp.where(below >= along, g_ref[...] * (1.0 / cells), raw)
         diagonal = jnp.sum(jnp.where(below == along, raw, 0.0), axis=0, keepdims=True)
-        p_ref[k:, :] = jnp.broadcast_to(diagonal, (8, k))
+        even = at_ref[7] == 0
+        for ref, first in ((mine_ref, even), (other_ref, jnp.logical_not(even))):
+            ref[: k // 2, :] = jnp.where(first, full[: k // 2, :], full[k // 2 :, :])
+            ref[k // 2 :, :] = jnp.broadcast_to(diagonal, (8, k))
 
     ins = [at, gram, own, w] + list(ghosts)
-    return call(body, [f32(k + 8, k)], ins, 6 * s.cells * k)[0]
-
-
-def total(value, axes):
-    for axis in axes:
-        count = lax.axis_size(axis)
-        bit = 1
-        while bit < count:
-            value = value + lax.ppermute(value, axis, [(i, i ^ bit) for i in range(count)])
+    return call(body, [f32(k // 2 + 8, k)] * 2, ins, 6 * s.cells * k)
+
+
+def total(mine, other):
+    axes = ("gx", "gy", "gz")
+    sizes = [lax.axis_size(a) for a in axes]
+
+    def swap(value, flip):
+        pairs = []
+        for i in range(sizes[0] * sizes[1] * sizes[2]):
+            x, y, z = i // (sizes[1] * sizes[2]), i // sizes[2] % sizes[1], i % sizes[2]
+            x, y, z = x ^ flip[0], y ^ flip[1], z ^ flip[2]
+            pairs.append((i, (x * sizes[1] + y) * sizes[2] + z))
+        return lax.ppermute(value, axes, pairs)
+
+    hops = []
+    for d, first in ((1, 2), (2, 1), (0, 1)):
+        bit = first
+        while bit < sizes[d]:
+            hops.append(tuple(bit if e == d else 0 for e in range(3)))
             bit *= 2
-    return value
+    pair = (0, 1, 0)
+    value = mine + swap(other, pair)
+    while hops:
+        a, *hops = hops
+        if hops:
+            b, *hops = hops
+            c = tuple(i ^ j for i, j in zip(a, b))
+            value = (value + swap(value, a)) + (swap(value, b) + swap(value, c))
+        else:
+            value = value + swap(value, a)
+    return value, swap(value, pair)
 
 
 PANEL = 32
@@ -361,21 +360,27 @@
             m_ref[top + PANEL :, :] = m_ref[top + PANEL :, :] - update[top + PANEL :, :]
 
 
-def orthonormal(packed, filtered, s):
+def orthonormal(own, got, filtered, at, s):
     k = s.k
-    rows = s.cells // 8
-
-    def body(p_ref, f_ref, b_ref, o_ref, m_ref, t_ref):
+    parts = 4
+    rows = s.cells // parts
+
+    def body(at_ref, own_ref, got_ref, f_ref, b_ref, o_ref, m_ref, t_ref):
         @pl.when(pl.program_id(0) == 0)
         def _():
-            upper = p_ref[:k, :]
+            even = at_ref[7] == 0
+            one, other = own_ref[: k // 2, :], got_ref[: k // 2, :]
+            upper = jnp.concatenate(
+                [jnp.where(even, one, other), jnp.where(even, other, one)], axis=0
+            )
+            diagonal = jnp.where(even, own_ref[k // 2 : k // 2 + 1, :], got_ref[k // 2 : k // 2 + 1, :])
             turned = upper.T
             below = lax.broadcasted_iota(jnp.int32, (k, k), 0)
             along = lax.broadcasted_iota(jnp.int32, (k, k), 1)
             m_ref[:, :k] = jnp.where(below >= along, upper, turned)
             m_ref[:, k:] = jnp.where(below == along, 1.0, 0.0)
             raw = jnp.where(below < along, upper, turned)
-            raw = jnp.where(below == along, p_ref[k : k + 1, :], raw)
+            raw = jnp.where(below == along, diagonal, raw)
             eliminate(m_ref, k)
             inverse = m_ref[:, k:]
             half = jnp.dot(inverse, raw, precision=HIGH, preferred_element_type=jnp.float32)
@@ -393,9 +398,9 @@
 
     return pl.pallas_call(
         body,
-        grid=(8,),
+        grid=(parts,),
         out_shape=[f32(s.cells, k), f32(k, k)],
-        in_specs=[VMEM, VMEM],
+        in_specs=[SMEM, VMEM, VMEM, VMEM],
         out_specs=(
             pl.BlockSpec((rows, k), lambda i: (i, 0)),
             pl.BlockSpec((k, k), lambda i: (0, 0)),
@@ -405,7 +410,7 @@
         cost_estimate=pl.CostEstimate(
             flops=8 * s.cells * k * k, bytes_accessed=8 * s.cells * k, transcendentals=0
         ),
-    )(packed, filtered)
+    )(at, own, got, filtered)
 
 
 def on_device(block, conductivity):
@@ -423,8 +428,8 @@
 
     flat = block.reshape(s.cells, s.k)
     turned = jnp.transpose(conductivity, (1, 2, 0))
-    w, wide, *rest = prepare(flat, turned, at, s, nz)
-    faces, edge = rest[: 4 + nz], rest[4 + nz :]
+    wide, *edge = spread(turned, at, s, nz)
+    w, *faces = prepare(flat, wide, at, s, nz)
     before = None
     for step in range(DEG):
         ghosts = exchange(faces, axes)
@@ -434,8 +439,8 @@
         w, *faces = finish(part, wide, edge, ghosts, at, s, nz, scale, step == DEG - 1)
     ghosts = one_way(faces, s, nz)
     filtered, gram, own = gather_terms(w, wide, at, s)
-    packed = total(pack_terms(gram, own, w, ghosts, at, s, nz, cells), ("gy", "gz", "gx"))
-    basis, projected = orthonormal(packed, filtered, s)
+    halves = total(*pack_terms(gram, own, w, ghosts, at, s, nz, cells))
+    basis, projected = orthonormal(*halves, filtered, at, s)
     return (basis.reshape(block.shape), projected)
 
 

time: 89 us -> 86.9 us (0.976)
  waiting for transfers between devices: 17.2 us -> 15.2 us
    pallas_call x2 -> x1, Pallas kernels: 10.8 us -> 7.5 us  [orthonormal(): pl.pallas_call(body, grid=(parts,), out_shape=[f32(s.cells, k), f32(k, k)...]
    pallas_call x9 -> x11, Pallas kernels: 11.8 us -> 14.7 us  [call(): pl.pallas_call(body, out_shape=outs, in_specs=[SMEM] + [VMEM] * (len(ins)...]
    ppermute x5 -> x8, waiting for transfers between devices: 11.8 us -> 9.72 us  [swap(): return lax.ppermute(value, axes, pairs)]
    ppermute x5 -> x8, starting transfers between devices: 10.1 us -> 10.5 us  [swap(): return lax.ppermute(value, axes, pairs)]
  transfers between devices with their start and end apart: 28 -> 31, of which waited for: 9 -> 11; matrix products, arithmetic and copies ran while one was open for 0% -> 0% of each run, Pallas kernels for 12% -> 12%
where the time goes in v6:
time: 86.9 us; the launch traced here: 86.5 us
  starting transfers between devices  42.8 us (49%)
  Pallas kernels  25 us (29%)
  waiting for transfers between devices  15.2 us (17%)
  local copies, waits for them, and re-layouts  2.51 us (3%)
  between operations  0.96 us (1%)
    ppermute x20, starting transfers between devices, exchange(): got.append(lax.ppermute(face, axis, pairs))  28.2 us
    pallas_call x11, Pallas kernels, call(): pl.pallas_call(body, out_shape=outs, in_specs=[SMEM] + [VMEM] * (len(ins)...  14.7 us
    ppermute x8, starting transfers between devices, swap(): return lax.ppermute(value, axes, pairs)  10.5 us
    ppermute x8, waiting for transfers between devices, swap(): return lax.ppermute(value, axes, pairs)  9.72 us
    pallas_call x1, Pallas kernels, orthonormal(): pl.pallas_call(body, grid=(parts,), out_shape=[f32(s.cells, k), f32(k, k)...  7.5 us
    ppermute x3, starting transfers between devices, one_way(): got.append(lax.ppermute(face, axis, pairs))  4.13 us
    ppermute x3, waiting for transfers between devices, one_way(): got.append(lax.ppermute(face, axis, pairs))  3.53 us
    pallas_call x1, Pallas kernels, gather_terms(): pl.pallas_call(body, out_shape=outs, in_specs=[SMEM, VMEM, VMEM], out_spe...  2.84 us
  transfers between devices with their start and end apart: 31, of which 11 were waited for; matrix products, arithmetic and copies ran while one was open for 0% of the time, Pallas kernels for 12%

profile of v6, /device:TPU:0, one launch (start us, length us, event | category | flops | bytes accessed | tf_op | source)
XLA Modules:
  0.0 86.5 jit_solution(3438973646084577859)
XLA Ops:
  1.6 1.6 %shard_map.41 = (f32[4104,128]{1,0:T(8,128)S(1)}, f32[512,128]{1,0:T(8,128)S(1)}) custom-call(s32[8]{0:T(128)S(1)} %stack.35.at_ref, f32[16,8,32]{2,1,0:T(8,128)S(1)} %bitcast.12), custom_call_target="tpu_custom_call" | custom-call | flops 524288 | bytes 2379808 | tf_op jit(solution)/shard_map/pallas_call | solution.py:21
  3.2 1.6 %copy-done = f32[32,16,8,128]{3,2,1,0:T(8,128)S(1)} copy-done((f32[32,16,8,128]{3,2,1,0:T(8,128)S(1)}, f32[32,16,8,128]{3,2,1,0:T(8,128)}, u32[]{:S(2)}) %copy-start) | copy-done | bytes 2097176
  4.8 1.3 %shard_map.42 = (f32[4104,128]{1,0:T(8,128)S(1)}, f32[128,128]{1,0:T(8,128)S(1)}, f32[128,128]{1,0:T(8,128)S(1)}, f32[256,128]{1,0:T(8,128)S(1)}, f32[256,128]{1,0:T(8,128)S(1)}, /*index=5*/f32[512,128]{1,0:T(8,128)S(1)}) custom-call(s32[8]{0:T(128)S(1)} %stack.35.at_ref, f32[4096,128]{1,0:T(8,128)S(1)} %bitcast.11, f32[4104,128]{1,0:T(8,128)S(1)} %get-tuple-element.39.k_ref), custom_call_target="tpu_custom_call" | custom-call | flops 2097152 | bytes 6955040 | tf_op jit(solution)/shard_map/pallas_call | solution.py:21
  6.1 3.0 %collective-permute-start.4 = (f32[512,128]{1,0:T(8,128)S(1)}, f32[512,128]{1,0:T(8,128)S(1)}, u32[]{:S(2)}, u32[]{:S(2)}) collective-permute-start(f32[512,128]{1,0:T(8,128)S(1)} %get-tuple-element.46), channel_id=1, source_target_pairs={{0,1},{1,0},{2,3},{3,2},{4,5},{5,4},{6,7},{7,6},{8,9},{9,8},{10,11... | collective-permute-start | bytes 786440 | tf_op jit(solution)/shard_map/ppermute | solution.py:210
  9.8 1.6 %collective-permute-start = (f32[128,128]{1,0:T(8,128)S(1)}, f32[128,128]{1,0:T(8,128)S(1)}, u32[]{:S(2)}, u32[]{:S(2)}) collective-permute-start(f32[128,128]{1,0:T(8,128)S(1)} %get-tuple-element.42), channel_id=1, source_target_pairs={{0,8},{8,0},{16,24},{24,16},{1,9},{9,1},{17,25},{25,17},{2,10},{10... | collective-permute-start | bytes 196616 | tf_op jit(solution)/shard_map/ppermute | solution.py:210
  12.1 1.8 %shard_map.43.p_ref = f32[4104,128]{1,0:T(8,128)S(1)} custom-call(s32[8]{0:T(128)S(1)} %stack.35.at_ref, f32[4104,128]{1,0:T(8,128)S(1)} %get-tuple-element.40.w_ref.rest_0_, f32[4104,128]{1,0:T(8,128)S(1)} %get-tuple-element.39.k_ref), custom_call_target="tpu_custom_call" | custom-call | flops 6291456 | bytes 6303776 | tf_op jit(solution)/shard_map/pallas_call | solution.py:21
  14.1 1.3 %collective-permute-done.4.refs_5_ = f32[512,128]{1,0:T(8,128)S(1)} collective-permute-done((f32[512,128]{1,0:T(8,128)S(1)}, f32[512,128]{1,0:T(8,128)S(1)}, u32[]{:S(2)}, u32[]{:S(2)}) %collective-permute-start.4) | collective-permute-done | bytes 262176 | tf_op jit(solution)/shard_map/ppermute | solution.py:210
  16.2 1.8 %collective-permute-start.9 = (f32[512,128]{1,0:T(8,128)S(1)}, f32[512,128]{1,0:T(8,128)S(1)}, u32[]{:S(2)}, u32[]{:S(2)}) collective-permute-start(f32[512,128]{1,0:T(8,128)S(1)} %get-tuple-element.52), channel_id=1, source_target_pairs={{0,1},{1,0},{2,3},{3,2},{4,5},{5,4},{6,7},{7,6},{8,9},{9,8},{10,11... | collective-permute-start | bytes 786440 | tf_op jit(solution)/shard_map/ppermute | solution.py:210
  18.7 3.8 %collective-permute-start.5 = (f32[128,128]{1,0:T(8,128)S(1)}, f32[128,128]{1,0:T(8,128)S(1)}, u32[]{:S(2)}, u32[]{:S(2)}) collective-permute-start(f32[128,128]{1,0:T(8,128)S(1)} %get-tuple-element.48), channel_id=1, source_target_pairs={{0,8},{8,0},{16,24},{24,16},{1,9},{9,1},{17,25},{25,17},{2,10},{10... | collective-permute-start | bytes 196616 | tf_op jit(solution)/shard_map/ppermute | solution.py:210
  23.1 1.8 %shard_map.45.p_ref = f32[4104,128]{1,0:T(8,128)S(1)} custom-call(s32[8]{0:T(128)S(1)} %stack.35.at_ref, f32[4104,128]{1,0:T(8,128)S(1)} %get-tuple-element.47.w_ref.rest_0_, f32[4104,128]{1,0:T(8,128)S(1)} %get-tuple-element.39.k_ref, f32[4104,128]{1,0:T(8,128)S(1)} %get-tuple-element.40.w_ref.rest_0_), custom_call_target="tpu_custom_call" | custom-call | flops 6291456 | bytes 8405024 | tf_op jit(solution)/shard_map/pallas_call | solution.py:21
  26.2 1.2 %collective-permute-start.14 = (f32[512,128]{1,0:T(8,128)S(1)}, f32[512,128]{1,0:T(8,128)S(1)}, u32[]{:S(2)}, u32[]{:S(2)}) collective-permute-start(f32[512,128]{1,0:T(8,128)S(1)} %get-tuple-element.58), channel_id=1, source_target_pairs={{0,1},{1,0},{2,3},{3,2},{4,5},{5,4},{6,7},{7,6},{8,9},{9,8},{10,11... | collective-permute-start | bytes 786440 | tf_op jit(solution)/shard_map/ppermute | solution.py:210
  27.4 2.6 %collective-permute-start.12 = (f32[256,128]{1,0:T(8,128)S(1)}, f32[256,128]{1,0:T(8,128)S(1)}, u32[]{:S(2)}, u32[]{:S(2)}) collective-permute-start(f32[256,128]{1,0:T(8,128)S(1)} %get-tuple-element.56), channel_id=1, source_target_pairs={{0,2},{2,0},{4,6},{6,4},{1,3},{3,1},{5,7},{7,5},{8,10},{10,8},{12,... | collective-permute-start | bytes 393224 | tf_op jit(solution)/shard_map/ppermute | solution.py:210
  30.6 3.3 %collective-permute-start.10 = (f32[128,128]{1,0:T(8,128)S(1)}, f32[128,128]{1,0:T(8,128)S(1)}, u32[]{:S(2)}, u32[]{:S(2)}) collective-permute-start(f32[128,128]{1,0:T(8,128)S(1)} %get-tuple-element.54), channel_id=1, source_target_pairs={{0,8},{8,0},{16,24},{24,16},{1,9},{9,1},{17,25},{25,17},{2,10},{10... | collective-permute-start | bytes 196616 | tf_op jit(solution)/shard_map/ppermute | solution.py:210
  34.7 1.9 %shard_map.47.p_ref = f32[4104,128]{1,0:T(8,128)S(1)} custom-call(s32[8]{0:T(128)S(1)} %stack.35.at_ref, f32[4104,128]{1,0:T(8,128)S(1)} %get-tuple-element.53.w_ref.rest_0_, f32[4104,128]{1,0:T(8,128)S(1)} %get-tuple-element.39.k_ref, f32[4104,128]{1,0:T(8,128)S(1)} %get-tuple-element.47.w_ref.rest_0_), custom_call_target="tpu_custom_call" | custom-call | flops 6291456 | bytes 8405024 | tf_op jit(solution)/shard_map/pallas_call | solution.py:21
  38.1 1.6 %collective-permute-start.17 = (f32[256,128]{1,0:T(8,128)S(1)}, f32[256,128]{1,0:T(8,128)S(1)}, u32[]{:S(2)}, u32[]{:S(2)}) collective-permute-start(f32[256,128]{1,0:T(8,128)S(1)} %get-tuple-element.62), channel_id=1, source_target_pairs={{0,2},{2,0},{4,6},{6,4},{1,3},{3,1},{5,7},{7,5},{8,10},{10,8},{12,... | collective-permute-start | bytes 393224 | tf_op jit(solution)/shard_map/ppermute | solution.py:210
  40.4 3.3 %collective-permute-start.15 = (f32[128,128]{1,0:T(8,128)S(1)}, f32[128,128]{1,0:T(8,128)S(1)}, u32[]{:S(2)}, u32[]{:S(2)}) collective-permute-start(f32[128,128]{1,0:T(8,128)S(1)} %get-tuple-element.60), channel_id=1, source_target_pairs={{0,8},{8,0},{16,24},{24,16},{1,9},{9,1},{17,25},{25,17},{2,10},{10... | collective-permute-start | bytes 196616 | tf_op jit(solution)/shard_map/ppermute | solution.py:210
  44.4 1.9 %shard_map.49.p_ref = f32[4104,128]{1,0:T(8,128)S(1)} custom-call(s32[8]{0:T(128)S(1)} %stack.35.at_ref, f32[4104,128]{1,0:T(8,128)S(1)} %get-tuple-element.59.w_ref, f32[4104,128]{1,0:T(8,128)S(1)} %get-tuple-element.39.k_ref, f32[4104,128]{1,0:T(8,128)S(1)} %get-tuple-element.53.w_ref.rest_0_), custom_call_target="tpu_custom_call" | custom-call | flops 6291456 | bytes 8405024 | tf_op jit(solution)/shard_map/pallas_call | solution.py:21
  47.2 1.3 %collective-permute-start.21 = (f32[256,128]{1,0:T(8,128)S(1)}, f32[256,128]{1,0:T(8,128)S(1)}, u32[]{:S(2)}, u32[]{:S(2)}) collective-permute-start(f32[256,128]{1,0:T(8,128)S(1)} %get-tuple-element.69), channel_id=1, source_target_pairs={{2,0},{4,2},{6,4},{3,1},{5,3},{7,5},{10,8},{12,10},{14,12},{11,9},... | collective-permute-start | bytes 393224 | tf_op jit(solution)/shard_map/ppermute | solution.py:199
  48.5 1.6 %collective-permute-start.22 = (f32[256,128]{1,0:T(8,128)S(1)}, f32[256,128]{1,0:T(8,128)S(1)}, u32[]{:S(2)}, u32[]{:S(2)}) collective-permute-start(f32[256,128]{1,0:T(8,128)S(1)} %get-tuple-element.70), channel_id=1, source_target_pairs={{0,1},{1,0},{2,3},{3,2},{4,5},{5,4},{6,7},{7,6},{8,9},{9,8},{10,11... | collective-permute-start | bytes 393224 | tf_op jit(solution)/shard_map/ppermute | solution.py:199
  50.1 1.3 %collective-permute-start.20 = (f32[128,128]{1,0:T(8,128)S(1)}, f32[128,128]{1,0:T(8,128)S(1)}, u32[]{:S(2)}, u32[]{:S(2)}) collective-permute-start(f32[128,128]{1,0:T(8,128)S(1)} %get-tuple-element.68), channel_id=1, source_target_pairs={{8,0},{16,8},{24,16},{9,1},{17,9},{25,17},{10,2},{18,10},{26,18},{... | collective-permute-start | bytes 196616 | tf_op jit(solution)/shard_map/ppermute | solution.py:199
  51.4 2.8 %shard_map.51 = (f32[4096,128]{1,0:T(8,128)S(1)}, f32[128,128]{1,0:T(8,128)S(1)}, f32[128,128]{1,0:T(8,128)S(1)}) custom-call(s32[8]{0:T(128)S(1)} %stack.35.at_ref, f32[4104,128]{1,0:T(8,128)S(1)} %get-tuple-element.65.w_ref, f32[4104,128]{1,0:T(8,128)S(1)} %get-tuple-element.39.k_ref), custom_call_target="tpu_custom_call" | custom-call | flops 1073741824 | bytes 8388608 | tf_op jit(solution)/shard_map/pallas_call | solution.py:254
  54.2 3.5 %collective-permute-done.20.x_ref = f32[128,128]{1,0:T(8,128)S(1)} collective-permute-done((f32[128,128]{1,0:T(8,128)S(1)}, f32[128,128]{1,0:T(8,128)S(1)}, u32[]{:S(2)}, u32[]{:S(2)}) %collective-permute-start.20) | collective-permute-done | bytes 65568 | tf_op jit(solution)/shard_map/ppermute | solution.py:199
  58.7 1.4 %collective-permute-start.23 = (f32[72,128]{1,0:T(8,128)S(1)}, f32[72,128]{1,0:T(8,128)S(1)}, u32[]{:S(2)}, u32[]{:S(2)}) collective-permute-start(f32[72,128]{1,0:T(8,128)S(1)} %get-tuple-element.72), channel_id=1, source_target_pairs={{0,2},{1,3},{2,0},{3,1},{4,6},{5,7},{6,4},{7,5},{8,10},{9,11},{10,... | collective-permute-start | bytes 110600 | tf_op jit(solution)/shard_map/ppermute | solution.py:306
  60.9 3.1 %collective-permute-start.26 = (f32[72,128]{1,0:T(8,128)S(1)}, f32[72,128]{1,0:T(8,128)S(1)}, u32[]{:S(2)}, u32[]{:S(2)}) collective-permute-start(f32[72,128]{1,0:T(8,128)S(1)} %add.21), channel_id=1, source_target_pairs={{0,5},{1,4},{2,7},{3,6},{4,1},{5,0},{6,3},{7,2},{8,13},{9,12},{10,... | collective-permute-start | bytes 110600 | tf_op jit(solution)/shard_map/ppermute | solution.py:306
  64.0 1.5 %collective-permute-start.25 = (f32[72,128]{1,0:T(8,128)S(1)}, f32[72,128]{1,0:T(8,128)S(1)}, u32[]{:S(2)}, u32[]{:S(2)}) collective-permute-start(f32[72,128]{1,0:T(8,128)S(1)} %add.21), channel_id=1, source_target_pairs={{0,1},{1,0},{2,3},{3,2},{4,5},{5,4},{6,7},{7,6},{8,9},{9,8},{10,11... | collective-permute-start | bytes 110600 | tf_op jit(solution)/shard_map/ppermute | solution.py:306
  66.0 2.0 %collective-permute-done.25 = f32[72,128]{1,0:T(8,128)S(1)} collective-permute-done((f32[72,128]{1,0:T(8,128)S(1)}, f32[72,128]{1,0:T(8,128)S(1)}, u32[]{:S(2)}, u32[]{:S(2)}) %collective-permute-start.25) | collective-permute-done | bytes 36896 | tf_op jit(solution)/shard_map/ppermute | solution.py:306
  68.0 1.5 %collective-permute-done.24 = f32[72,128]{1,0:T(8,128)S(1)} collective-permute-done((f32[72,128]{1,0:T(8,128)S(1)}, f32[72,128]{1,0:T(8,128)S(1)}, u32[]{:S(2)}, u32[]{:S(2)}) %collective-permute-start.24) | collective-permute-done | bytes 36896 | tf_op jit(solution)/shard_map/ppermute | solution.py:306
  69.5 3.0 %collective-permute-start.29 = (f32[72,128]{1,0:T(8,128)S(1)}, f32[72,128]{1,0:T(8,128)S(1)}, u32[]{:S(2)}, u32[]{:S(2)}) collective-permute-start(f32[72,128]{1,0:T(8,128)S(1)} %add_add_fusion.1), channel_id=1, source_target_pairs={{0,24},{1,25},{2,26},{3,27},{4,28},{5,29},{6,30},{7,31},{8,16},{9,... | collective-permute-start | bytes 110600 | tf_op jit(solution)/shard_map/ppermute | solution.py:306
  74.0 1.4 %collective-permute-done.29 = f32[72,128]{1,0:T(8,128)S(1)} collective-permute-done((f32[72,128]{1,0:T(8,128)S(1)}, f32[72,128]{1,0:T(8,128)S(1)}, u32[]{:S(2)}, u32[]{:S(2)}) %collective-permute-start.29) | collective-permute-done | bytes 36896 | tf_op jit(solution)/shard_map/ppermute | solution.py:306
  75.3 2.3 %collective-permute-done.28 = f32[72,128]{1,0:T(8,128)S(1)} collective-permute-done((f32[72,128]{1,0:T(8,128)S(1)}, f32[72,128]{1,0:T(8,128)S(1)}, u32[]{:S(2)}, u32[]{:S(2)}) %collective-permute-start.28) | collective-permute-done | bytes 36896 | tf_op jit(solution)/shard_map/ppermute | solution.py:306
  77.8 1.2 %collective-permute-done.30.got_ref = f32[72,128]{1,0:T(8,128)S(1)} collective-permute-done((f32[72,128]{1,0:T(8,128)S(1)}, f32[72,128]{1,0:T(8,128)S(1)}, u32[]{:S(2)}, u32[]{:S(2)}) %collective-permute-start.30) | collective-permute-done | bytes 36896 | tf_op jit(solution)/shard_map/ppermute | solution.py:306
  79.0 7.5 %shard_map.53 = (f32[4096,128]{1,0:T(8,128)}, f32[128,128]{1,0:T(8,128)}) custom-call(s32[8]{0:T(128)S(1)} %stack.35.at_ref, f32[72,128]{1,0:T(8,128)S(1)} %add_add_fusion.own_ref, f32[72,128]{1,0:T(8,128)S(1)} %collective-permute-done.30.got_ref, f32[4096,128]{1,0:T(8,128)S(1)} %get-tuple-element.73.f_ref), custom_call_target="tpu_custom_call" | custom-call | flops 536870912 | bytes 4194304 | tf_op jit(solution)/shard_map/pallas_call | solution.py:399
  (51 shorter events, 14.6 us)
Async XLA Ops:
  3.2 1.6 %copy-start = (f32[32,16,8,128]{3,2,1,0:T(8,128)S(1)}, f32[32,16,8,128]{3,2,1,0:T(8,128)}, u32[]{:S(2)}) copy-start(f32[32,16,8,128]{3,2,1,0:T(8,128)} %param.2) | copy-start | bytes 6291460
  6.1 9.3 %collective-permute-start.4 = (f32[512,128]{1,0:T(8,128)S(1)}, f32[512,128]{1,0:T(8,128)S(1)}, u32[]{:S(2)}, u32[]{:S(2)}) collective-permute-start(f32[512,128]{1,0:T(8,128)S(1)} %get-tuple-element.46), channel_id=1, source_target_pairs={{0,1},{1,0},{2,3},{3,2},{4,5},{5,4},{6,7},{7,6},{8,9},{9,8},{10,11... | collective-permute-start | bytes 786440 | tf_op jit(solution)/shard_map/ppermute | solution.py:210
  9.1 5.0 %collective-permute-start.2 = (f32[256,128]{1,0:T(8,128)S(1)}, f32[256,128]{1,0:T(8,128)S(1)}, u32[]{:S(2)}, u32[]{:S(2)}) collective-permute-start(f32[256,128]{1,0:T(8,128)S(1)} %get-tuple-element.44), channel_id=1, source_target_pairs={{0,2},{2,0},{4,6},{6,4},{1,3},{3,1},{5,7},{7,5},{8,10},{10,8},{12,... | collective-permute-start | bytes 393224 | tf_op jit(solution)/shard_map/ppermute | solution.py:210
  9.1 5.0 %collective-permute-start.3 = (f32[256,128]{1,0:T(8,128)S(1)}, f32[256,128]{1,0:T(8,128)S(1)}, u32[]{:S(2)}, u32[]{:S(2)}) collective-permute-start(f32[256,128]{1,0:T(8,128)S(1)} %get-tuple-element.45), channel_id=1, source_target_pairs={{2,4},{4,2},{3,5},{5,3},{10,12},{12,10},{11,13},{13,11},{18,20},{2... | collective-permute-start | bytes 393224 | tf_op jit(solution)/shard_map/ppermute | solution.py:210
  9.8 4.3 %collective-permute-start = (f32[128,128]{1,0:T(8,128)S(1)}, f32[128,128]{1,0:T(8,128)S(1)}, u32[]{:S(2)}, u32[]{:S(2)}) collective-permute-start(f32[128,128]{1,0:T(8,128)S(1)} %get-tuple-element.42), channel_id=1, source_target_pairs={{0,8},{8,0},{16,24},{24,16},{1,9},{9,1},{17,25},{25,17},{2,10},{10... | collective-permute-start | bytes 196616 | tf_op jit(solution)/shard_map/ppermute | solution.py:210
  11.4 2.7 %collective-permute-start.1 = (f32[128,128]{1,0:T(8,128)S(1)}, f32[128,128]{1,0:T(8,128)S(1)}, u32[]{:S(2)}, u32[]{:S(2)}) collective-permute-start(f32[128,128]{1,0:T(8,128)S(1)} %get-tuple-element.43), channel_id=1, source_target_pairs={{8,16},{16,8},{9,17},{17,9},{10,18},{18,10},{11,19},{19,11},{12,20... | collective-permute-start | bytes 196616 | tf_op jit(solution)/shard_map/ppermute | solution.py:210
  16.2 9.1 %collective-permute-start.9 = (f32[512,128]{1,0:T(8,128)S(1)}, f32[512,128]{1,0:T(8,128)S(1)}, u32[]{:S(2)}, u32[]{:S(2)}) collective-permute-start(f32[512,128]{1,0:T(8,128)S(1)} %get-tuple-element.52), channel_id=1, source_target_pairs={{0,1},{1,0},{2,3},{3,2},{4,5},{5,4},{6,7},{7,6},{8,9},{9,8},{10,11... | collective-permute-start | bytes 786440 | tf_op jit(solution)/shard_map/ppermute | solution.py:210
  18.0 7.0 %collective-permute-start.7 = (f32[256,128]{1,0:T(8,128)S(1)}, f32[256,128]{1,0:T(8,128)S(1)}, u32[]{:S(2)}, u32[]{:S(2)}) collective-permute-start(f32[256,128]{1,0:T(8,128)S(1)} %get-tuple-element.50), channel_id=1, source_target_pairs={{0,2},{2,0},{4,6},{6,4},{1,3},{3,1},{5,7},{7,5},{8,10},{10,8},{12,... | collective-permute-start | bytes 393224 | tf_op jit(solution)/shard_map/ppermute | solution.py:210
  18.0 7.0 %collective-permute-start.8 = (f32[256,128]{1,0:T(8,128)S(1)}, f32[256,128]{1,0:T(8,128)S(1)}, u32[]{:S(2)}, u32[]{:S(2)}) collective-permute-start(f32[256,128]{1,0:T(8,128)S(1)} %get-tuple-element.51), channel_id=1, source_target_pairs={{2,4},{4,2},{3,5},{5,3},{10,12},{12,10},{11,13},{13,11},{18,20},{2... | collective-permute-start | bytes 393224 | tf_op jit(solution)/shard_map/ppermute | solution.py:210
  18.7 6.3 %collective-permute-start.5 = (f32[128,128]{1,0:T(8,128)S(1)}, f32[128,128]{1,0:T(8,128)S(1)}, u32[]{:S(2)}, u32[]{:S(2)}) collective-permute-start(f32[128,128]{1,0:T(8,128)S(1)} %get-tuple-element.48), channel_id=1, source_target_pairs={{0,8},{8,0},{16,24},{24,16},{1,9},{9,1},{17,25},{25,17},{2,10},{10... | collective-permute-start | bytes 196616 | tf_op jit(solution)/shard_map/ppermute | solution.py:210
  22.5 2.5 %collective-permute-start.6 = (f32[128,128]{1,0:T(8,128)S(1)}, f32[128,128]{1,0:T(8,128)S(1)}, u32[]{:S(2)}, u32[]{:S(2)}) collective-permute-start(f32[128,128]{1,0:T(8,128)S(1)} %get-tuple-element.49), channel_id=1, source_target_pairs={{8,16},{16,8},{9,17},{17,9},{10,18},{18,10},{11,19},{19,11},{12,20... | collective-permute-start | bytes 196616 | tf_op jit(solution)/shard_map/ppermute | solution.py:210
  26.2 10.5 %collective-permute-start.14 = (f32[512,128]{1,0:T(8,128)S(1)}, f32[512,128]{1,0:T(8,128)S(1)}, u32[]{:S(2)}, u32[]{:S(2)}) collective-permute-start(f32[512,128]{1,0:T(8,128)S(1)} %get-tuple-element.58), channel_id=1, source_target_pairs={{0,1},{1,0},{2,3},{3,2},{4,5},{5,4},{6,7},{7,6},{8,9},{9,8},{10,11... | collective-permute-start | bytes 786440 | tf_op jit(solution)/shard_map/ppermute | solution.py:210
  27.4 9.2 %collective-permute-start.12 = (f32[256,128]{1,0:T(8,128)S(1)}, f32[256,128]{1,0:T(8,128)S(1)}, u32[]{:S(2)}, u32[]{:S(2)}) collective-permute-start(f32[256,128]{1,0:T(8,128)S(1)} %get-tuple-element.56), channel_id=1, source_target_pairs={{0,2},{2,0},{4,6},{6,4},{1,3},{3,1},{5,7},{7,5},{8,10},{10,8},{12,... | collective-permute-start | bytes 393224 | tf_op jit(solution)/shard_map/ppermute | solution.py:210
  30.0 6.7 %collective-permute-start.13 = (f32[256,128]{1,0:T(8,128)S(1)}, f32[256,128]{1,0:T(8,128)S(1)}, u32[]{:S(2)}, u32[]{:S(2)}) collective-permute-start(f32[256,128]{1,0:T(8,128)S(1)} %get-tuple-element.57), channel_id=1, source_target_pairs={{2,4},{4,2},{3,5},{5,3},{10,12},{12,10},{11,13},{13,11},{18,20},{2... | collective-permute-start | bytes 393224 | tf_op jit(solution)/shard_map/ppermute | solution.py:210
  30.6 6.0 %collective-permute-start.10 = (f32[128,128]{1,0:T(8,128)S(1)}, f32[128,128]{1,0:T(8,128)S(1)}, u32[]{:S(2)}, u32[]{:S(2)}) collective-permute-start(f32[128,128]{1,0:T(8,128)S(1)} %get-tuple-element.54), channel_id=1, source_target_pairs={{0,8},{8,0},{16,24},{24,16},{1,9},{9,1},{17,25},{25,17},{2,10},{10... | collective-permute-start | bytes 196616 | tf_op jit(solution)/shard_map/ppermute | solution.py:210
  34.0 2.6 %collective-permute-start.11 = (f32[128,128]{1,0:T(8,128)S(1)}, f32[128,128]{1,0:T(8,128)S(1)}, u32[]{:S(2)}, u32[]{:S(2)}) collective-permute-start(f32[128,128]{1,0:T(8,128)S(1)} %get-tuple-element.55), channel_id=1, source_target_pairs={{8,16},{16,8},{9,17},{17,9},{10,18},{18,10},{11,19},{19,11},{12,20... | collective-permute-start | bytes 196616 | tf_op jit(solution)/shard_map/ppermute | solution.py:210
  37.5 8.9 %collective-permute-start.19 = (f32[512,128]{1,0:T(8,128)S(1)}, f32[512,128]{1,0:T(8,128)S(1)}, u32[]{:S(2)}, u32[]{:S(2)}) collective-permute-start(f32[512,128]{1,0:T(8,128)S(1)} %get-tuple-element.64), channel_id=1, source_target_pairs={{0,1},{1,0},{2,3},{3,2},{4,5},{5,4},{6,7},{7,6},{8,9},{9,8},{10,11... | collective-permute-start | bytes 786440 | tf_op jit(solution)/shard_map/ppermute | solution.py:210
  38.1 8.2 %collective-permute-start.17 = (f32[256,128]{1,0:T(8,128)S(1)}, f32[256,128]{1,0:T(8,128)S(1)}, u32[]{:S(2)}, u32[]{:S(2)}) collective-permute-start(f32[256,128]{1,0:T(8,128)S(1)} %get-tuple-element.62), channel_id=1, source_target_pairs={{0,2},{2,0},{4,6},{6,4},{1,3},{3,1},{5,7},{7,5},{8,10},{10,8},{12,... | collective-permute-start | bytes 393224 | tf_op jit(solution)/shard_map/ppermute | solution.py:210
  39.7 6.7 %collective-permute-start.18 = (f32[256,128]{1,0:T(8,128)S(1)}, f32[256,128]{1,0:T(8,128)S(1)}, u32[]{:S(2)}, u32[]{:S(2)}) collective-permute-start(f32[256,128]{1,0:T(8,128)S(1)} %get-tuple-element.63), channel_id=1, source_target_pairs={{2,4},{4,2},{3,5},{5,3},{10,12},{12,10},{11,13},{13,11},{18,20},{2... | collective-permute-start | bytes 393224 | tf_op jit(solution)/shard_map/ppermute | solution.py:210
  40.4 6.0 %collective-permute-start.15 = (f32[128,128]{1,0:T(8,128)S(1)}, f32[128,128]{1,0:T(8,128)S(1)}, u32[]{:S(2)}, u32[]{:S(2)}) collective-permute-start(f32[128,128]{1,0:T(8,128)S(1)} %get-tuple-element.60), channel_id=1, source_target_pairs={{0,8},{8,0},{16,24},{24,16},{1,9},{9,1},{17,25},{25,17},{2,10},{10... | collective-permute-start | bytes 196616 | tf_op jit(solution)/shard_map/ppermute | solution.py:210
  43.7 2.6 %collective-permute-start.16 = (f32[128,128]{1,0:T(8,128)S(1)}, f32[128,128]{1,0:T(8,128)S(1)}, u32[]{:S(2)}, u32[]{:S(2)}) collective-permute-start(f32[128,128]{1,0:T(8,128)S(1)} %get-tuple-element.61), channel_id=1, source_target_pairs={{8,16},{16,8},{9,17},{17,9},{10,18},{18,10},{11,19},{19,11},{12,20... | collective-permute-start | bytes 196616 | tf_op jit(solution)/shard_map/ppermute | solution.py:210
  47.2 10.5 %collective-permute-start.21 = (f32[256,128]{1,0:T(8,128)S(1)}, f32[256,128]{1,0:T(8,128)S(1)}, u32[]{:S(2)}, u32[]{:S(2)}) collective-permute-start(f32[256,128]{1,0:T(8,128)S(1)} %get-tuple-element.69), channel_id=1, source_target_pairs={{2,0},{4,2},{6,4},{3,1},{5,3},{7,5},{10,8},{12,10},{14,12},{11,9},... | collective-permute-start | bytes 393224 | tf_op jit(solution)/shard_map/ppermute | solution.py:199
  48.5 9.2 %collective-permute-start.22 = (f32[256,128]{1,0:T(8,128)S(1)}, f32[256,128]{1,0:T(8,128)S(1)}, u32[]{:S(2)}, u32[]{:S(2)}) collective-permute-start(f32[256,128]{1,0:T(8,128)S(1)} %get-tuple-element.70), channel_id=1, source_target_pairs={{0,1},{1,0},{2,3},{3,2},{4,5},{5,4},{6,7},{7,6},{8,9},{9,8},{10,11... | collective-permute-start | bytes 393224 | tf_op jit(solution)/shard_map/ppermute | solution.py:199
  50.1 7.7 %collective-permute-start.20 = (f32[128,128]{1,0:T(8,128)S(1)}, f32[128,128]{1,0:T(8,128)S(1)}, u32[]{:S(2)}, u32[]{:S(2)}) collective-permute-start(f32[128,128]{1,0:T(8,128)S(1)} %get-tuple-element.68), channel_id=1, source_target_pairs={{8,0},{16,8},{24,16},{9,1},{17,9},{25,17},{10,2},{18,10},{26,18},{... | collective-permute-start | bytes 196616 | tf_op jit(solution)/shard_map/ppermute | solution.py:199
  58.7 2.2 %collective-permute-start.23 = (f32[72,128]{1,0:T(8,128)S(1)}, f32[72,128]{1,0:T(8,128)S(1)}, u32[]{:S(2)}, u32[]{:S(2)}) collective-permute-start(f32[72,128]{1,0:T(8,128)S(1)} %get-tuple-element.72), channel_id=1, source_target_pairs={{0,2},{1,3},{2,0},{3,1},{4,6},{5,7},{6,4},{7,5},{8,10},{9,11},{10,... | collective-permute-start | bytes 110600 | tf_op jit(solution)/shard_map/ppermute | solution.py:306
  60.9 5.0 %collective-permute-start.26 = (f32[72,128]{1,0:T(8,128)S(1)}, f32[72,128]{1,0:T(8,128)S(1)}, u32[]{:S(2)}, u32[]{:S(2)}) collective-permute-start(f32[72,128]{1,0:T(8,128)S(1)} %add.21), channel_id=1, source_target_pairs={{0,5},{1,4},{2,7},{3,6},{4,1},{5,0},{6,3},{7,2},{8,13},{9,12},{10,... | collective-permute-start | bytes 110600 | tf_op jit(solution)/shard_map/ppermute | solution.py:306
  64.0 4.0 %collective-permute-start.25 = (f32[72,128]{1,0:T(8,128)S(1)}, f32[72,128]{1,0:T(8,128)S(1)}, u32[]{:S(2)}, u32[]{:S(2)}) collective-permute-start(f32[72,128]{1,0:T(8,128)S(1)} %add.21), channel_id=1, source_target_pairs={{0,1},{1,0},{2,3},{3,2},{4,5},{5,4},{6,7},{7,6},{8,9},{9,8},{10,11... | collective-permute-start | bytes 110600 | tf_op jit(solution)/shard_map/ppermute | solution.py:306
  65.5 4.0 %collective-permute-start.24 = (f32[72,128]{1,0:T(8,128)S(1)}, f32[72,128]{1,0:T(8,128)S(1)}, u32[]{:S(2)}, u32[]{:S(2)}) collective-permute-start(f32[72,128]{1,0:T(8,128)S(1)} %add.21), channel_id=1, source_target_pairs={{0,4},{1,5},{2,6},{3,7},{4,0},{5,1},{6,2},{7,3},{8,12},{9,13},{10,... | collective-permute-start | bytes 110600 | tf_op jit(solution)/shard_map/ppermute | solution.py:306
  69.5 5.8 %collective-permute-start.29 = (f32[72,128]{1,0:T(8,128)S(1)}, f32[72,128]{1,0:T(8,128)S(1)}, u32[]{:S(2)}, u32[]{:S(2)}) collective-permute-start(f32[72,128]{1,0:T(8,128)S(1)} %add_add_fusion.1), channel_id=1, source_target_pairs={{0,24},{1,25},{2,26},{3,27},{4,28},{5,29},{6,30},{7,31},{8,16},{9,... | collective-permute-start | bytes 110600 | tf_op jit(solution)/shard_map/ppermute | solution.py:306
  72.5 5.2 %collective-permute-start.28 = (f32[72,128]{1,0:T(8,128)S(1)}, f32[72,128]{1,0:T(8,128)S(1)}, u32[]{:S(2)}, u32[]{:S(2)}) collective-permute-start(f32[72,128]{1,0:T(8,128)S(1)} %add_add_fusion.1), channel_id=1, source_target_pairs={{0,16},{1,17},{2,18},{3,19},{4,20},{5,21},{6,22},{7,23},{8,24},{9,... | collective-permute-start | bytes 110600 | tf_op jit(solution)/shard_map/ppermute | solution.py:306
  73.0 4.6 %collective-permute-start.27 = (f32[72,128]{1,0:T(8,128)S(1)}, f32[72,128]{1,0:T(8,128)S(1)}, u32[]{:S(2)}, u32[]{:S(2)}) collective-permute-start(f32[72,128]{1,0:T(8,128)S(1)} %add_add_fusion.1), channel_id=1, source_target_pairs={{0,8},{1,9},{2,10},{3,11},{4,12},{5,13},{6,14},{7,15},{8,0},{9,1},... | collective-permute-start | bytes 110600 | tf_op jit(solution)/shard_map/ppermute | solution.py:306
  77.7 1.3 %collective-permute-start.30 = (f32[72,128]{1,0:T(8,128)S(1)}, f32[72,128]{1,0:T(8,128)S(1)}, u32[]{:S(2)}, u32[]{:S(2)}) collective-permute-start(f32[72,128]{1,0:T(8,128)S(1)} %add_add_fusion.own_ref), channel_id=1, source_target_pairs={{0,2},{1,3},{2,0},{3,1},{4,6},{5,7},{6,4},{7,5},{8,10},{9,11},{10,... | collective-permute-start | bytes 110600 | tf_op jit(solution)/shard_map/ppermute | solution.py:306
  (1 other events, 0.8 us)

commit v7 on v6

--- a/solution.py
+++ b/solution.py
@@ -63,38 +63,28 @@
     return {"x": refs[0:2], "y": refs[2:4], "z": refs[4 : 4 + nz], "nz": nz}
 
 
-def spread(turned, at, s, nz):
-    def body(at_ref, k_ref, wide_ref, *edge):
+def prepare(block, turned, at, s, nz):
+    def body(at_ref, b_ref, k_ref, w_ref, wide_ref, *refs):
         for y in range(s.y):
             tile = k_ref[y]
             for x in range(s.x):
-                wide_ref[pl.ds(x * s.row + y * s.z, s.z), :] = jnp.broadcast_to(
-                    tile[:, x : x + 1], (s.z, s.k)
-                )
+                here = pl.ds(x * s.row + y * s.z, s.z)
+                k = jnp.broadcast_to(tile[:, x : x + 1], (s.z, s.k))
+                wide_ref[here, :] = k
+                w_ref[here, :] = jnp.sqrt(k) * b_ref[here, :]
         for i in range(nz):
-            edge[i][...] = wide_ref[pl.ds(at_ref[4 + i], s.x * s.y, stride=s.z), :]
-
-    outs = [f32(s.room, s.k)] + [f32(s.x * s.y, s.k)] * nz
-    return call(body, outs, [at, turned], s.cells * s.k)
-
-
-def prepare(block, wide, at, s, nz):
-    def body(at_ref, b_ref, k_ref, w_ref, *faces):
-        def step(x, _):
-            here = pl.ds(pl.multiple_of(x * s.row, s.row), s.row)
-            w_ref[here, :] = jnp.sqrt(k_ref[here, :]) * b_ref[here, :]
-            return 0
-
-        lax.fori_loop(0, s.x, step, 0, unroll=2)
-        faces_of(s, at_ref, w_ref, split_faces(faces, nz))
-
-    return call(body, [f32(s.room, s.k)] + face_shapes(s, nz), [at, block, wide], 4 * s.cells * s.k)
-
-
-def around(s, w_ref, x, low, high, emit):
+            refs[4 + nz + i][...] = wide_ref[pl.ds(at_ref[4 + i], s.x * s.y, stride=s.z), :]
+        faces_of(s, at_ref, w_ref, split_faces(refs, nz))
+
+    outs = [f32(s.room, s.k)] * 2 + face_shapes(s, nz) + [f32(s.x * s.y, s.k)] * nz
+    return call(body, outs, [at, block, turned], 4 * s.cells * s.k)
+
+
+def around(s, w_ref, o_ref, x, low, high, emit):
     base = pl.multiple_of(x * s.row, s.row)
     place = lax.broadcasted_iota(jnp.int32, (s.z, s.k), 0)
     tiles = [w_ref[pl.ds(base + y * s.z, s.z), :] for y in range(s.y)]
+    done = []
     for y in range(s.y):
         c = tiles[y]
         up = jnp.where(place == s.z - 1, 0.0, pltpu.roll(c, s.z - 1, 0))
@@ -108,18 +98,21 @@
             near = near + w_ref[pl.ds(base - s.row + y * s.z, s.z), :]
         if high:
             near = near + w_ref[pl.ds(base + s.row + y * s.z, s.z), :]
-        emit(pl.ds(base + y * s.z, s.z), c, near)
-
-
-def sweep(s, w_ref, emit):
-    around(s, w_ref, 0, False, True, emit)
+        here = pl.ds(base + y * s.z, s.z)
+        done.append((here, emit(here, c, near)))
+    for here, new in done:
+        o_ref[here, :] = new
+
+
+def sweep(s, w_ref, o_ref, emit):
+    around(s, w_ref, o_ref, 0, False, True, emit)
 
     def step(x, _):
-        around(s, w_ref, x, True, True, emit)
+        around(s, w_ref, o_ref, x, True, True, emit)
         return 0
 
-    lax.fori_loop(1, s.x - 1, step, 0)
-    around(s, w_ref, s.x - 1, True, False, emit)
+    lax.fori_loop(1, s.x - 1, step, 0, unroll=2)
+    around(s, w_ref, o_ref, s.x - 1, True, False, emit)
 
 
 def interior(w, before, wide, at, s):
@@ -132,9 +125,9 @@
             new = k_ref[here, :] * ((c - near * (1.0 / 6.0)) * scale) - (scale * center_value) * c
             if before is not None:
                 new = new - rest[0][here, :]
-            o_ref[here, :] = new
-
-        sweep(s, w_ref, emit)
+            return new
+
+        sweep(s, w_ref, o_ref, emit)
 
     ins = [at, w, wide] + ([] if before is None else [before])
     return call(body, [f32(s.room, s.k)], ins, 12 * s.cells * s.k)[0]
@@ -154,18 +147,25 @@
         for i in range(2):
             here = pl.ds(at_ref[i] * s.row, s.row)
             w_ref[here, :] = w_ref[here, :] - (k_ref[here, :] * factor) * ghost["x"][i][...]
+            done = []
             for x in range(s.x):
                 here = pl.ds(x * s.row + at_ref[2 + i] * s.z, s.z)
                 g = ghost["y"][i][pl.ds(x * s.z, s.z), :]
-                w_ref[here, :] = w_ref[here, :] - (k_ref[here, :] * factor) * g
+                done.append((here, w_ref[here, :] - (k_ref[here, :] * factor) * g))
+            for here, new in done:
+                w_ref[here, :] = new
         for i in range(nz):
-            for x in range(s.x):
-                here = pl.ds(x * s.row + at_ref[4 + i], s.y, stride=s.z)
-                flat = pl.ds(x * s.y, s.y)
-                new = w_ref[here, :] - (edges[i][flat, :] * factor) * ghost["z"][i][flat, :]
-                w_ref[here, :] = new
-                if not last:
-                    out["z"][i][flat, :] = new
+            for first in range(0, s.x, 8):
+                done = []
+                for x in range(first, min(first + 8, s.x)):
+                    here = pl.ds(x * s.row + at_ref[4 + i], s.y, stride=s.z)
+                    flat = pl.ds(x * s.y, s.y)
+                    new = w_ref[here, :] - (edges[i][flat, :] * factor) * ghost["z"][i][flat, :]
+                    done.append((here, flat, new))
+                for here, flat, new in done:
+                    w_ref[here, :] = new
+                    if not last:
+                        out["z"][i][flat, :] = new
         if last:
             out[0][...] = w_ref[: s.row, :]
             for x in range(s.x):
@@ -233,23 +233,22 @@
 
     def body(at_ref, w_ref, k_ref, f_ref, g_ref, m_ref, q_ref):
         def emit(here, c, near):
-            q_ref[here, :] = c - near * (1.0 / 6.0)
-
-        sweep(s, w_ref, emit)
+            return c - near * (1.0 / 6.0)
+
+        sweep(s, w_ref, q_ref, emit)
         sums = jnp.zeros((2 * s.k, 4 * s.k), jnp.float32)
         for i in range(s.cells // rows):
             here = pl.ds(i * rows, rows)
             k = k_ref[here, :]
             inverse = lax.rsqrt(k)
-            f = w_ref[here, :] * inverse
-            f_ref[here, :] = f
-            pair = two(f)
+            pair = two(w_ref[here, :] * inverse)
+            f_ref[here, :] = pair
             image = two((k * inverse) * q_ref[here, :])
             sums += transposed_dot(pair, jnp.concatenate([pair, image], axis=1))
         g_ref[...] = both(sums[:, : 2 * s.k])
         m_ref[...] = both(sums[:, 2 * s.k :])
 
-    outs = [f32(s.cells, s.k), f32(s.k, s.k), f32(s.k, s.k)]
+    outs = [jax.ShapeDtypeStruct((s.cells, 2 * s.k), BF), f32(s.k, s.k), f32(s.k, s.k)]
     moved = 4 * 4 * s.cells * s.k
     return pl.pallas_call(
         body,
@@ -325,7 +324,7 @@
 
 
 PANEL = 32
-GROUP = 8
+GROUP = 16
 
 
 def eliminate(m_ref, n):
@@ -365,47 +364,49 @@
     parts = 4
     rows = s.cells // parts
 
-    def body(at_ref, own_ref, got_ref, f_ref, b_ref, o_ref, m_ref, t_ref):
-        @pl.when(pl.program_id(0) == 0)
-        def _():
-            even = at_ref[7] == 0
-            one, other = own_ref[: k // 2, :], got_ref[: k // 2, :]
-            upper = jnp.concatenate(
-                [jnp.where(even, one, other), jnp.where(even, other, one)], axis=0
-            )
-            diagonal = jnp.where(even, own_ref[k // 2 : k // 2 + 1, :], got_ref[k // 2 : k // 2 + 1, :])
-            turned = upper.T
-            below = lax.broadcasted_iota(jnp.int32, (k, k), 0)
-            along = lax.broadcasted_iota(jnp.int32, (k, k), 1)
-            m_ref[:, :k] = jnp.where(below >= along, upper, turned)
-            m_ref[:, k:] = jnp.where(below == along, 1.0, 0.0)
-            raw = jnp.where(below < along, upper, turned)
-            raw = jnp.where(below == along, diagonal, raw)
-            eliminate(m_ref, k)
-            inverse = m_ref[:, k:]
-            half = jnp.dot(inverse, raw, precision=HIGH, preferred_element_type=jnp.float32)
-            o_ref[...] = lax.dot_general(
-                half, inverse, (((1,), (1,)), ((), ())),
-                precision=HIGH, preferred_element_type=jnp.float32,
-            )
-            pair = two(inverse.T)
-            t_ref[:k, :] = pair
-            t_ref[k:, :] = pair
-
-        f = f_ref[pl.ds(pl.multiple_of(pl.program_id(0) * rows, rows), rows), :]
-        out = jnp.dot(two(f), t_ref[...], preferred_element_type=jnp.float32)
-        b_ref[...] = out[:, :k] + out[:, k:]
+    def body(at_ref, own_ref, got_ref, f_ref, b_hbm, o_ref, m_ref, b_ref, sems):
+        even = at_ref[7] == 0
+        one, other = own_ref[: k // 2, :], got_ref[: k // 2, :]
+        upper = jnp.concatenate(
+            [jnp.where(even, one, other), jnp.where(even, other, one)], axis=0
+        )
+        low, high = own_ref[k // 2 : k // 2 + 1, :], got_ref[k // 2 : k // 2 + 1, :]
+        turned = upper.T
+        below = lax.broadcasted_iota(jnp.int32, (k, k), 0)
+        along = lax.broadcasted_iota(jnp.int32, (k, k), 1)
+        m_ref[:, :k] = jnp.where(below >= along, upper, turned)
+        m_ref[:, k:] = jnp.where(below == along, 1.0, 0.0)
+        eliminate(m_ref, k)
+        inverse = m_ref[:, k:]
+        pair = two(inverse.T)
+        pair = jnp.concatenate([pair, pair], axis=0)
+        copies = []
+        for i in range(parts):
+            here = pl.ds(i * rows, rows)
+            out = jnp.dot(f_ref[here, :], pair, preferred_element_type=jnp.float32)
+            b_ref[here, :] = out[:, :k] + out[:, k:]
+            copies.append(pltpu.make_async_copy(b_ref.at[here], b_hbm.at[here], sems.at[i]))
+            copies[-1].start()
+        raw = jnp.where(below < along, upper, turned)
+        raw = jnp.where(below == along, jnp.where(even, low, high), raw)
+        half = jnp.dot(inverse, raw, precision=HIGH, preferred_element_type=jnp.float32)
+        o_ref[...] = lax.dot_general(
+            half, inverse, (((1,), (1,)), ((), ())),
+            precision=HIGH, preferred_element_type=jnp.float32,
+        )
+        for copy in copies:
+            copy.wait()
 
     return pl.pallas_call(
         body,
-        grid=(parts,),
         out_shape=[f32(s.cells, k), f32(k, k)],
         in_specs=[SMEM, VMEM, VMEM, VMEM],
-        out_specs=(
-            pl.BlockSpec((rows, k), lambda i: (i, 0)),
-            pl.BlockSpec((k, k), lambda i: (0, 0)),
-        ),
-        scratch_shapes=[pltpu.VMEM((k, 2 * k), jnp.float32), pltpu.VMEM((2 * k, 2 * k), BF)],
+        out_specs=(pl.BlockSpec(memory_space=pl.ANY), VMEM),
+        scratch_shapes=[
+            pltpu.VMEM((k, 2 * k), jnp.float32),
+            pltpu.VMEM((s.cells, k), jnp.float32),
+            pltpu.SemaphoreType.DMA((parts,)),
+        ],
         compiler_params=pltpu.CompilerParams(vmem_limit_bytes=32 * 1024 * 1024),
         cost_estimate=pl.CostEstimate(
             flops=8 * s.cells * k * k, bytes_accessed=8 * s.cells * k, transcendentals=0
@@ -428,8 +429,8 @@
 
     flat = block.reshape(s.cells, s.k)
     turned = jnp.transpose(conductivity, (1, 2, 0))
-    wide, *edge = spread(turned, at, s, nz)
-    w, *faces = prepare(flat, wide, at, s, nz)
+    w, wide, *rest = prepare(flat, turned, at, s, nz)
+    faces, edge = rest[: 4 + nz], rest[4 + nz :]
     before = None
     for step in range(DEG):
         ghosts = exchange(faces, axes)

time: 86.9 us -> 84.6 us (0.974)
  Pallas kernels: 25 us -> 22.3 us
    pallas_call x11 -> x10, Pallas kernels: 14.7 us -> 13 us  [call(): pl.pallas_call(body, out_shape=outs, in_specs=[SMEM] + [VMEM] * (len(ins)...]
    pallas_call x1, Pallas kernels: 7.5 us -> 6.52 us  [orthonormal(): pl.pallas_call(body, out_shape=[f32(s.cells, k), f32(k, k)], in_specs=[SM...]
where the time goes in v7:
time: 84.6 us; the launch traced here: 84.2 us
  starting transfers between devices  42.5 us (50%)
  Pallas kernels  22.3 us (26%)
  waiting for transfers between devices  15.9 us (19%)
  local copies, waits for them, and re-layouts  2.52 us (3%)
  between operations  0.95 us (1%)
    ppermute x20, starting transfers between devices, exchange(): got.append(lax.ppermute(face, axis, pairs))  28 us
    pallas_call x10, Pallas kernels, call(): pl.pallas_call(body, out_shape=outs, in_specs=[SMEM] + [VMEM] * (len(ins)...  13 us
    ppermute x8, starting transfers between devices, swap(): return lax.ppermute(value, axes, pairs)  10.4 us
    ppermute x8, waiting for transfers between devices, swap(): return lax.ppermute(value, axes, pairs)  9.89 us
    pallas_call x1, Pallas kernels, orthonormal(): pl.pallas_call(body, out_shape=[f32(s.cells, k), f32(k, k)], in_specs=[SM...  6.52 us
    ppermute x3, starting transfers between devices, one_way(): got.append(lax.ppermute(face, axis, pairs))  4.13 us
    ppermute x3, waiting for transfers between devices, one_way(): got.append(lax.ppermute(face, axis, pairs))  3.79 us
    pallas_call x1, Pallas kernels, gather_terms(): pl.pallas_call(body, out_shape=outs, in_specs=[SMEM, VMEM, VMEM], out_spe...  2.76 us
  transfers between devices with their start and end apart: 31, of which 11 were waited for; matrix products, arithmetic and copies ran while one was open for 0% of the time, Pallas kernels for 12%

profile of v7, /device:TPU:0, one launch (start us, length us, event | category | flops | bytes accessed | tf_op | source)
XLA Modules:
  0.0 84.2 jit_solution(5651364098892591181)
XLA Ops:
  0.7 1.6 %copy-done = f32[32,16,8,128]{3,2,1,0:T(8,128)S(1)} copy-done((f32[32,16,8,128]{3,2,1,0:T(8,128)S(1)}, f32[32,16,8,128]{3,2,1,0:T(8,128)}, u32[]{:S(2)}) %copy-start) | copy-done | bytes 2097176
  3.2 1.7 %shard_map.41 = (f32[4104,128]{1,0:T(8,128)S(1)}, f32[4104,128]{1,0:T(8,128)S(1)}, f32[128,128]{1,0:T(8,128)S(1)}, f32[128,128]{1,0:T(8,128)S(1)}, f32[256,128]{...) custom-call(s32[8]{0:T(128)S(1)} %stack.35.at_ref, ...), custom_call_target="tpu_custom_call" | custom-call | flops 2097152 | bytes 7233568 | tf_op jit(solution)/shard_map/pallas_call | solution.py:21
  4.9 3.0 %collective-permute-start.4 = (f32[512,128]{1,0:T(8,128)S(1)}, f32[512,128]{1,0:T(8,128)S(1)}, u32[]{:S(2)}, u32[]{:S(2)}) collective-permute-start(f32[512,128]{1,0:T(8,128)S(1)} %get-tuple-element.46), channel_id=1, source_target_pairs={{0,1},{1,0},{2,3},{3,2},{4,5},{5,4},{6,7},{7,6},{8,9},{9,8},{10,11... | collective-permute-start | bytes 786440 | tf_op jit(solution)/shard_map/ppermute | solution.py:210
  8.5 1.6 %collective-permute-start = (f32[128,128]{1,0:T(8,128)S(1)}, f32[128,128]{1,0:T(8,128)S(1)}, u32[]{:S(2)}, u32[]{:S(2)}) collective-permute-start(f32[128,128]{1,0:T(8,128)S(1)} %get-tuple-element.42), channel_id=1, source_target_pairs={{0,8},{8,0},{16,24},{24,16},{1,9},{9,1},{17,25},{25,17},{2,10},{10... | collective-permute-start | bytes 196616 | tf_op jit(solution)/shard_map/ppermute | solution.py:210
  10.8 1.7 %shard_map.42.p_ref = f32[4104,128]{1,0:T(8,128)S(1)} custom-call(s32[8]{0:T(128)S(1)} %stack.35.at_ref, f32[4104,128]{1,0:T(8,128)S(1)} %get-tuple-element.39.w_ref.rest_0_, f32[4104,128]{1,0:T(8,128)S(1)} %get-tuple-element.40.k_ref), custom_call_target="tpu_custom_call" | custom-call | flops 6291456 | bytes 6303776 | tf_op jit(solution)/shard_map/pallas_call | solution.py:21
  12.9 1.3 %collective-permute-done.4.refs_5_ = f32[512,128]{1,0:T(8,128)S(1)} collective-permute-done((f32[512,128]{1,0:T(8,128)S(1)}, f32[512,128]{1,0:T(8,128)S(1)}, u32[]{:S(2)}, u32[]{:S(2)}) %collective-permute-start.4) | collective-permute-done | bytes 262176 | tf_op jit(solution)/shard_map/ppermute | solution.py:210
  15.0 1.8 %collective-permute-start.9 = (f32[512,128]{1,0:T(8,128)S(1)}, f32[512,128]{1,0:T(8,128)S(1)}, u32[]{:S(2)}, u32[]{:S(2)}) collective-permute-start(f32[512,128]{1,0:T(8,128)S(1)} %get-tuple-element.52), channel_id=1, source_target_pairs={{0,1},{1,0},{2,3},{3,2},{4,5},{5,4},{6,7},{7,6},{8,9},{9,8},{10,11... | collective-permute-start | bytes 786440 | tf_op jit(solution)/shard_map/ppermute | solution.py:210
  17.5 3.7 %collective-permute-start.5 = (f32[128,128]{1,0:T(8,128)S(1)}, f32[128,128]{1,0:T(8,128)S(1)}, u32[]{:S(2)}, u32[]{:S(2)}) collective-permute-start(f32[128,128]{1,0:T(8,128)S(1)} %get-tuple-element.48), channel_id=1, source_target_pairs={{0,8},{8,0},{16,24},{24,16},{1,9},{9,1},{17,25},{25,17},{2,10},{10... | collective-permute-start | bytes 196616 | tf_op jit(solution)/shard_map/ppermute | solution.py:210
  21.8 1.8 %shard_map.44.p_ref = f32[4104,128]{1,0:T(8,128)S(1)} custom-call(s32[8]{0:T(128)S(1)} %stack.35.at_ref, f32[4104,128]{1,0:T(8,128)S(1)} %get-tuple-element.47.w_ref.rest_0_, f32[4104,128]{1,0:T(8,128)S(1)} %get-tuple-element.40.k_ref, f32[4104,128]{1,0:T(8,128)S(1)} %get-tuple-element.39.w_ref.rest_0_), custom_call_target="tpu_custom_call" | custom-call | flops 6291456 | bytes 8405024 | tf_op jit(solution)/shard_map/pallas_call | solution.py:21
  25.0 1.0 %collective-permute-start.14 = (f32[512,128]{1,0:T(8,128)S(1)}, f32[512,128]{1,0:T(8,128)S(1)}, u32[]{:S(2)}, u32[]{:S(2)}) collective-permute-start(f32[512,128]{1,0:T(8,128)S(1)} %get-tuple-element.58), channel_id=1, source_target_pairs={{0,1},{1,0},{2,3},{3,2},{4,5},{5,4},{6,7},{7,6},{8,9},{9,8},{10,11... | collective-permute-start | bytes 786440 | tf_op jit(solution)/shard_map/ppermute | solution.py:210
  26.1 2.6 %collective-permute-start.12 = (f32[256,128]{1,0:T(8,128)S(1)}, f32[256,128]{1,0:T(8,128)S(1)}, u32[]{:S(2)}, u32[]{:S(2)}) collective-permute-start(f32[256,128]{1,0:T(8,128)S(1)} %get-tuple-element.56), channel_id=1, source_target_pairs={{0,2},{2,0},{4,6},{6,4},{1,3},{3,1},{5,7},{7,5},{8,10},{10,8},{12,... | collective-permute-start | bytes 393224 | tf_op jit(solution)/shard_map/ppermute | solution.py:210
  29.4 3.3 %collective-permute-start.10 = (f32[128,128]{1,0:T(8,128)S(1)}, f32[128,128]{1,0:T(8,128)S(1)}, u32[]{:S(2)}, u32[]{:S(2)}) collective-permute-start(f32[128,128]{1,0:T(8,128)S(1)} %get-tuple-element.54), channel_id=1, source_target_pairs={{0,8},{8,0},{16,24},{24,16},{1,9},{9,1},{17,25},{25,17},{2,10},{10... | collective-permute-start | bytes 196616 | tf_op jit(solution)/shard_map/ppermute | solution.py:210
  33.4 1.9 %shard_map.46.p_ref = f32[4104,128]{1,0:T(8,128)S(1)} custom-call(s32[8]{0:T(128)S(1)} %stack.35.at_ref, f32[4104,128]{1,0:T(8,128)S(1)} %get-tuple-element.53.w_ref.rest_0_, f32[4104,128]{1,0:T(8,128)S(1)} %get-tuple-element.40.k_ref, f32[4104,128]{1,0:T(8,128)S(1)} %get-tuple-element.47.w_ref.rest_0_), custom_call_target="tpu_custom_call" | custom-call | flops 6291456 | bytes 8405024 | tf_op jit(solution)/shard_map/pallas_call | solution.py:21
  36.7 1.7 %collective-permute-start.17 = (f32[256,128]{1,0:T(8,128)S(1)}, f32[256,128]{1,0:T(8,128)S(1)}, u32[]{:S(2)}, u32[]{:S(2)}) collective-permute-start(f32[256,128]{1,0:T(8,128)S(1)} %get-tuple-element.62), channel_id=1, source_target_pairs={{0,2},{2,0},{4,6},{6,4},{1,3},{3,1},{5,7},{7,5},{8,10},{10,8},{12,... | collective-permute-start | bytes 393224 | tf_op jit(solution)/shard_map/ppermute | solution.py:210
  39.1 3.3 %collective-permute-start.15 = (f32[128,128]{1,0:T(8,128)S(1)}, f32[128,128]{1,0:T(8,128)S(1)}, u32[]{:S(2)}, u32[]{:S(2)}) collective-permute-start(f32[128,128]{1,0:T(8,128)S(1)} %get-tuple-element.60), channel_id=1, source_target_pairs={{0,8},{8,0},{16,24},{24,16},{1,9},{9,1},{17,25},{25,17},{2,10},{10... | collective-permute-start | bytes 196616 | tf_op jit(solution)/shard_map/ppermute | solution.py:210
  43.1 1.8 %shard_map.48.p_ref = f32[4104,128]{1,0:T(8,128)S(1)} custom-call(s32[8]{0:T(128)S(1)} %stack.35.at_ref, f32[4104,128]{1,0:T(8,128)S(1)} %get-tuple-element.59.w_ref, f32[4104,128]{1,0:T(8,128)S(1)} %get-tuple-element.40.k_ref, f32[4104,128]{1,0:T(8,128)S(1)} %get-tuple-element.53.w_ref.rest_0_), custom_call_target="tpu_custom_call" | custom-call | flops 6291456 | bytes 8405024 | tf_op jit(solution)/shard_map/pallas_call | solution.py:21
  45.7 1.3 %collective-permute-start.21 = (f32[256,128]{1,0:T(8,128)S(1)}, f32[256,128]{1,0:T(8,128)S(1)}, u32[]{:S(2)}, u32[]{:S(2)}) collective-permute-start(f32[256,128]{1,0:T(8,128)S(1)} %get-tuple-element.69), channel_id=1, source_target_pairs={{2,0},{4,2},{6,4},{3,1},{5,3},{7,5},{10,8},{12,10},{14,12},{11,9},... | collective-permute-start | bytes 393224 | tf_op jit(solution)/shard_map/ppermute | solution.py:199
  47.0 1.6 %collective-permute-start.22 = (f32[256,128]{1,0:T(8,128)S(1)}, f32[256,128]{1,0:T(8,128)S(1)}, u32[]{:S(2)}, u32[]{:S(2)}) collective-permute-start(f32[256,128]{1,0:T(8,128)S(1)} %get-tuple-element.70), channel_id=1, source_target_pairs={{0,1},{1,0},{2,3},{3,2},{4,5},{5,4},{6,7},{7,6},{8,9},{9,8},{10,11... | collective-permute-start | bytes 393224 | tf_op jit(solution)/shard_map/ppermute | solution.py:199
  48.6 1.3 %collective-permute-start.20 = (f32[128,128]{1,0:T(8,128)S(1)}, f32[128,128]{1,0:T(8,128)S(1)}, u32[]{:S(2)}, u32[]{:S(2)}) collective-permute-start(f32[128,128]{1,0:T(8,128)S(1)} %get-tuple-element.68), channel_id=1, source_target_pairs={{8,0},{16,8},{24,16},{9,1},{17,9},{25,17},{10,2},{18,10},{26,18},{... | collective-permute-start | bytes 196616 | tf_op jit(solution)/shard_map/ppermute | solution.py:199
  49.9 2.8 %shard_map.50 = (bf16[4096,256]{1,0:T(8,128)(2,1)S(1)}, f32[128,128]{1,0:T(8,128)S(1)}, f32[128,128]{1,0:T(8,128)S(1)}) custom-call(s32[8]{0:T(128)S(1)} %stack.35.at_ref, f32[4104,128]{1,0:T(8,128)S(1)} %get-tuple-element.65.w_ref, f32[4104,128]{1,0:T(8,128)S(1)} %get-tuple-element.40.k_ref), custom_call_target="tpu_custom_call" | custom-call | flops 1073741824 | bytes 8388608 | tf_op jit(solution)/shard_map/pallas_call | solution.py:253
  52.6 3.8 %collective-permute-done.20.x_ref = f32[128,128]{1,0:T(8,128)S(1)} collective-permute-done((f32[128,128]{1,0:T(8,128)S(1)}, f32[128,128]{1,0:T(8,128)S(1)}, u32[]{:S(2)}, u32[]{:S(2)}) %collective-permute-start.20) | collective-permute-done | bytes 65568 | tf_op jit(solution)/shard_map/ppermute | solution.py:199
  56.4 1.0 %shard_map.51 = (f32[72,128]{1,0:T(8,128)S(1)}, f32[72,128]{1,0:T(8,128)S(1)}) custom-call(s32[8]{0:T(128)S(1)} %stack.35.at_ref, f32[128,128]{1,0:T(8,128)S(1)} %get-tuple-element.66.g_ref, f32[128,128]{1,0:T(8,128)S(1)} %get-tuple-element.67.m_ref, f32[4104,128]{1,0:T(8,128)S(1)} %get-tuple-element.65.w_ref, f32[128,128]{1,0:T(8,128)S(1)} %collective-permute-done.20.x_ref, ...), custom_call_target="tpu_custom_call" | custom-call | flops 3145728 | bytes 2633760 | tf_op jit(solution)/shard_map/pallas_call | solution.py:21
  57.4 1.3 %collective-permute-start.23 = (f32[72,128]{1,0:T(8,128)S(1)}, f32[72,128]{1,0:T(8,128)S(1)}, u32[]{:S(2)}, u32[]{:S(2)}) collective-permute-start(f32[72,128]{1,0:T(8,128)S(1)} %get-tuple-element.72), channel_id=1, source_target_pairs={{0,2},{1,3},{2,0},{3,1},{4,6},{5,7},{6,4},{7,5},{8,10},{9,11},{10,... | collective-permute-start | bytes 110600 | tf_op jit(solution)/shard_map/ppermute | solution.py:305
  59.5 3.1 %collective-permute-start.26 = (f32[72,128]{1,0:T(8,128)S(1)}, f32[72,128]{1,0:T(8,128)S(1)}, u32[]{:S(2)}, u32[]{:S(2)}) collective-permute-start(f32[72,128]{1,0:T(8,128)S(1)} %add.21), channel_id=1, source_target_pairs={{0,5},{1,4},{2,7},{3,6},{4,1},{5,0},{6,3},{7,2},{8,13},{9,12},{10,... | collective-permute-start | bytes 110600 | tf_op jit(solution)/shard_map/ppermute | solution.py:305
  62.6 1.5 %collective-permute-start.25 = (f32[72,128]{1,0:T(8,128)S(1)}, f32[72,128]{1,0:T(8,128)S(1)}, u32[]{:S(2)}, u32[]{:S(2)}) collective-permute-start(f32[72,128]{1,0:T(8,128)S(1)} %add.21), channel_id=1, source_target_pairs={{0,1},{1,0},{2,3},{3,2},{4,5},{5,4},{6,7},{7,6},{8,9},{9,8},{10,11... | collective-permute-start | bytes 110600 | tf_op jit(solution)/shard_map/ppermute | solution.py:305
  64.5 2.0 %collective-permute-done.25 = f32[72,128]{1,0:T(8,128)S(1)} collective-permute-done((f32[72,128]{1,0:T(8,128)S(1)}, f32[72,128]{1,0:T(8,128)S(1)}, u32[]{:S(2)}, u32[]{:S(2)}) %collective-permute-start.25) | collective-permute-done | bytes 36896 | tf_op jit(solution)/shard_map/ppermute | solution.py:305
  66.6 1.5 %collective-permute-done.24 = f32[72,128]{1,0:T(8,128)S(1)} collective-permute-done((f32[72,128]{1,0:T(8,128)S(1)}, f32[72,128]{1,0:T(8,128)S(1)}, u32[]{:S(2)}, u32[]{:S(2)}) %collective-permute-start.24) | collective-permute-done | bytes 36896 | tf_op jit(solution)/shard_map/ppermute | solution.py:305
  68.1 3.1 %collective-permute-start.29 = (f32[72,128]{1,0:T(8,128)S(1)}, f32[72,128]{1,0:T(8,128)S(1)}, u32[]{:S(2)}, u32[]{:S(2)}) collective-permute-start(f32[72,128]{1,0:T(8,128)S(1)} %add_add_fusion.1), channel_id=1, source_target_pairs={{0,24},{1,25},{2,26},{3,27},{4,28},{5,29},{6,30},{7,31},{8,16},{9,... | collective-permute-start | bytes 110600 | tf_op jit(solution)/shard_map/ppermute | solution.py:305
  72.5 1.4 %collective-permute-done.29 = f32[72,128]{1,0:T(8,128)S(1)} collective-permute-done((f32[72,128]{1,0:T(8,128)S(1)}, f32[72,128]{1,0:T(8,128)S(1)}, u32[]{:S(2)}, u32[]{:S(2)}) %collective-permute-start.29) | collective-permute-done | bytes 36896 | tf_op jit(solution)/shard_map/ppermute | solution.py:305
  73.9 2.5 %collective-permute-done.28 = f32[72,128]{1,0:T(8,128)S(1)} collective-permute-done((f32[72,128]{1,0:T(8,128)S(1)}, f32[72,128]{1,0:T(8,128)S(1)}, u32[]{:S(2)}, u32[]{:S(2)}) %collective-permute-start.28) | collective-permute-done | bytes 36896 | tf_op jit(solution)/shard_map/ppermute | solution.py:305
  76.5 1.2 %collective-permute-done.30.got_ref = f32[72,128]{1,0:T(8,128)S(1)} collective-permute-done((f32[72,128]{1,0:T(8,128)S(1)}, f32[72,128]{1,0:T(8,128)S(1)}, u32[]{:S(2)}, u32[]{:S(2)}) %collective-permute-start.30) | collective-permute-done | bytes 36896 | tf_op jit(solution)/shard_map/ppermute | solution.py:305
  77.7 6.5 %shard_map.52 = (f32[4096,128]{1,0:T(8,128)}, f32[128,128]{1,0:T(8,128)}) custom-call(s32[8]{0:T(128)S(1)} %stack.35.at_ref, f32[72,128]{1,0:T(8,128)S(1)} %add_add_fusion.own_ref, f32[72,128]{1,0:T(8,128)S(1)} %collective-permute-done.30.got_ref, bf16[4096,256]{1,0:T(8,128)(2,1)S(1)} %get-tuple-element.73.f_ref), custom_call_target="tpu_custom_call" | custom-call | flops 536870912 | bytes 4194304 | tf_op jit(solution)/shard_map/pallas_call | solution.py:400
  (50 shorter events, 13.7 us)
Async XLA Ops:
  0.7 1.6 %copy-start = (f32[32,16,8,128]{3,2,1,0:T(8,128)S(1)}, f32[32,16,8,128]{3,2,1,0:T(8,128)}, u32[]{:S(2)}) copy-start(f32[32,16,8,128]{3,2,1,0:T(8,128)} %param.2) | copy-start | bytes 6291460
  4.9 9.3 %collective-permute-start.4 = (f32[512,128]{1,0:T(8,128)S(1)}, f32[512,128]{1,0:T(8,128)S(1)}, u32[]{:S(2)}, u32[]{:S(2)}) collective-permute-start(f32[512,128]{1,0:T(8,128)S(1)} %get-tuple-element.46), channel_id=1, source_target_pairs={{0,1},{1,0},{2,3},{3,2},{4,5},{5,4},{6,7},{7,6},{8,9},{9,8},{10,11... | collective-permute-start | bytes 786440 | tf_op jit(solution)/shard_map/ppermute | solution.py:210
  7.9 5.0 %collective-permute-start.2 = (f32[256,128]{1,0:T(8,128)S(1)}, f32[256,128]{1,0:T(8,128)S(1)}, u32[]{:S(2)}, u32[]{:S(2)}) collective-permute-start(f32[256,128]{1,0:T(8,128)S(1)} %get-tuple-element.44), channel_id=1, source_target_pairs={{0,2},{2,0},{4,6},{6,4},{1,3},{3,1},{5,7},{7,5},{8,10},{10,8},{12,... | collective-permute-start | bytes 393224 | tf_op jit(solution)/shard_map/ppermute | solution.py:210
  7.9 5.0 %collective-permute-start.3 = (f32[256,128]{1,0:T(8,128)S(1)}, f32[256,128]{1,0:T(8,128)S(1)}, u32[]{:S(2)}, u32[]{:S(2)}) collective-permute-start(f32[256,128]{1,0:T(8,128)S(1)} %get-tuple-element.45), channel_id=1, source_target_pairs={{2,4},{4,2},{3,5},{5,3},{10,12},{12,10},{11,13},{13,11},{18,20},{2... | collective-permute-start | bytes 393224 | tf_op jit(solution)/shard_map/ppermute | solution.py:210
  8.5 4.3 %collective-permute-start = (f32[128,128]{1,0:T(8,128)S(1)}, f32[128,128]{1,0:T(8,128)S(1)}, u32[]{:S(2)}, u32[]{:S(2)}) collective-permute-start(f32[128,128]{1,0:T(8,128)S(1)} %get-tuple-element.42), channel_id=1, source_target_pairs={{0,8},{8,0},{16,24},{24,16},{1,9},{9,1},{17,25},{25,17},{2,10},{10... | collective-permute-start | bytes 196616 | tf_op jit(solution)/shard_map/ppermute | solution.py:210
  10.2 2.7 %collective-permute-start.1 = (f32[128,128]{1,0:T(8,128)S(1)}, f32[128,128]{1,0:T(8,128)S(1)}, u32[]{:S(2)}, u32[]{:S(2)}) collective-permute-start(f32[128,128]{1,0:T(8,128)S(1)} %get-tuple-element.43), channel_id=1, source_target_pairs={{8,16},{16,8},{9,17},{17,9},{10,18},{18,10},{11,19},{19,11},{12,20... | collective-permute-start | bytes 196616 | tf_op jit(solution)/shard_map/ppermute | solution.py:210
  15.0 9.2 %collective-permute-start.9 = (f32[512,128]{1,0:T(8,128)S(1)}, f32[512,128]{1,0:T(8,128)S(1)}, u32[]{:S(2)}, u32[]{:S(2)}) collective-permute-start(f32[512,128]{1,0:T(8,128)S(1)} %get-tuple-element.52), channel_id=1, source_target_pairs={{0,1},{1,0},{2,3},{3,2},{4,5},{5,4},{6,7},{7,6},{8,9},{9,8},{10,11... | collective-permute-start | bytes 786440 | tf_op jit(solution)/shard_map/ppermute | solution.py:210
  16.8 6.8 %collective-permute-start.7 = (f32[256,128]{1,0:T(8,128)S(1)}, f32[256,128]{1,0:T(8,128)S(1)}, u32[]{:S(2)}, u32[]{:S(2)}) collective-permute-start(f32[256,128]{1,0:T(8,128)S(1)} %get-tuple-element.50), channel_id=1, source_target_pairs={{0,2},{2,0},{4,6},{6,4},{1,3},{3,1},{5,7},{7,5},{8,10},{10,8},{12,... | collective-permute-start | bytes 393224 | tf_op jit(solution)/shard_map/ppermute | solution.py:210
  16.8 6.9 %collective-permute-start.8 = (f32[256,128]{1,0:T(8,128)S(1)}, f32[256,128]{1,0:T(8,128)S(1)}, u32[]{:S(2)}, u32[]{:S(2)}) collective-permute-start(f32[256,128]{1,0:T(8,128)S(1)} %get-tuple-element.51), channel_id=1, source_target_pairs={{2,4},{4,2},{3,5},{5,3},{10,12},{12,10},{11,13},{13,11},{18,20},{2... | collective-permute-start | bytes 393224 | tf_op jit(solution)/shard_map/ppermute | solution.py:210
  17.5 6.2 %collective-permute-start.5 = (f32[128,128]{1,0:T(8,128)S(1)}, f32[128,128]{1,0:T(8,128)S(1)}, u32[]{:S(2)}, u32[]{:S(2)}) collective-permute-start(f32[128,128]{1,0:T(8,128)S(1)} %get-tuple-element.48), channel_id=1, source_target_pairs={{0,8},{8,0},{16,24},{24,16},{1,9},{9,1},{17,25},{25,17},{2,10},{10... | collective-permute-start | bytes 196616 | tf_op jit(solution)/shard_map/ppermute | solution.py:210
  21.2 2.5 %collective-permute-start.6 = (f32[128,128]{1,0:T(8,128)S(1)}, f32[128,128]{1,0:T(8,128)S(1)}, u32[]{:S(2)}, u32[]{:S(2)}) collective-permute-start(f32[128,128]{1,0:T(8,128)S(1)} %get-tuple-element.49), channel_id=1, source_target_pairs={{8,16},{16,8},{9,17},{17,9},{10,18},{18,10},{11,19},{19,11},{12,20... | collective-permute-start | bytes 196616 | tf_op jit(solution)/shard_map/ppermute | solution.py:210
  25.0 10.3 %collective-permute-start.14 = (f32[512,128]{1,0:T(8,128)S(1)}, f32[512,128]{1,0:T(8,128)S(1)}, u32[]{:S(2)}, u32[]{:S(2)}) collective-permute-start(f32[512,128]{1,0:T(8,128)S(1)} %get-tuple-element.58), channel_id=1, source_target_pairs={{0,1},{1,0},{2,3},{3,2},{4,5},{5,4},{6,7},{7,6},{8,9},{9,8},{10,11... | collective-permute-start | bytes 786440 | tf_op jit(solution)/shard_map/ppermute | solution.py:210
  26.1 9.2 %collective-permute-start.12 = (f32[256,128]{1,0:T(8,128)S(1)}, f32[256,128]{1,0:T(8,128)S(1)}, u32[]{:S(2)}, u32[]{:S(2)}) collective-permute-start(f32[256,128]{1,0:T(8,128)S(1)} %get-tuple-element.56), channel_id=1, source_target_pairs={{0,2},{2,0},{4,6},{6,4},{1,3},{3,1},{5,7},{7,5},{8,10},{10,8},{12,... | collective-permute-start | bytes 393224 | tf_op jit(solution)/shard_map/ppermute | solution.py:210
  28.7 6.6 %collective-permute-start.13 = (f32[256,128]{1,0:T(8,128)S(1)}, f32[256,128]{1,0:T(8,128)S(1)}, u32[]{:S(2)}, u32[]{:S(2)}) collective-permute-start(f32[256,128]{1,0:T(8,128)S(1)} %get-tuple-element.57), channel_id=1, source_target_pairs={{2,4},{4,2},{3,5},{5,3},{10,12},{12,10},{11,13},{13,11},{18,20},{2... | collective-permute-start | bytes 393224 | tf_op jit(solution)/shard_map/ppermute | solution.py:210
  29.4 5.9 %collective-permute-start.10 = (f32[128,128]{1,0:T(8,128)S(1)}, f32[128,128]{1,0:T(8,128)S(1)}, u32[]{:S(2)}, u32[]{:S(2)}) collective-permute-start(f32[128,128]{1,0:T(8,128)S(1)} %get-tuple-element.54), channel_id=1, source_target_pairs={{0,8},{8,0},{16,24},{24,16},{1,9},{9,1},{17,25},{25,17},{2,10},{10... | collective-permute-start | bytes 196616 | tf_op jit(solution)/shard_map/ppermute | solution.py:210
  32.7 2.6 %collective-permute-start.11 = (f32[128,128]{1,0:T(8,128)S(1)}, f32[128,128]{1,0:T(8,128)S(1)}, u32[]{:S(2)}, u32[]{:S(2)}) collective-permute-start(f32[128,128]{1,0:T(8,128)S(1)} %get-tuple-element.55), channel_id=1, source_target_pairs={{8,16},{16,8},{9,17},{17,9},{10,18},{18,10},{11,19},{19,11},{12,20... | collective-permute-start | bytes 196616 | tf_op jit(solution)/shard_map/ppermute | solution.py:210
  36.1 8.7 %collective-permute-start.19 = (f32[512,128]{1,0:T(8,128)S(1)}, f32[512,128]{1,0:T(8,128)S(1)}, u32[]{:S(2)}, u32[]{:S(2)}) collective-permute-start(f32[512,128]{1,0:T(8,128)S(1)} %get-tuple-element.64), channel_id=1, source_target_pairs={{0,1},{1,0},{2,3},{3,2},{4,5},{5,4},{6,7},{7,6},{8,9},{9,8},{10,11... | collective-permute-start | bytes 786440 | tf_op jit(solution)/shard_map/ppermute | solution.py:210
  36.7 8.1 %collective-permute-start.17 = (f32[256,128]{1,0:T(8,128)S(1)}, f32[256,128]{1,0:T(8,128)S(1)}, u32[]{:S(2)}, u32[]{:S(2)}) collective-permute-start(f32[256,128]{1,0:T(8,128)S(1)} %get-tuple-element.62), channel_id=1, source_target_pairs={{0,2},{2,0},{4,6},{6,4},{1,3},{3,1},{5,7},{7,5},{8,10},{10,8},{12,... | collective-permute-start | bytes 393224 | tf_op jit(solution)/shard_map/ppermute | solution.py:210
  38.4 6.5 %collective-permute-start.18 = (f32[256,128]{1,0:T(8,128)S(1)}, f32[256,128]{1,0:T(8,128)S(1)}, u32[]{:S(2)}, u32[]{:S(2)}) collective-permute-start(f32[256,128]{1,0:T(8,128)S(1)} %get-tuple-element.63), channel_id=1, source_target_pairs={{2,4},{4,2},{3,5},{5,3},{10,12},{12,10},{11,13},{13,11},{18,20},{2... | collective-permute-start | bytes 393224 | tf_op jit(solution)/shard_map/ppermute | solution.py:210
  39.1 5.8 %collective-permute-start.15 = (f32[128,128]{1,0:T(8,128)S(1)}, f32[128,128]{1,0:T(8,128)S(1)}, u32[]{:S(2)}, u32[]{:S(2)}) collective-permute-start(f32[128,128]{1,0:T(8,128)S(1)} %get-tuple-element.60), channel_id=1, source_target_pairs={{0,8},{8,0},{16,24},{24,16},{1,9},{9,1},{17,25},{25,17},{2,10},{10... | collective-permute-start | bytes 196616 | tf_op jit(solution)/shard_map/ppermute | solution.py:210
  42.4 2.4 %collective-permute-start.16 = (f32[128,128]{1,0:T(8,128)S(1)}, f32[128,128]{1,0:T(8,128)S(1)}, u32[]{:S(2)}, u32[]{:S(2)}) collective-permute-start(f32[128,128]{1,0:T(8,128)S(1)} %get-tuple-element.61), channel_id=1, source_target_pairs={{8,16},{16,8},{9,17},{17,9},{10,18},{18,10},{11,19},{19,11},{12,20... | collective-permute-start | bytes 196616 | tf_op jit(solution)/shard_map/ppermute | solution.py:210
  45.7 10.7 %collective-permute-start.21 = (f32[256,128]{1,0:T(8,128)S(1)}, f32[256,128]{1,0:T(8,128)S(1)}, u32[]{:S(2)}, u32[]{:S(2)}) collective-permute-start(f32[256,128]{1,0:T(8,128)S(1)} %get-tuple-element.69), channel_id=1, source_target_pairs={{2,0},{4,2},{6,4},{3,1},{5,3},{7,5},{10,8},{12,10},{14,12},{11,9},... | collective-permute-start | bytes 393224 | tf_op jit(solution)/shard_map/ppermute | solution.py:199
  47.0 9.4 %collective-permute-start.22 = (f32[256,128]{1,0:T(8,128)S(1)}, f32[256,128]{1,0:T(8,128)S(1)}, u32[]{:S(2)}, u32[]{:S(2)}) collective-permute-start(f32[256,128]{1,0:T(8,128)S(1)} %get-tuple-element.70), channel_id=1, source_target_pairs={{0,1},{1,0},{2,3},{3,2},{4,5},{5,4},{6,7},{7,6},{8,9},{9,8},{10,11... | collective-permute-start | bytes 393224 | tf_op jit(solution)/shard_map/ppermute | solution.py:199
  48.6 7.8 %collective-permute-start.20 = (f32[128,128]{1,0:T(8,128)S(1)}, f32[128,128]{1,0:T(8,128)S(1)}, u32[]{:S(2)}, u32[]{:S(2)}) collective-permute-start(f32[128,128]{1,0:T(8,128)S(1)} %get-tuple-element.68), channel_id=1, source_target_pairs={{8,0},{16,8},{24,16},{9,1},{17,9},{25,17},{10,2},{18,10},{26,18},{... | collective-permute-start | bytes 196616 | tf_op jit(solution)/shard_map/ppermute | solution.py:199
  57.4 2.1 %collective-permute-start.23 = (f32[72,128]{1,0:T(8,128)S(1)}, f32[72,128]{1,0:T(8,128)S(1)}, u32[]{:S(2)}, u32[]{:S(2)}) collective-permute-start(f32[72,128]{1,0:T(8,128)S(1)} %get-tuple-element.72), channel_id=1, source_target_pairs={{0,2},{1,3},{2,0},{3,1},{4,6},{5,7},{6,4},{7,5},{8,10},{9,11},{10,... | collective-permute-start | bytes 110600 | tf_op jit(solution)/shard_map/ppermute | solution.py:305
  59.5 5.0 %collective-permute-start.26 = (f32[72,128]{1,0:T(8,128)S(1)}, f32[72,128]{1,0:T(8,128)S(1)}, u32[]{:S(2)}, u32[]{:S(2)}) collective-permute-start(f32[72,128]{1,0:T(8,128)S(1)} %add.21), channel_id=1, source_target_pairs={{0,5},{1,4},{2,7},{3,6},{4,1},{5,0},{6,3},{7,2},{8,13},{9,12},{10,... | collective-permute-start | bytes 110600 | tf_op jit(solution)/shard_map/ppermute | solution.py:305
  62.6 4.0 %collective-permute-start.25 = (f32[72,128]{1,0:T(8,128)S(1)}, f32[72,128]{1,0:T(8,128)S(1)}, u32[]{:S(2)}, u32[]{:S(2)}) collective-permute-start(f32[72,128]{1,0:T(8,128)S(1)} %add.21), channel_id=1, source_target_pairs={{0,1},{1,0},{2,3},{3,2},{4,5},{5,4},{6,7},{7,6},{8,9},{9,8},{10,11... | collective-permute-start | bytes 110600 | tf_op jit(solution)/shard_map/ppermute | solution.py:305
  64.1 4.0 %collective-permute-start.24 = (f32[72,128]{1,0:T(8,128)S(1)}, f32[72,128]{1,0:T(8,128)S(1)}, u32[]{:S(2)}, u32[]{:S(2)}) collective-permute-start(f32[72,128]{1,0:T(8,128)S(1)} %add.21), channel_id=1, source_target_pairs={{0,4},{1,5},{2,6},{3,7},{4,0},{5,1},{6,2},{7,3},{8,12},{9,13},{10,... | collective-permute-start | bytes 110600 | tf_op jit(solution)/shard_map/ppermute | solution.py:305
  68.1 5.8 %collective-permute-start.29 = (f32[72,128]{1,0:T(8,128)S(1)}, f32[72,128]{1,0:T(8,128)S(1)}, u32[]{:S(2)}, u32[]{:S(2)}) collective-permute-start(f32[72,128]{1,0:T(8,128)S(1)} %add_add_fusion.1), channel_id=1, source_target_pairs={{0,24},{1,25},{2,26},{3,27},{4,28},{5,29},{6,30},{7,31},{8,16},{9,... | collective-permute-start | bytes 110600 | tf_op jit(solution)/shard_map/ppermute | solution.py:305
  71.1 5.2 %collective-permute-start.28 = (f32[72,128]{1,0:T(8,128)S(1)}, f32[72,128]{1,0:T(8,128)S(1)}, u32[]{:S(2)}, u32[]{:S(2)}) collective-permute-start(f32[72,128]{1,0:T(8,128)S(1)} %add_add_fusion.1), channel_id=1, source_target_pairs={{0,16},{1,17},{2,18},{3,19},{4,20},{5,21},{6,22},{7,23},{8,24},{9,... | collective-permute-start | bytes 110600 | tf_op jit(solution)/shard_map/ppermute | solution.py:305
  71.6 4.8 %collective-permute-start.27 = (f32[72,128]{1,0:T(8,128)S(1)}, f32[72,128]{1,0:T(8,128)S(1)}, u32[]{:S(2)}, u32[]{:S(2)}) collective-permute-start(f32[72,128]{1,0:T(8,128)S(1)} %add_add_fusion.1), channel_id=1, source_target_pairs={{0,8},{1,9},{2,10},{3,11},{4,12},{5,13},{6,14},{7,15},{8,0},{9,1},... | collective-permute-start | bytes 110600 | tf_op jit(solution)/shard_map/ppermute | solution.py:305
  76.4 1.3 %collective-permute-start.30 = (f32[72,128]{1,0:T(8,128)S(1)}, f32[72,128]{1,0:T(8,128)S(1)}, u32[]{:S(2)}, u32[]{:S(2)}) collective-permute-start(f32[72,128]{1,0:T(8,128)S(1)} %add_add_fusion.own_ref), channel_id=1, source_target_pairs={{0,2},{1,3},{2,0},{3,1},{4,6},{5,7},{6,4},{7,5},{8,10},{9,11},{10,... | collective-permute-start | bytes 110600 | tf_op jit(solution)/shard_map/ppermute | solution.py:305
  (1 other events, 0.8 us)

commit v8 on v7

--- a/solution.py
+++ b/solution.py
@@ -12,7 +12,6 @@
 center_value = 3.25
 half_value = 2.75
 VMEM = pl.BlockSpec(memory_space=pltpu.VMEM)
-SMEM = pl.BlockSpec(memory_space=pltpu.SMEM)
 BF = jnp.bfloat16
 
 
@@ -21,7 +20,7 @@
     return pl.pallas_call(
         body,
         out_shape=outs,
-        in_specs=[SMEM] + [VMEM] * (len(ins) - 1),
+        in_specs=[VMEM] * len(ins),
         out_specs=tuple(VMEM for _ in outs),
         input_output_aliases=aliases or {},
         compiler_params=pltpu.CompilerParams(vmem_limit_bytes=32 * 1024 * 1024),
@@ -39,6 +38,13 @@
         self.row = self.y * self.z
         self.cells = self.x * self.row
         self.room = self.cells + self.z
+
+
+def places(s):
+    odd = [lax.rem(lax.axis_index(a), 2) for a in ("gx", "gy", "gz")]
+    tops = (s.x - 1, s.y - 1, s.z - 1)
+    at = [jnp.where(odd[d] == first, tops[d], 0) for d in range(3) for first in range(2)]
+    return at + [odd[2], odd[1]]
 
 
 def faces_of(s, at, w_ref, out, with_z=True):
@@ -63,8 +69,9 @@
     return {"x": refs[0:2], "y": refs[2:4], "z": refs[4 : 4 + nz], "nz": nz}
 
 
-def prepare(block, turned, at, s, nz):
-    def body(at_ref, b_ref, k_ref, w_ref, wide_ref, *refs):
+def prepare(block, turned, s, nz):
+    def body(b_ref, k_ref, w_ref, wide_ref, *refs):
+        at_ref = places(s)
         for y in range(s.y):
             tile = k_ref[y]
             for x in range(s.x):
@@ -77,7 +84,7 @@
         faces_of(s, at_ref, w_ref, split_faces(refs, nz))
 
     outs = [f32(s.room, s.k)] * 2 + face_shapes(s, nz) + [f32(s.x * s.y, s.k)] * nz
-    return call(body, outs, [at, block, turned], 4 * s.cells * s.k)
+    return call(body, outs, [block, turned], 4 * s.cells * s.k)
 
 
 def around(s, w_ref, o_ref, x, low, high, emit):
@@ -115,10 +122,10 @@
     around(s, w_ref, o_ref, s.x - 1, True, False, emit)
 
 
-def interior(w, before, wide, at, s):
+def interior(w, before, wide, s):
     scale = (1.0 if before is None else 2.0) / half_value
 
-    def body(at_ref, w_ref, k_ref, *rest):
+    def body(w_ref, k_ref, *rest):
         o_ref = rest[-1]
 
         def emit(here, c, near):
@@ -129,13 +136,14 @@
 
         sweep(s, w_ref, o_ref, emit)
 
-    ins = [at, w, wide] + ([] if before is None else [before])
+    ins = [w, wide] + ([] if before is None else [before])
     return call(body, [f32(s.room, s.k)], ins, 12 * s.cells * s.k)[0]
 
 
-def finish(part, wide, edge, ghosts, at, s, nz, scale, last):
-    def body(at_ref, p_ref, k_ref, *refs):
+def finish(part, wide, edge, ghosts, s, nz, scale, last):
+    def body(p_ref, k_ref, *refs):
         del p_ref
+        at_ref = places(s)
         edges = refs[:nz]
         ghost = split_faces(refs[nz : 4 + 2 * nz], nz)
         w_ref = refs[4 + 2 * nz]
@@ -182,8 +190,8 @@
         outs = [f32(s.room, s.k), f32(s.row, s.k), f32(s.x * s.z, s.k), f32(s.x * s.y // (2 if halved(s, nz) else 1), s.k)]
     else:
         outs = [f32(s.room, s.k)] + face_shapes(s, nz)
-    ins = [at, part, wide] + list(edge) + list(ghosts)
-    return call(body, outs, ins, 4 * s.x * s.y * s.k, {1: 0})
+    ins = [part, wide] + list(edge) + list(ghosts)
+    return call(body, outs, ins, 4 * s.x * s.y * s.k, {0: 0})
 
 
 def halved(s, nz):
@@ -228,10 +236,10 @@
     return full[:k, :k] + (full[:k, k:] + full[k:, :k]) + full[k:, k:]
 
 
-def gather_terms(w, wide, at, s):
+def gather_terms(w, wide, s):
     rows = s.cells // 4
 
-    def body(at_ref, w_ref, k_ref, f_ref, g_ref, m_ref, q_ref):
+    def body(w_ref, k_ref, f_ref, g_ref, m_ref, q_ref):
         def emit(here, c, near):
             return c - near * (1.0 / 6.0)
 
@@ -253,20 +261,21 @@
     return pl.pallas_call(
         body,
         out_shape=outs,
-        in_specs=[SMEM, VMEM, VMEM],
+        in_specs=[VMEM, VMEM],
         out_specs=(VMEM, VMEM, VMEM),
         scratch_shapes=[pltpu.VMEM((s.cells, s.k), jnp.float32)],
         compiler_params=pltpu.CompilerParams(vmem_limit_bytes=32 * 1024 * 1024),
         cost_estimate=pl.CostEstimate(
             flops=16 * s.cells * s.k * s.k, bytes_accessed=moved, transcendentals=0
         ),
-    )(at, w, wide)
-
-
-def pack_terms(gram, own, w, ghosts, at, s, nz, cells):
+    )(w, wide)
+
+
+def pack_terms(gram, own, w, ghosts, s, nz, cells):
     k = s.k
 
-    def body(at_ref, g_ref, m_ref, w_ref, x_ref, y_ref, z_ref, mine_ref, other_ref):
+    def body(g_ref, m_ref, w_ref, x_ref, y_ref, z_ref, mine_ref, other_ref):
+        at_ref = places(s)
         lefts = [w_ref[s.cells - s.row : s.cells, :]]
         tops = [w_ref[(x + 1) * s.row - s.z : (x + 1) * s.row, :] for x in range(s.x)]
         lefts.append(jnp.concatenate(tops, axis=0))
@@ -288,7 +297,7 @@
             ref[: k // 2, :] = jnp.where(first, full[: k // 2, :], full[k // 2 :, :])
             ref[k // 2 :, :] = jnp.broadcast_to(diagonal, (8, k))
 
-    ins = [at, gram, own, w] + list(ghosts)
+    ins = [gram, own, w] + list(ghosts)
     return call(body, [f32(k // 2 + 8, k)] * 2, ins, 6 * s.cells * k)
 
 
@@ -359,13 +368,13 @@
             m_ref[top + PANEL :, :] = m_ref[top + PANEL :, :] - update[top + PANEL :, :]
 
 
-def orthonormal(own, got, filtered, at, s):
+def orthonormal(own, got, filtered, s):
     k = s.k
     parts = 4
     rows = s.cells // parts
 
-    def body(at_ref, own_ref, got_ref, f_ref, b_hbm, o_ref, m_ref, b_ref, sems):
-        even = at_ref[7] == 0
+    def body(own_ref, got_ref, f_ref, b_hbm, o_ref, m_ref, b_ref, sems):
+        even = places(s)[7] == 0
         one, other = own_ref[: k // 2, :], got_ref[: k // 2, :]
         upper = jnp.concatenate(
             [jnp.where(even, one, other), jnp.where(even, other, one)], axis=0
@@ -400,7 +409,7 @@
     return pl.pallas_call(
         body,
         out_shape=[f32(s.cells, k), f32(k, k)],
-        in_specs=[SMEM, VMEM, VMEM, VMEM],
+        in_specs=[VMEM, VMEM, VMEM],
         out_specs=(pl.BlockSpec(memory_space=pl.ANY), VMEM),
         scratch_shapes=[
             pltpu.VMEM((k, 2 * k), jnp.float32),
@@ -411,7 +420,7 @@
         cost_estimate=pl.CostEstimate(
             flops=8 * s.cells * k * k, bytes_accessed=8 * s.cells * k, transcendentals=0
         ),
-    )(at, own, got, filtered)
+    )(own, got, filtered)
 
 
 def on_device(block, conductivity):
@@ -419,29 +428,23 @@
     sizes = [lax.axis_size(a) for a in ("gx", "gy", "gz")]
     nz = 1 if sizes[2] == 2 else 2
     cells = float(s.cells * sizes[0] * sizes[1] * sizes[2])
-    odd = [lax.rem(lax.axis_index(a), 2) for a in ("gx", "gy", "gz")]
-    tops = (s.x - 1, s.y - 1, s.z - 1)
-    at = jnp.stack(
-        [jnp.where(odd[d] == first, tops[d], 0) for d in range(3) for first in range(2)]
-        + [odd[2], odd[1]]
-    ).astype(jnp.int32)
     axes = [("gx", 0), ("gx", 1), ("gy", 0), ("gy", 1), ("gz", 0), ("gz", 1)][: 4 + nz]
 
     flat = block.reshape(s.cells, s.k)
     turned = jnp.transpose(conductivity, (1, 2, 0))
-    w, wide, *rest = prepare(flat, turned, at, s, nz)
+    w, wide, *rest = prepare(flat, turned, s, nz)
     faces, edge = rest[: 4 + nz], rest[4 + nz :]
     before = None
     for step in range(DEG):
         ghosts = exchange(faces, axes)
-        part = interior(w, before, wide, at, s)
+        part = interior(w, before, wide, s)
         scale = (1.0 if before is None else 2.0) / half_value
         before = w
-        w, *faces = finish(part, wide, edge, ghosts, at, s, nz, scale, step == DEG - 1)
+        w, *faces = finish(part, wide, edge, ghosts, s, nz, scale, step == DEG - 1)
     ghosts = one_way(faces, s, nz)
-    filtered, gram, own = gather_terms(w, wide, at, s)
-    halves = total(*pack_terms(gram, own, w, ghosts, at, s, nz, cells))
-    basis, projected = orthonormal(*halves, filtered, at, s)
+    filtered, gram, own = gather_terms(w, wide, s)
+    halves = total(*pack_terms(gram, own, w, ghosts, s, nz, cells))
+    basis, projected = orthonormal(*halves, filtered, s)
     return (basis.reshape(block.shape), projected)
 
 

time: 84.6 us -> 80.1 us (0.947)
  Pallas kernels: 22.3 us -> 15.8 us
  waiting for transfers between devices: 15.9 us -> 17.6 us
    pallas_call x12, Pallas kernels: 22.3 us -> 15.8 us  [the longest x10 7.63 us: call(): pl.pallas_call(body, out_shape=outs, in_specs=[VMEM] * len(ins), out_spec...]
    ppermute x20, waiting for transfers between devices: 2.2 us -> 3.54 us  [exchange(): got.append(lax.ppermute(face, axis, pairs))]
  transfers between devices with their start and end apart: 31 -> 31, of which waited for: 11 -> 15; matrix products, arithmetic and copies ran while one was open for 0% -> 0% of each run, Pallas kernels for 12% -> 9%
where the time goes in v8:
time: 80.1 us; the launch traced here: 79.7 us
  starting transfers between devices  43 us (54%)
  waiting for transfers between devices  17.6 us (22%)
  Pallas kernels  15.8 us (20%)
  local copies, waits for them, and re-layouts  2.42 us (3%)
  between operations  0.85 us (1%)
    ppermute x20, starting transfers between devices, exchange(): got.append(lax.ppermute(face, axis, pairs))  28.4 us
    ppermute x8, starting transfers between devices, swap(): return lax.ppermute(value, axes, pairs)  10.5 us
    ppermute x8, waiting for transfers between devices, swap(): return lax.ppermute(value, axes, pairs)  9.46 us
    pallas_call x10, Pallas kernels, call(): pl.pallas_call(body, out_shape=outs, in_specs=[VMEM] * len(ins), out_spec...  7.63 us
    pallas_call x1, Pallas kernels, orthonormal(): pl.pallas_call(body, out_shape=[f32(s.cells, k), f32(k, k)], in_specs=[VM...  5.98 us
    ppermute x3, waiting for transfers between devices, one_way(): got.append(lax.ppermute(face, axis, pairs))  4.57 us
    ppermute x3, starting transfers between devices, one_way(): got.append(lax.ppermute(face, axis, pairs))  4.13 us
    ppermute x20, waiting for transfers between devices, exchange(): got.append(lax.ppermute(face, axis, pairs))  3.54 us
  transfers between devices with their start and end apart: 31, of which 15 were waited for; matrix products, arithmetic and copies ran while one was open for 0% of the time, Pallas kernels for 9%

profile of v8, /device:TPU:0, one launch (start us, length us, event | category | flops | bytes accessed | tf_op | source)
XLA Modules:
  0.0 79.7 jit_solution(2472434061387945427)
XLA Ops:
  0.6 1.6 %copy-done = f32[32,16,8,128]{3,2,1,0:T(8,128)S(1)} copy-done((f32[32,16,8,128]{3,2,1,0:T(8,128)S(1)}, f32[32,16,8,128]{3,2,1,0:T(8,128)}, u32[]{:S(2)}) %copy-start) | copy-done | bytes 2097176
  3.1 1.1 %shard_map.41 = (f32[4104,128]{1,0:T(8,128)S(1)}, f32[4104,128]{1,0:T(8,128)S(1)}, f32[128,128]{1,0:T(8,128)S(1)}, f32[128,128]{1,0:T(8,128)S(1)}, f32[256,128]{...) custom-call(f32[4096,128]{1,0:T(8,128)S(1)} %bitcast.3, ...), custom_call_target="tpu_custom_call" | custom-call | flops 2097152 | bytes 7233536 | tf_op jit(solution)/shard_map/pallas_call | solution.py:20
  4.2 3.0 %collective-permute-start.4 = (f32[512,128]{1,0:T(8,128)S(1)}, f32[512,128]{1,0:T(8,128)S(1)}, u32[]{:S(2)}, u32[]{:S(2)}) collective-permute-start(f32[512,128]{1,0:T(8,128)S(1)} %get-tuple-element.46), channel_id=1, source_target_pairs={{0,1},{1,0},{2,3},{3,2},{4,5},{5,4},{6,7},{7,6},{8,9},{9,8},{10,11... | collective-permute-start | bytes 786440 | tf_op jit(solution)/shard_map/ppermute | solution.py:218
  7.9 1.6 %collective-permute-start = (f32[128,128]{1,0:T(8,128)S(1)}, f32[128,128]{1,0:T(8,128)S(1)}, u32[]{:S(2)}, u32[]{:S(2)}) collective-permute-start(f32[128,128]{1,0:T(8,128)S(1)} %get-tuple-element.42), channel_id=1, source_target_pairs={{0,8},{8,0},{16,24},{24,16},{1,9},{9,1},{17,25},{25,17},{2,10},{10... | collective-permute-start | bytes 196616 | tf_op jit(solution)/shard_map/ppermute | solution.py:218
  10.2 1.2 %shard_map.42.p_ref = f32[4104,128]{1,0:T(8,128)S(1)} custom-call(f32[4104,128]{1,0:T(8,128)S(1)} %get-tuple-element.39.w_ref.rest_0_, f32[4104,128]{1,0:T(8,128)S(1)} %get-tuple-element.40.k_ref), custom_call_target="tpu_custom_call" | custom-call | flops 6291456 | bytes 6303744 | tf_op jit(solution)/shard_map/pallas_call | solution.py:20
  12.2 1.3 %collective-permute-done.4.refs_5_ = f32[512,128]{1,0:T(8,128)S(1)} collective-permute-done((f32[512,128]{1,0:T(8,128)S(1)}, f32[512,128]{1,0:T(8,128)S(1)}, u32[]{:S(2)}, u32[]{:S(2)}) %collective-permute-start.4) | collective-permute-done | bytes 262176 | tf_op jit(solution)/shard_map/ppermute | solution.py:218
  13.8 1.8 %collective-permute-start.9 = (f32[512,128]{1,0:T(8,128)S(1)}, f32[512,128]{1,0:T(8,128)S(1)}, u32[]{:S(2)}, u32[]{:S(2)}) collective-permute-start(f32[512,128]{1,0:T(8,128)S(1)} %get-tuple-element.52), channel_id=1, source_target_pairs={{0,1},{1,0},{2,3},{3,2},{4,5},{5,4},{6,7},{7,6},{8,9},{9,8},{10,11... | collective-permute-start | bytes 786440 | tf_op jit(solution)/shard_map/ppermute | solution.py:218
  16.3 3.6 %collective-permute-start.5 = (f32[128,128]{1,0:T(8,128)S(1)}, f32[128,128]{1,0:T(8,128)S(1)}, u32[]{:S(2)}, u32[]{:S(2)}) collective-permute-start(f32[128,128]{1,0:T(8,128)S(1)} %get-tuple-element.48), channel_id=1, source_target_pairs={{0,8},{8,0},{16,24},{24,16},{1,9},{9,1},{17,25},{25,17},{2,10},{10... | collective-permute-start | bytes 196616 | tf_op jit(solution)/shard_map/ppermute | solution.py:218
  20.5 1.2 %shard_map.44.p_ref = f32[4104,128]{1,0:T(8,128)S(1)} custom-call(f32[4104,128]{1,0:T(8,128)S(1)} %get-tuple-element.47.w_ref.rest_0_, f32[4104,128]{1,0:T(8,128)S(1)} %get-tuple-element.40.k_ref, f32[4104,128]{1,0:T(8,128)S(1)} %get-tuple-element.39.w_ref.rest_0_), custom_call_target="tpu_custom_call" | custom-call | flops 6291456 | bytes 8404992 | tf_op jit(solution)/shard_map/pallas_call | solution.py:20
  22.8 1.2 %collective-permute-start.14 = (f32[512,128]{1,0:T(8,128)S(1)}, f32[512,128]{1,0:T(8,128)S(1)}, u32[]{:S(2)}, u32[]{:S(2)}) collective-permute-start(f32[512,128]{1,0:T(8,128)S(1)} %get-tuple-element.58), channel_id=1, source_target_pairs={{0,1},{1,0},{2,3},{3,2},{4,5},{5,4},{6,7},{7,6},{8,9},{9,8},{10,11... | collective-permute-start | bytes 786440 | tf_op jit(solution)/shard_map/ppermute | solution.py:218
  24.0 2.4 %collective-permute-start.12 = (f32[256,128]{1,0:T(8,128)S(1)}, f32[256,128]{1,0:T(8,128)S(1)}, u32[]{:S(2)}, u32[]{:S(2)}) collective-permute-start(f32[256,128]{1,0:T(8,128)S(1)} %get-tuple-element.56), channel_id=1, source_target_pairs={{0,2},{2,0},{4,6},{6,4},{1,3},{3,1},{5,7},{7,5},{8,10},{10,8},{12,... | collective-permute-start | bytes 393224 | tf_op jit(solution)/shard_map/ppermute | solution.py:218
  27.1 3.7 %collective-permute-start.10 = (f32[128,128]{1,0:T(8,128)S(1)}, f32[128,128]{1,0:T(8,128)S(1)}, u32[]{:S(2)}, u32[]{:S(2)}) collective-permute-start(f32[128,128]{1,0:T(8,128)S(1)} %get-tuple-element.54), channel_id=1, source_target_pairs={{0,8},{8,0},{16,24},{24,16},{1,9},{9,1},{17,25},{25,17},{2,10},{10... | collective-permute-start | bytes 196616 | tf_op jit(solution)/shard_map/ppermute | solution.py:218
  31.5 1.4 %shard_map.46.p_ref = f32[4104,128]{1,0:T(8,128)S(1)} custom-call(f32[4104,128]{1,0:T(8,128)S(1)} %get-tuple-element.53.w_ref.rest_0_, f32[4104,128]{1,0:T(8,128)S(1)} %get-tuple-element.40.k_ref, f32[4104,128]{1,0:T(8,128)S(1)} %get-tuple-element.47.w_ref.rest_0_), custom_call_target="tpu_custom_call" | custom-call | flops 6291456 | bytes 8404992 | tf_op jit(solution)/shard_map/pallas_call | solution.py:20
  34.0 1.6 %collective-permute-start.17 = (f32[256,128]{1,0:T(8,128)S(1)}, f32[256,128]{1,0:T(8,128)S(1)}, u32[]{:S(2)}, u32[]{:S(2)}) collective-permute-start(f32[256,128]{1,0:T(8,128)S(1)} %get-tuple-element.62), channel_id=1, source_target_pairs={{0,2},{2,0},{4,6},{6,4},{1,3},{3,1},{5,7},{7,5},{8,10},{10,8},{12,... | collective-permute-start | bytes 393224 | tf_op jit(solution)/shard_map/ppermute | solution.py:218
  36.3 3.6 %collective-permute-start.15 = (f32[128,128]{1,0:T(8,128)S(1)}, f32[128,128]{1,0:T(8,128)S(1)}, u32[]{:S(2)}, u32[]{:S(2)}) collective-permute-start(f32[128,128]{1,0:T(8,128)S(1)} %get-tuple-element.60), channel_id=1, source_target_pairs={{0,8},{8,0},{16,24},{24,16},{1,9},{9,1},{17,25},{25,17},{2,10},{10... | collective-permute-start | bytes 196616 | tf_op jit(solution)/shard_map/ppermute | solution.py:218
  40.5 1.2 %shard_map.48.p_ref = f32[4104,128]{1,0:T(8,128)S(1)} custom-call(f32[4104,128]{1,0:T(8,128)S(1)} %get-tuple-element.59.w_ref, f32[4104,128]{1,0:T(8,128)S(1)} %get-tuple-element.40.k_ref, f32[4104,128]{1,0:T(8,128)S(1)} %get-tuple-element.53.w_ref.rest_0_), custom_call_target="tpu_custom_call" | custom-call | flops 6291456 | bytes 8404992 | tf_op jit(solution)/shard_map/pallas_call | solution.py:20
  42.4 1.3 %collective-permute-start.21 = (f32[256,128]{1,0:T(8,128)S(1)}, f32[256,128]{1,0:T(8,128)S(1)}, u32[]{:S(2)}, u32[]{:S(2)}) collective-permute-start(f32[256,128]{1,0:T(8,128)S(1)} %get-tuple-element.69), channel_id=1, source_target_pairs={{2,0},{4,2},{6,4},{3,1},{5,3},{7,5},{10,8},{12,10},{14,12},{11,9},... | collective-permute-start | bytes 393224 | tf_op jit(solution)/shard_map/ppermute | solution.py:207
  43.7 1.6 %collective-permute-start.22 = (f32[256,128]{1,0:T(8,128)S(1)}, f32[256,128]{1,0:T(8,128)S(1)}, u32[]{:S(2)}, u32[]{:S(2)}) collective-permute-start(f32[256,128]{1,0:T(8,128)S(1)} %get-tuple-element.70), channel_id=1, source_target_pairs={{0,1},{1,0},{2,3},{3,2},{4,5},{5,4},{6,7},{7,6},{8,9},{9,8},{10,11... | collective-permute-start | bytes 393224 | tf_op jit(solution)/shard_map/ppermute | solution.py:207
  45.3 1.3 %collective-permute-start.20 = (f32[128,128]{1,0:T(8,128)S(1)}, f32[128,128]{1,0:T(8,128)S(1)}, u32[]{:S(2)}, u32[]{:S(2)}) collective-permute-start(f32[128,128]{1,0:T(8,128)S(1)} %get-tuple-element.68), channel_id=1, source_target_pairs={{8,0},{16,8},{24,16},{9,1},{17,9},{25,17},{10,2},{18,10},{26,18},{... | collective-permute-start | bytes 196616 | tf_op jit(solution)/shard_map/ppermute | solution.py:207
  46.6 2.2 %shard_map.50 = (bf16[4096,256]{1,0:T(8,128)(2,1)S(1)}, f32[128,128]{1,0:T(8,128)S(1)}, f32[128,128]{1,0:T(8,128)S(1)}) custom-call(f32[4104,128]{1,0:T(8,128)S(1)} %get-tuple-element.65.w_ref, f32[4104,128]{1,0:T(8,128)S(1)} %get-tuple-element.40.k_ref), custom_call_target="tpu_custom_call" | custom-call | flops 1073741824 | bytes 8388608 | tf_op jit(solution)/shard_map/pallas_call | solution.py:261
  48.8 4.6 %collective-permute-done.20.x_ref = f32[128,128]{1,0:T(8,128)S(1)} collective-permute-done((f32[128,128]{1,0:T(8,128)S(1)}, f32[128,128]{1,0:T(8,128)S(1)}, u32[]{:S(2)}, u32[]{:S(2)}) %collective-permute-start.20) | collective-permute-done | bytes 65568 | tf_op jit(solution)/shard_map/ppermute | solution.py:207
  53.7 1.4 %collective-permute-start.23 = (f32[72,128]{1,0:T(8,128)S(1)}, f32[72,128]{1,0:T(8,128)S(1)}, u32[]{:S(2)}, u32[]{:S(2)}) collective-permute-start(f32[72,128]{1,0:T(8,128)S(1)} %get-tuple-element.72), channel_id=1, source_target_pairs={{0,2},{1,3},{2,0},{3,1},{4,6},{5,7},{6,4},{7,5},{8,10},{9,11},{10,... | collective-permute-start | bytes 110600 | tf_op jit(solution)/shard_map/ppermute | solution.py:314
  56.0 3.1 %collective-permute-start.26 = (f32[72,128]{1,0:T(8,128)S(1)}, f32[72,128]{1,0:T(8,128)S(1)}, u32[]{:S(2)}, u32[]{:S(2)}) collective-permute-start(f32[72,128]{1,0:T(8,128)S(1)} %add.21), channel_id=1, source_target_pairs={{0,5},{1,4},{2,7},{3,6},{4,1},{5,0},{6,3},{7,2},{8,13},{9,12},{10,... | collective-permute-start | bytes 110600 | tf_op jit(solution)/shard_map/ppermute | solution.py:314
  59.1 1.5 %collective-permute-start.25 = (f32[72,128]{1,0:T(8,128)S(1)}, f32[72,128]{1,0:T(8,128)S(1)}, u32[]{:S(2)}, u32[]{:S(2)}) collective-permute-start(f32[72,128]{1,0:T(8,128)S(1)} %add.21), channel_id=1, source_target_pairs={{0,1},{1,0},{2,3},{3,2},{4,5},{5,4},{6,7},{7,6},{8,9},{9,8},{10,11... | collective-permute-start | bytes 110600 | tf_op jit(solution)/shard_map/ppermute | solution.py:314
  61.0 2.0 %collective-permute-done.25 = f32[72,128]{1,0:T(8,128)S(1)} collective-permute-done((f32[72,128]{1,0:T(8,128)S(1)}, f32[72,128]{1,0:T(8,128)S(1)}, u32[]{:S(2)}, u32[]{:S(2)}) %collective-permute-start.25) | collective-permute-done | bytes 36896 | tf_op jit(solution)/shard_map/ppermute | solution.py:314
  63.0 1.5 %collective-permute-done.24 = f32[72,128]{1,0:T(8,128)S(1)} collective-permute-done((f32[72,128]{1,0:T(8,128)S(1)}, f32[72,128]{1,0:T(8,128)S(1)}, u32[]{:S(2)}, u32[]{:S(2)}) %collective-permute-start.24) | collective-permute-done | bytes 36896 | tf_op jit(solution)/shard_map/ppermute | solution.py:314
  64.5 2.7 %collective-permute-start.29 = (f32[72,128]{1,0:T(8,128)S(1)}, f32[72,128]{1,0:T(8,128)S(1)}, u32[]{:S(2)}, u32[]{:S(2)}) collective-permute-start(f32[72,128]{1,0:T(8,128)S(1)} %add_add_fusion.1), channel_id=1, source_target_pairs={{0,24},{1,25},{2,26},{3,27},{4,28},{5,29},{6,30},{7,31},{8,16},{9,... | collective-permute-start | bytes 110600 | tf_op jit(solution)/shard_map/ppermute | solution.py:314
  68.1 0.9 %collective-permute-start.27 = (f32[72,128]{1,0:T(8,128)S(1)}, f32[72,128]{1,0:T(8,128)S(1)}, u32[]{:S(2)}, u32[]{:S(2)}) collective-permute-start(f32[72,128]{1,0:T(8,128)S(1)} %add_add_fusion.1), channel_id=1, source_target_pairs={{0,8},{1,9},{2,10},{3,11},{4,12},{5,13},{6,14},{7,15},{8,0},{9,1},... | collective-permute-start | bytes 110600 | tf_op jit(solution)/shard_map/ppermute | solution.py:314
  69.0 1.6 %collective-permute-done.29 = f32[72,128]{1,0:T(8,128)S(1)} collective-permute-done((f32[72,128]{1,0:T(8,128)S(1)}, f32[72,128]{1,0:T(8,128)S(1)}, u32[]{:S(2)}, u32[]{:S(2)}) %collective-permute-start.29) | collective-permute-done | bytes 36896 | tf_op jit(solution)/shard_map/ppermute | solution.py:314
  70.6 1.6 %collective-permute-done.28 = f32[72,128]{1,0:T(8,128)S(1)} collective-permute-done((f32[72,128]{1,0:T(8,128)S(1)}, f32[72,128]{1,0:T(8,128)S(1)}, u32[]{:S(2)}, u32[]{:S(2)}) %collective-permute-start.28) | collective-permute-done | bytes 36896 | tf_op jit(solution)/shard_map/ppermute | solution.py:314
  72.5 1.2 %collective-permute-done.30.got_ref = f32[72,128]{1,0:T(8,128)S(1)} collective-permute-done((f32[72,128]{1,0:T(8,128)S(1)}, f32[72,128]{1,0:T(8,128)S(1)}, u32[]{:S(2)}, u32[]{:S(2)}) %collective-permute-start.30) | collective-permute-done | bytes 36896 | tf_op jit(solution)/shard_map/ppermute | solution.py:314
  73.7 6.0 %shard_map.52 = (f32[4096,128]{1,0:T(8,128)}, f32[128,128]{1,0:T(8,128)}) custom-call(f32[72,128]{1,0:T(8,128)S(1)} %add_add_fusion.own_ref, f32[72,128]{1,0:T(8,128)S(1)} %collective-permute-done.30.got_ref, bf16[4096,256]{1,0:T(8,128)(2,1)S(1)} %get-tuple-element.73.f_ref), custom_call_target="tpu_custom_call" | custom-call | flops 536870912 | bytes 4194304 | tf_op jit(solution)/shard_map/pallas_call | solution.py:409
  (49 shorter events, 13.0 us)
Async XLA Ops:
  0.6 1.6 %copy-start = (f32[32,16,8,128]{3,2,1,0:T(8,128)S(1)}, f32[32,16,8,128]{3,2,1,0:T(8,128)}, u32[]{:S(2)}) copy-start(f32[32,16,8,128]{3,2,1,0:T(8,128)} %param.2) | copy-start | bytes 6291460
  4.2 9.3 %collective-permute-start.4 = (f32[512,128]{1,0:T(8,128)S(1)}, f32[512,128]{1,0:T(8,128)S(1)}, u32[]{:S(2)}, u32[]{:S(2)}) collective-permute-start(f32[512,128]{1,0:T(8,128)S(1)} %get-tuple-element.46), channel_id=1, source_target_pairs={{0,1},{1,0},{2,3},{3,2},{4,5},{5,4},{6,7},{7,6},{8,9},{9,8},{10,11... | collective-permute-start | bytes 786440 | tf_op jit(solution)/shard_map/ppermute | solution.py:218
  7.2 5.0 %collective-permute-start.2 = (f32[256,128]{1,0:T(8,128)S(1)}, f32[256,128]{1,0:T(8,128)S(1)}, u32[]{:S(2)}, u32[]{:S(2)}) collective-permute-start(f32[256,128]{1,0:T(8,128)S(1)} %get-tuple-element.44), channel_id=1, source_target_pairs={{0,2},{2,0},{4,6},{6,4},{1,3},{3,1},{5,7},{7,5},{8,10},{10,8},{12,... | collective-permute-start | bytes 393224 | tf_op jit(solution)/shard_map/ppermute | solution.py:218
  7.2 5.0 %collective-permute-start.3 = (f32[256,128]{1,0:T(8,128)S(1)}, f32[256,128]{1,0:T(8,128)S(1)}, u32[]{:S(2)}, u32[]{:S(2)}) collective-permute-start(f32[256,128]{1,0:T(8,128)S(1)} %get-tuple-element.45), channel_id=1, source_target_pairs={{2,4},{4,2},{3,5},{5,3},{10,12},{12,10},{11,13},{13,11},{18,20},{2... | collective-permute-start | bytes 393224 | tf_op jit(solution)/shard_map/ppermute | solution.py:218
  7.9 4.3 %collective-permute-start = (f32[128,128]{1,0:T(8,128)S(1)}, f32[128,128]{1,0:T(8,128)S(1)}, u32[]{:S(2)}, u32[]{:S(2)}) collective-permute-start(f32[128,128]{1,0:T(8,128)S(1)} %get-tuple-element.42), channel_id=1, source_target_pairs={{0,8},{8,0},{16,24},{24,16},{1,9},{9,1},{17,25},{25,17},{2,10},{10... | collective-permute-start | bytes 196616 | tf_op jit(solution)/shard_map/ppermute | solution.py:218
  9.5 2.7 %collective-permute-start.1 = (f32[128,128]{1,0:T(8,128)S(1)}, f32[128,128]{1,0:T(8,128)S(1)}, u32[]{:S(2)}, u32[]{:S(2)}) collective-permute-start(f32[128,128]{1,0:T(8,128)S(1)} %get-tuple-element.43), channel_id=1, source_target_pairs={{8,16},{16,8},{9,17},{17,9},{10,18},{18,10},{11,19},{19,11},{12,20... | collective-permute-start | bytes 196616 | tf_op jit(solution)/shard_map/ppermute | solution.py:218
  13.8 8.8 %collective-permute-start.9 = (f32[512,128]{1,0:T(8,128)S(1)}, f32[512,128]{1,0:T(8,128)S(1)}, u32[]{:S(2)}, u32[]{:S(2)}) collective-permute-start(f32[512,128]{1,0:T(8,128)S(1)} %get-tuple-element.52), channel_id=1, source_target_pairs={{0,1},{1,0},{2,3},{3,2},{4,5},{5,4},{6,7},{7,6},{8,9},{9,8},{10,11... | collective-permute-start | bytes 786440 | tf_op jit(solution)/shard_map/ppermute | solution.py:218
  15.6 6.5 %collective-permute-start.7 = (f32[256,128]{1,0:T(8,128)S(1)}, f32[256,128]{1,0:T(8,128)S(1)}, u32[]{:S(2)}, u32[]{:S(2)}) collective-permute-start(f32[256,128]{1,0:T(8,128)S(1)} %get-tuple-element.50), channel_id=1, source_target_pairs={{0,2},{2,0},{4,6},{6,4},{1,3},{3,1},{5,7},{7,5},{8,10},{10,8},{12,... | collective-permute-start | bytes 393224 | tf_op jit(solution)/shard_map/ppermute | solution.py:218
  15.6 6.5 %collective-permute-start.8 = (f32[256,128]{1,0:T(8,128)S(1)}, f32[256,128]{1,0:T(8,128)S(1)}, u32[]{:S(2)}, u32[]{:S(2)}) collective-permute-start(f32[256,128]{1,0:T(8,128)S(1)} %get-tuple-element.51), channel_id=1, source_target_pairs={{2,4},{4,2},{3,5},{5,3},{10,12},{12,10},{11,13},{13,11},{18,20},{2... | collective-permute-start | bytes 393224 | tf_op jit(solution)/shard_map/ppermute | solution.py:218
  16.3 5.9 %collective-permute-start.5 = (f32[128,128]{1,0:T(8,128)S(1)}, f32[128,128]{1,0:T(8,128)S(1)}, u32[]{:S(2)}, u32[]{:S(2)}) collective-permute-start(f32[128,128]{1,0:T(8,128)S(1)} %get-tuple-element.48), channel_id=1, source_target_pairs={{0,8},{8,0},{16,24},{24,16},{1,9},{9,1},{17,25},{25,17},{2,10},{10... | collective-permute-start | bytes 196616 | tf_op jit(solution)/shard_map/ppermute | solution.py:218
  19.9 2.2 %collective-permute-start.6 = (f32[128,128]{1,0:T(8,128)S(1)}, f32[128,128]{1,0:T(8,128)S(1)}, u32[]{:S(2)}, u32[]{:S(2)}) collective-permute-start(f32[128,128]{1,0:T(8,128)S(1)} %get-tuple-element.49), channel_id=1, source_target_pairs={{8,16},{16,8},{9,17},{17,9},{10,18},{18,10},{11,19},{19,11},{12,20... | collective-permute-start | bytes 196616 | tf_op jit(solution)/shard_map/ppermute | solution.py:218
  22.8 10.2 %collective-permute-start.14 = (f32[512,128]{1,0:T(8,128)S(1)}, f32[512,128]{1,0:T(8,128)S(1)}, u32[]{:S(2)}, u32[]{:S(2)}) collective-permute-start(f32[512,128]{1,0:T(8,128)S(1)} %get-tuple-element.58), channel_id=1, source_target_pairs={{0,1},{1,0},{2,3},{3,2},{4,5},{5,4},{6,7},{7,6},{8,9},{9,8},{10,11... | collective-permute-start | bytes 786440 | tf_op jit(solution)/shard_map/ppermute | solution.py:218
  24.0 9.0 %collective-permute-start.12 = (f32[256,128]{1,0:T(8,128)S(1)}, f32[256,128]{1,0:T(8,128)S(1)}, u32[]{:S(2)}, u32[]{:S(2)}) collective-permute-start(f32[256,128]{1,0:T(8,128)S(1)} %get-tuple-element.56), channel_id=1, source_target_pairs={{0,2},{2,0},{4,6},{6,4},{1,3},{3,1},{5,7},{7,5},{8,10},{10,8},{12,... | collective-permute-start | bytes 393224 | tf_op jit(solution)/shard_map/ppermute | solution.py:218
  26.4 6.6 %collective-permute-start.13 = (f32[256,128]{1,0:T(8,128)S(1)}, f32[256,128]{1,0:T(8,128)S(1)}, u32[]{:S(2)}, u32[]{:S(2)}) collective-permute-start(f32[256,128]{1,0:T(8,128)S(1)} %get-tuple-element.57), channel_id=1, source_target_pairs={{2,4},{4,2},{3,5},{5,3},{10,12},{12,10},{11,13},{13,11},{18,20},{2... | collective-permute-start | bytes 393224 | tf_op jit(solution)/shard_map/ppermute | solution.py:218
  27.1 5.9 %collective-permute-start.10 = (f32[128,128]{1,0:T(8,128)S(1)}, f32[128,128]{1,0:T(8,128)S(1)}, u32[]{:S(2)}, u32[]{:S(2)}) collective-permute-start(f32[128,128]{1,0:T(8,128)S(1)} %get-tuple-element.54), channel_id=1, source_target_pairs={{0,8},{8,0},{16,24},{24,16},{1,9},{9,1},{17,25},{25,17},{2,10},{10... | collective-permute-start | bytes 196616 | tf_op jit(solution)/shard_map/ppermute | solution.py:218
  30.8 2.2 %collective-permute-start.11 = (f32[128,128]{1,0:T(8,128)S(1)}, f32[128,128]{1,0:T(8,128)S(1)}, u32[]{:S(2)}, u32[]{:S(2)}) collective-permute-start(f32[128,128]{1,0:T(8,128)S(1)} %get-tuple-element.55), channel_id=1, source_target_pairs={{8,16},{16,8},{9,17},{17,9},{10,18},{18,10},{11,19},{19,11},{12,20... | collective-permute-start | bytes 196616 | tf_op jit(solution)/shard_map/ppermute | solution.py:218
  33.4 8.8 %collective-permute-start.19 = (f32[512,128]{1,0:T(8,128)S(1)}, f32[512,128]{1,0:T(8,128)S(1)}, u32[]{:S(2)}, u32[]{:S(2)}) collective-permute-start(f32[512,128]{1,0:T(8,128)S(1)} %get-tuple-element.64), channel_id=1, source_target_pairs={{0,1},{1,0},{2,3},{3,2},{4,5},{5,4},{6,7},{7,6},{8,9},{9,8},{10,11... | collective-permute-start | bytes 786440 | tf_op jit(solution)/shard_map/ppermute | solution.py:218
  34.0 8.2 %collective-permute-start.17 = (f32[256,128]{1,0:T(8,128)S(1)}, f32[256,128]{1,0:T(8,128)S(1)}, u32[]{:S(2)}, u32[]{:S(2)}) collective-permute-start(f32[256,128]{1,0:T(8,128)S(1)} %get-tuple-element.62), channel_id=1, source_target_pairs={{0,2},{2,0},{4,6},{6,4},{1,3},{3,1},{5,7},{7,5},{8,10},{10,8},{12,... | collective-permute-start | bytes 393224 | tf_op jit(solution)/shard_map/ppermute | solution.py:218
  35.6 6.5 %collective-permute-start.18 = (f32[256,128]{1,0:T(8,128)S(1)}, f32[256,128]{1,0:T(8,128)S(1)}, u32[]{:S(2)}, u32[]{:S(2)}) collective-permute-start(f32[256,128]{1,0:T(8,128)S(1)} %get-tuple-element.63), channel_id=1, source_target_pairs={{2,4},{4,2},{3,5},{5,3},{10,12},{12,10},{11,13},{13,11},{18,20},{2... | collective-permute-start | bytes 393224 | tf_op jit(solution)/shard_map/ppermute | solution.py:218
  36.3 5.8 %collective-permute-start.15 = (f32[128,128]{1,0:T(8,128)S(1)}, f32[128,128]{1,0:T(8,128)S(1)}, u32[]{:S(2)}, u32[]{:S(2)}) collective-permute-start(f32[128,128]{1,0:T(8,128)S(1)} %get-tuple-element.60), channel_id=1, source_target_pairs={{0,8},{8,0},{16,24},{24,16},{1,9},{9,1},{17,25},{25,17},{2,10},{10... | collective-permute-start | bytes 196616 | tf_op jit(solution)/shard_map/ppermute | solution.py:218
  39.9 2.2 %collective-permute-start.16 = (f32[128,128]{1,0:T(8,128)S(1)}, f32[128,128]{1,0:T(8,128)S(1)}, u32[]{:S(2)}, u32[]{:S(2)}) collective-permute-start(f32[128,128]{1,0:T(8,128)S(1)} %get-tuple-element.61), channel_id=1, source_target_pairs={{8,16},{16,8},{9,17},{17,9},{10,18},{18,10},{11,19},{19,11},{12,20... | collective-permute-start | bytes 196616 | tf_op jit(solution)/shard_map/ppermute | solution.py:218
  42.4 10.9 %collective-permute-start.21 = (f32[256,128]{1,0:T(8,128)S(1)}, f32[256,128]{1,0:T(8,128)S(1)}, u32[]{:S(2)}, u32[]{:S(2)}) collective-permute-start(f32[256,128]{1,0:T(8,128)S(1)} %get-tuple-element.69), channel_id=1, source_target_pairs={{2,0},{4,2},{6,4},{3,1},{5,3},{7,5},{10,8},{12,10},{14,12},{11,9},... | collective-permute-start | bytes 393224 | tf_op jit(solution)/shard_map/ppermute | solution.py:207
  43.7 9.6 %collective-permute-start.22 = (f32[256,128]{1,0:T(8,128)S(1)}, f32[256,128]{1,0:T(8,128)S(1)}, u32[]{:S(2)}, u32[]{:S(2)}) collective-permute-start(f32[256,128]{1,0:T(8,128)S(1)} %get-tuple-element.70), channel_id=1, source_target_pairs={{0,1},{1,0},{2,3},{3,2},{4,5},{5,4},{6,7},{7,6},{8,9},{9,8},{10,11... | collective-permute-start | bytes 393224 | tf_op jit(solution)/shard_map/ppermute | solution.py:207
  45.3 8.1 %collective-permute-start.20 = (f32[128,128]{1,0:T(8,128)S(1)}, f32[128,128]{1,0:T(8,128)S(1)}, u32[]{:S(2)}, u32[]{:S(2)}) collective-permute-start(f32[128,128]{1,0:T(8,128)S(1)} %get-tuple-element.68), channel_id=1, source_target_pairs={{8,0},{16,8},{24,16},{9,1},{17,9},{25,17},{10,2},{18,10},{26,18},{... | collective-permute-start | bytes 196616 | tf_op jit(solution)/shard_map/ppermute | solution.py:207
  53.7 2.2 %collective-permute-start.23 = (f32[72,128]{1,0:T(8,128)S(1)}, f32[72,128]{1,0:T(8,128)S(1)}, u32[]{:S(2)}, u32[]{:S(2)}) collective-permute-start(f32[72,128]{1,0:T(8,128)S(1)} %get-tuple-element.72), channel_id=1, source_target_pairs={{0,2},{1,3},{2,0},{3,1},{4,6},{5,7},{6,4},{7,5},{8,10},{9,11},{10,... | collective-permute-start | bytes 110600 | tf_op jit(solution)/shard_map/ppermute | solution.py:314
  56.0 5.0 %collective-permute-start.26 = (f32[72,128]{1,0:T(8,128)S(1)}, f32[72,128]{1,0:T(8,128)S(1)}, u32[]{:S(2)}, u32[]{:S(2)}) collective-permute-start(f32[72,128]{1,0:T(8,128)S(1)} %add.21), channel_id=1, source_target_pairs={{0,5},{1,4},{2,7},{3,6},{4,1},{5,0},{6,3},{7,2},{8,13},{9,12},{10,... | collective-permute-start | bytes 110600 | tf_op jit(solution)/shard_map/ppermute | solution.py:314
  59.1 4.0 %collective-permute-start.25 = (f32[72,128]{1,0:T(8,128)S(1)}, f32[72,128]{1,0:T(8,128)S(1)}, u32[]{:S(2)}, u32[]{:S(2)}) collective-permute-start(f32[72,128]{1,0:T(8,128)S(1)} %add.21), channel_id=1, source_target_pairs={{0,1},{1,0},{2,3},{3,2},{4,5},{5,4},{6,7},{7,6},{8,9},{9,8},{10,11... | collective-permute-start | bytes 110600 | tf_op jit(solution)/shard_map/ppermute | solution.py:314
  60.6 4.0 %collective-permute-start.24 = (f32[72,128]{1,0:T(8,128)S(1)}, f32[72,128]{1,0:T(8,128)S(1)}, u32[]{:S(2)}, u32[]{:S(2)}) collective-permute-start(f32[72,128]{1,0:T(8,128)S(1)} %add.21), channel_id=1, source_target_pairs={{0,4},{1,5},{2,6},{3,7},{4,0},{5,1},{6,2},{7,3},{8,12},{9,13},{10,... | collective-permute-start | bytes 110600 | tf_op jit(solution)/shard_map/ppermute | solution.py:314
  64.5 6.0 %collective-permute-start.29 = (f32[72,128]{1,0:T(8,128)S(1)}, f32[72,128]{1,0:T(8,128)S(1)}, u32[]{:S(2)}, u32[]{:S(2)}) collective-permute-start(f32[72,128]{1,0:T(8,128)S(1)} %add_add_fusion.1), channel_id=1, source_target_pairs={{0,24},{1,25},{2,26},{3,27},{4,28},{5,29},{6,30},{7,31},{8,16},{9,... | collective-permute-start | bytes 110600 | tf_op jit(solution)/shard_map/ppermute | solution.py:314
  67.2 5.0 %collective-permute-start.28 = (f32[72,128]{1,0:T(8,128)S(1)}, f32[72,128]{1,0:T(8,128)S(1)}, u32[]{:S(2)}, u32[]{:S(2)}) collective-permute-start(f32[72,128]{1,0:T(8,128)S(1)} %add_add_fusion.1), channel_id=1, source_target_pairs={{0,16},{1,17},{2,18},{3,19},{4,20},{5,21},{6,22},{7,23},{8,24},{9,... | collective-permute-start | bytes 110600 | tf_op jit(solution)/shard_map/ppermute | solution.py:314
  68.1 4.4 %collective-permute-start.27 = (f32[72,128]{1,0:T(8,128)S(1)}, f32[72,128]{1,0:T(8,128)S(1)}, u32[]{:S(2)}, u32[]{:S(2)}) collective-permute-start(f32[72,128]{1,0:T(8,128)S(1)} %add_add_fusion.1), channel_id=1, source_target_pairs={{0,8},{1,9},{2,10},{3,11},{4,12},{5,13},{6,14},{7,15},{8,0},{9,1},... | collective-permute-start | bytes 110600 | tf_op jit(solution)/shard_map/ppermute | solution.py:314
  72.5 1.3 %collective-permute-start.30 = (f32[72,128]{1,0:T(8,128)S(1)}, f32[72,128]{1,0:T(8,128)S(1)}, u32[]{:S(2)}, u32[]{:S(2)}) collective-permute-start(f32[72,128]{1,0:T(8,128)S(1)} %add_add_fusion.own_ref), channel_id=1, source_target_pairs={{0,2},{1,3},{2,0},{3,1},{4,6},{5,7},{6,4},{7,5},{8,10},{9,11},{10,... | collective-permute-start | bytes 110600 | tf_op jit(solution)/shard_map/ppermute | solution.py:314
  (1 other events, 0.8 us)

commit v9 on v8

--- a/solution.py
+++ b/solution.py
@@ -70,7 +70,11 @@
 
 
 def prepare(block, turned, s, nz):
-    def body(b_ref, k_ref, w_ref, wide_ref, *refs):
+    parts = 4
+    each = s.x // parts
+
+    def body(k_ref, *all_refs):
+        b_refs, (w_ref, wide_ref, *refs) = all_refs[:parts], all_refs[parts:]
         at_ref = places(s)
         for y in range(s.y):
             tile = k_ref[y]
@@ -78,13 +82,15 @@
                 here = pl.ds(x * s.row + y * s.z, s.z)
                 k = jnp.broadcast_to(tile[:, x : x + 1], (s.z, s.k))
                 wide_ref[here, :] = k
-                w_ref[here, :] = jnp.sqrt(k) * b_ref[here, :]
+                b = b_refs[x // each][(x % each) * s.row + y * s.z : (x % each) * s.row + (y + 1) * s.z, :]
+                w_ref[here, :] = jnp.sqrt(k) * b
         for i in range(nz):
             refs[4 + nz + i][...] = wide_ref[pl.ds(at_ref[4 + i], s.x * s.y, stride=s.z), :]
         faces_of(s, at_ref, w_ref, split_faces(refs, nz))
 
     outs = [f32(s.room, s.k)] * 2 + face_shapes(s, nz) + [f32(s.x * s.y, s.k)] * nz
-    return call(body, outs, [block, turned], 4 * s.cells * s.k)
+    slices = [block[i * each * s.row : (i + 1) * each * s.row] for i in range(parts)]
+    return call(body, outs, [turned] + slices, 4 * s.cells * s.k)
 
 
 def around(s, w_ref, o_ref, x, low, high, emit):
@@ -176,22 +182,30 @@
                         out["z"][i][flat, :] = new
         if last:
             out[0][...] = w_ref[: s.row, :]
-            for x in range(s.x):
-                out[1][x * s.z : (x + 1) * s.z, :] = w_ref[x * s.row : x * s.row + s.z, :]
-            if halved(s, nz):
-                start = (1 - at_ref[6]) * (s.cells // 2) + at_ref[4]
-                out[2][...] = w_ref[pl.ds(start, s.x * s.y // 2, stride=s.z), :]
-            else:
-                out[2][...] = w_ref[pl.ds(0, s.x * s.y, stride=s.z), :]
         else:
             faces_of(s, at_ref, w_ref, out, with_z=False)
 
     if last:
-        outs = [f32(s.room, s.k), f32(s.row, s.k), f32(s.x * s.z, s.k), f32(s.x * s.y // (2 if halved(s, nz) else 1), s.k)]
+        outs = [f32(s.room, s.k), f32(s.row, s.k)]
     else:
         outs = [f32(s.room, s.k)] + face_shapes(s, nz)
     ins = [part, wide] + list(edge) + list(ghosts)
     return call(body, outs, ins, 4 * s.x * s.y * s.k, {0: 0})
+
+
+def last_faces(w, s, nz):
+    def body(w_ref, *out):
+        at_ref = places(s)
+        for x in range(s.x):
+            out[0][x * s.z : (x + 1) * s.z, :] = w_ref[x * s.row : x * s.row + s.z, :]
+        if halved(s, nz):
+            start = (1 - at_ref[6]) * (s.cells // 2) + at_ref[4]
+            out[1][...] = w_ref[pl.ds(start, s.x * s.y // 2, stride=s.z), :]
+        else:
+            out[1][...] = w_ref[pl.ds(0, s.x * s.y, stride=s.z), :]
+
+    outs = [f32(s.x * s.z, s.k), f32(s.x * s.y // (2 if halved(s, nz) else 1), s.k)]
+    return list(call(body, outs, [w], s.x * s.y * s.k))
 
 
 def halved(s, nz):
@@ -332,7 +346,7 @@
     return value, swap(value, pair)
 
 
-PANEL = 32
+PANEL = 64
 GROUP = 16
 
 
@@ -370,7 +384,7 @@
 
 def orthonormal(own, got, filtered, s):
     k = s.k
-    parts = 4
+    parts = 8
     rows = s.cells // parts
 
     def body(own_ref, got_ref, f_ref, b_hbm, o_ref, m_ref, b_ref, sems):
@@ -441,7 +455,7 @@
         scale = (1.0 if before is None else 2.0) / half_value
         before = w
         w, *faces = finish(part, wide, edge, ghosts, s, nz, scale, step == DEG - 1)
-    ghosts = one_way(faces, s, nz)
+    ghosts = one_way(faces + last_faces(w, s, nz), s, nz)
     filtered, gram, own = gather_terms(w, wide, s)
     halves = total(*pack_terms(gram, own, w, ghosts, s, nz, cells))
     basis, projected = orthonormal(*halves, filtered, s)

time: 80.1 us -> 78.9 us (0.985)
    unnamed x4 -> x2, local copies, waits for them, and re-layouts: 2.42 us -> 0.01 us
    slice x0 -> x1, local copies, waits for them, and re-layouts: none -> 1.76 us  [prepare(): block[i * each * s.row:(i + 1) * each * s.row]]
    pallas_call x10 -> x11, Pallas kernels: 7.63 us -> 7.63 us  [call(): pl.pallas_call(body, out_shape=outs, in_specs=[VMEM] * len(ins), out_spec...]
where the time goes in v9:
time: 78.9 us; the launch traced here: 78.5 us
  starting transfers between devices  43 us (54%)
  waiting for transfers between devices  17.6 us (22%)
  Pallas kernels  15.3 us (19%)
  local copies, waits for them, and re-layouts  1.77 us (2%)
  between operations  0.87 us (1%)
    ppermute x20, starting transfers between devices, exchange(): got.append(lax.ppermute(face, axis, pairs))  28.4 us
    ppermute x8, starting transfers between devices, swap(): return lax.ppermute(value, axes, pairs)  10.5 us
    ppermute x8, waiting for transfers between devices, swap(): return lax.ppermute(value, axes, pairs)  9.46 us
    pallas_call x11, Pallas kernels, call(): pl.pallas_call(body, out_shape=outs, in_specs=[VMEM] * len(ins), out_spec...  7.63 us
    pallas_call x1, Pallas kernels, orthonormal(): pl.pallas_call(body, out_shape=[f32(s.cells, k), f32(k, k)], in_specs=[VM...  5.44 us
    ppermute x3, waiting for transfers between devices, one_way(): got.append(lax.ppermute(face, axis, pairs))  4.57 us
    ppermute x3, starting transfers between devices, one_way(): got.append(lax.ppermute(face, axis, pairs))  4.13 us
    ppermute x20, waiting for transfers between devices, exchange(): got.append(lax.ppermute(face, axis, pairs))  3.54 us
  transfers between devices with their start and end apart: 31, of which 15 were waited for; matrix products, arithmetic and copies ran while one was open for 0% of the time, Pallas kernels for 9%

profile of v9, /device:TPU:0, one launch (start us, length us, event | category | flops | bytes accessed | tf_op | source)
XLA Modules:
  0.0 78.5 jit_solution(6919411189153730548)
XLA Ops:
  0.6 1.8 %fusion = (f32[8,16,8,128]{3,2,1,0:T(8,128)S(1)}, f32[8,16,8,128]{3,2,1,0:T(8,128)S(1)}, f32[8,16,8,128]{3,2,1,0:T(8,128)S(1)}, f32[8,16,8,128]{3,2,1,0:T(8,128)S(1)}) fusion(f32[32,16,8,128]{3,2,1,0:T(8,128)} %param.2), kind=kLoop, calls=%fused_computation.2 | loop fusion | bytes 4194304 | tf_op jit(solution)/shard_map/slice | solution.py:92
  2.4 1.1 %shard_map.41 = (f32[4104,128]{1,0:T(8,128)S(1)}, f32[4104,128]{1,0:T(8,128)S(1)}, f32[128,128]{1,0:T(8,128)S(1)}, f32[128,128]{1,0:T(8,128)S(1)}, f32[256,128]{...) custom-call(f32[16,8,32]{2,1,0:T(8,128)S(1)} %bitcast.10, ...), custom_call_target="tpu_custom_call" | custom-call | flops 2097152 | bytes 7233536 | tf_op jit(solution)/shard_map/pallas_call | solution.py:20
  3.5 3.0 %collective-permute-start.4 = (f32[512,128]{1,0:T(8,128)S(1)}, f32[512,128]{1,0:T(8,128)S(1)}, u32[]{:S(2)}, u32[]{:S(2)}) collective-permute-start(f32[512,128]{1,0:T(8,128)S(1)} %get-tuple-element.46), channel_id=1, source_target_pairs={{0,1},{1,0},{2,3},{3,2},{4,5},{5,4},{6,7},{7,6},{8,9},{9,8},{10,11... | collective-permute-start | bytes 786440 | tf_op jit(solution)/shard_map/ppermute | solution.py:232
  7.2 1.6 %collective-permute-start = (f32[128,128]{1,0:T(8,128)S(1)}, f32[128,128]{1,0:T(8,128)S(1)}, u32[]{:S(2)}, u32[]{:S(2)}) collective-permute-start(f32[128,128]{1,0:T(8,128)S(1)} %get-tuple-element.42), channel_id=1, source_target_pairs={{0,8},{8,0},{16,24},{24,16},{1,9},{9,1},{17,25},{25,17},{2,10},{10... | collective-permute-start | bytes 196616 | tf_op jit(solution)/shard_map/ppermute | solution.py:232
  9.5 1.2 %shard_map.42.p_ref = f32[4104,128]{1,0:T(8,128)S(1)} custom-call(f32[4104,128]{1,0:T(8,128)S(1)} %get-tuple-element.39.w_ref.rest_0_, f32[4104,128]{1,0:T(8,128)S(1)} %get-tuple-element.40.k_ref), custom_call_target="tpu_custom_call" | custom-call | flops 6291456 | bytes 6303744 | tf_op jit(solution)/shard_map/pallas_call | solution.py:20
  11.6 1.3 %collective-permute-done.4.refs_5_ = f32[512,128]{1,0:T(8,128)S(1)} collective-permute-done((f32[512,128]{1,0:T(8,128)S(1)}, f32[512,128]{1,0:T(8,128)S(1)}, u32[]{:S(2)}, u32[]{:S(2)}) %collective-permute-start.4) | collective-permute-done | bytes 262176 | tf_op jit(solution)/shard_map/ppermute | solution.py:232
  13.1 1.8 %collective-permute-start.9 = (f32[512,128]{1,0:T(8,128)S(1)}, f32[512,128]{1,0:T(8,128)S(1)}, u32[]{:S(2)}, u32[]{:S(2)}) collective-permute-start(f32[512,128]{1,0:T(8,128)S(1)} %get-tuple-element.52), channel_id=1, source_target_pairs={{0,1},{1,0},{2,3},{3,2},{4,5},{5,4},{6,7},{7,6},{8,9},{9,8},{10,11... | collective-permute-start | bytes 786440 | tf_op jit(solution)/shard_map/ppermute | solution.py:232
  15.6 3.6 %collective-permute-start.5 = (f32[128,128]{1,0:T(8,128)S(1)}, f32[128,128]{1,0:T(8,128)S(1)}, u32[]{:S(2)}, u32[]{:S(2)}) collective-permute-start(f32[128,128]{1,0:T(8,128)S(1)} %get-tuple-element.48), channel_id=1, source_target_pairs={{0,8},{8,0},{16,24},{24,16},{1,9},{9,1},{17,25},{25,17},{2,10},{10... | collective-permute-start | bytes 196616 | tf_op jit(solution)/shard_map/ppermute | solution.py:232
  19.9 1.2 %shard_map.44.p_ref = f32[4104,128]{1,0:T(8,128)S(1)} custom-call(f32[4104,128]{1,0:T(8,128)S(1)} %get-tuple-element.47.w_ref.rest_0_, f32[4104,128]{1,0:T(8,128)S(1)} %get-tuple-element.40.k_ref, f32[4104,128]{1,0:T(8,128)S(1)} %get-tuple-element.39.w_ref.rest_0_), custom_call_target="tpu_custom_call" | custom-call | flops 6291456 | bytes 8404992 | tf_op jit(solution)/shard_map/pallas_call | solution.py:20
  22.2 1.2 %collective-permute-start.14 = (f32[512,128]{1,0:T(8,128)S(1)}, f32[512,128]{1,0:T(8,128)S(1)}, u32[]{:S(2)}, u32[]{:S(2)}) collective-permute-start(f32[512,128]{1,0:T(8,128)S(1)} %get-tuple-element.58), channel_id=1, source_target_pairs={{0,1},{1,0},{2,3},{3,2},{4,5},{5,4},{6,7},{7,6},{8,9},{9,8},{10,11... | collective-permute-start | bytes 786440 | tf_op jit(solution)/shard_map/ppermute | solution.py:232
  23.4 2.4 %collective-permute-start.12 = (f32[256,128]{1,0:T(8,128)S(1)}, f32[256,128]{1,0:T(8,128)S(1)}, u32[]{:S(2)}, u32[]{:S(2)}) collective-permute-start(f32[256,128]{1,0:T(8,128)S(1)} %get-tuple-element.56), channel_id=1, source_target_pairs={{0,2},{2,0},{4,6},{6,4},{1,3},{3,1},{5,7},{7,5},{8,10},{10,8},{12,... | collective-permute-start | bytes 393224 | tf_op jit(solution)/shard_map/ppermute | solution.py:232
  26.4 3.7 %collective-permute-start.10 = (f32[128,128]{1,0:T(8,128)S(1)}, f32[128,128]{1,0:T(8,128)S(1)}, u32[]{:S(2)}, u32[]{:S(2)}) collective-permute-start(f32[128,128]{1,0:T(8,128)S(1)} %get-tuple-element.54), channel_id=1, source_target_pairs={{0,8},{8,0},{16,24},{24,16},{1,9},{9,1},{17,25},{25,17},{2,10},{10... | collective-permute-start | bytes 196616 | tf_op jit(solution)/shard_map/ppermute | solution.py:232
  30.8 1.4 %shard_map.46.p_ref = f32[4104,128]{1,0:T(8,128)S(1)} custom-call(f32[4104,128]{1,0:T(8,128)S(1)} %get-tuple-element.53.w_ref.rest_0_, f32[4104,128]{1,0:T(8,128)S(1)} %get-tuple-element.40.k_ref, f32[4104,128]{1,0:T(8,128)S(1)} %get-tuple-element.47.w_ref.rest_0_), custom_call_target="tpu_custom_call" | custom-call | flops 6291456 | bytes 8404992 | tf_op jit(solution)/shard_map/pallas_call | solution.py:20
  33.3 1.6 %collective-permute-start.17 = (f32[256,128]{1,0:T(8,128)S(1)}, f32[256,128]{1,0:T(8,128)S(1)}, u32[]{:S(2)}, u32[]{:S(2)}) collective-permute-start(f32[256,128]{1,0:T(8,128)S(1)} %get-tuple-element.62), channel_id=1, source_target_pairs={{0,2},{2,0},{4,6},{6,4},{1,3},{3,1},{5,7},{7,5},{8,10},{10,8},{12,... | collective-permute-start | bytes 393224 | tf_op jit(solution)/shard_map/ppermute | solution.py:232
  35.6 3.6 %collective-permute-start.15 = (f32[128,128]{1,0:T(8,128)S(1)}, f32[128,128]{1,0:T(8,128)S(1)}, u32[]{:S(2)}, u32[]{:S(2)}) collective-permute-start(f32[128,128]{1,0:T(8,128)S(1)} %get-tuple-element.60), channel_id=1, source_target_pairs={{0,8},{8,0},{16,24},{24,16},{1,9},{9,1},{17,25},{25,17},{2,10},{10... | collective-permute-start | bytes 196616 | tf_op jit(solution)/shard_map/ppermute | solution.py:232
  39.9 1.2 %shard_map.48.p_ref = f32[4104,128]{1,0:T(8,128)S(1)} custom-call(f32[4104,128]{1,0:T(8,128)S(1)} %get-tuple-element.59.w_ref, f32[4104,128]{1,0:T(8,128)S(1)} %get-tuple-element.40.k_ref, f32[4104,128]{1,0:T(8,128)S(1)} %get-tuple-element.53.w_ref.rest_0_), custom_call_target="tpu_custom_call" | custom-call | flops 6291456 | bytes 8404992 | tf_op jit(solution)/shard_map/pallas_call | solution.py:20
  41.8 1.3 %collective-permute-start.21 = (f32[256,128]{1,0:T(8,128)S(1)}, f32[256,128]{1,0:T(8,128)S(1)}, u32[]{:S(2)}, u32[]{:S(2)}) collective-permute-start(f32[256,128]{1,0:T(8,128)S(1)} %get-tuple-element.69), channel_id=1, source_target_pairs={{2,0},{4,2},{6,4},{3,1},{5,3},{7,5},{10,8},{12,10},{14,12},{11,9},... | collective-permute-start | bytes 393224 | tf_op jit(solution)/shard_map/ppermute | solution.py:221
  43.1 1.6 %collective-permute-start.22 = (f32[256,128]{1,0:T(8,128)S(1)}, f32[256,128]{1,0:T(8,128)S(1)}, u32[]{:S(2)}, u32[]{:S(2)}) collective-permute-start(f32[256,128]{1,0:T(8,128)S(1)} %get-tuple-element.70), channel_id=1, source_target_pairs={{0,1},{1,0},{2,3},{3,2},{4,5},{5,4},{6,7},{7,6},{8,9},{9,8},{10,11... | collective-permute-start | bytes 393224 | tf_op jit(solution)/shard_map/ppermute | solution.py:221
  44.7 1.3 %collective-permute-start.20 = (f32[128,128]{1,0:T(8,128)S(1)}, f32[128,128]{1,0:T(8,128)S(1)}, u32[]{:S(2)}, u32[]{:S(2)}) collective-permute-start(f32[128,128]{1,0:T(8,128)S(1)} %get-tuple-element.68), channel_id=1, source_target_pairs={{8,0},{16,8},{24,16},{9,1},{17,9},{25,17},{10,2},{18,10},{26,18},{... | collective-permute-start | bytes 196616 | tf_op jit(solution)/shard_map/ppermute | solution.py:221
  45.9 2.2 %shard_map.50 = (bf16[4096,256]{1,0:T(8,128)(2,1)S(1)}, f32[128,128]{1,0:T(8,128)S(1)}, f32[128,128]{1,0:T(8,128)S(1)}) custom-call(f32[4104,128]{1,0:T(8,128)S(1)} %get-tuple-element.65.w_ref, f32[4104,128]{1,0:T(8,128)S(1)} %get-tuple-element.40.k_ref), custom_call_target="tpu_custom_call" | custom-call | flops 1073741824 | bytes 8388608 | tf_op jit(solution)/shard_map/pallas_call | solution.py:275
  48.1 4.6 %collective-permute-done.20.x_ref = f32[128,128]{1,0:T(8,128)S(1)} collective-permute-done((f32[128,128]{1,0:T(8,128)S(1)}, f32[128,128]{1,0:T(8,128)S(1)}, u32[]{:S(2)}, u32[]{:S(2)}) %collective-permute-start.20) | collective-permute-done | bytes 65568 | tf_op jit(solution)/shard_map/ppermute | solution.py:221
  53.1 1.4 %collective-permute-start.23 = (f32[72,128]{1,0:T(8,128)S(1)}, f32[72,128]{1,0:T(8,128)S(1)}, u32[]{:S(2)}, u32[]{:S(2)}) collective-permute-start(f32[72,128]{1,0:T(8,128)S(1)} %get-tuple-element.72), channel_id=1, source_target_pairs={{0,2},{1,3},{2,0},{3,1},{4,6},{5,7},{6,4},{7,5},{8,10},{9,11},{10,... | collective-permute-start | bytes 110600 | tf_op jit(solution)/shard_map/ppermute | solution.py:328
  55.4 3.1 %collective-permute-start.26 = (f32[72,128]{1,0:T(8,128)S(1)}, f32[72,128]{1,0:T(8,128)S(1)}, u32[]{:S(2)}, u32[]{:S(2)}) collective-permute-start(f32[72,128]{1,0:T(8,128)S(1)} %add.21), channel_id=1, source_target_pairs={{0,5},{1,4},{2,7},{3,6},{4,1},{5,0},{6,3},{7,2},{8,13},{9,12},{10,... | collective-permute-start | bytes 110600 | tf_op jit(solution)/shard_map/ppermute | solution.py:328
  58.4 1.5 %collective-permute-start.25 = (f32[72,128]{1,0:T(8,128)S(1)}, f32[72,128]{1,0:T(8,128)S(1)}, u32[]{:S(2)}, u32[]{:S(2)}) collective-permute-start(f32[72,128]{1,0:T(8,128)S(1)} %add.21), channel_id=1, source_target_pairs={{0,1},{1,0},{2,3},{3,2},{4,5},{5,4},{6,7},{7,6},{8,9},{9,8},{10,11... | collective-permute-start | bytes 110600 | tf_op jit(solution)/shard_map/ppermute | solution.py:328
  60.4 2.0 %collective-permute-done.25 = f32[72,128]{1,0:T(8,128)S(1)} collective-permute-done((f32[72,128]{1,0:T(8,128)S(1)}, f32[72,128]{1,0:T(8,128)S(1)}, u32[]{:S(2)}, u32[]{:S(2)}) %collective-permute-start.25) | collective-permute-done | bytes 36896 | tf_op jit(solution)/shard_map/ppermute | solution.py:328
  62.4 1.5 %collective-permute-done.24 = f32[72,128]{1,0:T(8,128)S(1)} collective-permute-done((f32[72,128]{1,0:T(8,128)S(1)}, f32[72,128]{1,0:T(8,128)S(1)}, u32[]{:S(2)}, u32[]{:S(2)}) %collective-permute-start.24) | collective-permute-done | bytes 36896 | tf_op jit(solution)/shard_map/ppermute | solution.py:328
  63.9 2.7 %collective-permute-start.29 = (f32[72,128]{1,0:T(8,128)S(1)}, f32[72,128]{1,0:T(8,128)S(1)}, u32[]{:S(2)}, u32[]{:S(2)}) collective-permute-start(f32[72,128]{1,0:T(8,128)S(1)} %add_add_fusion.1), channel_id=1, source_target_pairs={{0,24},{1,25},{2,26},{3,27},{4,28},{5,29},{6,30},{7,31},{8,16},{9,... | collective-permute-start | bytes 110600 | tf_op jit(solution)/shard_map/ppermute | solution.py:328
  67.5 0.9 %collective-permute-start.27 = (f32[72,128]{1,0:T(8,128)S(1)}, f32[72,128]{1,0:T(8,128)S(1)}, u32[]{:S(2)}, u32[]{:S(2)}) collective-permute-start(f32[72,128]{1,0:T(8,128)S(1)} %add_add_fusion.1), channel_id=1, source_target_pairs={{0,8},{1,9},{2,10},{3,11},{4,12},{5,13},{6,14},{7,15},{8,0},{9,1},... | collective-permute-start | bytes 110600 | tf_op jit(solution)/shard_map/ppermute | solution.py:328
  68.4 1.6 %collective-permute-done.29 = f32[72,128]{1,0:T(8,128)S(1)} collective-permute-done((f32[72,128]{1,0:T(8,128)S(1)}, f32[72,128]{1,0:T(8,128)S(1)}, u32[]{:S(2)}, u32[]{:S(2)}) %collective-permute-start.29) | collective-permute-done | bytes 36896 | tf_op jit(solution)/shard_map/ppermute | solution.py:328
  70.0 1.6 %collective-permute-done.28 = f32[72,128]{1,0:T(8,128)S(1)} collective-permute-done((f32[72,128]{1,0:T(8,128)S(1)}, f32[72,128]{1,0:T(8,128)S(1)}, u32[]{:S(2)}, u32[]{:S(2)}) %collective-permute-start.28) | collective-permute-done | bytes 36896 | tf_op jit(solution)/shard_map/ppermute | solution.py:328
  71.9 1.2 %collective-permute-done.30.got_ref = f32[72,128]{1,0:T(8,128)S(1)} collective-permute-done((f32[72,128]{1,0:T(8,128)S(1)}, f32[72,128]{1,0:T(8,128)S(1)}, u32[]{:S(2)}, u32[]{:S(2)}) %collective-permute-start.30) | collective-permute-done | bytes 36896 | tf_op jit(solution)/shard_map/ppermute | solution.py:328
  73.1 5.4 %shard_map.53 = (f32[4096,128]{1,0:T(8,128)}, f32[128,128]{1,0:T(8,128)}) custom-call(f32[72,128]{1,0:T(8,128)S(1)} %add_add_fusion.own_ref, f32[72,128]{1,0:T(8,128)S(1)} %collective-permute-done.30.got_ref, bf16[4096,256]{1,0:T(8,128)(2,1)S(1)} %get-tuple-element.73.f_ref), custom_call_target="tpu_custom_call" | custom-call | flops 536870912 | bytes 4194304 | tf_op jit(solution)/shard_map/pallas_call | solution.py:423
  (49 shorter events, 12.2 us)
Async XLA Ops:
  0.6 1.8 %copy-start = (f32[32,16,8]{0,2,1:T(8,128)S(1)}, f32[32,16,8]{0,2,1:T(8,128)}, u32[]{:S(2)}) copy-start(f32[32,16,8]{0,2,1:T(8,128)} %param.3) | copy-start | bytes 49156
  3.5 9.3 %collective-permute-start.4 = (f32[512,128]{1,0:T(8,128)S(1)}, f32[512,128]{1,0:T(8,128)S(1)}, u32[]{:S(2)}, u32[]{:S(2)}) collective-permute-start(f32[512,128]{1,0:T(8,128)S(1)} %get-tuple-element.46), channel_id=1, source_target_pairs={{0,1},{1,0},{2,3},{3,2},{4,5},{5,4},{6,7},{7,6},{8,9},{9,8},{10,11... | collective-permute-start | bytes 786440 | tf_op jit(solution)/shard_map/ppermute | solution.py:232
  6.5 5.0 %collective-permute-start.2 = (f32[256,128]{1,0:T(8,128)S(1)}, f32[256,128]{1,0:T(8,128)S(1)}, u32[]{:S(2)}, u32[]{:S(2)}) collective-permute-start(f32[256,128]{1,0:T(8,128)S(1)} %get-tuple-element.44), channel_id=1, source_target_pairs={{0,2},{2,0},{4,6},{6,4},{1,3},{3,1},{5,7},{7,5},{8,10},{10,8},{12,... | collective-permute-start | bytes 393224 | tf_op jit(solution)/shard_map/ppermute | solution.py:232
  6.5 5.0 %collective-permute-start.3 = (f32[256,128]{1,0:T(8,128)S(1)}, f32[256,128]{1,0:T(8,128)S(1)}, u32[]{:S(2)}, u32[]{:S(2)}) collective-permute-start(f32[256,128]{1,0:T(8,128)S(1)} %get-tuple-element.45), channel_id=1, source_target_pairs={{2,4},{4,2},{3,5},{5,3},{10,12},{12,10},{11,13},{13,11},{18,20},{2... | collective-permute-start | bytes 393224 | tf_op jit(solution)/shard_map/ppermute | solution.py:232
  7.2 4.3 %collective-permute-start = (f32[128,128]{1,0:T(8,128)S(1)}, f32[128,128]{1,0:T(8,128)S(1)}, u32[]{:S(2)}, u32[]{:S(2)}) collective-permute-start(f32[128,128]{1,0:T(8,128)S(1)} %get-tuple-element.42), channel_id=1, source_target_pairs={{0,8},{8,0},{16,24},{24,16},{1,9},{9,1},{17,25},{25,17},{2,10},{10... | collective-permute-start | bytes 196616 | tf_op jit(solution)/shard_map/ppermute | solution.py:232
  8.9 2.7 %collective-permute-start.1 = (f32[128,128]{1,0:T(8,128)S(1)}, f32[128,128]{1,0:T(8,128)S(1)}, u32[]{:S(2)}, u32[]{:S(2)}) collective-permute-start(f32[128,128]{1,0:T(8,128)S(1)} %get-tuple-element.43), channel_id=1, source_target_pairs={{8,16},{16,8},{9,17},{17,9},{10,18},{18,10},{11,19},{19,11},{12,20... | collective-permute-start | bytes 196616 | tf_op jit(solution)/shard_map/ppermute | solution.py:232
  13.1 8.8 %collective-permute-start.9 = (f32[512,128]{1,0:T(8,128)S(1)}, f32[512,128]{1,0:T(8,128)S(1)}, u32[]{:S(2)}, u32[]{:S(2)}) collective-permute-start(f32[512,128]{1,0:T(8,128)S(1)} %get-tuple-element.52), channel_id=1, source_target_pairs={{0,1},{1,0},{2,3},{3,2},{4,5},{5,4},{6,7},{7,6},{8,9},{9,8},{10,11... | collective-permute-start | bytes 786440 | tf_op jit(solution)/shard_map/ppermute | solution.py:232
  14.9 6.5 %collective-permute-start.7 = (f32[256,128]{1,0:T(8,128)S(1)}, f32[256,128]{1,0:T(8,128)S(1)}, u32[]{:S(2)}, u32[]{:S(2)}) collective-permute-start(f32[256,128]{1,0:T(8,128)S(1)} %get-tuple-element.50), channel_id=1, source_target_pairs={{0,2},{2,0},{4,6},{6,4},{1,3},{3,1},{5,7},{7,5},{8,10},{10,8},{12,... | collective-permute-start | bytes 393224 | tf_op jit(solution)/shard_map/ppermute | solution.py:232
  14.9 6.5 %collective-permute-start.8 = (f32[256,128]{1,0:T(8,128)S(1)}, f32[256,128]{1,0:T(8,128)S(1)}, u32[]{:S(2)}, u32[]{:S(2)}) collective-permute-start(f32[256,128]{1,0:T(8,128)S(1)} %get-tuple-element.51), channel_id=1, source_target_pairs={{2,4},{4,2},{3,5},{5,3},{10,12},{12,10},{11,13},{13,11},{18,20},{2... | collective-permute-start | bytes 393224 | tf_op jit(solution)/shard_map/ppermute | solution.py:232
  15.6 5.9 %collective-permute-start.5 = (f32[128,128]{1,0:T(8,128)S(1)}, f32[128,128]{1,0:T(8,128)S(1)}, u32[]{:S(2)}, u32[]{:S(2)}) collective-permute-start(f32[128,128]{1,0:T(8,128)S(1)} %get-tuple-element.48), channel_id=1, source_target_pairs={{0,8},{8,0},{16,24},{24,16},{1,9},{9,1},{17,25},{25,17},{2,10},{10... | collective-permute-start | bytes 196616 | tf_op jit(solution)/shard_map/ppermute | solution.py:232
  19.2 2.2 %collective-permute-start.6 = (f32[128,128]{1,0:T(8,128)S(1)}, f32[128,128]{1,0:T(8,128)S(1)}, u32[]{:S(2)}, u32[]{:S(2)}) collective-permute-start(f32[128,128]{1,0:T(8,128)S(1)} %get-tuple-element.49), channel_id=1, source_target_pairs={{8,16},{16,8},{9,17},{17,9},{10,18},{18,10},{11,19},{19,11},{12,20... | collective-permute-start | bytes 196616 | tf_op jit(solution)/shard_map/ppermute | solution.py:232
  22.2 10.2 %collective-permute-start.14 = (f32[512,128]{1,0:T(8,128)S(1)}, f32[512,128]{1,0:T(8,128)S(1)}, u32[]{:S(2)}, u32[]{:S(2)}) collective-permute-start(f32[512,128]{1,0:T(8,128)S(1)} %get-tuple-element.58), channel_id=1, source_target_pairs={{0,1},{1,0},{2,3},{3,2},{4,5},{5,4},{6,7},{7,6},{8,9},{9,8},{10,11... | collective-permute-start | bytes 786440 | tf_op jit(solution)/shard_map/ppermute | solution.py:232
  23.4 9.0 %collective-permute-start.12 = (f32[256,128]{1,0:T(8,128)S(1)}, f32[256,128]{1,0:T(8,128)S(1)}, u32[]{:S(2)}, u32[]{:S(2)}) collective-permute-start(f32[256,128]{1,0:T(8,128)S(1)} %get-tuple-element.56), channel_id=1, source_target_pairs={{0,2},{2,0},{4,6},{6,4},{1,3},{3,1},{5,7},{7,5},{8,10},{10,8},{12,... | collective-permute-start | bytes 393224 | tf_op jit(solution)/shard_map/ppermute | solution.py:232
  25.8 6.6 %collective-permute-start.13 = (f32[256,128]{1,0:T(8,128)S(1)}, f32[256,128]{1,0:T(8,128)S(1)}, u32[]{:S(2)}, u32[]{:S(2)}) collective-permute-start(f32[256,128]{1,0:T(8,128)S(1)} %get-tuple-element.57), channel_id=1, source_target_pairs={{2,4},{4,2},{3,5},{5,3},{10,12},{12,10},{11,13},{13,11},{18,20},{2... | collective-permute-start | bytes 393224 | tf_op jit(solution)/shard_map/ppermute | solution.py:232
  26.4 5.9 %collective-permute-start.10 = (f32[128,128]{1,0:T(8,128)S(1)}, f32[128,128]{1,0:T(8,128)S(1)}, u32[]{:S(2)}, u32[]{:S(2)}) collective-permute-start(f32[128,128]{1,0:T(8,128)S(1)} %get-tuple-element.54), channel_id=1, source_target_pairs={{0,8},{8,0},{16,24},{24,16},{1,9},{9,1},{17,25},{25,17},{2,10},{10... | collective-permute-start | bytes 196616 | tf_op jit(solution)/shard_map/ppermute | solution.py:232
  30.2 2.2 %collective-permute-start.11 = (f32[128,128]{1,0:T(8,128)S(1)}, f32[128,128]{1,0:T(8,128)S(1)}, u32[]{:S(2)}, u32[]{:S(2)}) collective-permute-start(f32[128,128]{1,0:T(8,128)S(1)} %get-tuple-element.55), channel_id=1, source_target_pairs={{8,16},{16,8},{9,17},{17,9},{10,18},{18,10},{11,19},{19,11},{12,20... | collective-permute-start | bytes 196616 | tf_op jit(solution)/shard_map/ppermute | solution.py:232
  32.7 8.8 %collective-permute-start.19 = (f32[512,128]{1,0:T(8,128)S(1)}, f32[512,128]{1,0:T(8,128)S(1)}, u32[]{:S(2)}, u32[]{:S(2)}) collective-permute-start(f32[512,128]{1,0:T(8,128)S(1)} %get-tuple-element.64), channel_id=1, source_target_pairs={{0,1},{1,0},{2,3},{3,2},{4,5},{5,4},{6,7},{7,6},{8,9},{9,8},{10,11... | collective-permute-start | bytes 786440 | tf_op jit(solution)/shard_map/ppermute | solution.py:232
  33.3 8.2 %collective-permute-start.17 = (f32[256,128]{1,0:T(8,128)S(1)}, f32[256,128]{1,0:T(8,128)S(1)}, u32[]{:S(2)}, u32[]{:S(2)}) collective-permute-start(f32[256,128]{1,0:T(8,128)S(1)} %get-tuple-element.62), channel_id=1, source_target_pairs={{0,2},{2,0},{4,6},{6,4},{1,3},{3,1},{5,7},{7,5},{8,10},{10,8},{12,... | collective-permute-start | bytes 393224 | tf_op jit(solution)/shard_map/ppermute | solution.py:232
  35.0 6.5 %collective-permute-start.18 = (f32[256,128]{1,0:T(8,128)S(1)}, f32[256,128]{1,0:T(8,128)S(1)}, u32[]{:S(2)}, u32[]{:S(2)}) collective-permute-start(f32[256,128]{1,0:T(8,128)S(1)} %get-tuple-element.63), channel_id=1, source_target_pairs={{2,4},{4,2},{3,5},{5,3},{10,12},{12,10},{11,13},{13,11},{18,20},{2... | collective-permute-start | bytes 393224 | tf_op jit(solution)/shard_map/ppermute | solution.py:232
  35.6 5.8 %collective-permute-start.15 = (f32[128,128]{1,0:T(8,128)S(1)}, f32[128,128]{1,0:T(8,128)S(1)}, u32[]{:S(2)}, u32[]{:S(2)}) collective-permute-start(f32[128,128]{1,0:T(8,128)S(1)} %get-tuple-element.60), channel_id=1, source_target_pairs={{0,8},{8,0},{16,24},{24,16},{1,9},{9,1},{17,25},{25,17},{2,10},{10... | collective-permute-start | bytes 196616 | tf_op jit(solution)/shard_map/ppermute | solution.py:232
  39.2 2.2 %collective-permute-start.16 = (f32[128,128]{1,0:T(8,128)S(1)}, f32[128,128]{1,0:T(8,128)S(1)}, u32[]{:S(2)}, u32[]{:S(2)}) collective-permute-start(f32[128,128]{1,0:T(8,128)S(1)} %get-tuple-element.61), channel_id=1, source_target_pairs={{8,16},{16,8},{9,17},{17,9},{10,18},{18,10},{11,19},{19,11},{12,20... | collective-permute-start | bytes 196616 | tf_op jit(solution)/shard_map/ppermute | solution.py:232
  41.8 10.9 %collective-permute-start.21 = (f32[256,128]{1,0:T(8,128)S(1)}, f32[256,128]{1,0:T(8,128)S(1)}, u32[]{:S(2)}, u32[]{:S(2)}) collective-permute-start(f32[256,128]{1,0:T(8,128)S(1)} %get-tuple-element.69), channel_id=1, source_target_pairs={{2,0},{4,2},{6,4},{3,1},{5,3},{7,5},{10,8},{12,10},{14,12},{11,9},... | collective-permute-start | bytes 393224 | tf_op jit(solution)/shard_map/ppermute | solution.py:221
  43.1 9.6 %collective-permute-start.22 = (f32[256,128]{1,0:T(8,128)S(1)}, f32[256,128]{1,0:T(8,128)S(1)}, u32[]{:S(2)}, u32[]{:S(2)}) collective-permute-start(f32[256,128]{1,0:T(8,128)S(1)} %get-tuple-element.70), channel_id=1, source_target_pairs={{0,1},{1,0},{2,3},{3,2},{4,5},{5,4},{6,7},{7,6},{8,9},{9,8},{10,11... | collective-permute-start | bytes 393224 | tf_op jit(solution)/shard_map/ppermute | solution.py:221
  44.7 8.1 %collective-permute-start.20 = (f32[128,128]{1,0:T(8,128)S(1)}, f32[128,128]{1,0:T(8,128)S(1)}, u32[]{:S(2)}, u32[]{:S(2)}) collective-permute-start(f32[128,128]{1,0:T(8,128)S(1)} %get-tuple-element.68), channel_id=1, source_target_pairs={{8,0},{16,8},{24,16},{9,1},{17,9},{25,17},{10,2},{18,10},{26,18},{... | collective-permute-start | bytes 196616 | tf_op jit(solution)/shard_map/ppermute | solution.py:221
  53.1 2.2 %collective-permute-start.23 = (f32[72,128]{1,0:T(8,128)S(1)}, f32[72,128]{1,0:T(8,128)S(1)}, u32[]{:S(2)}, u32[]{:S(2)}) collective-permute-start(f32[72,128]{1,0:T(8,128)S(1)} %get-tuple-element.72), channel_id=1, source_target_pairs={{0,2},{1,3},{2,0},{3,1},{4,6},{5,7},{6,4},{7,5},{8,10},{9,11},{10,... | collective-permute-start | bytes 110600 | tf_op jit(solution)/shard_map/ppermute | solution.py:328
  55.4 5.0 %collective-permute-start.26 = (f32[72,128]{1,0:T(8,128)S(1)}, f32[72,128]{1,0:T(8,128)S(1)}, u32[]{:S(2)}, u32[]{:S(2)}) collective-permute-start(f32[72,128]{1,0:T(8,128)S(1)} %add.21), channel_id=1, source_target_pairs={{0,5},{1,4},{2,7},{3,6},{4,1},{5,0},{6,3},{7,2},{8,13},{9,12},{10,... | collective-permute-start | bytes 110600 | tf_op jit(solution)/shard_map/ppermute | solution.py:328
  58.4 4.0 %collective-permute-start.25 = (f32[72,128]{1,0:T(8,128)S(1)}, f32[72,128]{1,0:T(8,128)S(1)}, u32[]{:S(2)}, u32[]{:S(2)}) collective-permute-start(f32[72,128]{1,0:T(8,128)S(1)} %add.21), channel_id=1, source_target_pairs={{0,1},{1,0},{2,3},{3,2},{4,5},{5,4},{6,7},{7,6},{8,9},{9,8},{10,11... | collective-permute-start | bytes 110600 | tf_op jit(solution)/shard_map/ppermute | solution.py:328
  59.9 4.0 %collective-permute-start.24 = (f32[72,128]{1,0:T(8,128)S(1)}, f32[72,128]{1,0:T(8,128)S(1)}, u32[]{:S(2)}, u32[]{:S(2)}) collective-permute-start(f32[72,128]{1,0:T(8,128)S(1)} %add.21), channel_id=1, source_target_pairs={{0,4},{1,5},{2,6},{3,7},{4,0},{5,1},{6,2},{7,3},{8,12},{9,13},{10,... | collective-permute-start | bytes 110600 | tf_op jit(solution)/shard_map/ppermute | solution.py:328
  63.9 6.0 %collective-permute-start.29 = (f32[72,128]{1,0:T(8,128)S(1)}, f32[72,128]{1,0:T(8,128)S(1)}, u32[]{:S(2)}, u32[]{:S(2)}) collective-permute-start(f32[72,128]{1,0:T(8,128)S(1)} %add_add_fusion.1), channel_id=1, source_target_pairs={{0,24},{1,25},{2,26},{3,27},{4,28},{5,29},{6,30},{7,31},{8,16},{9,... | collective-permute-start | bytes 110600 | tf_op jit(solution)/shard_map/ppermute | solution.py:328
  66.6 5.0 %collective-permute-start.28 = (f32[72,128]{1,0:T(8,128)S(1)}, f32[72,128]{1,0:T(8,128)S(1)}, u32[]{:S(2)}, u32[]{:S(2)}) collective-permute-start(f32[72,128]{1,0:T(8,128)S(1)} %add_add_fusion.1), channel_id=1, source_target_pairs={{0,16},{1,17},{2,18},{3,19},{4,20},{5,21},{6,22},{7,23},{8,24},{9,... | collective-permute-start | bytes 110600 | tf_op jit(solution)/shard_map/ppermute | solution.py:328
  67.5 4.4 %collective-permute-start.27 = (f32[72,128]{1,0:T(8,128)S(1)}, f32[72,128]{1,0:T(8,128)S(1)}, u32[]{:S(2)}, u32[]{:S(2)}) collective-permute-start(f32[72,128]{1,0:T(8,128)S(1)} %add_add_fusion.1), channel_id=1, source_target_pairs={{0,8},{1,9},{2,10},{3,11},{4,12},{5,13},{6,14},{7,15},{8,0},{9,1},... | collective-permute-start | bytes 110600 | tf_op jit(solution)/shard_map/ppermute | solution.py:328
  71.8 1.3 %collective-permute-start.30 = (f32[72,128]{1,0:T(8,128)S(1)}, f32[72,128]{1,0:T(8,128)S(1)}, u32[]{:S(2)}, u32[]{:S(2)}) collective-permute-start(f32[72,128]{1,0:T(8,128)S(1)} %add_add_fusion.own_ref), channel_id=1, source_target_pairs={{0,2},{1,3},{2,0},{3,1},{4,6},{5,7},{6,4},{7,5},{8,10},{9,11},{10,... | collective-permute-start | bytes 110600 | tf_op jit(solution)/shard_map/ppermute | solution.py:328

commit v10 on v9

--- a/solution.py
+++ b/solution.py
@@ -153,10 +153,8 @@
         edges = refs[:nz]
         ghost = split_faces(refs[nz : 4 + 2 * nz], nz)
         w_ref = refs[4 + 2 * nz]
-        if last:
-            out = refs[5 + 2 * nz :]
-        else:
-            out = split_faces(refs[5 + 2 * nz :], nz)
+        out = split_faces(refs[5 + 2 * nz :], nz)
+        half = last and halved(s, nz)
         factor = scale / 6.0
         for i in range(2):
             here = pl.ds(at_ref[i] * s.row, s.row)
@@ -178,48 +176,22 @@
                     done.append((here, flat, new))
                 for here, flat, new in done:
                     w_ref[here, :] = new
-                    if not last:
+                    if not half:
                         out["z"][i][flat, :] = new
-        if last:
-            out[0][...] = w_ref[: s.row, :]
-        else:
-            faces_of(s, at_ref, w_ref, out, with_z=False)
-
-    if last:
-        outs = [f32(s.room, s.k), f32(s.row, s.k)]
-    else:
-        outs = [f32(s.room, s.k)] + face_shapes(s, nz)
+        faces_of(s, at_ref, w_ref, out, with_z=False)
+        if half:
+            start = (1 - at_ref[6]) * (s.cells // 2) + at_ref[4]
+            out["z"][0][...] = w_ref[pl.ds(start, s.x * s.y // 2, stride=s.z), :]
+
+    outs = [f32(s.room, s.k)] + face_shapes(s, nz)
+    if last and halved(s, nz):
+        outs[5] = f32(s.x * s.y // 2, s.k)
     ins = [part, wide] + list(edge) + list(ghosts)
     return call(body, outs, ins, 4 * s.x * s.y * s.k, {0: 0})
 
 
-def last_faces(w, s, nz):
-    def body(w_ref, *out):
-        at_ref = places(s)
-        for x in range(s.x):
-            out[0][x * s.z : (x + 1) * s.z, :] = w_ref[x * s.row : x * s.row + s.z, :]
-        if halved(s, nz):
-            start = (1 - at_ref[6]) * (s.cells // 2) + at_ref[4]
-            out[1][...] = w_ref[pl.ds(start, s.x * s.y // 2, stride=s.z), :]
-        else:
-            out[1][...] = w_ref[pl.ds(0, s.x * s.y, stride=s.z), :]
-
-    outs = [f32(s.x * s.z, s.k), f32(s.x * s.y // (2 if halved(s, nz) else 1), s.k)]
-    return list(call(body, outs, [w], s.x * s.y * s.k))
-
-
 def halved(s, nz):
     return nz == 1 and s.x % 2 == 0
-
-
-def one_way(faces, s, nz):
-    got = []
-    for face, axis in zip(faces, ("gx", "gy", "gz")):
-        pairs = [(i, i - 1) for i in range(1, lax.axis_size(axis))]
-        if axis == "gz" and halved(s, nz):
-            pairs = [(0, 1), (1, 0)]
-        got.append(lax.ppermute(face, axis, pairs))
-    return got
 
 
 def exchange(faces, axes):
@@ -288,19 +260,27 @@
 def pack_terms(gram, own, w, ghosts, s, nz, cells):
     k = s.k
 
-    def body(g_ref, m_ref, w_ref, x_ref, y_ref, z_ref, mine_ref, other_ref):
+    def body(g_ref, m_ref, w_ref, *refs):
         at_ref = places(s)
-        lefts = [w_ref[s.cells - s.row : s.cells, :]]
-        tops = [w_ref[(x + 1) * s.row - s.z : (x + 1) * s.row, :] for x in range(s.x)]
-        lefts.append(jnp.concatenate(tops, axis=0))
+        ghost = split_faces(refs[: 4 + nz], nz)
+        mine_ref, other_ref = refs[4 + nz :]
+        lefts = [w_ref[pl.ds(at_ref[i] * s.row, s.row), :] for i in range(2)]
+        for i in range(2):
+            lefts += [
+                w_ref[pl.ds(x * s.row + at_ref[2 + i] * s.z, s.z), :] for x in range(s.x)
+            ]
+        rights = [g[...] for g in list(ghost["x"]) + list(ghost["y"])]
         if halved(s, nz):
             start = at_ref[6] * (s.cells // 2) + at_ref[4]
             lefts.append(w_ref[pl.ds(start, s.x * s.y // 2, stride=s.z), :])
+            rights.append(2.0 * ghost["z"][0][...])
         else:
-            lefts.append(w_ref[pl.ds(s.z - 1, s.x * s.y, stride=s.z), :])
+            for i in range(nz):
+                lefts.append(w_ref[pl.ds(at_ref[4 + i], s.x * s.y, stride=s.z), :])
+                rights.append(ghost["z"][i][...])
         left = jnp.concatenate(lefts, axis=0)
-        right = jnp.concatenate([x_ref[...], y_ref[...], z_ref[...]], axis=0)
-        m = m_ref[...] - both(transposed_dot(two(left), two(right))) * (2.0 / 6.0)
+        right = jnp.concatenate(rights, axis=0)
+        m = m_ref[...] - both(transposed_dot(two(left), two(right))) * (1.0 / 6.0)
         raw = (m + m.T) * (0.5 / cells)
         below = lax.broadcasted_iota(jnp.int32, (k, k), 0)
         along = lax.broadcasted_iota(jnp.int32, (k, k), 1)
@@ -455,7 +435,7 @@
         scale = (1.0 if before is None else 2.0) / half_value
         before = w
         w, *faces = finish(part, wide, edge, ghosts, s, nz, scale, step == DEG - 1)
-    ghosts = one_way(faces + last_faces(w, s, nz), s, nz)
+    ghosts = exchange(faces, axes)
     filtered, gram, own = gather_terms(w, wide, s)
     halves = total(*pack_terms(gram, own, w, ghosts, s, nz, cells))
     basis, projected = orthonormal(*halves, filtered, s)

time: 78.9 us -> 78.7 us (level)
  waiting for transfers between devices: 17.6 us -> 12.6 us
  starting transfers between devices: 43 us -> 47.7 us
    ppermute x20 -> x25, starting transfers between devices: 28.4 us -> 37.1 us  [exchange(): got.append(lax.ppermute(face, axis, pairs))]
    ppermute x3 -> x0, waiting for transfers between devices: 4.57 us -> none  [one_way(): got.append(lax.ppermute(face, axis, pairs))]
    ppermute x3 -> x0, starting transfers between devices: 4.13 us -> none  [one_way(): got.append(lax.ppermute(face, axis, pairs))]
    pallas_call x11 -> x10, Pallas kernels: 7.63 us -> 7.71 us  [call(): pl.pallas_call(body, out_shape=outs, in_specs=[VMEM] * len(ins), out_spec...]
    ppermute x20 -> x25, waiting for transfers between devices: 3.54 us -> 3.55 us  [exchange(): got.append(lax.ppermute(face, axis, pairs))]
  transfers between devices with their start and end apart: 31 -> 33, of which waited for: 15 -> 14; matrix products, arithmetic and copies ran while one was open for 0% -> 0% of each run, Pallas kernels for 9% -> 9%
where the time goes in v10:
time: 78.7 us; the launch traced here: 78.3 us
  starting transfers between devices  47.7 us (61%)
  Pallas kernels  15.4 us (20%)
  waiting for transfers between devices  12.6 us (16%)
  local copies, waits for them, and re-layouts  1.77 us (2%)
  between operations  0.9 us (1%)
    ppermute x25, starting transfers between devices, exchange(): got.append(lax.ppermute(face, axis, pairs))  37.1 us
    ppermute x8, starting transfers between devices, swap(): return lax.ppermute(value, axes, pairs)  10.5 us
    ppermute x8, waiting for transfers between devices, swap(): return lax.ppermute(value, axes, pairs)  9.05 us
    pallas_call x10, Pallas kernels, call(): pl.pallas_call(body, out_shape=outs, in_specs=[VMEM] * len(ins), out_spec...  7.71 us
    pallas_call x1, Pallas kernels, orthonormal(): pl.pallas_call(body, out_shape=[f32(s.cells, k), f32(k, k)], in_specs=[VM...  5.44 us
    ppermute x25, waiting for transfers between devices, exchange(): got.append(lax.ppermute(face, axis, pairs))  3.55 us
    pallas_call x1, Pallas kernels, gather_terms(): pl.pallas_call(body, out_shape=outs, in_specs=[VMEM, VMEM], out_specs=(VM...  2.2 us
    slice x1, local copies, waits for them, and re-layouts, prepare(): block[i * each * s.row:(i + 1) * each * s.row]  1.76 us
  transfers between devices with their start and end apart: 33, of which 14 were waited for; matrix products, arithmetic and copies ran while one was open for 0% of the time, Pallas kernels for 9%

profile of v10, /device:TPU:0, one launch (start us, length us, event | category | flops | bytes accessed | tf_op | source)
XLA Modules:
  0.0 78.3 jit_solution(1507718827095345199)
XLA Ops:
  0.6 1.8 %fusion = (f32[8,16,8,128]{3,2,1,0:T(8,128)S(1)}, f32[8,16,8,128]{3,2,1,0:T(8,128)S(1)}, f32[8,16,8,128]{3,2,1,0:T(8,128)S(1)}, f32[8,16,8,128]{3,2,1,0:T(8,128)S(1)}) fusion(f32[32,16,8,128]{3,2,1,0:T(8,128)} %param.2), kind=kLoop, calls=%fused_computation.2 | loop fusion | bytes 4194304 | tf_op jit(solution)/shard_map/slice | solution.py:92
  2.4 1.1 %shard_map.41 = (f32[4104,128]{1,0:T(8,128)S(1)}, f32[4104,128]{1,0:T(8,128)S(1)}, f32[128,128]{1,0:T(8,128)S(1)}, f32[128,128]{1,0:T(8,128)S(1)}, f32[256,128]{...) custom-call(f32[16,8,32]{2,1,0:T(8,128)S(1)} %bitcast.10, ...), custom_call_target="tpu_custom_call" | custom-call | flops 2097152 | bytes 7233536 | tf_op jit(solution)/shard_map/pallas_call | solution.py:20
  3.5 3.0 %collective-permute-start.4 = (f32[512,128]{1,0:T(8,128)S(1)}, f32[512,128]{1,0:T(8,128)S(1)}, u32[]{:S(2)}, u32[]{:S(2)}) collective-permute-start(f32[512,128]{1,0:T(8,128)S(1)} %get-tuple-element.48), channel_id=1, source_target_pairs={{0,1},{1,0},{2,3},{3,2},{4,5},{5,4},{6,7},{7,6},{8,9},{9,8},{10,11... | collective-permute-start | bytes 786440 | tf_op jit(solution)/shard_map/ppermute | solution.py:204
  7.2 1.6 %collective-permute-start = (f32[128,128]{1,0:T(8,128)S(1)}, f32[128,128]{1,0:T(8,128)S(1)}, u32[]{:S(2)}, u32[]{:S(2)}) collective-permute-start(f32[128,128]{1,0:T(8,128)S(1)} %get-tuple-element.44), channel_id=1, source_target_pairs={{0,8},{8,0},{16,24},{24,16},{1,9},{9,1},{17,25},{25,17},{2,10},{10... | collective-permute-start | bytes 196616 | tf_op jit(solution)/shard_map/ppermute | solution.py:204
  9.5 1.2 %shard_map.42.p_ref = f32[4104,128]{1,0:T(8,128)S(1)} custom-call(f32[4104,128]{1,0:T(8,128)S(1)} %get-tuple-element.41.w_ref.rest_0_, f32[4104,128]{1,0:T(8,128)S(1)} %get-tuple-element.42.k_ref), custom_call_target="tpu_custom_call" | custom-call | flops 6291456 | bytes 6303744 | tf_op jit(solution)/shard_map/pallas_call | solution.py:20
  10.7 0.9 %collective-permute-done.refs_1_ = f32[128,128]{1,0:T(8,128)S(1)} collective-permute-done((f32[128,128]{1,0:T(8,128)S(1)}, f32[128,128]{1,0:T(8,128)S(1)}, u32[]{:S(2)}, u32[]{:S(2)}) %collective-permute-start) | collective-permute-done | bytes 65568 | tf_op jit(solution)/shard_map/ppermute | solution.py:204
  11.6 1.3 %collective-permute-done.4.refs_5_ = f32[512,128]{1,0:T(8,128)S(1)} collective-permute-done((f32[512,128]{1,0:T(8,128)S(1)}, f32[512,128]{1,0:T(8,128)S(1)}, u32[]{:S(2)}, u32[]{:S(2)}) %collective-permute-start.4) | collective-permute-done | bytes 262176 | tf_op jit(solution)/shard_map/ppermute | solution.py:204
  13.1 1.8 %collective-permute-start.9 = (f32[512,128]{1,0:T(8,128)S(1)}, f32[512,128]{1,0:T(8,128)S(1)}, u32[]{:S(2)}, u32[]{:S(2)}) collective-permute-start(f32[512,128]{1,0:T(8,128)S(1)} %get-tuple-element.54), channel_id=1, source_target_pairs={{0,1},{1,0},{2,3},{3,2},{4,5},{5,4},{6,7},{7,6},{8,9},{9,8},{10,11... | collective-permute-start | bytes 786440 | tf_op jit(solution)/shard_map/ppermute | solution.py:204
  15.6 3.6 %collective-permute-start.5 = (f32[128,128]{1,0:T(8,128)S(1)}, f32[128,128]{1,0:T(8,128)S(1)}, u32[]{:S(2)}, u32[]{:S(2)}) collective-permute-start(f32[128,128]{1,0:T(8,128)S(1)} %get-tuple-element.50), channel_id=1, source_target_pairs={{0,8},{8,0},{16,24},{24,16},{1,9},{9,1},{17,25},{25,17},{2,10},{10... | collective-permute-start | bytes 196616 | tf_op jit(solution)/shard_map/ppermute | solution.py:204
  19.9 1.2 %shard_map.44.p_ref = f32[4104,128]{1,0:T(8,128)S(1)} custom-call(f32[4104,128]{1,0:T(8,128)S(1)} %get-tuple-element.49.w_ref.rest_0_, f32[4104,128]{1,0:T(8,128)S(1)} %get-tuple-element.42.k_ref, f32[4104,128]{1,0:T(8,128)S(1)} %get-tuple-element.41.w_ref.rest_0_), custom_call_target="tpu_custom_call" | custom-call | flops 6291456 | bytes 8404992 | tf_op jit(solution)/shard_map/pallas_call | solution.py:20
  22.2 1.2 %collective-permute-start.14 = (f32[512,128]{1,0:T(8,128)S(1)}, f32[512,128]{1,0:T(8,128)S(1)}, u32[]{:S(2)}, u32[]{:S(2)}) collective-permute-start(f32[512,128]{1,0:T(8,128)S(1)} %get-tuple-element.60), channel_id=1, source_target_pairs={{0,1},{1,0},{2,3},{3,2},{4,5},{5,4},{6,7},{7,6},{8,9},{9,8},{10,11... | collective-permute-start | bytes 786440 | tf_op jit(solution)/shard_map/ppermute | solution.py:204
  23.4 2.4 %collective-permute-start.12 = (f32[256,128]{1,0:T(8,128)S(1)}, f32[256,128]{1,0:T(8,128)S(1)}, u32[]{:S(2)}, u32[]{:S(2)}) collective-permute-start(f32[256,128]{1,0:T(8,128)S(1)} %get-tuple-element.58), channel_id=1, source_target_pairs={{0,2},{2,0},{4,6},{6,4},{1,3},{3,1},{5,7},{7,5},{8,10},{10,8},{12,... | collective-permute-start | bytes 393224 | tf_op jit(solution)/shard_map/ppermute | solution.py:204
  26.4 3.7 %collective-permute-start.10 = (f32[128,128]{1,0:T(8,128)S(1)}, f32[128,128]{1,0:T(8,128)S(1)}, u32[]{:S(2)}, u32[]{:S(2)}) collective-permute-start(f32[128,128]{1,0:T(8,128)S(1)} %get-tuple-element.56), channel_id=1, source_target_pairs={{0,8},{8,0},{16,24},{24,16},{1,9},{9,1},{17,25},{25,17},{2,10},{10... | collective-permute-start | bytes 196616 | tf_op jit(solution)/shard_map/ppermute | solution.py:204
  30.8 1.4 %shard_map.46.p_ref = f32[4104,128]{1,0:T(8,128)S(1)} custom-call(f32[4104,128]{1,0:T(8,128)S(1)} %get-tuple-element.55.w_ref.rest_0_, f32[4104,128]{1,0:T(8,128)S(1)} %get-tuple-element.42.k_ref, f32[4104,128]{1,0:T(8,128)S(1)} %get-tuple-element.49.w_ref.rest_0_), custom_call_target="tpu_custom_call" | custom-call | flops 6291456 | bytes 8404992 | tf_op jit(solution)/shard_map/pallas_call | solution.py:20
  33.3 1.6 %collective-permute-start.17 = (f32[256,128]{1,0:T(8,128)S(1)}, f32[256,128]{1,0:T(8,128)S(1)}, u32[]{:S(2)}, u32[]{:S(2)}) collective-permute-start(f32[256,128]{1,0:T(8,128)S(1)} %get-tuple-element.64), channel_id=1, source_target_pairs={{0,2},{2,0},{4,6},{6,4},{1,3},{3,1},{5,7},{7,5},{8,10},{10,8},{12,... | collective-permute-start | bytes 393224 | tf_op jit(solution)/shard_map/ppermute | solution.py:204
  35.6 3.6 %collective-permute-start.15 = (f32[128,128]{1,0:T(8,128)S(1)}, f32[128,128]{1,0:T(8,128)S(1)}, u32[]{:S(2)}, u32[]{:S(2)}) collective-permute-start(f32[128,128]{1,0:T(8,128)S(1)} %get-tuple-element.62), channel_id=1, source_target_pairs={{0,8},{8,0},{16,24},{24,16},{1,9},{9,1},{17,25},{25,17},{2,10},{10... | collective-permute-start | bytes 196616 | tf_op jit(solution)/shard_map/ppermute | solution.py:204
  39.9 1.2 %shard_map.48.p_ref = f32[4104,128]{1,0:T(8,128)S(1)} custom-call(f32[4104,128]{1,0:T(8,128)S(1)} %get-tuple-element.61.w_ref, f32[4104,128]{1,0:T(8,128)S(1)} %get-tuple-element.42.k_ref, f32[4104,128]{1,0:T(8,128)S(1)} %get-tuple-element.55.w_ref.rest_0_), custom_call_target="tpu_custom_call" | custom-call | flops 6291456 | bytes 8404992 | tf_op jit(solution)/shard_map/pallas_call | solution.py:20
  41.8 2.4 %collective-permute-start.22 = (f32[256,128]{1,0:T(8,128)S(1)}, f32[256,128]{1,0:T(8,128)S(1)}, u32[]{:S(2)}, u32[]{:S(2)}) collective-permute-start(f32[256,128]{1,0:T(8,128)S(1)} %get-tuple-element.72), channel_id=1, source_target_pairs={{0,2},{2,0},{4,6},{6,4},{1,3},{3,1},{5,7},{7,5},{8,10},{10,8},{12,... | collective-permute-start | bytes 393224 | tf_op jit(solution)/shard_map/ppermute | solution.py:204
  44.9 1.6 %collective-permute-start.24 = (f32[256,128]{1,0:T(8,128)S(1)}, f32[256,128]{1,0:T(8,128)S(1)}, u32[]{:S(2)}, u32[]{:S(2)}) collective-permute-start(f32[256,128]{1,0:T(8,128)S(1)} %get-tuple-element.74), channel_id=1, source_target_pairs={{0,1},{1,0},{2,3},{3,2},{4,5},{5,4},{6,7},{7,6},{8,9},{9,8},{10,11... | collective-permute-start | bytes 393224 | tf_op jit(solution)/shard_map/ppermute | solution.py:204
  46.5 3.4 %collective-permute-start.20 = (f32[128,128]{1,0:T(8,128)S(1)}, f32[128,128]{1,0:T(8,128)S(1)}, u32[]{:S(2)}, u32[]{:S(2)}) collective-permute-start(f32[128,128]{1,0:T(8,128)S(1)} %get-tuple-element.70), channel_id=1, source_target_pairs={{0,8},{8,0},{16,24},{24,16},{1,9},{9,1},{17,25},{25,17},{2,10},{10... | collective-permute-start | bytes 196616 | tf_op jit(solution)/shard_map/ppermute | solution.py:204
  50.5 2.2 %shard_map.50 = (bf16[4096,256]{1,0:T(8,128)(2,1)S(1)}, f32[128,128]{1,0:T(8,128)S(1)}, f32[128,128]{1,0:T(8,128)S(1)}) custom-call(f32[4104,128]{1,0:T(8,128)S(1)} %get-tuple-element.67.w_ref, f32[4104,128]{1,0:T(8,128)S(1)} %get-tuple-element.42.k_ref), custom_call_target="tpu_custom_call" | custom-call | flops 1073741824 | bytes 8388608 | tf_op jit(solution)/shard_map/pallas_call | solution.py:247
  53.2 1.9 %collective-permute-start.25 = (f32[72,128]{1,0:T(8,128)S(1)}, f32[72,128]{1,0:T(8,128)S(1)}, u32[]{:S(2)}, u32[]{:S(2)}) collective-permute-start(f32[72,128]{1,0:T(8,128)S(1)} %get-tuple-element.76), channel_id=1, source_target_pairs={{0,2},{1,3},{2,0},{3,1},{4,6},{5,7},{6,4},{7,5},{8,10},{9,11},{10,... | collective-permute-start | bytes 110600 | tf_op jit(solution)/shard_map/ppermute | solution.py:308
  56.0 1.4 %collective-permute-start.28 = (f32[72,128]{1,0:T(8,128)S(1)}, f32[72,128]{1,0:T(8,128)S(1)}, u32[]{:S(2)}, u32[]{:S(2)}) collective-permute-start(f32[72,128]{1,0:T(8,128)S(1)} %add.21), channel_id=1, source_target_pairs={{0,5},{1,4},{2,7},{3,6},{4,1},{5,0},{6,3},{7,2},{8,13},{9,12},{10,... | collective-permute-start | bytes 110600 | tf_op jit(solution)/shard_map/ppermute | solution.py:308
  57.4 1.5 %collective-permute-start.27 = (f32[72,128]{1,0:T(8,128)S(1)}, f32[72,128]{1,0:T(8,128)S(1)}, u32[]{:S(2)}, u32[]{:S(2)}) collective-permute-start(f32[72,128]{1,0:T(8,128)S(1)} %add.21), channel_id=1, source_target_pairs={{0,1},{1,0},{2,3},{3,2},{4,5},{5,4},{6,7},{7,6},{8,9},{9,8},{10,11... | collective-permute-start | bytes 110600 | tf_op jit(solution)/shard_map/ppermute | solution.py:308
  59.5 1.5 %collective-permute-done.28 = f32[72,128]{1,0:T(8,128)S(1)} collective-permute-done((f32[72,128]{1,0:T(8,128)S(1)}, f32[72,128]{1,0:T(8,128)S(1)}, u32[]{:S(2)}, u32[]{:S(2)}) %collective-permute-start.28) | collective-permute-done | bytes 36896 | tf_op jit(solution)/shard_map/ppermute | solution.py:308
  61.3 1.5 %collective-permute-done.26 = f32[72,128]{1,0:T(8,128)S(1)} collective-permute-done((f32[72,128]{1,0:T(8,128)S(1)}, f32[72,128]{1,0:T(8,128)S(1)}, u32[]{:S(2)}, u32[]{:S(2)}) %collective-permute-start.26) | collective-permute-done | bytes 36896 | tf_op jit(solution)/shard_map/ppermute | solution.py:308
  62.8 2.7 %collective-permute-start.31 = (f32[72,128]{1,0:T(8,128)S(1)}, f32[72,128]{1,0:T(8,128)S(1)}, u32[]{:S(2)}, u32[]{:S(2)}) collective-permute-start(f32[72,128]{1,0:T(8,128)S(1)} %add_add_fusion.1), channel_id=1, source_target_pairs={{0,24},{1,25},{2,26},{3,27},{4,28},{5,29},{6,30},{7,31},{8,16},{9,... | collective-permute-start | bytes 110600 | tf_op jit(solution)/shard_map/ppermute | solution.py:308
  65.5 2.1 %collective-permute-start.30 = (f32[72,128]{1,0:T(8,128)S(1)}, f32[72,128]{1,0:T(8,128)S(1)}, u32[]{:S(2)}, u32[]{:S(2)}) collective-permute-start(f32[72,128]{1,0:T(8,128)S(1)} %add_add_fusion.1), channel_id=1, source_target_pairs={{0,16},{1,17},{2,18},{3,19},{4,20},{5,21},{6,22},{7,23},{8,24},{9,... | collective-permute-start | bytes 110600 | tf_op jit(solution)/shard_map/ppermute | solution.py:308
  68.7 1.7 %collective-permute-done.30 = f32[72,128]{1,0:T(8,128)S(1)} collective-permute-done((f32[72,128]{1,0:T(8,128)S(1)}, f32[72,128]{1,0:T(8,128)S(1)}, u32[]{:S(2)}, u32[]{:S(2)}) %collective-permute-start.30) | collective-permute-done | bytes 36896 | tf_op jit(solution)/shard_map/ppermute | solution.py:308
  70.4 1.2 %collective-permute-done.29 = f32[72,128]{1,0:T(8,128)S(1)} collective-permute-done((f32[72,128]{1,0:T(8,128)S(1)}, f32[72,128]{1,0:T(8,128)S(1)}, u32[]{:S(2)}, u32[]{:S(2)}) %collective-permute-start.29) | collective-permute-done | bytes 36896 | tf_op jit(solution)/shard_map/ppermute | solution.py:308
  71.7 1.2 %collective-permute-done.32.got_ref = f32[72,128]{1,0:T(8,128)S(1)} collective-permute-done((f32[72,128]{1,0:T(8,128)S(1)}, f32[72,128]{1,0:T(8,128)S(1)}, u32[]{:S(2)}, u32[]{:S(2)}) %collective-permute-start.32) | collective-permute-done | bytes 36896 | tf_op jit(solution)/shard_map/ppermute | solution.py:308
  72.9 5.4 %shard_map.52 = (f32[4096,128]{1,0:T(8,128)}, f32[128,128]{1,0:T(8,128)}) custom-call(f32[72,128]{1,0:T(8,128)S(1)} %add_add_fusion.own_ref, f32[72,128]{1,0:T(8,128)S(1)} %collective-permute-done.32.got_ref, bf16[4096,256]{1,0:T(8,128)(2,1)S(1)} %get-tuple-element.77.f_ref), custom_call_target="tpu_custom_call" | custom-call | flops 536870912 | bytes 4194304 | tf_op jit(solution)/shard_map/pallas_call | solution.py:403
  (52 shorter events, 13.1 us)
Async XLA Ops:
  3.5 9.3 %collective-permute-start.4 = (f32[512,128]{1,0:T(8,128)S(1)}, f32[512,128]{1,0:T(8,128)S(1)}, u32[]{:S(2)}, u32[]{:S(2)}) collective-permute-start(f32[512,128]{1,0:T(8,128)S(1)} %get-tuple-element.48), channel_id=1, source_target_pairs={{0,1},{1,0},{2,3},{3,2},{4,5},{5,4},{6,7},{7,6},{8,9},{9,8},{10,11... | collective-permute-start | bytes 786440 | tf_op jit(solution)/shard_map/ppermute | solution.py:204
  6.5 5.0 %collective-permute-start.2 = (f32[256,128]{1,0:T(8,128)S(1)}, f32[256,128]{1,0:T(8,128)S(1)}, u32[]{:S(2)}, u32[]{:S(2)}) collective-permute-start(f32[256,128]{1,0:T(8,128)S(1)} %get-tuple-element.46), channel_id=1, source_target_pairs={{0,2},{2,0},{4,6},{6,4},{1,3},{3,1},{5,7},{7,5},{8,10},{10,8},{12,... | collective-permute-start | bytes 393224 | tf_op jit(solution)/shard_map/ppermute | solution.py:204
  6.5 5.0 %collective-permute-start.3 = (f32[256,128]{1,0:T(8,128)S(1)}, f32[256,128]{1,0:T(8,128)S(1)}, u32[]{:S(2)}, u32[]{:S(2)}) collective-permute-start(f32[256,128]{1,0:T(8,128)S(1)} %get-tuple-element.47), channel_id=1, source_target_pairs={{2,4},{4,2},{3,5},{5,3},{10,12},{12,10},{11,13},{13,11},{18,20},{2... | collective-permute-start | bytes 393224 | tf_op jit(solution)/shard_map/ppermute | solution.py:204
  7.2 4.3 %collective-permute-start = (f32[128,128]{1,0:T(8,128)S(1)}, f32[128,128]{1,0:T(8,128)S(1)}, u32[]{:S(2)}, u32[]{:S(2)}) collective-permute-start(f32[128,128]{1,0:T(8,128)S(1)} %get-tuple-element.44), channel_id=1, source_target_pairs={{0,8},{8,0},{16,24},{24,16},{1,9},{9,1},{17,25},{25,17},{2,10},{10... | collective-permute-start | bytes 196616 | tf_op jit(solution)/shard_map/ppermute | solution.py:204
  8.9 2.7 %collective-permute-start.1 = (f32[128,128]{1,0:T(8,128)S(1)}, f32[128,128]{1,0:T(8,128)S(1)}, u32[]{:S(2)}, u32[]{:S(2)}) collective-permute-start(f32[128,128]{1,0:T(8,128)S(1)} %get-tuple-element.45), channel_id=1, source_target_pairs={{8,16},{16,8},{9,17},{17,9},{10,18},{18,10},{11,19},{19,11},{12,20... | collective-permute-start | bytes 196616 | tf_op jit(solution)/shard_map/ppermute | solution.py:204
  13.1 8.8 %collective-permute-start.9 = (f32[512,128]{1,0:T(8,128)S(1)}, f32[512,128]{1,0:T(8,128)S(1)}, u32[]{:S(2)}, u32[]{:S(2)}) collective-permute-start(f32[512,128]{1,0:T(8,128)S(1)} %get-tuple-element.54), channel_id=1, source_target_pairs={{0,1},{1,0},{2,3},{3,2},{4,5},{5,4},{6,7},{7,6},{8,9},{9,8},{10,11... | collective-permute-start | bytes 786440 | tf_op jit(solution)/shard_map/ppermute | solution.py:204
  14.9 6.5 %collective-permute-start.7 = (f32[256,128]{1,0:T(8,128)S(1)}, f32[256,128]{1,0:T(8,128)S(1)}, u32[]{:S(2)}, u32[]{:S(2)}) collective-permute-start(f32[256,128]{1,0:T(8,128)S(1)} %get-tuple-element.52), channel_id=1, source_target_pairs={{0,2},{2,0},{4,6},{6,4},{1,3},{3,1},{5,7},{7,5},{8,10},{10,8},{12,... | collective-permute-start | bytes 393224 | tf_op jit(solution)/shard_map/ppermute | solution.py:204
  14.9 6.5 %collective-permute-start.8 = (f32[256,128]{1,0:T(8,128)S(1)}, f32[256,128]{1,0:T(8,128)S(1)}, u32[]{:S(2)}, u32[]{:S(2)}) collective-permute-start(f32[256,128]{1,0:T(8,128)S(1)} %get-tuple-element.53), channel_id=1, source_target_pairs={{2,4},{4,2},{3,5},{5,3},{10,12},{12,10},{11,13},{13,11},{18,20},{2... | collective-permute-start | bytes 393224 | tf_op jit(solution)/shard_map/ppermute | solution.py:204
  15.6 5.9 %collective-permute-start.5 = (f32[128,128]{1,0:T(8,128)S(1)}, f32[128,128]{1,0:T(8,128)S(1)}, u32[]{:S(2)}, u32[]{:S(2)}) collective-permute-start(f32[128,128]{1,0:T(8,128)S(1)} %get-tuple-element.50), channel_id=1, source_target_pairs={{0,8},{8,0},{16,24},{24,16},{1,9},{9,1},{17,25},{25,17},{2,10},{10... | collective-permute-start | bytes 196616 | tf_op jit(solution)/shard_map/ppermute | solution.py:204
  19.2 2.2 %collective-permute-start.6 = (f32[128,128]{1,0:T(8,128)S(1)}, f32[128,128]{1,0:T(8,128)S(1)}, u32[]{:S(2)}, u32[]{:S(2)}) collective-permute-start(f32[128,128]{1,0:T(8,128)S(1)} %get-tuple-element.51), channel_id=1, source_target_pairs={{8,16},{16,8},{9,17},{17,9},{10,18},{18,10},{11,19},{19,11},{12,20... | collective-permute-start | bytes 196616 | tf_op jit(solution)/shard_map/ppermute | solution.py:204
  22.2 10.2 %collective-permute-start.14 = (f32[512,128]{1,0:T(8,128)S(1)}, f32[512,128]{1,0:T(8,128)S(1)}, u32[]{:S(2)}, u32[]{:S(2)}) collective-permute-start(f32[512,128]{1,0:T(8,128)S(1)} %get-tuple-element.60), channel_id=1, source_target_pairs={{0,1},{1,0},{2,3},{3,2},{4,5},{5,4},{6,7},{7,6},{8,9},{9,8},{10,11... | collective-permute-start | bytes 786440 | tf_op jit(solution)/shard_map/ppermute | solution.py:204
  23.4 9.0 %collective-permute-start.12 = (f32[256,128]{1,0:T(8,128)S(1)}, f32[256,128]{1,0:T(8,128)S(1)}, u32[]{:S(2)}, u32[]{:S(2)}) collective-permute-start(f32[256,128]{1,0:T(8,128)S(1)} %get-tuple-element.58), channel_id=1, source_target_pairs={{0,2},{2,0},{4,6},{6,4},{1,3},{3,1},{5,7},{7,5},{8,10},{10,8},{12,... | collective-permute-start | bytes 393224 | tf_op jit(solution)/shard_map/ppermute | solution.py:204
  25.8 6.6 %collective-permute-start.13 = (f32[256,128]{1,0:T(8,128)S(1)}, f32[256,128]{1,0:T(8,128)S(1)}, u32[]{:S(2)}, u32[]{:S(2)}) collective-permute-start(f32[256,128]{1,0:T(8,128)S(1)} %get-tuple-element.59), channel_id=1, source_target_pairs={{2,4},{4,2},{3,5},{5,3},{10,12},{12,10},{11,13},{13,11},{18,20},{2... | collective-permute-start | bytes 393224 | tf_op jit(solution)/shard_map/ppermute | solution.py:204
  26.4 5.9 %collective-permute-start.10 = (f32[128,128]{1,0:T(8,128)S(1)}, f32[128,128]{1,0:T(8,128)S(1)}, u32[]{:S(2)}, u32[]{:S(2)}) collective-permute-start(f32[128,128]{1,0:T(8,128)S(1)} %get-tuple-element.56), channel_id=1, source_target_pairs={{0,8},{8,0},{16,24},{24,16},{1,9},{9,1},{17,25},{25,17},{2,10},{10... | collective-permute-start | bytes 196616 | tf_op jit(solution)/shard_map/ppermute | solution.py:204
  30.2 2.2 %collective-permute-start.11 = (f32[128,128]{1,0:T(8,128)S(1)}, f32[128,128]{1,0:T(8,128)S(1)}, u32[]{:S(2)}, u32[]{:S(2)}) collective-permute-start(f32[128,128]{1,0:T(8,128)S(1)} %get-tuple-element.57), channel_id=1, source_target_pairs={{8,16},{16,8},{9,17},{17,9},{10,18},{18,10},{11,19},{19,11},{12,20... | collective-permute-start | bytes 196616 | tf_op jit(solution)/shard_map/ppermute | solution.py:204
  32.7 8.8 %collective-permute-start.19 = (f32[512,128]{1,0:T(8,128)S(1)}, f32[512,128]{1,0:T(8,128)S(1)}, u32[]{:S(2)}, u32[]{:S(2)}) collective-permute-start(f32[512,128]{1,0:T(8,128)S(1)} %get-tuple-element.66), channel_id=1, source_target_pairs={{0,1},{1,0},{2,3},{3,2},{4,5},{5,4},{6,7},{7,6},{8,9},{9,8},{10,11... | collective-permute-start | bytes 786440 | tf_op jit(solution)/shard_map/ppermute | solution.py:204
  33.3 8.2 %collective-permute-start.17 = (f32[256,128]{1,0:T(8,128)S(1)}, f32[256,128]{1,0:T(8,128)S(1)}, u32[]{:S(2)}, u32[]{:S(2)}) collective-permute-start(f32[256,128]{1,0:T(8,128)S(1)} %get-tuple-element.64), channel_id=1, source_target_pairs={{0,2},{2,0},{4,6},{6,4},{1,3},{3,1},{5,7},{7,5},{8,10},{10,8},{12,... | collective-permute-start | bytes 393224 | tf_op jit(solution)/shard_map/ppermute | solution.py:204
  35.0 6.5 %collective-permute-start.18 = (f32[256,128]{1,0:T(8,128)S(1)}, f32[256,128]{1,0:T(8,128)S(1)}, u32[]{:S(2)}, u32[]{:S(2)}) collective-permute-start(f32[256,128]{1,0:T(8,128)S(1)} %get-tuple-element.65), channel_id=1, source_target_pairs={{2,4},{4,2},{3,5},{5,3},{10,12},{12,10},{11,13},{13,11},{18,20},{2... | collective-permute-start | bytes 393224 | tf_op jit(solution)/shard_map/ppermute | solution.py:204
  35.6 5.8 %collective-permute-start.15 = (f32[128,128]{1,0:T(8,128)S(1)}, f32[128,128]{1,0:T(8,128)S(1)}, u32[]{:S(2)}, u32[]{:S(2)}) collective-permute-start(f32[128,128]{1,0:T(8,128)S(1)} %get-tuple-element.62), channel_id=1, source_target_pairs={{0,8},{8,0},{16,24},{24,16},{1,9},{9,1},{17,25},{25,17},{2,10},{10... | collective-permute-start | bytes 196616 | tf_op jit(solution)/shard_map/ppermute | solution.py:204
  39.2 2.2 %collective-permute-start.16 = (f32[128,128]{1,0:T(8,128)S(1)}, f32[128,128]{1,0:T(8,128)S(1)}, u32[]{:S(2)}, u32[]{:S(2)}) collective-permute-start(f32[128,128]{1,0:T(8,128)S(1)} %get-tuple-element.63), channel_id=1, source_target_pairs={{8,16},{16,8},{9,17},{17,9},{10,18},{18,10},{11,19},{19,11},{12,20... | collective-permute-start | bytes 196616 | tf_op jit(solution)/shard_map/ppermute | solution.py:204
  41.8 10.9 %collective-permute-start.22 = (f32[256,128]{1,0:T(8,128)S(1)}, f32[256,128]{1,0:T(8,128)S(1)}, u32[]{:S(2)}, u32[]{:S(2)}) collective-permute-start(f32[256,128]{1,0:T(8,128)S(1)} %get-tuple-element.72), channel_id=1, source_target_pairs={{0,2},{2,0},{4,6},{6,4},{1,3},{3,1},{5,7},{7,5},{8,10},{10,8},{12,... | collective-permute-start | bytes 393224 | tf_op jit(solution)/shard_map/ppermute | solution.py:204
  44.2 8.5 %collective-permute-start.23 = (f32[256,128]{1,0:T(8,128)S(1)}, f32[256,128]{1,0:T(8,128)S(1)}, u32[]{:S(2)}, u32[]{:S(2)}) collective-permute-start(f32[256,128]{1,0:T(8,128)S(1)} %get-tuple-element.73), channel_id=1, source_target_pairs={{2,4},{4,2},{3,5},{5,3},{10,12},{12,10},{11,13},{13,11},{18,20},{2... | collective-permute-start | bytes 393224 | tf_op jit(solution)/shard_map/ppermute | solution.py:204
  44.9 7.8 %collective-permute-start.24 = (f32[256,128]{1,0:T(8,128)S(1)}, f32[256,128]{1,0:T(8,128)S(1)}, u32[]{:S(2)}, u32[]{:S(2)}) collective-permute-start(f32[256,128]{1,0:T(8,128)S(1)} %get-tuple-element.74), channel_id=1, source_target_pairs={{0,1},{1,0},{2,3},{3,2},{4,5},{5,4},{6,7},{7,6},{8,9},{9,8},{10,11... | collective-permute-start | bytes 393224 | tf_op jit(solution)/shard_map/ppermute | solution.py:204
  46.5 6.2 %collective-permute-start.20 = (f32[128,128]{1,0:T(8,128)S(1)}, f32[128,128]{1,0:T(8,128)S(1)}, u32[]{:S(2)}, u32[]{:S(2)}) collective-permute-start(f32[128,128]{1,0:T(8,128)S(1)} %get-tuple-element.70), channel_id=1, source_target_pairs={{0,8},{8,0},{16,24},{24,16},{1,9},{9,1},{17,25},{25,17},{2,10},{10... | collective-permute-start | bytes 196616 | tf_op jit(solution)/shard_map/ppermute | solution.py:204
  49.8 2.9 %collective-permute-start.21 = (f32[128,128]{1,0:T(8,128)S(1)}, f32[128,128]{1,0:T(8,128)S(1)}, u32[]{:S(2)}, u32[]{:S(2)}) collective-permute-start(f32[128,128]{1,0:T(8,128)S(1)} %get-tuple-element.71), channel_id=1, source_target_pairs={{8,16},{16,8},{9,17},{17,9},{10,18},{18,10},{11,19},{19,11},{12,20... | collective-permute-start | bytes 196616 | tf_op jit(solution)/shard_map/ppermute | solution.py:204
  53.2 2.8 %collective-permute-start.25 = (f32[72,128]{1,0:T(8,128)S(1)}, f32[72,128]{1,0:T(8,128)S(1)}, u32[]{:S(2)}, u32[]{:S(2)}) collective-permute-start(f32[72,128]{1,0:T(8,128)S(1)} %get-tuple-element.76), channel_id=1, source_target_pairs={{0,2},{1,3},{2,0},{3,1},{4,6},{5,7},{6,4},{7,5},{8,10},{9,11},{10,... | collective-permute-start | bytes 110600 | tf_op jit(solution)/shard_map/ppermute | solution.py:308
  56.0 5.0 %collective-permute-start.28 = (f32[72,128]{1,0:T(8,128)S(1)}, f32[72,128]{1,0:T(8,128)S(1)}, u32[]{:S(2)}, u32[]{:S(2)}) collective-permute-start(f32[72,128]{1,0:T(8,128)S(1)} %add.21), channel_id=1, source_target_pairs={{0,5},{1,4},{2,7},{3,6},{4,1},{5,0},{6,3},{7,2},{8,13},{9,12},{10,... | collective-permute-start | bytes 110600 | tf_op jit(solution)/shard_map/ppermute | solution.py:308
  57.4 4.0 %collective-permute-start.27 = (f32[72,128]{1,0:T(8,128)S(1)}, f32[72,128]{1,0:T(8,128)S(1)}, u32[]{:S(2)}, u32[]{:S(2)}) collective-permute-start(f32[72,128]{1,0:T(8,128)S(1)} %add.21), channel_id=1, source_target_pairs={{0,1},{1,0},{2,3},{3,2},{4,5},{5,4},{6,7},{7,6},{8,9},{9,8},{10,11... | collective-permute-start | bytes 110600 | tf_op jit(solution)/shard_map/ppermute | solution.py:308
  58.8 4.0 %collective-permute-start.26 = (f32[72,128]{1,0:T(8,128)S(1)}, f32[72,128]{1,0:T(8,128)S(1)}, u32[]{:S(2)}, u32[]{:S(2)}) collective-permute-start(f32[72,128]{1,0:T(8,128)S(1)} %add.21), channel_id=1, source_target_pairs={{0,4},{1,5},{2,6},{3,7},{4,0},{5,1},{6,2},{7,3},{8,12},{9,13},{10,... | collective-permute-start | bytes 110600 | tf_op jit(solution)/shard_map/ppermute | solution.py:308
  62.8 5.8 %collective-permute-start.31 = (f32[72,128]{1,0:T(8,128)S(1)}, f32[72,128]{1,0:T(8,128)S(1)}, u32[]{:S(2)}, u32[]{:S(2)}) collective-permute-start(f32[72,128]{1,0:T(8,128)S(1)} %add_add_fusion.1), channel_id=1, source_target_pairs={{0,24},{1,25},{2,26},{3,27},{4,28},{5,29},{6,30},{7,31},{8,16},{9,... | collective-permute-start | bytes 110600 | tf_op jit(solution)/shard_map/ppermute | solution.py:308
  65.5 4.9 %collective-permute-start.30 = (f32[72,128]{1,0:T(8,128)S(1)}, f32[72,128]{1,0:T(8,128)S(1)}, u32[]{:S(2)}, u32[]{:S(2)}) collective-permute-start(f32[72,128]{1,0:T(8,128)S(1)} %add_add_fusion.1), channel_id=1, source_target_pairs={{0,16},{1,17},{2,18},{3,19},{4,20},{5,21},{6,22},{7,23},{8,24},{9,... | collective-permute-start | bytes 110600 | tf_op jit(solution)/shard_map/ppermute | solution.py:308
  67.6 4.0 %collective-permute-start.29 = (f32[72,128]{1,0:T(8,128)S(1)}, f32[72,128]{1,0:T(8,128)S(1)}, u32[]{:S(2)}, u32[]{:S(2)}) collective-permute-start(f32[72,128]{1,0:T(8,128)S(1)} %add_add_fusion.1), channel_id=1, source_target_pairs={{0,8},{1,9},{2,10},{3,11},{4,12},{5,13},{6,14},{7,15},{8,0},{9,1},... | collective-permute-start | bytes 110600 | tf_op jit(solution)/shard_map/ppermute | solution.py:308
  (2 other events, 3.1 us)

commit v11 on v10

--- a/solution.py
+++ b/solution.py
@@ -263,7 +263,7 @@
     def body(g_ref, m_ref, w_ref, *refs):
         at_ref = places(s)
         ghost = split_faces(refs[: 4 + nz], nz)
-        mine_ref, other_ref = refs[4 + nz :]
+        p_ref = refs[4 + nz]
         lefts = [w_ref[pl.ds(at_ref[i] * s.row, s.row), :] for i in range(2)]
         for i in range(2):
             lefts += [
@@ -286,16 +286,14 @@
         along = lax.broadcasted_iota(jnp.int32, (k, k), 1)
         full = jnp.where(below >= along, g_ref[...] * (1.0 / cells), raw)
         diagonal = jnp.sum(jnp.where(below == along, raw, 0.0), axis=0, keepdims=True)
-        even = at_ref[7] == 0
-        for ref, first in ((mine_ref, even), (other_ref, jnp.logical_not(even))):
-            ref[: k // 2, :] = jnp.where(first, full[: k // 2, :], full[k // 2 :, :])
-            ref[k // 2 :, :] = jnp.broadcast_to(diagonal, (8, k))
+        p_ref[:k, :] = full
+        p_ref[k:, :] = jnp.broadcast_to(diagonal, (8, k))
 
     ins = [gram, own, w] + list(ghosts)
-    return call(body, [f32(k // 2 + 8, k)] * 2, ins, 6 * s.cells * k)
-
-
-def total(mine, other):
+    return call(body, [f32(k + 8, k)], ins, 6 * s.cells * k)[0]
+
+
+def total(mine):
     axes = ("gx", "gy", "gz")
     sizes = [lax.axis_size(a) for a in axes]
 
@@ -314,7 +312,7 @@
             hops.append(tuple(bit if e == d else 0 for e in range(3)))
             bit *= 2
     pair = (0, 1, 0)
-    value = mine + swap(other, pair)
+    value = mine + swap(mine, pair)
     while hops:
         a, *hops = hops
         if hops:
@@ -323,7 +321,7 @@
             value = (value + swap(value, a)) + (swap(value, b) + swap(value, c))
         else:
             value = value + swap(value, a)
-    return value, swap(value, pair)
+    return value
 
 
 PANEL = 64
@@ -362,18 +360,13 @@
             m_ref[top + PANEL :, :] = m_ref[top + PANEL :, :] - update[top + PANEL :, :]
 
 
-def orthonormal(own, got, filtered, s):
+def orthonormal(packed, filtered, s):
     k = s.k
     parts = 8
     rows = s.cells // parts
 
-    def body(own_ref, got_ref, f_ref, b_hbm, o_ref, m_ref, b_ref, sems):
-        even = places(s)[7] == 0
-        one, other = own_ref[: k // 2, :], got_ref[: k // 2, :]
-        upper = jnp.concatenate(
-            [jnp.where(even, one, other), jnp.where(even, other, one)], axis=0
-        )
-        low, high = own_ref[k // 2 : k // 2 + 1, :], got_ref[k // 2 : k // 2 + 1, :]
+    def body(p_ref, f_ref, b_hbm, o_ref, m_ref, b_ref, sems):
+        upper = p_ref[:k, :]
         turned = upper.T
         below = lax.broadcasted_iota(jnp.int32, (k, k), 0)
         along = lax.broadcasted_iota(jnp.int32, (k, k), 1)
@@ -391,7 +384,7 @@
             copies.append(pltpu.make_async_copy(b_ref.at[here], b_hbm.at[here], sems.at[i]))
             copies[-1].start()
         raw = jnp.where(below < along, upper, turned)
-        raw = jnp.where(below == along, jnp.where(even, low, high), raw)
+        raw = jnp.where(below == along, p_ref[k : k + 1, :], raw)
         half = jnp.dot(inverse, raw, precision=HIGH, preferred_element_type=jnp.float32)
         o_ref[...] = lax.dot_general(
             half, inverse, (((1,), (1,)), ((), ())),
@@ -403,7 +396,7 @@
     return pl.pallas_call(
         body,
         out_shape=[f32(s.cells, k), f32(k, k)],
-        in_specs=[VMEM, VMEM, VMEM],
+        in_specs=[VMEM, VMEM],
         out_specs=(pl.BlockSpec(memory_space=pl.ANY), VMEM),
         scratch_shapes=[
             pltpu.VMEM((k, 2 * k), jnp.float32),
@@ -414,7 +407,7 @@
         cost_estimate=pl.CostEstimate(
             flops=8 * s.cells * k * k, bytes_accessed=8 * s.cells * k, transcendentals=0
         ),
-    )(own, got, filtered)
+    )(packed, filtered)
 
 
 def on_device(block, conductivity):
@@ -437,8 +430,8 @@
         w, *faces = finish(part, wide, edge, ghosts, s, nz, scale, step == DEG - 1)
     ghosts = exchange(faces, axes)
     filtered, gram, own = gather_terms(w, wide, s)
-    halves = total(*pack_terms(gram, own, w, ghosts, s, nz, cells))
-    basis, projected = orthonormal(*halves, filtered, s)
+    packed = total(pack_terms(gram, own, w, ghosts, s, nz, cells))
+    basis, projected = orthonormal(packed, filtered, s)
     return (basis.reshape(block.shape), projected)
 
 

time: 78.7 us -> 78.8 us (level)
    ppermute x8 -> x7, waiting for transfers between devices: 9.05 us -> 9.11 us  [swap(): return lax.ppermute(value, axes, pairs)]
    ppermute x8 -> x7, starting transfers between devices: 10.5 us -> 10.5 us  [swap(): return lax.ppermute(value, axes, pairs)]
  transfers between devices with their start and end apart: 33 -> 32, of which waited for: 14 -> 13; matrix products, arithmetic and copies ran while one was open for 0% -> 0% of each run, Pallas kernels for 9% -> 9%
where the time goes in v11:
time: 78.8 us; the launch traced here: 78.4 us
  starting transfers between devices  47.7 us (61%)
  Pallas kernels  15.3 us (19%)
  waiting for transfers between devices  12.7 us (16%)
  local copies, waits for them, and re-layouts  1.77 us (2%)
  between operations  0.89 us (1%)
    ppermute x25, starting transfers between devices, exchange(): got.append(lax.ppermute(face, axis, pairs))  37.1 us
    ppermute x7, starting transfers between devices, swap(): return lax.ppermute(value, axes, pairs)  10.5 us
    ppermute x7, waiting for transfers between devices, swap(): return lax.ppermute(value, axes, pairs)  9.11 us
    pallas_call x10, Pallas kernels, call(): pl.pallas_call(body, out_shape=outs, in_specs=[VMEM] * len(ins), out_spec...  7.71 us
    pallas_call x1, Pallas kernels, orthonormal(): pl.pallas_call(body, out_shape=[f32(s.cells, k), f32(k, k)], in_specs=[VM...  5.44 us
    ppermute x25, waiting for transfers between devices, exchange(): got.append(lax.ppermute(face, axis, pairs))  3.55 us
    pallas_call x1, Pallas kernels, gather_terms(): pl.pallas_call(body, out_shape=outs, in_specs=[VMEM, VMEM], out_specs=(VM...  2.2 us
    slice x1, local copies, waits for them, and re-layouts, prepare(): block[i * each * s.row:(i + 1) * each * s.row]  1.76 us
  transfers between devices with their start and end apart: 32, of which 13 were waited for; matrix products, arithmetic and copies ran while one was open for 0% of the time, Pallas kernels for 9%

profile of v11, /device:TPU:0, one launch (start us, length us, event | category | flops | bytes accessed | tf_op | source)
XLA Modules:
  0.0 78.4 jit_solution(15012627524248447924)
XLA Ops:
  0.6 1.8 %fusion = (f32[8,16,8,128]{3,2,1,0:T(8,128)S(1)}, f32[8,16,8,128]{3,2,1,0:T(8,128)S(1)}, f32[8,16,8,128]{3,2,1,0:T(8,128)S(1)}, f32[8,16,8,128]{3,2,1,0:T(8,128)S(1)}) fusion(f32[32,16,8,128]{3,2,1,0:T(8,128)} %param.2), kind=kLoop, calls=%fused_computation.2 | loop fusion | bytes 4194304 | tf_op jit(solution)/shard_map/slice | solution.py:92
  2.4 1.1 %shard_map.41 = (f32[4104,128]{1,0:T(8,128)S(1)}, f32[4104,128]{1,0:T(8,128)S(1)}, f32[128,128]{1,0:T(8,128)S(1)}, f32[128,128]{1,0:T(8,128)S(1)}, f32[256,128]{...) custom-call(f32[16,8,32]{2,1,0:T(8,128)S(1)} %bitcast.10, ...), custom_call_target="tpu_custom_call" | custom-call | flops 2097152 | bytes 7233536 | tf_op jit(solution)/shard_map/pallas_call | solution.py:20
  3.5 3.0 %collective-permute-start.4 = (f32[512,128]{1,0:T(8,128)S(1)}, f32[512,128]{1,0:T(8,128)S(1)}, u32[]{:S(2)}, u32[]{:S(2)}) collective-permute-start(f32[512,128]{1,0:T(8,128)S(1)} %get-tuple-element.46), channel_id=1, source_target_pairs={{0,1},{1,0},{2,3},{3,2},{4,5},{5,4},{6,7},{7,6},{8,9},{9,8},{10,11... | collective-permute-start | bytes 786440 | tf_op jit(solution)/shard_map/ppermute | solution.py:204
  7.2 1.6 %collective-permute-start = (f32[128,128]{1,0:T(8,128)S(1)}, f32[128,128]{1,0:T(8,128)S(1)}, u32[]{:S(2)}, u32[]{:S(2)}) collective-permute-start(f32[128,128]{1,0:T(8,128)S(1)} %get-tuple-element.42), channel_id=1, source_target_pairs={{0,8},{8,0},{16,24},{24,16},{1,9},{9,1},{17,25},{25,17},{2,10},{10... | collective-permute-start | bytes 196616 | tf_op jit(solution)/shard_map/ppermute | solution.py:204
  9.5 1.2 %shard_map.42.p_ref = f32[4104,128]{1,0:T(8,128)S(1)} custom-call(f32[4104,128]{1,0:T(8,128)S(1)} %get-tuple-element.39.w_ref.rest_0_, f32[4104,128]{1,0:T(8,128)S(1)} %get-tuple-element.40.k_ref), custom_call_target="tpu_custom_call" | custom-call | flops 6291456 | bytes 6303744 | tf_op jit(solution)/shard_map/pallas_call | solution.py:20
  10.7 0.9 %collective-permute-done.refs_1_ = f32[128,128]{1,0:T(8,128)S(1)} collective-permute-done((f32[128,128]{1,0:T(8,128)S(1)}, f32[128,128]{1,0:T(8,128)S(1)}, u32[]{:S(2)}, u32[]{:S(2)}) %collective-permute-start) | collective-permute-done | bytes 65568 | tf_op jit(solution)/shard_map/ppermute | solution.py:204
  11.6 1.3 %collective-permute-done.4.refs_5_ = f32[512,128]{1,0:T(8,128)S(1)} collective-permute-done((f32[512,128]{1,0:T(8,128)S(1)}, f32[512,128]{1,0:T(8,128)S(1)}, u32[]{:S(2)}, u32[]{:S(2)}) %collective-permute-start.4) | collective-permute-done | bytes 262176 | tf_op jit(solution)/shard_map/ppermute | solution.py:204
  13.1 1.8 %collective-permute-start.9 = (f32[512,128]{1,0:T(8,128)S(1)}, f32[512,128]{1,0:T(8,128)S(1)}, u32[]{:S(2)}, u32[]{:S(2)}) collective-permute-start(f32[512,128]{1,0:T(8,128)S(1)} %get-tuple-element.52), channel_id=1, source_target_pairs={{0,1},{1,0},{2,3},{3,2},{4,5},{5,4},{6,7},{7,6},{8,9},{9,8},{10,11... | collective-permute-start | bytes 786440 | tf_op jit(solution)/shard_map/ppermute | solution.py:204
  15.6 3.6 %collective-permute-start.5 = (f32[128,128]{1,0:T(8,128)S(1)}, f32[128,128]{1,0:T(8,128)S(1)}, u32[]{:S(2)}, u32[]{:S(2)}) collective-permute-start(f32[128,128]{1,0:T(8,128)S(1)} %get-tuple-element.48), channel_id=1, source_target_pairs={{0,8},{8,0},{16,24},{24,16},{1,9},{9,1},{17,25},{25,17},{2,10},{10... | collective-permute-start | bytes 196616 | tf_op jit(solution)/shard_map/ppermute | solution.py:204
  19.9 1.2 %shard_map.44.p_ref = f32[4104,128]{1,0:T(8,128)S(1)} custom-call(f32[4104,128]{1,0:T(8,128)S(1)} %get-tuple-element.47.w_ref.rest_0_, f32[4104,128]{1,0:T(8,128)S(1)} %get-tuple-element.40.k_ref, f32[4104,128]{1,0:T(8,128)S(1)} %get-tuple-element.39.w_ref.rest_0_), custom_call_target="tpu_custom_call" | custom-call | flops 6291456 | bytes 8404992 | tf_op jit(solution)/shard_map/pallas_call | solution.py:20
  22.2 1.2 %collective-permute-start.14 = (f32[512,128]{1,0:T(8,128)S(1)}, f32[512,128]{1,0:T(8,128)S(1)}, u32[]{:S(2)}, u32[]{:S(2)}) collective-permute-start(f32[512,128]{1,0:T(8,128)S(1)} %get-tuple-element.58), channel_id=1, source_target_pairs={{0,1},{1,0},{2,3},{3,2},{4,5},{5,4},{6,7},{7,6},{8,9},{9,8},{10,11... | collective-permute-start | bytes 786440 | tf_op jit(solution)/shard_map/ppermute | solution.py:204
  23.4 2.4 %collective-permute-start.12 = (f32[256,128]{1,0:T(8,128)S(1)}, f32[256,128]{1,0:T(8,128)S(1)}, u32[]{:S(2)}, u32[]{:S(2)}) collective-permute-start(f32[256,128]{1,0:T(8,128)S(1)} %get-tuple-element.56), channel_id=1, source_target_pairs={{0,2},{2,0},{4,6},{6,4},{1,3},{3,1},{5,7},{7,5},{8,10},{10,8},{12,... | collective-permute-start | bytes 393224 | tf_op jit(solution)/shard_map/ppermute | solution.py:204
  26.4 3.7 %collective-permute-start.10 = (f32[128,128]{1,0:T(8,128)S(1)}, f32[128,128]{1,0:T(8,128)S(1)}, u32[]{:S(2)}, u32[]{:S(2)}) collective-permute-start(f32[128,128]{1,0:T(8,128)S(1)} %get-tuple-element.54), channel_id=1, source_target_pairs={{0,8},{8,0},{16,24},{24,16},{1,9},{9,1},{17,25},{25,17},{2,10},{10... | collective-permute-start | bytes 196616 | tf_op jit(solution)/shard_map/ppermute | solution.py:204
  30.8 1.4 %shard_map.46.p_ref = f32[4104,128]{1,0:T(8,128)S(1)} custom-call(f32[4104,128]{1,0:T(8,128)S(1)} %get-tuple-element.53.w_ref.rest_0_, f32[4104,128]{1,0:T(8,128)S(1)} %get-tuple-element.40.k_ref, f32[4104,128]{1,0:T(8,128)S(1)} %get-tuple-element.47.w_ref.rest_0_), custom_call_target="tpu_custom_call" | custom-call | flops 6291456 | bytes 8404992 | tf_op jit(solution)/shard_map/pallas_call | solution.py:20
  33.3 1.6 %collective-permute-start.17 = (f32[256,128]{1,0:T(8,128)S(1)}, f32[256,128]{1,0:T(8,128)S(1)}, u32[]{:S(2)}, u32[]{:S(2)}) collective-permute-start(f32[256,128]{1,0:T(8,128)S(1)} %get-tuple-element.62), channel_id=1, source_target_pairs={{0,2},{2,0},{4,6},{6,4},{1,3},{3,1},{5,7},{7,5},{8,10},{10,8},{12,... | collective-permute-start | bytes 393224 | tf_op jit(solution)/shard_map/ppermute | solution.py:204
  35.6 3.6 %collective-permute-start.15 = (f32[128,128]{1,0:T(8,128)S(1)}, f32[128,128]{1,0:T(8,128)S(1)}, u32[]{:S(2)}, u32[]{:S(2)}) collective-permute-start(f32[128,128]{1,0:T(8,128)S(1)} %get-tuple-element.60), channel_id=1, source_target_pairs={{0,8},{8,0},{16,24},{24,16},{1,9},{9,1},{17,25},{25,17},{2,10},{10... | collective-permute-start | bytes 196616 | tf_op jit(solution)/shard_map/ppermute | solution.py:204
  39.9 1.2 %shard_map.48.p_ref = f32[4104,128]{1,0:T(8,128)S(1)} custom-call(f32[4104,128]{1,0:T(8,128)S(1)} %get-tuple-element.59.w_ref, f32[4104,128]{1,0:T(8,128)S(1)} %get-tuple-element.40.k_ref, f32[4104,128]{1,0:T(8,128)S(1)} %get-tuple-element.53.w_ref.rest_0_), custom_call_target="tpu_custom_call" | custom-call | flops 6291456 | bytes 8404992 | tf_op jit(solution)/shard_map/pallas_call | solution.py:20
  41.8 2.4 %collective-permute-start.22 = (f32[256,128]{1,0:T(8,128)S(1)}, f32[256,128]{1,0:T(8,128)S(1)}, u32[]{:S(2)}, u32[]{:S(2)}) collective-permute-start(f32[256,128]{1,0:T(8,128)S(1)} %get-tuple-element.70), channel_id=1, source_target_pairs={{0,2},{2,0},{4,6},{6,4},{1,3},{3,1},{5,7},{7,5},{8,10},{10,8},{12,... | collective-permute-start | bytes 393224 | tf_op jit(solution)/shard_map/ppermute | solution.py:204
  44.9 1.6 %collective-permute-start.24 = (f32[256,128]{1,0:T(8,128)S(1)}, f32[256,128]{1,0:T(8,128)S(1)}, u32[]{:S(2)}, u32[]{:S(2)}) collective-permute-start(f32[256,128]{1,0:T(8,128)S(1)} %get-tuple-element.72), channel_id=1, source_target_pairs={{0,1},{1,0},{2,3},{3,2},{4,5},{5,4},{6,7},{7,6},{8,9},{9,8},{10,11... | collective-permute-start | bytes 393224 | tf_op jit(solution)/shard_map/ppermute | solution.py:204
  46.5 3.4 %collective-permute-start.20 = (f32[128,128]{1,0:T(8,128)S(1)}, f32[128,128]{1,0:T(8,128)S(1)}, u32[]{:S(2)}, u32[]{:S(2)}) collective-permute-start(f32[128,128]{1,0:T(8,128)S(1)} %get-tuple-element.68), channel_id=1, source_target_pairs={{0,8},{8,0},{16,24},{24,16},{1,9},{9,1},{17,25},{25,17},{2,10},{10... | collective-permute-start | bytes 196616 | tf_op jit(solution)/shard_map/ppermute | solution.py:204
  50.5 2.2 %shard_map.50 = (bf16[4096,256]{1,0:T(8,128)(2,1)S(1)}, f32[128,128]{1,0:T(8,128)S(1)}, f32[128,128]{1,0:T(8,128)S(1)}) custom-call(f32[4104,128]{1,0:T(8,128)S(1)} %get-tuple-element.65.w_ref, f32[4104,128]{1,0:T(8,128)S(1)} %get-tuple-element.40.k_ref), custom_call_target="tpu_custom_call" | custom-call | flops 1073741824 | bytes 8388608 | tf_op jit(solution)/shard_map/pallas_call | solution.py:247
  53.2 1.9 %collective-permute-start.25 = (f32[136,128]{1,0:T(8,128)S(1)}, f32[136,128]{1,0:T(8,128)S(1)}, u32[]{:S(2)}, u32[]{:S(2)}) collective-permute-start(f32[136,128]{1,0:T(8,128)S(1)} %shard_map.51), channel_id=1, source_target_pairs={{0,2},{1,3},{2,0},{3,1},{4,6},{5,7},{6,4},{7,5},{8,10},{9,11},{10,... | collective-permute-start | bytes 208904 | tf_op jit(solution)/shard_map/ppermute | solution.py:306
  55.1 0.9 %collective-permute-done.25 = f32[136,128]{1,0:T(8,128)S(1)} collective-permute-done((f32[136,128]{1,0:T(8,128)S(1)}, f32[136,128]{1,0:T(8,128)S(1)}, u32[]{:S(2)}, u32[]{:S(2)}) %collective-permute-start.25) | collective-permute-done | bytes 69664 | tf_op jit(solution)/shard_map/ppermute | solution.py:306
  56.1 1.4 %collective-permute-start.28 = (f32[136,128]{1,0:T(8,128)S(1)}, f32[136,128]{1,0:T(8,128)S(1)}, u32[]{:S(2)}, u32[]{:S(2)}) collective-permute-start(f32[136,128]{1,0:T(8,128)S(1)} %add.21), channel_id=1, source_target_pairs={{0,5},{1,4},{2,7},{3,6},{4,1},{5,0},{6,3},{7,2},{8,13},{9,12},{10,... | collective-permute-start | bytes 208904 | tf_op jit(solution)/shard_map/ppermute | solution.py:306
  57.5 1.5 %collective-permute-start.27 = (f32[136,128]{1,0:T(8,128)S(1)}, f32[136,128]{1,0:T(8,128)S(1)}, u32[]{:S(2)}, u32[]{:S(2)}) collective-permute-start(f32[136,128]{1,0:T(8,128)S(1)} %add.21), channel_id=1, source_target_pairs={{0,1},{1,0},{2,3},{3,2},{4,5},{5,4},{6,7},{7,6},{8,9},{9,8},{10,11... | collective-permute-start | bytes 208904 | tf_op jit(solution)/shard_map/ppermute | solution.py:306
  59.6 2.4 %collective-permute-done.28 = f32[136,128]{1,0:T(8,128)S(1)} collective-permute-done((f32[136,128]{1,0:T(8,128)S(1)}, f32[136,128]{1,0:T(8,128)S(1)}, u32[]{:S(2)}, u32[]{:S(2)}) %collective-permute-start.28) | collective-permute-done | bytes 69664 | tf_op jit(solution)/shard_map/ppermute | solution.py:306
  63.3 2.7 %collective-permute-start.31 = (f32[136,128]{1,0:T(8,128)S(1)}, f32[136,128]{1,0:T(8,128)S(1)}, u32[]{:S(2)}, u32[]{:S(2)}) collective-permute-start(f32[136,128]{1,0:T(8,128)S(1)} %add_add_fusion.1), channel_id=1, source_target_pairs={{0,24},{1,25},{2,26},{3,27},{4,28},{5,29},{6,30},{7,31},{8,16},{9,... | collective-permute-start | bytes 208904 | tf_op jit(solution)/shard_map/ppermute | solution.py:306
  66.0 2.1 %collective-permute-start.30 = (f32[136,128]{1,0:T(8,128)S(1)}, f32[136,128]{1,0:T(8,128)S(1)}, u32[]{:S(2)}, u32[]{:S(2)}) collective-permute-start(f32[136,128]{1,0:T(8,128)S(1)} %add_add_fusion.1), channel_id=1, source_target_pairs={{0,16},{1,17},{2,18},{3,19},{4,20},{5,21},{6,22},{7,23},{8,24},{9,... | collective-permute-start | bytes 208904 | tf_op jit(solution)/shard_map/ppermute | solution.py:306
  68.4 1.2 %collective-permute-done.31 = f32[136,128]{1,0:T(8,128)S(1)} collective-permute-done((f32[136,128]{1,0:T(8,128)S(1)}, f32[136,128]{1,0:T(8,128)S(1)}, u32[]{:S(2)}, u32[]{:S(2)}) %collective-permute-start.31) | collective-permute-done | bytes 69664 | tf_op jit(solution)/shard_map/ppermute | solution.py:306
  69.6 2.6 %collective-permute-done.30 = f32[136,128]{1,0:T(8,128)S(1)} collective-permute-done((f32[136,128]{1,0:T(8,128)S(1)}, f32[136,128]{1,0:T(8,128)S(1)}, u32[]{:S(2)}, u32[]{:S(2)}) %collective-permute-start.30) | collective-permute-done | bytes 69664 | tf_op jit(solution)/shard_map/ppermute | solution.py:306
  72.2 0.7 collective-permute-done.29
  72.9 5.4 %shard_map.52 = (f32[4096,128]{1,0:T(8,128)}, f32[128,128]{1,0:T(8,128)}) custom-call(f32[136,128]{1,0:T(8,128)S(1)} %add_add_fusion.p_ref, bf16[4096,256]{1,0:T(8,128)(2,1)S(1)} %get-tuple-element.73.f_ref), custom_call_target="tpu_custom_call" | custom-call | flops 536870912 | bytes 4194304 | tf_op jit(solution)/shard_map/pallas_call | solution.py:396
  (50 shorter events, 12.4 us)
Async XLA Ops:
  3.5 9.3 %collective-permute-start.4 = (f32[512,128]{1,0:T(8,128)S(1)}, f32[512,128]{1,0:T(8,128)S(1)}, u32[]{:S(2)}, u32[]{:S(2)}) collective-permute-start(f32[512,128]{1,0:T(8,128)S(1)} %get-tuple-element.46), channel_id=1, source_target_pairs={{0,1},{1,0},{2,3},{3,2},{4,5},{5,4},{6,7},{7,6},{8,9},{9,8},{10,11... | collective-permute-start | bytes 786440 | tf_op jit(solution)/shard_map/ppermute | solution.py:204
  6.5 5.0 %collective-permute-start.2 = (f32[256,128]{1,0:T(8,128)S(1)}, f32[256,128]{1,0:T(8,128)S(1)}, u32[]{:S(2)}, u32[]{:S(2)}) collective-permute-start(f32[256,128]{1,0:T(8,128)S(1)} %get-tuple-element.44), channel_id=1, source_target_pairs={{0,2},{2,0},{4,6},{6,4},{1,3},{3,1},{5,7},{7,5},{8,10},{10,8},{12,... | collective-permute-start | bytes 393224 | tf_op jit(solution)/shard_map/ppermute | solution.py:204
  6.5 5.0 %collective-permute-start.3 = (f32[256,128]{1,0:T(8,128)S(1)}, f32[256,128]{1,0:T(8,128)S(1)}, u32[]{:S(2)}, u32[]{:S(2)}) collective-permute-start(f32[256,128]{1,0:T(8,128)S(1)} %get-tuple-element.45), channel_id=1, source_target_pairs={{2,4},{4,2},{3,5},{5,3},{10,12},{12,10},{11,13},{13,11},{18,20},{2... | collective-permute-start | bytes 393224 | tf_op jit(solution)/shard_map/ppermute | solution.py:204
  7.2 4.3 %collective-permute-start = (f32[128,128]{1,0:T(8,128)S(1)}, f32[128,128]{1,0:T(8,128)S(1)}, u32[]{:S(2)}, u32[]{:S(2)}) collective-permute-start(f32[128,128]{1,0:T(8,128)S(1)} %get-tuple-element.42), channel_id=1, source_target_pairs={{0,8},{8,0},{16,24},{24,16},{1,9},{9,1},{17,25},{25,17},{2,10},{10... | collective-permute-start | bytes 196616 | tf_op jit(solution)/shard_map/ppermute | solution.py:204
  8.9 2.7 %collective-permute-start.1 = (f32[128,128]{1,0:T(8,128)S(1)}, f32[128,128]{1,0:T(8,128)S(1)}, u32[]{:S(2)}, u32[]{:S(2)}) collective-permute-start(f32[128,128]{1,0:T(8,128)S(1)} %get-tuple-element.43), channel_id=1, source_target_pairs={{8,16},{16,8},{9,17},{17,9},{10,18},{18,10},{11,19},{19,11},{12,20... | collective-permute-start | bytes 196616 | tf_op jit(solution)/shard_map/ppermute | solution.py:204
  13.1 8.8 %collective-permute-start.9 = (f32[512,128]{1,0:T(8,128)S(1)}, f32[512,128]{1,0:T(8,128)S(1)}, u32[]{:S(2)}, u32[]{:S(2)}) collective-permute-start(f32[512,128]{1,0:T(8,128)S(1)} %get-tuple-element.52), channel_id=1, source_target_pairs={{0,1},{1,0},{2,3},{3,2},{4,5},{5,4},{6,7},{7,6},{8,9},{9,8},{10,11... | collective-permute-start | bytes 786440 | tf_op jit(solution)/shard_map/ppermute | solution.py:204
  14.9 6.5 %collective-permute-start.7 = (f32[256,128]{1,0:T(8,128)S(1)}, f32[256,128]{1,0:T(8,128)S(1)}, u32[]{:S(2)}, u32[]{:S(2)}) collective-permute-start(f32[256,128]{1,0:T(8,128)S(1)} %get-tuple-element.50), channel_id=1, source_target_pairs={{0,2},{2,0},{4,6},{6,4},{1,3},{3,1},{5,7},{7,5},{8,10},{10,8},{12,... | collective-permute-start | bytes 393224 | tf_op jit(solution)/shard_map/ppermute | solution.py:204
  14.9 6.5 %collective-permute-start.8 = (f32[256,128]{1,0:T(8,128)S(1)}, f32[256,128]{1,0:T(8,128)S(1)}, u32[]{:S(2)}, u32[]{:S(2)}) collective-permute-start(f32[256,128]{1,0:T(8,128)S(1)} %get-tuple-element.51), channel_id=1, source_target_pairs={{2,4},{4,2},{3,5},{5,3},{10,12},{12,10},{11,13},{13,11},{18,20},{2... | collective-permute-start | bytes 393224 | tf_op jit(solution)/shard_map/ppermute | solution.py:204
  15.6 5.9 %collective-permute-start.5 = (f32[128,128]{1,0:T(8,128)S(1)}, f32[128,128]{1,0:T(8,128)S(1)}, u32[]{:S(2)}, u32[]{:S(2)}) collective-permute-start(f32[128,128]{1,0:T(8,128)S(1)} %get-tuple-element.48), channel_id=1, source_target_pairs={{0,8},{8,0},{16,24},{24,16},{1,9},{9,1},{17,25},{25,17},{2,10},{10... | collective-permute-start | bytes 196616 | tf_op jit(solution)/shard_map/ppermute | solution.py:204
  19.2 2.2 %collective-permute-start.6 = (f32[128,128]{1,0:T(8,128)S(1)}, f32[128,128]{1,0:T(8,128)S(1)}, u32[]{:S(2)}, u32[]{:S(2)}) collective-permute-start(f32[128,128]{1,0:T(8,128)S(1)} %get-tuple-element.49), channel_id=1, source_target_pairs={{8,16},{16,8},{9,17},{17,9},{10,18},{18,10},{11,19},{19,11},{12,20... | collective-permute-start | bytes 196616 | tf_op jit(solution)/shard_map/ppermute | solution.py:204
  22.2 10.2 %collective-permute-start.14 = (f32[512,128]{1,0:T(8,128)S(1)}, f32[512,128]{1,0:T(8,128)S(1)}, u32[]{:S(2)}, u32[]{:S(2)}) collective-permute-start(f32[512,128]{1,0:T(8,128)S(1)} %get-tuple-element.58), channel_id=1, source_target_pairs={{0,1},{1,0},{2,3},{3,2},{4,5},{5,4},{6,7},{7,6},{8,9},{9,8},{10,11... | collective-permute-start | bytes 786440 | tf_op jit(solution)/shard_map/ppermute | solution.py:204
  23.4 9.0 %collective-permute-start.12 = (f32[256,128]{1,0:T(8,128)S(1)}, f32[256,128]{1,0:T(8,128)S(1)}, u32[]{:S(2)}, u32[]{:S(2)}) collective-permute-start(f32[256,128]{1,0:T(8,128)S(1)} %get-tuple-element.56), channel_id=1, source_target_pairs={{0,2},{2,0},{4,6},{6,4},{1,3},{3,1},{5,7},{7,5},{8,10},{10,8},{12,... | collective-permute-start | bytes 393224 | tf_op jit(solution)/shard_map/ppermute | solution.py:204
  25.8 6.6 %collective-permute-start.13 = (f32[256,128]{1,0:T(8,128)S(1)}, f32[256,128]{1,0:T(8,128)S(1)}, u32[]{:S(2)}, u32[]{:S(2)}) collective-permute-start(f32[256,128]{1,0:T(8,128)S(1)} %get-tuple-element.57), channel_id=1, source_target_pairs={{2,4},{4,2},{3,5},{5,3},{10,12},{12,10},{11,13},{13,11},{18,20},{2... | collective-permute-start | bytes 393224 | tf_op jit(solution)/shard_map/ppermute | solution.py:204
  26.4 5.9 %collective-permute-start.10 = (f32[128,128]{1,0:T(8,128)S(1)}, f32[128,128]{1,0:T(8,128)S(1)}, u32[]{:S(2)}, u32[]{:S(2)}) collective-permute-start(f32[128,128]{1,0:T(8,128)S(1)} %get-tuple-element.54), channel_id=1, source_target_pairs={{0,8},{8,0},{16,24},{24,16},{1,9},{9,1},{17,25},{25,17},{2,10},{10... | collective-permute-start | bytes 196616 | tf_op jit(solution)/shard_map/ppermute | solution.py:204
  30.2 2.2 %collective-permute-start.11 = (f32[128,128]{1,0:T(8,128)S(1)}, f32[128,128]{1,0:T(8,128)S(1)}, u32[]{:S(2)}, u32[]{:S(2)}) collective-permute-start(f32[128,128]{1,0:T(8,128)S(1)} %get-tuple-element.55), channel_id=1, source_target_pairs={{8,16},{16,8},{9,17},{17,9},{10,18},{18,10},{11,19},{19,11},{12,20... | collective-permute-start | bytes 196616 | tf_op jit(solution)/shard_map/ppermute | solution.py:204
  32.7 8.8 %collective-permute-start.19 = (f32[512,128]{1,0:T(8,128)S(1)}, f32[512,128]{1,0:T(8,128)S(1)}, u32[]{:S(2)}, u32[]{:S(2)}) collective-permute-start(f32[512,128]{1,0:T(8,128)S(1)} %get-tuple-element.64), channel_id=1, source_target_pairs={{0,1},{1,0},{2,3},{3,2},{4,5},{5,4},{6,7},{7,6},{8,9},{9,8},{10,11... | collective-permute-start | bytes 786440 | tf_op jit(solution)/shard_map/ppermute | solution.py:204
  33.3 8.2 %collective-permute-start.17 = (f32[256,128]{1,0:T(8,128)S(1)}, f32[256,128]{1,0:T(8,128)S(1)}, u32[]{:S(2)}, u32[]{:S(2)}) collective-permute-start(f32[256,128]{1,0:T(8,128)S(1)} %get-tuple-element.62), channel_id=1, source_target_pairs={{0,2},{2,0},{4,6},{6,4},{1,3},{3,1},{5,7},{7,5},{8,10},{10,8},{12,... | collective-permute-start | bytes 393224 | tf_op jit(solution)/shard_map/ppermute | solution.py:204
  35.0 6.5 %collective-permute-start.18 = (f32[256,128]{1,0:T(8,128)S(1)}, f32[256,128]{1,0:T(8,128)S(1)}, u32[]{:S(2)}, u32[]{:S(2)}) collective-permute-start(f32[256,128]{1,0:T(8,128)S(1)} %get-tuple-element.63), channel_id=1, source_target_pairs={{2,4},{4,2},{3,5},{5,3},{10,12},{12,10},{11,13},{13,11},{18,20},{2... | collective-permute-start | bytes 393224 | tf_op jit(solution)/shard_map/ppermute | solution.py:204
  35.6 5.8 %collective-permute-start.15 = (f32[128,128]{1,0:T(8,128)S(1)}, f32[128,128]{1,0:T(8,128)S(1)}, u32[]{:S(2)}, u32[]{:S(2)}) collective-permute-start(f32[128,128]{1,0:T(8,128)S(1)} %get-tuple-element.60), channel_id=1, source_target_pairs={{0,8},{8,0},{16,24},{24,16},{1,9},{9,1},{17,25},{25,17},{2,10},{10... | collective-permute-start | bytes 196616 | tf_op jit(solution)/shard_map/ppermute | solution.py:204
  39.2 2.2 %collective-permute-start.16 = (f32[128,128]{1,0:T(8,128)S(1)}, f32[128,128]{1,0:T(8,128)S(1)}, u32[]{:S(2)}, u32[]{:S(2)}) collective-permute-start(f32[128,128]{1,0:T(8,128)S(1)} %get-tuple-element.61), channel_id=1, source_target_pairs={{8,16},{16,8},{9,17},{17,9},{10,18},{18,10},{11,19},{19,11},{12,20... | collective-permute-start | bytes 196616 | tf_op jit(solution)/shard_map/ppermute | solution.py:204
  41.8 10.9 %collective-permute-start.22 = (f32[256,128]{1,0:T(8,128)S(1)}, f32[256,128]{1,0:T(8,128)S(1)}, u32[]{:S(2)}, u32[]{:S(2)}) collective-permute-start(f32[256,128]{1,0:T(8,128)S(1)} %get-tuple-element.70), channel_id=1, source_target_pairs={{0,2},{2,0},{4,6},{6,4},{1,3},{3,1},{5,7},{7,5},{8,10},{10,8},{12,... | collective-permute-start | bytes 393224 | tf_op jit(solution)/shard_map/ppermute | solution.py:204
  44.2 8.5 %collective-permute-start.23 = (f32[256,128]{1,0:T(8,128)S(1)}, f32[256,128]{1,0:T(8,128)S(1)}, u32[]{:S(2)}, u32[]{:S(2)}) collective-permute-start(f32[256,128]{1,0:T(8,128)S(1)} %get-tuple-element.71), channel_id=1, source_target_pairs={{2,4},{4,2},{3,5},{5,3},{10,12},{12,10},{11,13},{13,11},{18,20},{2... | collective-permute-start | bytes 393224 | tf_op jit(solution)/shard_map/ppermute | solution.py:204
  44.9 7.8 %collective-permute-start.24 = (f32[256,128]{1,0:T(8,128)S(1)}, f32[256,128]{1,0:T(8,128)S(1)}, u32[]{:S(2)}, u32[]{:S(2)}) collective-permute-start(f32[256,128]{1,0:T(8,128)S(1)} %get-tuple-element.72), channel_id=1, source_target_pairs={{0,1},{1,0},{2,3},{3,2},{4,5},{5,4},{6,7},{7,6},{8,9},{9,8},{10,11... | collective-permute-start | bytes 393224 | tf_op jit(solution)/shard_map/ppermute | solution.py:204
  46.5 6.2 %collective-permute-start.20 = (f32[128,128]{1,0:T(8,128)S(1)}, f32[128,128]{1,0:T(8,128)S(1)}, u32[]{:S(2)}, u32[]{:S(2)}) collective-permute-start(f32[128,128]{1,0:T(8,128)S(1)} %get-tuple-element.68), channel_id=1, source_target_pairs={{0,8},{8,0},{16,24},{24,16},{1,9},{9,1},{17,25},{25,17},{2,10},{10... | collective-permute-start | bytes 196616 | tf_op jit(solution)/shard_map/ppermute | solution.py:204
  49.8 2.9 %collective-permute-start.21 = (f32[128,128]{1,0:T(8,128)S(1)}, f32[128,128]{1,0:T(8,128)S(1)}, u32[]{:S(2)}, u32[]{:S(2)}) collective-permute-start(f32[128,128]{1,0:T(8,128)S(1)} %get-tuple-element.69), channel_id=1, source_target_pairs={{8,16},{16,8},{9,17},{17,9},{10,18},{18,10},{11,19},{19,11},{12,20... | collective-permute-start | bytes 196616 | tf_op jit(solution)/shard_map/ppermute | solution.py:204
  53.2 2.8 %collective-permute-start.25 = (f32[136,128]{1,0:T(8,128)S(1)}, f32[136,128]{1,0:T(8,128)S(1)}, u32[]{:S(2)}, u32[]{:S(2)}) collective-permute-start(f32[136,128]{1,0:T(8,128)S(1)} %shard_map.51), channel_id=1, source_target_pairs={{0,2},{1,3},{2,0},{3,1},{4,6},{5,7},{6,4},{7,5},{8,10},{9,11},{10,... | collective-permute-start | bytes 208904 | tf_op jit(solution)/shard_map/ppermute | solution.py:306
  56.1 6.0 %collective-permute-start.28 = (f32[136,128]{1,0:T(8,128)S(1)}, f32[136,128]{1,0:T(8,128)S(1)}, u32[]{:S(2)}, u32[]{:S(2)}) collective-permute-start(f32[136,128]{1,0:T(8,128)S(1)} %add.21), channel_id=1, source_target_pairs={{0,5},{1,4},{2,7},{3,6},{4,1},{5,0},{6,3},{7,2},{8,13},{9,12},{10,... | collective-permute-start | bytes 208904 | tf_op jit(solution)/shard_map/ppermute | solution.py:306
  57.5 5.2 %collective-permute-start.27 = (f32[136,128]{1,0:T(8,128)S(1)}, f32[136,128]{1,0:T(8,128)S(1)}, u32[]{:S(2)}, u32[]{:S(2)}) collective-permute-start(f32[136,128]{1,0:T(8,128)S(1)} %add.21), channel_id=1, source_target_pairs={{0,1},{1,0},{2,3},{3,2},{4,5},{5,4},{6,7},{7,6},{8,9},{9,8},{10,11... | collective-permute-start | bytes 208904 | tf_op jit(solution)/shard_map/ppermute | solution.py:306
  59.0 4.3 %collective-permute-start.26 = (f32[136,128]{1,0:T(8,128)S(1)}, f32[136,128]{1,0:T(8,128)S(1)}, u32[]{:S(2)}, u32[]{:S(2)}) collective-permute-start(f32[136,128]{1,0:T(8,128)S(1)} %add.21), channel_id=1, source_target_pairs={{0,4},{1,5},{2,6},{3,7},{4,0},{5,1},{6,2},{7,3},{8,12},{9,13},{10,... | collective-permute-start | bytes 208904 | tf_op jit(solution)/shard_map/ppermute | solution.py:306
  63.3 6.3 %collective-permute-start.31 = (f32[136,128]{1,0:T(8,128)S(1)}, f32[136,128]{1,0:T(8,128)S(1)}, u32[]{:S(2)}, u32[]{:S(2)}) collective-permute-start(f32[136,128]{1,0:T(8,128)S(1)} %add_add_fusion.1), channel_id=1, source_target_pairs={{0,24},{1,25},{2,26},{3,27},{4,28},{5,29},{6,30},{7,31},{8,16},{9,... | collective-permute-start | bytes 208904 | tf_op jit(solution)/shard_map/ppermute | solution.py:306
  66.0 6.2 %collective-permute-start.30 = (f32[136,128]{1,0:T(8,128)S(1)}, f32[136,128]{1,0:T(8,128)S(1)}, u32[]{:S(2)}, u32[]{:S(2)}) collective-permute-start(f32[136,128]{1,0:T(8,128)S(1)} %add_add_fusion.1), channel_id=1, source_target_pairs={{0,16},{1,17},{2,18},{3,19},{4,20},{5,21},{6,22},{7,23},{8,24},{9,... | collective-permute-start | bytes 208904 | tf_op jit(solution)/shard_map/ppermute | solution.py:306
  68.1 4.8 %collective-permute-start.29 = (f32[136,128]{1,0:T(8,128)S(1)}, f32[136,128]{1,0:T(8,128)S(1)}, u32[]{:S(2)}, u32[]{:S(2)}) collective-permute-start(f32[136,128]{1,0:T(8,128)S(1)} %add_add_fusion.1), channel_id=1, source_target_pairs={{0,8},{1,9},{2,10},{3,11},{4,12},{5,13},{6,14},{7,15},{8,0},{9,1},... | collective-permute-start | bytes 208904 | tf_op jit(solution)/shard_map/ppermute | solution.py:306
  (1 other events, 1.8 us)

commit v12 on v11

--- a/solution.py
+++ b/solution.py
@@ -124,7 +124,7 @@
         around(s, w_ref, o_ref, x, True, True, emit)
         return 0
 
-    lax.fori_loop(1, s.x - 1, step, 0, unroll=2)
+    lax.fori_loop(1, s.x - 1, step, 0, unroll=5)
     around(s, w_ref, o_ref, s.x - 1, True, False, emit)
 
 

time: 78.8 us -> 78.7 us (level)
  no operation moved by 1% of the time
where the time goes in v12:
time: 78.7 us; the launch traced here: 78.3 us
  starting transfers between devices  47.7 us (61%)
  Pallas kernels  15.1 us (19%)
  waiting for transfers between devices  12.8 us (16%)
  local copies, waits for them, and re-layouts  1.77 us (2%)
  between operations  0.89 us (1%)
    ppermute x25, starting transfers between devices, exchange(): got.append(lax.ppermute(face, axis, pairs))  37.1 us
    ppermute x7, starting transfers between devices, swap(): return lax.ppermute(value, axes, pairs)  10.6 us
    ppermute x7, waiting for transfers between devices, swap(): return lax.ppermute(value, axes, pairs)  9.08 us
    pallas_call x10, Pallas kernels, call(): pl.pallas_call(body, out_shape=outs, in_specs=[VMEM] * len(ins), out_spec...  7.51 us
    pallas_call x1, Pallas kernels, orthonormal(): pl.pallas_call(body, out_shape=[f32(s.cells, k), f32(k, k)], in_specs=[VM...  5.44 us
    ppermute x25, waiting for transfers between devices, exchange(): got.append(lax.ppermute(face, axis, pairs))  3.76 us
    pallas_call x1, Pallas kernels, gather_terms(): pl.pallas_call(body, out_shape=outs, in_specs=[VMEM, VMEM], out_specs=(VM...  2.12 us
    slice x1, local copies, waits for them, and re-layouts, prepare(): block[i * each * s.row:(i + 1) * each * s.row]  1.76 us
  transfers between devices with their start and end apart: 32, of which 13 were waited for; matrix products, arithmetic and copies ran while one was open for 0% of the time, Pallas kernels for 9%

profile of v12, /device:TPU:0, one launch (start us, length us, event | category | flops | bytes accessed | tf_op | source)
XLA Modules:
  0.0 78.3 jit_solution(1678587001059662466)
XLA Ops:
  0.6 1.8 %fusion = (f32[8,16,8,128]{3,2,1,0:T(8,128)S(1)}, f32[8,16,8,128]{3,2,1,0:T(8,128)S(1)}, f32[8,16,8,128]{3,2,1,0:T(8,128)S(1)}, f32[8,16,8,128]{3,2,1,0:T(8,128)S(1)}) fusion(f32[32,16,8,128]{3,2,1,0:T(8,128)} %param.2), kind=kLoop, calls=%fused_computation.2 | loop fusion | bytes 4194304 | tf_op jit(solution)/shard_map/slice | solution.py:92
  2.4 1.1 %shard_map.41 = (f32[4104,128]{1,0:T(8,128)S(1)}, f32[4104,128]{1,0:T(8,128)S(1)}, f32[128,128]{1,0:T(8,128)S(1)}, f32[128,128]{1,0:T(8,128)S(1)}, f32[256,128]{...) custom-call(f32[16,8,32]{2,1,0:T(8,128)S(1)} %bitcast.10, ...), custom_call_target="tpu_custom_call" | custom-call | flops 2097152 | bytes 7233536 | tf_op jit(solution)/shard_map/pallas_call | solution.py:20
  3.5 3.0 %collective-permute-start.4 = (f32[512,128]{1,0:T(8,128)S(1)}, f32[512,128]{1,0:T(8,128)S(1)}, u32[]{:S(2)}, u32[]{:S(2)}) collective-permute-start(f32[512,128]{1,0:T(8,128)S(1)} %get-tuple-element.46), channel_id=1, source_target_pairs={{0,1},{1,0},{2,3},{3,2},{4,5},{5,4},{6,7},{7,6},{8,9},{9,8},{10,11... | collective-permute-start | bytes 786440 | tf_op jit(solution)/shard_map/ppermute | solution.py:204
  7.2 1.6 %collective-permute-start = (f32[128,128]{1,0:T(8,128)S(1)}, f32[128,128]{1,0:T(8,128)S(1)}, u32[]{:S(2)}, u32[]{:S(2)}) collective-permute-start(f32[128,128]{1,0:T(8,128)S(1)} %get-tuple-element.42), channel_id=1, source_target_pairs={{0,8},{8,0},{16,24},{24,16},{1,9},{9,1},{17,25},{25,17},{2,10},{10... | collective-permute-start | bytes 196616 | tf_op jit(solution)/shard_map/ppermute | solution.py:204
  9.5 1.1 %shard_map.42.p_ref = f32[4104,128]{1,0:T(8,128)S(1)} custom-call(f32[4104,128]{1,0:T(8,128)S(1)} %get-tuple-element.39.w_ref.rest_0_, f32[4104,128]{1,0:T(8,128)S(1)} %get-tuple-element.40.k_ref), custom_call_target="tpu_custom_call" | custom-call | flops 6291456 | bytes 6303744 | tf_op jit(solution)/shard_map/pallas_call | solution.py:20
  10.6 0.9 %collective-permute-done.refs_1_ = f32[128,128]{1,0:T(8,128)S(1)} collective-permute-done((f32[128,128]{1,0:T(8,128)S(1)}, f32[128,128]{1,0:T(8,128)S(1)}, u32[]{:S(2)}, u32[]{:S(2)}) %collective-permute-start) | collective-permute-done | bytes 65568 | tf_op jit(solution)/shard_map/ppermute | solution.py:204
  11.6 1.3 %collective-permute-done.4.refs_5_ = f32[512,128]{1,0:T(8,128)S(1)} collective-permute-done((f32[512,128]{1,0:T(8,128)S(1)}, f32[512,128]{1,0:T(8,128)S(1)}, u32[]{:S(2)}, u32[]{:S(2)}) %collective-permute-start.4) | collective-permute-done | bytes 262176 | tf_op jit(solution)/shard_map/ppermute | solution.py:204
  13.1 1.8 %collective-permute-start.9 = (f32[512,128]{1,0:T(8,128)S(1)}, f32[512,128]{1,0:T(8,128)S(1)}, u32[]{:S(2)}, u32[]{:S(2)}) collective-permute-start(f32[512,128]{1,0:T(8,128)S(1)} %get-tuple-element.52), channel_id=1, source_target_pairs={{0,1},{1,0},{2,3},{3,2},{4,5},{5,4},{6,7},{7,6},{8,9},{9,8},{10,11... | collective-permute-start | bytes 786440 | tf_op jit(solution)/shard_map/ppermute | solution.py:204
  15.6 3.6 %collective-permute-start.5 = (f32[128,128]{1,0:T(8,128)S(1)}, f32[128,128]{1,0:T(8,128)S(1)}, u32[]{:S(2)}, u32[]{:S(2)}) collective-permute-start(f32[128,128]{1,0:T(8,128)S(1)} %get-tuple-element.48), channel_id=1, source_target_pairs={{0,8},{8,0},{16,24},{24,16},{1,9},{9,1},{17,25},{25,17},{2,10},{10... | collective-permute-start | bytes 196616 | tf_op jit(solution)/shard_map/ppermute | solution.py:204
  19.9 1.2 %shard_map.44.p_ref = f32[4104,128]{1,0:T(8,128)S(1)} custom-call(f32[4104,128]{1,0:T(8,128)S(1)} %get-tuple-element.47.w_ref.rest_0_, f32[4104,128]{1,0:T(8,128)S(1)} %get-tuple-element.40.k_ref, f32[4104,128]{1,0:T(8,128)S(1)} %get-tuple-element.39.w_ref.rest_0_), custom_call_target="tpu_custom_call" | custom-call | flops 6291456 | bytes 8404992 | tf_op jit(solution)/shard_map/pallas_call | solution.py:20
  22.2 1.2 %collective-permute-start.14 = (f32[512,128]{1,0:T(8,128)S(1)}, f32[512,128]{1,0:T(8,128)S(1)}, u32[]{:S(2)}, u32[]{:S(2)}) collective-permute-start(f32[512,128]{1,0:T(8,128)S(1)} %get-tuple-element.58), channel_id=1, source_target_pairs={{0,1},{1,0},{2,3},{3,2},{4,5},{5,4},{6,7},{7,6},{8,9},{9,8},{10,11... | collective-permute-start | bytes 786440 | tf_op jit(solution)/shard_map/ppermute | solution.py:204
  23.4 2.4 %collective-permute-start.12 = (f32[256,128]{1,0:T(8,128)S(1)}, f32[256,128]{1,0:T(8,128)S(1)}, u32[]{:S(2)}, u32[]{:S(2)}) collective-permute-start(f32[256,128]{1,0:T(8,128)S(1)} %get-tuple-element.56), channel_id=1, source_target_pairs={{0,2},{2,0},{4,6},{6,4},{1,3},{3,1},{5,7},{7,5},{8,10},{10,8},{12,... | collective-permute-start | bytes 393224 | tf_op jit(solution)/shard_map/ppermute | solution.py:204
  26.4 3.7 %collective-permute-start.10 = (f32[128,128]{1,0:T(8,128)S(1)}, f32[128,128]{1,0:T(8,128)S(1)}, u32[]{:S(2)}, u32[]{:S(2)}) collective-permute-start(f32[128,128]{1,0:T(8,128)S(1)} %get-tuple-element.54), channel_id=1, source_target_pairs={{0,8},{8,0},{16,24},{24,16},{1,9},{9,1},{17,25},{25,17},{2,10},{10... | collective-permute-start | bytes 196616 | tf_op jit(solution)/shard_map/ppermute | solution.py:204
  30.8 1.3 %shard_map.46.p_ref = f32[4104,128]{1,0:T(8,128)S(1)} custom-call(f32[4104,128]{1,0:T(8,128)S(1)} %get-tuple-element.53.w_ref.rest_0_, f32[4104,128]{1,0:T(8,128)S(1)} %get-tuple-element.40.k_ref, f32[4104,128]{1,0:T(8,128)S(1)} %get-tuple-element.47.w_ref.rest_0_), custom_call_target="tpu_custom_call" | custom-call | flops 6291456 | bytes 8404992 | tf_op jit(solution)/shard_map/pallas_call | solution.py:20
  33.3 1.6 %collective-permute-start.17 = (f32[256,128]{1,0:T(8,128)S(1)}, f32[256,128]{1,0:T(8,128)S(1)}, u32[]{:S(2)}, u32[]{:S(2)}) collective-permute-start(f32[256,128]{1,0:T(8,128)S(1)} %get-tuple-element.62), channel_id=1, source_target_pairs={{0,2},{2,0},{4,6},{6,4},{1,3},{3,1},{5,7},{7,5},{8,10},{10,8},{12,... | collective-permute-start | bytes 393224 | tf_op jit(solution)/shard_map/ppermute | solution.py:204
  35.6 3.6 %collective-permute-start.15 = (f32[128,128]{1,0:T(8,128)S(1)}, f32[128,128]{1,0:T(8,128)S(1)}, u32[]{:S(2)}, u32[]{:S(2)}) collective-permute-start(f32[128,128]{1,0:T(8,128)S(1)} %get-tuple-element.60), channel_id=1, source_target_pairs={{0,8},{8,0},{16,24},{24,16},{1,9},{9,1},{17,25},{25,17},{2,10},{10... | collective-permute-start | bytes 196616 | tf_op jit(solution)/shard_map/ppermute | solution.py:204
  39.9 1.2 %shard_map.48.p_ref = f32[4104,128]{1,0:T(8,128)S(1)} custom-call(f32[4104,128]{1,0:T(8,128)S(1)} %get-tuple-element.59.w_ref, f32[4104,128]{1,0:T(8,128)S(1)} %get-tuple-element.40.k_ref, f32[4104,128]{1,0:T(8,128)S(1)} %get-tuple-element.53.w_ref.rest_0_), custom_call_target="tpu_custom_call" | custom-call | flops 6291456 | bytes 8404992 | tf_op jit(solution)/shard_map/pallas_call | solution.py:20
  41.8 2.4 %collective-permute-start.22 = (f32[256,128]{1,0:T(8,128)S(1)}, f32[256,128]{1,0:T(8,128)S(1)}, u32[]{:S(2)}, u32[]{:S(2)}) collective-permute-start(f32[256,128]{1,0:T(8,128)S(1)} %get-tuple-element.70), channel_id=1, source_target_pairs={{0,2},{2,0},{4,6},{6,4},{1,3},{3,1},{5,7},{7,5},{8,10},{10,8},{12,... | collective-permute-start | bytes 393224 | tf_op jit(solution)/shard_map/ppermute | solution.py:204
  44.8 1.6 %collective-permute-start.24 = (f32[256,128]{1,0:T(8,128)S(1)}, f32[256,128]{1,0:T(8,128)S(1)}, u32[]{:S(2)}, u32[]{:S(2)}) collective-permute-start(f32[256,128]{1,0:T(8,128)S(1)} %get-tuple-element.72), channel_id=1, source_target_pairs={{0,1},{1,0},{2,3},{3,2},{4,5},{5,4},{6,7},{7,6},{8,9},{9,8},{10,11... | collective-permute-start | bytes 393224 | tf_op jit(solution)/shard_map/ppermute | solution.py:204
  46.4 3.4 %collective-permute-start.20 = (f32[128,128]{1,0:T(8,128)S(1)}, f32[128,128]{1,0:T(8,128)S(1)}, u32[]{:S(2)}, u32[]{:S(2)}) collective-permute-start(f32[128,128]{1,0:T(8,128)S(1)} %get-tuple-element.68), channel_id=1, source_target_pairs={{0,8},{8,0},{16,24},{24,16},{1,9},{9,1},{17,25},{25,17},{2,10},{10... | collective-permute-start | bytes 196616 | tf_op jit(solution)/shard_map/ppermute | solution.py:204
  50.5 2.1 %shard_map.50 = (bf16[4096,256]{1,0:T(8,128)(2,1)S(1)}, f32[128,128]{1,0:T(8,128)S(1)}, f32[128,128]{1,0:T(8,128)S(1)}) custom-call(f32[4104,128]{1,0:T(8,128)S(1)} %get-tuple-element.65.w_ref, f32[4104,128]{1,0:T(8,128)S(1)} %get-tuple-element.40.k_ref), custom_call_target="tpu_custom_call" | custom-call | flops 1073741824 | bytes 8388608 | tf_op jit(solution)/shard_map/pallas_call | solution.py:247
  53.1 1.9 %collective-permute-start.25 = (f32[136,128]{1,0:T(8,128)S(1)}, f32[136,128]{1,0:T(8,128)S(1)}, u32[]{:S(2)}, u32[]{:S(2)}) collective-permute-start(f32[136,128]{1,0:T(8,128)S(1)} %shard_map.51), channel_id=1, source_target_pairs={{0,2},{1,3},{2,0},{3,1},{4,6},{5,7},{6,4},{7,5},{8,10},{9,11},{10,... | collective-permute-start | bytes 208904 | tf_op jit(solution)/shard_map/ppermute | solution.py:306
  55.1 0.9 %collective-permute-done.25 = f32[136,128]{1,0:T(8,128)S(1)} collective-permute-done((f32[136,128]{1,0:T(8,128)S(1)}, f32[136,128]{1,0:T(8,128)S(1)}, u32[]{:S(2)}, u32[]{:S(2)}) %collective-permute-start.25) | collective-permute-done | bytes 69664 | tf_op jit(solution)/shard_map/ppermute | solution.py:306
  56.0 1.4 %collective-permute-start.28 = (f32[136,128]{1,0:T(8,128)S(1)}, f32[136,128]{1,0:T(8,128)S(1)}, u32[]{:S(2)}, u32[]{:S(2)}) collective-permute-start(f32[136,128]{1,0:T(8,128)S(1)} %add.21), channel_id=1, source_target_pairs={{0,5},{1,4},{2,7},{3,6},{4,1},{5,0},{6,3},{7,2},{8,13},{9,12},{10,... | collective-permute-start | bytes 208904 | tf_op jit(solution)/shard_map/ppermute | solution.py:306
  57.4 1.5 %collective-permute-start.27 = (f32[136,128]{1,0:T(8,128)S(1)}, f32[136,128]{1,0:T(8,128)S(1)}, u32[]{:S(2)}, u32[]{:S(2)}) collective-permute-start(f32[136,128]{1,0:T(8,128)S(1)} %add.21), channel_id=1, source_target_pairs={{0,1},{1,0},{2,3},{3,2},{4,5},{5,4},{6,7},{7,6},{8,9},{9,8},{10,11... | collective-permute-start | bytes 208904 | tf_op jit(solution)/shard_map/ppermute | solution.py:306
  59.6 2.4 %collective-permute-done.28 = f32[136,128]{1,0:T(8,128)S(1)} collective-permute-done((f32[136,128]{1,0:T(8,128)S(1)}, f32[136,128]{1,0:T(8,128)S(1)}, u32[]{:S(2)}, u32[]{:S(2)}) %collective-permute-start.28) | collective-permute-done | bytes 69664 | tf_op jit(solution)/shard_map/ppermute | solution.py:306
  63.2 2.7 %collective-permute-start.31 = (f32[136,128]{1,0:T(8,128)S(1)}, f32[136,128]{1,0:T(8,128)S(1)}, u32[]{:S(2)}, u32[]{:S(2)}) collective-permute-start(f32[136,128]{1,0:T(8,128)S(1)} %add_add_fusion.1), channel_id=1, source_target_pairs={{0,24},{1,25},{2,26},{3,27},{4,28},{5,29},{6,30},{7,31},{8,16},{9,... | collective-permute-start | bytes 208904 | tf_op jit(solution)/shard_map/ppermute | solution.py:306
  66.0 2.1 %collective-permute-start.30 = (f32[136,128]{1,0:T(8,128)S(1)}, f32[136,128]{1,0:T(8,128)S(1)}, u32[]{:S(2)}, u32[]{:S(2)}) collective-permute-start(f32[136,128]{1,0:T(8,128)S(1)} %add_add_fusion.1), channel_id=1, source_target_pairs={{0,16},{1,17},{2,18},{3,19},{4,20},{5,21},{6,22},{7,23},{8,24},{9,... | collective-permute-start | bytes 208904 | tf_op jit(solution)/shard_map/ppermute | solution.py:306
  68.4 1.2 %collective-permute-done.31 = f32[136,128]{1,0:T(8,128)S(1)} collective-permute-done((f32[136,128]{1,0:T(8,128)S(1)}, f32[136,128]{1,0:T(8,128)S(1)}, u32[]{:S(2)}, u32[]{:S(2)}) %collective-permute-start.31) | collective-permute-done | bytes 69664 | tf_op jit(solution)/shard_map/ppermute | solution.py:306
  69.5 2.6 %collective-permute-done.30 = f32[136,128]{1,0:T(8,128)S(1)} collective-permute-done((f32[136,128]{1,0:T(8,128)S(1)}, f32[136,128]{1,0:T(8,128)S(1)}, u32[]{:S(2)}, u32[]{:S(2)}) %collective-permute-start.30) | collective-permute-done | bytes 69664 | tf_op jit(solution)/shard_map/ppermute | solution.py:306
  72.2 0.7 collective-permute-done.29
  72.9 5.4 %shard_map.52 = (f32[4096,128]{1,0:T(8,128)}, f32[128,128]{1,0:T(8,128)}) custom-call(f32[136,128]{1,0:T(8,128)S(1)} %add_add_fusion.p_ref, bf16[4096,256]{1,0:T(8,128)(2,1)S(1)} %get-tuple-element.73.f_ref), custom_call_target="tpu_custom_call" | custom-call | flops 536870912 | bytes 4194304 | tf_op jit(solution)/shard_map/pallas_call | solution.py:396
  (50 shorter events, 12.5 us)
Async XLA Ops:
  3.5 9.3 %collective-permute-start.4 = (f32[512,128]{1,0:T(8,128)S(1)}, f32[512,128]{1,0:T(8,128)S(1)}, u32[]{:S(2)}, u32[]{:S(2)}) collective-permute-start(f32[512,128]{1,0:T(8,128)S(1)} %get-tuple-element.46), channel_id=1, source_target_pairs={{0,1},{1,0},{2,3},{3,2},{4,5},{5,4},{6,7},{7,6},{8,9},{9,8},{10,11... | collective-permute-start | bytes 786440 | tf_op jit(solution)/shard_map/ppermute | solution.py:204
  6.5 5.0 %collective-permute-start.2 = (f32[256,128]{1,0:T(8,128)S(1)}, f32[256,128]{1,0:T(8,128)S(1)}, u32[]{:S(2)}, u32[]{:S(2)}) collective-permute-start(f32[256,128]{1,0:T(8,128)S(1)} %get-tuple-element.44), channel_id=1, source_target_pairs={{0,2},{2,0},{4,6},{6,4},{1,3},{3,1},{5,7},{7,5},{8,10},{10,8},{12,... | collective-permute-start | bytes 393224 | tf_op jit(solution)/shard_map/ppermute | solution.py:204
  6.5 5.0 %collective-permute-start.3 = (f32[256,128]{1,0:T(8,128)S(1)}, f32[256,128]{1,0:T(8,128)S(1)}, u32[]{:S(2)}, u32[]{:S(2)}) collective-permute-start(f32[256,128]{1,0:T(8,128)S(1)} %get-tuple-element.45), channel_id=1, source_target_pairs={{2,4},{4,2},{3,5},{5,3},{10,12},{12,10},{11,13},{13,11},{18,20},{2... | collective-permute-start | bytes 393224 | tf_op jit(solution)/shard_map/ppermute | solution.py:204
  7.2 4.3 %collective-permute-start = (f32[128,128]{1,0:T(8,128)S(1)}, f32[128,128]{1,0:T(8,128)S(1)}, u32[]{:S(2)}, u32[]{:S(2)}) collective-permute-start(f32[128,128]{1,0:T(8,128)S(1)} %get-tuple-element.42), channel_id=1, source_target_pairs={{0,8},{8,0},{16,24},{24,16},{1,9},{9,1},{17,25},{25,17},{2,10},{10... | collective-permute-start | bytes 196616 | tf_op jit(solution)/shard_map/ppermute | solution.py:204
  8.9 2.7 %collective-permute-start.1 = (f32[128,128]{1,0:T(8,128)S(1)}, f32[128,128]{1,0:T(8,128)S(1)}, u32[]{:S(2)}, u32[]{:S(2)}) collective-permute-start(f32[128,128]{1,0:T(8,128)S(1)} %get-tuple-element.43), channel_id=1, source_target_pairs={{8,16},{16,8},{9,17},{17,9},{10,18},{18,10},{11,19},{19,11},{12,20... | collective-permute-start | bytes 196616 | tf_op jit(solution)/shard_map/ppermute | solution.py:204
  13.1 8.8 %collective-permute-start.9 = (f32[512,128]{1,0:T(8,128)S(1)}, f32[512,128]{1,0:T(8,128)S(1)}, u32[]{:S(2)}, u32[]{:S(2)}) collective-permute-start(f32[512,128]{1,0:T(8,128)S(1)} %get-tuple-element.52), channel_id=1, source_target_pairs={{0,1},{1,0},{2,3},{3,2},{4,5},{5,4},{6,7},{7,6},{8,9},{9,8},{10,11... | collective-permute-start | bytes 786440 | tf_op jit(solution)/shard_map/ppermute | solution.py:204
  14.9 6.5 %collective-permute-start.7 = (f32[256,128]{1,0:T(8,128)S(1)}, f32[256,128]{1,0:T(8,128)S(1)}, u32[]{:S(2)}, u32[]{:S(2)}) collective-permute-start(f32[256,128]{1,0:T(8,128)S(1)} %get-tuple-element.50), channel_id=1, source_target_pairs={{0,2},{2,0},{4,6},{6,4},{1,3},{3,1},{5,7},{7,5},{8,10},{10,8},{12,... | collective-permute-start | bytes 393224 | tf_op jit(solution)/shard_map/ppermute | solution.py:204
  14.9 6.5 %collective-permute-start.8 = (f32[256,128]{1,0:T(8,128)S(1)}, f32[256,128]{1,0:T(8,128)S(1)}, u32[]{:S(2)}, u32[]{:S(2)}) collective-permute-start(f32[256,128]{1,0:T(8,128)S(1)} %get-tuple-element.51), channel_id=1, source_target_pairs={{2,4},{4,2},{3,5},{5,3},{10,12},{12,10},{11,13},{13,11},{18,20},{2... | collective-permute-start | bytes 393224 | tf_op jit(solution)/shard_map/ppermute | solution.py:204
  15.6 5.9 %collective-permute-start.5 = (f32[128,128]{1,0:T(8,128)S(1)}, f32[128,128]{1,0:T(8,128)S(1)}, u32[]{:S(2)}, u32[]{:S(2)}) collective-permute-start(f32[128,128]{1,0:T(8,128)S(1)} %get-tuple-element.48), channel_id=1, source_target_pairs={{0,8},{8,0},{16,24},{24,16},{1,9},{9,1},{17,25},{25,17},{2,10},{10... | collective-permute-start | bytes 196616 | tf_op jit(solution)/shard_map/ppermute | solution.py:204
  19.2 2.2 %collective-permute-start.6 = (f32[128,128]{1,0:T(8,128)S(1)}, f32[128,128]{1,0:T(8,128)S(1)}, u32[]{:S(2)}, u32[]{:S(2)}) collective-permute-start(f32[128,128]{1,0:T(8,128)S(1)} %get-tuple-element.49), channel_id=1, source_target_pairs={{8,16},{16,8},{9,17},{17,9},{10,18},{18,10},{11,19},{19,11},{12,20... | collective-permute-start | bytes 196616 | tf_op jit(solution)/shard_map/ppermute | solution.py:204
  22.2 10.2 %collective-permute-start.14 = (f32[512,128]{1,0:T(8,128)S(1)}, f32[512,128]{1,0:T(8,128)S(1)}, u32[]{:S(2)}, u32[]{:S(2)}) collective-permute-start(f32[512,128]{1,0:T(8,128)S(1)} %get-tuple-element.58), channel_id=1, source_target_pairs={{0,1},{1,0},{2,3},{3,2},{4,5},{5,4},{6,7},{7,6},{8,9},{9,8},{10,11... | collective-permute-start | bytes 786440 | tf_op jit(solution)/shard_map/ppermute | solution.py:204
  23.4 9.0 %collective-permute-start.12 = (f32[256,128]{1,0:T(8,128)S(1)}, f32[256,128]{1,0:T(8,128)S(1)}, u32[]{:S(2)}, u32[]{:S(2)}) collective-permute-start(f32[256,128]{1,0:T(8,128)S(1)} %get-tuple-element.56), channel_id=1, source_target_pairs={{0,2},{2,0},{4,6},{6,4},{1,3},{3,1},{5,7},{7,5},{8,10},{10,8},{12,... | collective-permute-start | bytes 393224 | tf_op jit(solution)/shard_map/ppermute | solution.py:204
  25.8 6.6 %collective-permute-start.13 = (f32[256,128]{1,0:T(8,128)S(1)}, f32[256,128]{1,0:T(8,128)S(1)}, u32[]{:S(2)}, u32[]{:S(2)}) collective-permute-start(f32[256,128]{1,0:T(8,128)S(1)} %get-tuple-element.57), channel_id=1, source_target_pairs={{2,4},{4,2},{3,5},{5,3},{10,12},{12,10},{11,13},{13,11},{18,20},{2... | collective-permute-start | bytes 393224 | tf_op jit(solution)/shard_map/ppermute | solution.py:204
  26.4 6.0 %collective-permute-start.10 = (f32[128,128]{1,0:T(8,128)S(1)}, f32[128,128]{1,0:T(8,128)S(1)}, u32[]{:S(2)}, u32[]{:S(2)}) collective-permute-start(f32[128,128]{1,0:T(8,128)S(1)} %get-tuple-element.54), channel_id=1, source_target_pairs={{0,8},{8,0},{16,24},{24,16},{1,9},{9,1},{17,25},{25,17},{2,10},{10... | collective-permute-start | bytes 196616 | tf_op jit(solution)/shard_map/ppermute | solution.py:204
  30.2 2.2 %collective-permute-start.11 = (f32[128,128]{1,0:T(8,128)S(1)}, f32[128,128]{1,0:T(8,128)S(1)}, u32[]{:S(2)}, u32[]{:S(2)}) collective-permute-start(f32[128,128]{1,0:T(8,128)S(1)} %get-tuple-element.55), channel_id=1, source_target_pairs={{8,16},{16,8},{9,17},{17,9},{10,18},{18,10},{11,19},{19,11},{12,20... | collective-permute-start | bytes 196616 | tf_op jit(solution)/shard_map/ppermute | solution.py:204
  32.7 8.8 %collective-permute-start.19 = (f32[512,128]{1,0:T(8,128)S(1)}, f32[512,128]{1,0:T(8,128)S(1)}, u32[]{:S(2)}, u32[]{:S(2)}) collective-permute-start(f32[512,128]{1,0:T(8,128)S(1)} %get-tuple-element.64), channel_id=1, source_target_pairs={{0,1},{1,0},{2,3},{3,2},{4,5},{5,4},{6,7},{7,6},{8,9},{9,8},{10,11... | collective-permute-start | bytes 786440 | tf_op jit(solution)/shard_map/ppermute | solution.py:204
  33.3 8.2 %collective-permute-start.17 = (f32[256,128]{1,0:T(8,128)S(1)}, f32[256,128]{1,0:T(8,128)S(1)}, u32[]{:S(2)}, u32[]{:S(2)}) collective-permute-start(f32[256,128]{1,0:T(8,128)S(1)} %get-tuple-element.62), channel_id=1, source_target_pairs={{0,2},{2,0},{4,6},{6,4},{1,3},{3,1},{5,7},{7,5},{8,10},{10,8},{12,... | collective-permute-start | bytes 393224 | tf_op jit(solution)/shard_map/ppermute | solution.py:204
  34.9 6.6 %collective-permute-start.18 = (f32[256,128]{1,0:T(8,128)S(1)}, f32[256,128]{1,0:T(8,128)S(1)}, u32[]{:S(2)}, u32[]{:S(2)}) collective-permute-start(f32[256,128]{1,0:T(8,128)S(1)} %get-tuple-element.63), channel_id=1, source_target_pairs={{2,4},{4,2},{3,5},{5,3},{10,12},{12,10},{11,13},{13,11},{18,20},{2... | collective-permute-start | bytes 393224 | tf_op jit(solution)/shard_map/ppermute | solution.py:204
  35.6 5.9 %collective-permute-start.15 = (f32[128,128]{1,0:T(8,128)S(1)}, f32[128,128]{1,0:T(8,128)S(1)}, u32[]{:S(2)}, u32[]{:S(2)}) collective-permute-start(f32[128,128]{1,0:T(8,128)S(1)} %get-tuple-element.60), channel_id=1, source_target_pairs={{0,8},{8,0},{16,24},{24,16},{1,9},{9,1},{17,25},{25,17},{2,10},{10... | collective-permute-start | bytes 196616 | tf_op jit(solution)/shard_map/ppermute | solution.py:204
  39.2 2.2 %collective-permute-start.16 = (f32[128,128]{1,0:T(8,128)S(1)}, f32[128,128]{1,0:T(8,128)S(1)}, u32[]{:S(2)}, u32[]{:S(2)}) collective-permute-start(f32[128,128]{1,0:T(8,128)S(1)} %get-tuple-element.61), channel_id=1, source_target_pairs={{8,16},{16,8},{9,17},{17,9},{10,18},{18,10},{11,19},{19,11},{12,20... | collective-permute-start | bytes 196616 | tf_op jit(solution)/shard_map/ppermute | solution.py:204
  41.8 10.8 %collective-permute-start.22 = (f32[256,128]{1,0:T(8,128)S(1)}, f32[256,128]{1,0:T(8,128)S(1)}, u32[]{:S(2)}, u32[]{:S(2)}) collective-permute-start(f32[256,128]{1,0:T(8,128)S(1)} %get-tuple-element.70), channel_id=1, source_target_pairs={{0,2},{2,0},{4,6},{6,4},{1,3},{3,1},{5,7},{7,5},{8,10},{10,8},{12,... | collective-permute-start | bytes 393224 | tf_op jit(solution)/shard_map/ppermute | solution.py:204
  44.2 8.5 %collective-permute-start.23 = (f32[256,128]{1,0:T(8,128)S(1)}, f32[256,128]{1,0:T(8,128)S(1)}, u32[]{:S(2)}, u32[]{:S(2)}) collective-permute-start(f32[256,128]{1,0:T(8,128)S(1)} %get-tuple-element.71), channel_id=1, source_target_pairs={{2,4},{4,2},{3,5},{5,3},{10,12},{12,10},{11,13},{13,11},{18,20},{2... | collective-permute-start | bytes 393224 | tf_op jit(solution)/shard_map/ppermute | solution.py:204
  44.8 7.8 %collective-permute-start.24 = (f32[256,128]{1,0:T(8,128)S(1)}, f32[256,128]{1,0:T(8,128)S(1)}, u32[]{:S(2)}, u32[]{:S(2)}) collective-permute-start(f32[256,128]{1,0:T(8,128)S(1)} %get-tuple-element.72), channel_id=1, source_target_pairs={{0,1},{1,0},{2,3},{3,2},{4,5},{5,4},{6,7},{7,6},{8,9},{9,8},{10,11... | collective-permute-start | bytes 393224 | tf_op jit(solution)/shard_map/ppermute | solution.py:204
  46.4 6.2 %collective-permute-start.20 = (f32[128,128]{1,0:T(8,128)S(1)}, f32[128,128]{1,0:T(8,128)S(1)}, u32[]{:S(2)}, u32[]{:S(2)}) collective-permute-start(f32[128,128]{1,0:T(8,128)S(1)} %get-tuple-element.68), channel_id=1, source_target_pairs={{0,8},{8,0},{16,24},{24,16},{1,9},{9,1},{17,25},{25,17},{2,10},{10... | collective-permute-start | bytes 196616 | tf_op jit(solution)/shard_map/ppermute | solution.py:204
  49.8 2.8 %collective-permute-start.21 = (f32[128,128]{1,0:T(8,128)S(1)}, f32[128,128]{1,0:T(8,128)S(1)}, u32[]{:S(2)}, u32[]{:S(2)}) collective-permute-start(f32[128,128]{1,0:T(8,128)S(1)} %get-tuple-element.69), channel_id=1, source_target_pairs={{8,16},{16,8},{9,17},{17,9},{10,18},{18,10},{11,19},{19,11},{12,20... | collective-permute-start | bytes 196616 | tf_op jit(solution)/shard_map/ppermute | solution.py:204
  53.1 2.8 %collective-permute-start.25 = (f32[136,128]{1,0:T(8,128)S(1)}, f32[136,128]{1,0:T(8,128)S(1)}, u32[]{:S(2)}, u32[]{:S(2)}) collective-permute-start(f32[136,128]{1,0:T(8,128)S(1)} %shard_map.51), channel_id=1, source_target_pairs={{0,2},{1,3},{2,0},{3,1},{4,6},{5,7},{6,4},{7,5},{8,10},{9,11},{10,... | collective-permute-start | bytes 208904 | tf_op jit(solution)/shard_map/ppermute | solution.py:306
  56.0 6.0 %collective-permute-start.28 = (f32[136,128]{1,0:T(8,128)S(1)}, f32[136,128]{1,0:T(8,128)S(1)}, u32[]{:S(2)}, u32[]{:S(2)}) collective-permute-start(f32[136,128]{1,0:T(8,128)S(1)} %add.21), channel_id=1, source_target_pairs={{0,5},{1,4},{2,7},{3,6},{4,1},{5,0},{6,3},{7,2},{8,13},{9,12},{10,... | collective-permute-start | bytes 208904 | tf_op jit(solution)/shard_map/ppermute | solution.py:306
  57.4 5.2 %collective-permute-start.27 = (f32[136,128]{1,0:T(8,128)S(1)}, f32[136,128]{1,0:T(8,128)S(1)}, u32[]{:S(2)}, u32[]{:S(2)}) collective-permute-start(f32[136,128]{1,0:T(8,128)S(1)} %add.21), channel_id=1, source_target_pairs={{0,1},{1,0},{2,3},{3,2},{4,5},{5,4},{6,7},{7,6},{8,9},{9,8},{10,11... | collective-permute-start | bytes 208904 | tf_op jit(solution)/shard_map/ppermute | solution.py:306
  58.9 4.3 %collective-permute-start.26 = (f32[136,128]{1,0:T(8,128)S(1)}, f32[136,128]{1,0:T(8,128)S(1)}, u32[]{:S(2)}, u32[]{:S(2)}) collective-permute-start(f32[136,128]{1,0:T(8,128)S(1)} %add.21), channel_id=1, source_target_pairs={{0,4},{1,5},{2,6},{3,7},{4,0},{5,1},{6,2},{7,3},{8,12},{9,13},{10,... | collective-permute-start | bytes 208904 | tf_op jit(solution)/shard_map/ppermute | solution.py:306
  63.2 6.3 %collective-permute-start.31 = (f32[136,128]{1,0:T(8,128)S(1)}, f32[136,128]{1,0:T(8,128)S(1)}, u32[]{:S(2)}, u32[]{:S(2)}) collective-permute-start(f32[136,128]{1,0:T(8,128)S(1)} %add_add_fusion.1), channel_id=1, source_target_pairs={{0,24},{1,25},{2,26},{3,27},{4,28},{5,29},{6,30},{7,31},{8,16},{9,... | collective-permute-start | bytes 208904 | tf_op jit(solution)/shard_map/ppermute | solution.py:306
  66.0 6.2 %collective-permute-start.30 = (f32[136,128]{1,0:T(8,128)S(1)}, f32[136,128]{1,0:T(8,128)S(1)}, u32[]{:S(2)}, u32[]{:S(2)}) collective-permute-start(f32[136,128]{1,0:T(8,128)S(1)} %add_add_fusion.1), channel_id=1, source_target_pairs={{0,16},{1,17},{2,18},{3,19},{4,20},{5,21},{6,22},{7,23},{8,24},{9,... | collective-permute-start | bytes 208904 | tf_op jit(solution)/shard_map/ppermute | solution.py:306
  68.1 4.8 %collective-permute-start.29 = (f32[136,128]{1,0:T(8,128)S(1)}, f32[136,128]{1,0:T(8,128)S(1)}, u32[]{:S(2)}, u32[]{:S(2)}) collective-permute-start(f32[136,128]{1,0:T(8,128)S(1)} %add_add_fusion.1), channel_id=1, source_target_pairs={{0,8},{1,9},{2,10},{3,11},{4,12},{5,13},{6,14},{7,15},{8,0},{9,1},... | collective-permute-start | bytes 208904 | tf_op jit(solution)/shard_map/ppermute | solution.py:306
  (1 other events, 1.8 us)

commit v13 on v11

--- a/solution.py
+++ b/solution.py
@@ -70,7 +70,7 @@
 
 
 def prepare(block, turned, s, nz):
-    parts = 4
+    parts = 2
     each = s.x // parts
 
     def body(k_ref, *all_refs):

time: 78.8 us -> 78.8 us (level)
  no operation moved by 1% of the time
where the time goes in v13:
time: 78.8 us; the launch traced here: 78.4 us
  starting transfers between devices  47.7 us (61%)
  Pallas kernels  15.3 us (19%)
  waiting for transfers between devices  12.7 us (16%)
  local copies, waits for them, and re-layouts  1.79 us (2%)
  between operations  0.89 us (1%)
    ppermute x25, starting transfers between devices, exchange(): got.append(lax.ppermute(face, axis, pairs))  37.1 us
    ppermute x7, starting transfers between devices, swap(): return lax.ppermute(value, axes, pairs)  10.5 us
    ppermute x7, waiting for transfers between devices, swap(): return lax.ppermute(value, axes, pairs)  9.13 us
    pallas_call x10, Pallas kernels, call(): pl.pallas_call(body, out_shape=outs, in_specs=[VMEM] * len(ins), out_spec...  7.71 us
    pallas_call x1, Pallas kernels, orthonormal(): pl.pallas_call(body, out_shape=[f32(s.cells, k), f32(k, k)], in_specs=[VM...  5.44 us
    ppermute x25, waiting for transfers between devices, exchange(): got.append(lax.ppermute(face, axis, pairs))  3.55 us
    pallas_call x1, Pallas kernels, gather_terms(): pl.pallas_call(body, out_shape=outs, in_specs=[VMEM, VMEM], out_specs=(VM...  2.17 us
    slice x1, local copies, waits for them, and re-layouts, prepare(): block[i * each * s.row:(i + 1) * each * s.row]  1.79 us
  transfers between devices with their start and end apart: 32, of which 13 were waited for; matrix products, arithmetic and copies ran while one was open for 0% of the time, Pallas kernels for 9%

profile of v13, /device:TPU:0, one launch (start us, length us, event | category | flops | bytes accessed | tf_op | source)
XLA Modules:
  0.0 78.4 jit_solution(10904325917780291620)
XLA Ops:
  0.6 1.8 %fusion = (f32[16,16,8,128]{3,2,1,0:T(8,128)S(1)}, f32[16,16,8,128]{3,2,1,0:T(8,128)S(1)}) fusion(f32[32,16,8,128]{3,2,1,0:T(8,128)} %param.2), kind=kLoop, calls=%fused_computation.2 | loop fusion | bytes 4194304 | tf_op jit(solution)/shard_map/slice | solution.py:92
  2.4 1.1 %shard_map.41 = (f32[4104,128]{1,0:T(8,128)S(1)}, f32[4104,128]{1,0:T(8,128)S(1)}, f32[128,128]{1,0:T(8,128)S(1)}, f32[128,128]{1,0:T(8,128)S(1)}, f32[256,128]{...) custom-call(f32[16,8,32]{2,1,0:T(8,128)S(1)} %bitcast.6, ...), custom_call_target="tpu_custom_call" | custom-call | flops 2097152 | bytes 7233536 | tf_op jit(solution)/shard_map/pallas_call | solution.py:20
  3.6 3.0 %collective-permute-start.4 = (f32[512,128]{1,0:T(8,128)S(1)}, f32[512,128]{1,0:T(8,128)S(1)}, u32[]{:S(2)}, u32[]{:S(2)}) collective-permute-start(f32[512,128]{1,0:T(8,128)S(1)} %get-tuple-element.46), channel_id=1, source_target_pairs={{0,1},{1,0},{2,3},{3,2},{4,5},{5,4},{6,7},{7,6},{8,9},{9,8},{10,11... | collective-permute-start | bytes 786440 | tf_op jit(solution)/shard_map/ppermute | solution.py:204
  7.2 1.6 %collective-permute-start = (f32[128,128]{1,0:T(8,128)S(1)}, f32[128,128]{1,0:T(8,128)S(1)}, u32[]{:S(2)}, u32[]{:S(2)}) collective-permute-start(f32[128,128]{1,0:T(8,128)S(1)} %get-tuple-element.42), channel_id=1, source_target_pairs={{0,8},{8,0},{16,24},{24,16},{1,9},{9,1},{17,25},{25,17},{2,10},{10... | collective-permute-start | bytes 196616 | tf_op jit(solution)/shard_map/ppermute | solution.py:204
  9.5 1.2 %shard_map.42.p_ref = f32[4104,128]{1,0:T(8,128)S(1)} custom-call(f32[4104,128]{1,0:T(8,128)S(1)} %get-tuple-element.39.w_ref.rest_0_, f32[4104,128]{1,0:T(8,128)S(1)} %get-tuple-element.40.k_ref), custom_call_target="tpu_custom_call" | custom-call | flops 6291456 | bytes 6303744 | tf_op jit(solution)/shard_map/pallas_call | solution.py:20
  10.7 0.9 %collective-permute-done.refs_1_ = f32[128,128]{1,0:T(8,128)S(1)} collective-permute-done((f32[128,128]{1,0:T(8,128)S(1)}, f32[128,128]{1,0:T(8,128)S(1)}, u32[]{:S(2)}, u32[]{:S(2)}) %collective-permute-start) | collective-permute-done | bytes 65568 | tf_op jit(solution)/shard_map/ppermute | solution.py:204
  11.6 1.3 %collective-permute-done.4.refs_5_ = f32[512,128]{1,0:T(8,128)S(1)} collective-permute-done((f32[512,128]{1,0:T(8,128)S(1)}, f32[512,128]{1,0:T(8,128)S(1)}, u32[]{:S(2)}, u32[]{:S(2)}) %collective-permute-start.4) | collective-permute-done | bytes 262176 | tf_op jit(solution)/shard_map/ppermute | solution.py:204
  13.2 1.8 %collective-permute-start.9 = (f32[512,128]{1,0:T(8,128)S(1)}, f32[512,128]{1,0:T(8,128)S(1)}, u32[]{:S(2)}, u32[]{:S(2)}) collective-permute-start(f32[512,128]{1,0:T(8,128)S(1)} %get-tuple-element.52), channel_id=1, source_target_pairs={{0,1},{1,0},{2,3},{3,2},{4,5},{5,4},{6,7},{7,6},{8,9},{9,8},{10,11... | collective-permute-start | bytes 786440 | tf_op jit(solution)/shard_map/ppermute | solution.py:204
  15.6 3.6 %collective-permute-start.5 = (f32[128,128]{1,0:T(8,128)S(1)}, f32[128,128]{1,0:T(8,128)S(1)}, u32[]{:S(2)}, u32[]{:S(2)}) collective-permute-start(f32[128,128]{1,0:T(8,128)S(1)} %get-tuple-element.48), channel_id=1, source_target_pairs={{0,8},{8,0},{16,24},{24,16},{1,9},{9,1},{17,25},{25,17},{2,10},{10... | collective-permute-start | bytes 196616 | tf_op jit(solution)/shard_map/ppermute | solution.py:204
  19.9 1.2 %shard_map.44.p_ref = f32[4104,128]{1,0:T(8,128)S(1)} custom-call(f32[4104,128]{1,0:T(8,128)S(1)} %get-tuple-element.47.w_ref.rest_0_, f32[4104,128]{1,0:T(8,128)S(1)} %get-tuple-element.40.k_ref, f32[4104,128]{1,0:T(8,128)S(1)} %get-tuple-element.39.w_ref.rest_0_), custom_call_target="tpu_custom_call" | custom-call | flops 6291456 | bytes 8404992 | tf_op jit(solution)/shard_map/pallas_call | solution.py:20
  22.2 1.2 %collective-permute-start.14 = (f32[512,128]{1,0:T(8,128)S(1)}, f32[512,128]{1,0:T(8,128)S(1)}, u32[]{:S(2)}, u32[]{:S(2)}) collective-permute-start(f32[512,128]{1,0:T(8,128)S(1)} %get-tuple-element.58), channel_id=1, source_target_pairs={{0,1},{1,0},{2,3},{3,2},{4,5},{5,4},{6,7},{7,6},{8,9},{9,8},{10,11... | collective-permute-start | bytes 786440 | tf_op jit(solution)/shard_map/ppermute | solution.py:204
  23.4 2.4 %collective-permute-start.12 = (f32[256,128]{1,0:T(8,128)S(1)}, f32[256,128]{1,0:T(8,128)S(1)}, u32[]{:S(2)}, u32[]{:S(2)}) collective-permute-start(f32[256,128]{1,0:T(8,128)S(1)} %get-tuple-element.56), channel_id=1, source_target_pairs={{0,2},{2,0},{4,6},{6,4},{1,3},{3,1},{5,7},{7,5},{8,10},{10,8},{12,... | collective-permute-start | bytes 393224 | tf_op jit(solution)/shard_map/ppermute | solution.py:204
  26.5 3.7 %collective-permute-start.10 = (f32[128,128]{1,0:T(8,128)S(1)}, f32[128,128]{1,0:T(8,128)S(1)}, u32[]{:S(2)}, u32[]{:S(2)}) collective-permute-start(f32[128,128]{1,0:T(8,128)S(1)} %get-tuple-element.54), channel_id=1, source_target_pairs={{0,8},{8,0},{16,24},{24,16},{1,9},{9,1},{17,25},{25,17},{2,10},{10... | collective-permute-start | bytes 196616 | tf_op jit(solution)/shard_map/ppermute | solution.py:204
  30.8 1.4 %shard_map.46.p_ref = f32[4104,128]{1,0:T(8,128)S(1)} custom-call(f32[4104,128]{1,0:T(8,128)S(1)} %get-tuple-element.53.w_ref.rest_0_, f32[4104,128]{1,0:T(8,128)S(1)} %get-tuple-element.40.k_ref, f32[4104,128]{1,0:T(8,128)S(1)} %get-tuple-element.47.w_ref.rest_0_), custom_call_target="tpu_custom_call" | custom-call | flops 6291456 | bytes 8404992 | tf_op jit(solution)/shard_map/pallas_call | solution.py:20
  33.3 1.6 %collective-permute-start.17 = (f32[256,128]{1,0:T(8,128)S(1)}, f32[256,128]{1,0:T(8,128)S(1)}, u32[]{:S(2)}, u32[]{:S(2)}) collective-permute-start(f32[256,128]{1,0:T(8,128)S(1)} %get-tuple-element.62), channel_id=1, source_target_pairs={{0,2},{2,0},{4,6},{6,4},{1,3},{3,1},{5,7},{7,5},{8,10},{10,8},{12,... | collective-permute-start | bytes 393224 | tf_op jit(solution)/shard_map/ppermute | solution.py:204
  35.6 3.6 %collective-permute-start.15 = (f32[128,128]{1,0:T(8,128)S(1)}, f32[128,128]{1,0:T(8,128)S(1)}, u32[]{:S(2)}, u32[]{:S(2)}) collective-permute-start(f32[128,128]{1,0:T(8,128)S(1)} %get-tuple-element.60), channel_id=1, source_target_pairs={{0,8},{8,0},{16,24},{24,16},{1,9},{9,1},{17,25},{25,17},{2,10},{10... | collective-permute-start | bytes 196616 | tf_op jit(solution)/shard_map/ppermute | solution.py:204
  39.9 1.2 %shard_map.48.p_ref = f32[4104,128]{1,0:T(8,128)S(1)} custom-call(f32[4104,128]{1,0:T(8,128)S(1)} %get-tuple-element.59.w_ref, f32[4104,128]{1,0:T(8,128)S(1)} %get-tuple-element.40.k_ref, f32[4104,128]{1,0:T(8,128)S(1)} %get-tuple-element.53.w_ref.rest_0_), custom_call_target="tpu_custom_call" | custom-call | flops 6291456 | bytes 8404992 | tf_op jit(solution)/shard_map/pallas_call | solution.py:20
  41.8 2.4 %collective-permute-start.22 = (f32[256,128]{1,0:T(8,128)S(1)}, f32[256,128]{1,0:T(8,128)S(1)}, u32[]{:S(2)}, u32[]{:S(2)}) collective-permute-start(f32[256,128]{1,0:T(8,128)S(1)} %get-tuple-element.70), channel_id=1, source_target_pairs={{0,2},{2,0},{4,6},{6,4},{1,3},{3,1},{5,7},{7,5},{8,10},{10,8},{12,... | collective-permute-start | bytes 393224 | tf_op jit(solution)/shard_map/ppermute | solution.py:204
  44.9 1.6 %collective-permute-start.24 = (f32[256,128]{1,0:T(8,128)S(1)}, f32[256,128]{1,0:T(8,128)S(1)}, u32[]{:S(2)}, u32[]{:S(2)}) collective-permute-start(f32[256,128]{1,0:T(8,128)S(1)} %get-tuple-element.72), channel_id=1, source_target_pairs={{0,1},{1,0},{2,3},{3,2},{4,5},{5,4},{6,7},{7,6},{8,9},{9,8},{10,11... | collective-permute-start | bytes 393224 | tf_op jit(solution)/shard_map/ppermute | solution.py:204
  46.5 3.4 %collective-permute-start.20 = (f32[128,128]{1,0:T(8,128)S(1)}, f32[128,128]{1,0:T(8,128)S(1)}, u32[]{:S(2)}, u32[]{:S(2)}) collective-permute-start(f32[128,128]{1,0:T(8,128)S(1)} %get-tuple-element.68), channel_id=1, source_target_pairs={{0,8},{8,0},{16,24},{24,16},{1,9},{9,1},{17,25},{25,17},{2,10},{10... | collective-permute-start | bytes 196616 | tf_op jit(solution)/shard_map/ppermute | solution.py:204
  50.5 2.2 %shard_map.50 = (bf16[4096,256]{1,0:T(8,128)(2,1)S(1)}, f32[128,128]{1,0:T(8,128)S(1)}, f32[128,128]{1,0:T(8,128)S(1)}) custom-call(f32[4104,128]{1,0:T(8,128)S(1)} %get-tuple-element.65.w_ref, f32[4104,128]{1,0:T(8,128)S(1)} %get-tuple-element.40.k_ref), custom_call_target="tpu_custom_call" | custom-call | flops 1073741824 | bytes 8388608 | tf_op jit(solution)/shard_map/pallas_call | solution.py:247
  53.2 1.9 %collective-permute-start.25 = (f32[136,128]{1,0:T(8,128)S(1)}, f32[136,128]{1,0:T(8,128)S(1)}, u32[]{:S(2)}, u32[]{:S(2)}) collective-permute-start(f32[136,128]{1,0:T(8,128)S(1)} %shard_map.51), channel_id=1, source_target_pairs={{0,2},{1,3},{2,0},{3,1},{4,6},{5,7},{6,4},{7,5},{8,10},{9,11},{10,... | collective-permute-start | bytes 208904 | tf_op jit(solution)/shard_map/ppermute | solution.py:306
  55.2 0.9 %collective-permute-done.25 = f32[136,128]{1,0:T(8,128)S(1)} collective-permute-done((f32[136,128]{1,0:T(8,128)S(1)}, f32[136,128]{1,0:T(8,128)S(1)}, u32[]{:S(2)}, u32[]{:S(2)}) %collective-permute-start.25) | collective-permute-done | bytes 69664 | tf_op jit(solution)/shard_map/ppermute | solution.py:306
  56.1 1.4 %collective-permute-start.28 = (f32[136,128]{1,0:T(8,128)S(1)}, f32[136,128]{1,0:T(8,128)S(1)}, u32[]{:S(2)}, u32[]{:S(2)}) collective-permute-start(f32[136,128]{1,0:T(8,128)S(1)} %add.21), channel_id=1, source_target_pairs={{0,5},{1,4},{2,7},{3,6},{4,1},{5,0},{6,3},{7,2},{8,13},{9,12},{10,... | collective-permute-start | bytes 208904 | tf_op jit(solution)/shard_map/ppermute | solution.py:306
  57.5 1.5 %collective-permute-start.27 = (f32[136,128]{1,0:T(8,128)S(1)}, f32[136,128]{1,0:T(8,128)S(1)}, u32[]{:S(2)}, u32[]{:S(2)}) collective-permute-start(f32[136,128]{1,0:T(8,128)S(1)} %add.21), channel_id=1, source_target_pairs={{0,1},{1,0},{2,3},{3,2},{4,5},{5,4},{6,7},{7,6},{8,9},{9,8},{10,11... | collective-permute-start | bytes 208904 | tf_op jit(solution)/shard_map/ppermute | solution.py:306
  59.6 2.4 %collective-permute-done.28 = f32[136,128]{1,0:T(8,128)S(1)} collective-permute-done((f32[136,128]{1,0:T(8,128)S(1)}, f32[136,128]{1,0:T(8,128)S(1)}, u32[]{:S(2)}, u32[]{:S(2)}) %collective-permute-start.28) | collective-permute-done | bytes 69664 | tf_op jit(solution)/shard_map/ppermute | solution.py:306
  63.3 2.7 %collective-permute-start.31 = (f32[136,128]{1,0:T(8,128)S(1)}, f32[136,128]{1,0:T(8,128)S(1)}, u32[]{:S(2)}, u32[]{:S(2)}) collective-permute-start(f32[136,128]{1,0:T(8,128)S(1)} %add_add_fusion.1), channel_id=1, source_target_pairs={{0,24},{1,25},{2,26},{3,27},{4,28},{5,29},{6,30},{7,31},{8,16},{9,... | collective-permute-start | bytes 208904 | tf_op jit(solution)/shard_map/ppermute | solution.py:306
  66.0 2.1 %collective-permute-start.30 = (f32[136,128]{1,0:T(8,128)S(1)}, f32[136,128]{1,0:T(8,128)S(1)}, u32[]{:S(2)}, u32[]{:S(2)}) collective-permute-start(f32[136,128]{1,0:T(8,128)S(1)} %add_add_fusion.1), channel_id=1, source_target_pairs={{0,16},{1,17},{2,18},{3,19},{4,20},{5,21},{6,22},{7,23},{8,24},{9,... | collective-permute-start | bytes 208904 | tf_op jit(solution)/shard_map/ppermute | solution.py:306
  68.4 1.3 %collective-permute-done.31 = f32[136,128]{1,0:T(8,128)S(1)} collective-permute-done((f32[136,128]{1,0:T(8,128)S(1)}, f32[136,128]{1,0:T(8,128)S(1)}, u32[]{:S(2)}, u32[]{:S(2)}) %collective-permute-start.31) | collective-permute-done | bytes 69664 | tf_op jit(solution)/shard_map/ppermute | solution.py:306
  69.7 2.6 %collective-permute-done.30 = f32[136,128]{1,0:T(8,128)S(1)} collective-permute-done((f32[136,128]{1,0:T(8,128)S(1)}, f32[136,128]{1,0:T(8,128)S(1)}, u32[]{:S(2)}, u32[]{:S(2)}) %collective-permute-start.30) | collective-permute-done | bytes 69664 | tf_op jit(solution)/shard_map/ppermute | solution.py:306
  72.2 0.7 collective-permute-done.29
  73.0 5.4 %shard_map.52 = (f32[4096,128]{1,0:T(8,128)}, f32[128,128]{1,0:T(8,128)}) custom-call(f32[136,128]{1,0:T(8,128)S(1)} %add_add_fusion.p_ref, bf16[4096,256]{1,0:T(8,128)(2,1)S(1)} %get-tuple-element.73.f_ref), custom_call_target="tpu_custom_call" | custom-call | flops 536870912 | bytes 4194304 | tf_op jit(solution)/shard_map/pallas_call | solution.py:396
  (50 shorter events, 12.4 us)
Async XLA Ops:
  3.6 9.3 %collective-permute-start.4 = (f32[512,128]{1,0:T(8,128)S(1)}, f32[512,128]{1,0:T(8,128)S(1)}, u32[]{:S(2)}, u32[]{:S(2)}) collective-permute-start(f32[512,128]{1,0:T(8,128)S(1)} %get-tuple-element.46), channel_id=1, source_target_pairs={{0,1},{1,0},{2,3},{3,2},{4,5},{5,4},{6,7},{7,6},{8,9},{9,8},{10,11... | collective-permute-start | bytes 786440 | tf_op jit(solution)/shard_map/ppermute | solution.py:204
  6.6 5.0 %collective-permute-start.2 = (f32[256,128]{1,0:T(8,128)S(1)}, f32[256,128]{1,0:T(8,128)S(1)}, u32[]{:S(2)}, u32[]{:S(2)}) collective-permute-start(f32[256,128]{1,0:T(8,128)S(1)} %get-tuple-element.44), channel_id=1, source_target_pairs={{0,2},{2,0},{4,6},{6,4},{1,3},{3,1},{5,7},{7,5},{8,10},{10,8},{12,... | collective-permute-start | bytes 393224 | tf_op jit(solution)/shard_map/ppermute | solution.py:204
  6.6 5.0 %collective-permute-start.3 = (f32[256,128]{1,0:T(8,128)S(1)}, f32[256,128]{1,0:T(8,128)S(1)}, u32[]{:S(2)}, u32[]{:S(2)}) collective-permute-start(f32[256,128]{1,0:T(8,128)S(1)} %get-tuple-element.45), channel_id=1, source_target_pairs={{2,4},{4,2},{3,5},{5,3},{10,12},{12,10},{11,13},{13,11},{18,20},{2... | collective-permute-start | bytes 393224 | tf_op jit(solution)/shard_map/ppermute | solution.py:204
  7.2 4.3 %collective-permute-start = (f32[128,128]{1,0:T(8,128)S(1)}, f32[128,128]{1,0:T(8,128)S(1)}, u32[]{:S(2)}, u32[]{:S(2)}) collective-permute-start(f32[128,128]{1,0:T(8,128)S(1)} %get-tuple-element.42), channel_id=1, source_target_pairs={{0,8},{8,0},{16,24},{24,16},{1,9},{9,1},{17,25},{25,17},{2,10},{10... | collective-permute-start | bytes 196616 | tf_op jit(solution)/shard_map/ppermute | solution.py:204
  8.9 2.7 %collective-permute-start.1 = (f32[128,128]{1,0:T(8,128)S(1)}, f32[128,128]{1,0:T(8,128)S(1)}, u32[]{:S(2)}, u32[]{:S(2)}) collective-permute-start(f32[128,128]{1,0:T(8,128)S(1)} %get-tuple-element.43), channel_id=1, source_target_pairs={{8,16},{16,8},{9,17},{17,9},{10,18},{18,10},{11,19},{19,11},{12,20... | collective-permute-start | bytes 196616 | tf_op jit(solution)/shard_map/ppermute | solution.py:204
  13.2 8.8 %collective-permute-start.9 = (f32[512,128]{1,0:T(8,128)S(1)}, f32[512,128]{1,0:T(8,128)S(1)}, u32[]{:S(2)}, u32[]{:S(2)}) collective-permute-start(f32[512,128]{1,0:T(8,128)S(1)} %get-tuple-element.52), channel_id=1, source_target_pairs={{0,1},{1,0},{2,3},{3,2},{4,5},{5,4},{6,7},{7,6},{8,9},{9,8},{10,11... | collective-permute-start | bytes 786440 | tf_op jit(solution)/shard_map/ppermute | solution.py:204
  15.0 6.5 %collective-permute-start.7 = (f32[256,128]{1,0:T(8,128)S(1)}, f32[256,128]{1,0:T(8,128)S(1)}, u32[]{:S(2)}, u32[]{:S(2)}) collective-permute-start(f32[256,128]{1,0:T(8,128)S(1)} %get-tuple-element.50), channel_id=1, source_target_pairs={{0,2},{2,0},{4,6},{6,4},{1,3},{3,1},{5,7},{7,5},{8,10},{10,8},{12,... | collective-permute-start | bytes 393224 | tf_op jit(solution)/shard_map/ppermute | solution.py:204
  15.0 6.5 %collective-permute-start.8 = (f32[256,128]{1,0:T(8,128)S(1)}, f32[256,128]{1,0:T(8,128)S(1)}, u32[]{:S(2)}, u32[]{:S(2)}) collective-permute-start(f32[256,128]{1,0:T(8,128)S(1)} %get-tuple-element.51), channel_id=1, source_target_pairs={{2,4},{4,2},{3,5},{5,3},{10,12},{12,10},{11,13},{13,11},{18,20},{2... | collective-permute-start | bytes 393224 | tf_op jit(solution)/shard_map/ppermute | solution.py:204
  15.6 5.9 %collective-permute-start.5 = (f32[128,128]{1,0:T(8,128)S(1)}, f32[128,128]{1,0:T(8,128)S(1)}, u32[]{:S(2)}, u32[]{:S(2)}) collective-permute-start(f32[128,128]{1,0:T(8,128)S(1)} %get-tuple-element.48), channel_id=1, source_target_pairs={{0,8},{8,0},{16,24},{24,16},{1,9},{9,1},{17,25},{25,17},{2,10},{10... | collective-permute-start | bytes 196616 | tf_op jit(solution)/shard_map/ppermute | solution.py:204
  19.3 2.2 %collective-permute-start.6 = (f32[128,128]{1,0:T(8,128)S(1)}, f32[128,128]{1,0:T(8,128)S(1)}, u32[]{:S(2)}, u32[]{:S(2)}) collective-permute-start(f32[128,128]{1,0:T(8,128)S(1)} %get-tuple-element.49), channel_id=1, source_target_pairs={{8,16},{16,8},{9,17},{17,9},{10,18},{18,10},{11,19},{19,11},{12,20... | collective-permute-start | bytes 196616 | tf_op jit(solution)/shard_map/ppermute | solution.py:204
  22.2 10.2 %collective-permute-start.14 = (f32[512,128]{1,0:T(8,128)S(1)}, f32[512,128]{1,0:T(8,128)S(1)}, u32[]{:S(2)}, u32[]{:S(2)}) collective-permute-start(f32[512,128]{1,0:T(8,128)S(1)} %get-tuple-element.58), channel_id=1, source_target_pairs={{0,1},{1,0},{2,3},{3,2},{4,5},{5,4},{6,7},{7,6},{8,9},{9,8},{10,11... | collective-permute-start | bytes 786440 | tf_op jit(solution)/shard_map/ppermute | solution.py:204
  23.4 9.0 %collective-permute-start.12 = (f32[256,128]{1,0:T(8,128)S(1)}, f32[256,128]{1,0:T(8,128)S(1)}, u32[]{:S(2)}, u32[]{:S(2)}) collective-permute-start(f32[256,128]{1,0:T(8,128)S(1)} %get-tuple-element.56), channel_id=1, source_target_pairs={{0,2},{2,0},{4,6},{6,4},{1,3},{3,1},{5,7},{7,5},{8,10},{10,8},{12,... | collective-permute-start | bytes 393224 | tf_op jit(solution)/shard_map/ppermute | solution.py:204
  25.8 6.6 %collective-permute-start.13 = (f32[256,128]{1,0:T(8,128)S(1)}, f32[256,128]{1,0:T(8,128)S(1)}, u32[]{:S(2)}, u32[]{:S(2)}) collective-permute-start(f32[256,128]{1,0:T(8,128)S(1)} %get-tuple-element.57), channel_id=1, source_target_pairs={{2,4},{4,2},{3,5},{5,3},{10,12},{12,10},{11,13},{13,11},{18,20},{2... | collective-permute-start | bytes 393224 | tf_op jit(solution)/shard_map/ppermute | solution.py:204
  26.5 5.9 %collective-permute-start.10 = (f32[128,128]{1,0:T(8,128)S(1)}, f32[128,128]{1,0:T(8,128)S(1)}, u32[]{:S(2)}, u32[]{:S(2)}) collective-permute-start(f32[128,128]{1,0:T(8,128)S(1)} %get-tuple-element.54), channel_id=1, source_target_pairs={{0,8},{8,0},{16,24},{24,16},{1,9},{9,1},{17,25},{25,17},{2,10},{10... | collective-permute-start | bytes 196616 | tf_op jit(solution)/shard_map/ppermute | solution.py:204
  30.2 2.2 %collective-permute-start.11 = (f32[128,128]{1,0:T(8,128)S(1)}, f32[128,128]{1,0:T(8,128)S(1)}, u32[]{:S(2)}, u32[]{:S(2)}) collective-permute-start(f32[128,128]{1,0:T(8,128)S(1)} %get-tuple-element.55), channel_id=1, source_target_pairs={{8,16},{16,8},{9,17},{17,9},{10,18},{18,10},{11,19},{19,11},{12,20... | collective-permute-start | bytes 196616 | tf_op jit(solution)/shard_map/ppermute | solution.py:204
  32.7 8.8 %collective-permute-start.19 = (f32[512,128]{1,0:T(8,128)S(1)}, f32[512,128]{1,0:T(8,128)S(1)}, u32[]{:S(2)}, u32[]{:S(2)}) collective-permute-start(f32[512,128]{1,0:T(8,128)S(1)} %get-tuple-element.64), channel_id=1, source_target_pairs={{0,1},{1,0},{2,3},{3,2},{4,5},{5,4},{6,7},{7,6},{8,9},{9,8},{10,11... | collective-permute-start | bytes 786440 | tf_op jit(solution)/shard_map/ppermute | solution.py:204
  33.3 8.2 %collective-permute-start.17 = (f32[256,128]{1,0:T(8,128)S(1)}, f32[256,128]{1,0:T(8,128)S(1)}, u32[]{:S(2)}, u32[]{:S(2)}) collective-permute-start(f32[256,128]{1,0:T(8,128)S(1)} %get-tuple-element.62), channel_id=1, source_target_pairs={{0,2},{2,0},{4,6},{6,4},{1,3},{3,1},{5,7},{7,5},{8,10},{10,8},{12,... | collective-permute-start | bytes 393224 | tf_op jit(solution)/shard_map/ppermute | solution.py:204
  35.0 6.5 %collective-permute-start.18 = (f32[256,128]{1,0:T(8,128)S(1)}, f32[256,128]{1,0:T(8,128)S(1)}, u32[]{:S(2)}, u32[]{:S(2)}) collective-permute-start(f32[256,128]{1,0:T(8,128)S(1)} %get-tuple-element.63), channel_id=1, source_target_pairs={{2,4},{4,2},{3,5},{5,3},{10,12},{12,10},{11,13},{13,11},{18,20},{2... | collective-permute-start | bytes 393224 | tf_op jit(solution)/shard_map/ppermute | solution.py:204
  35.6 5.8 %collective-permute-start.15 = (f32[128,128]{1,0:T(8,128)S(1)}, f32[128,128]{1,0:T(8,128)S(1)}, u32[]{:S(2)}, u32[]{:S(2)}) collective-permute-start(f32[128,128]{1,0:T(8,128)S(1)} %get-tuple-element.60), channel_id=1, source_target_pairs={{0,8},{8,0},{16,24},{24,16},{1,9},{9,1},{17,25},{25,17},{2,10},{10... | collective-permute-start | bytes 196616 | tf_op jit(solution)/shard_map/ppermute | solution.py:204
  39.2 2.2 %collective-permute-start.16 = (f32[128,128]{1,0:T(8,128)S(1)}, f32[128,128]{1,0:T(8,128)S(1)}, u32[]{:S(2)}, u32[]{:S(2)}) collective-permute-start(f32[128,128]{1,0:T(8,128)S(1)} %get-tuple-element.61), channel_id=1, source_target_pairs={{8,16},{16,8},{9,17},{17,9},{10,18},{18,10},{11,19},{19,11},{12,20... | collective-permute-start | bytes 196616 | tf_op jit(solution)/shard_map/ppermute | solution.py:204
  41.8 10.9 %collective-permute-start.22 = (f32[256,128]{1,0:T(8,128)S(1)}, f32[256,128]{1,0:T(8,128)S(1)}, u32[]{:S(2)}, u32[]{:S(2)}) collective-permute-start(f32[256,128]{1,0:T(8,128)S(1)} %get-tuple-element.70), channel_id=1, source_target_pairs={{0,2},{2,0},{4,6},{6,4},{1,3},{3,1},{5,7},{7,5},{8,10},{10,8},{12,... | collective-permute-start | bytes 393224 | tf_op jit(solution)/shard_map/ppermute | solution.py:204
  44.3 8.5 %collective-permute-start.23 = (f32[256,128]{1,0:T(8,128)S(1)}, f32[256,128]{1,0:T(8,128)S(1)}, u32[]{:S(2)}, u32[]{:S(2)}) collective-permute-start(f32[256,128]{1,0:T(8,128)S(1)} %get-tuple-element.71), channel_id=1, source_target_pairs={{2,4},{4,2},{3,5},{5,3},{10,12},{12,10},{11,13},{13,11},{18,20},{2... | collective-permute-start | bytes 393224 | tf_op jit(solution)/shard_map/ppermute | solution.py:204
  44.9 7.8 %collective-permute-start.24 = (f32[256,128]{1,0:T(8,128)S(1)}, f32[256,128]{1,0:T(8,128)S(1)}, u32[]{:S(2)}, u32[]{:S(2)}) collective-permute-start(f32[256,128]{1,0:T(8,128)S(1)} %get-tuple-element.72), channel_id=1, source_target_pairs={{0,1},{1,0},{2,3},{3,2},{4,5},{5,4},{6,7},{7,6},{8,9},{9,8},{10,11... | collective-permute-start | bytes 393224 | tf_op jit(solution)/shard_map/ppermute | solution.py:204
  46.5 6.2 %collective-permute-start.20 = (f32[128,128]{1,0:T(8,128)S(1)}, f32[128,128]{1,0:T(8,128)S(1)}, u32[]{:S(2)}, u32[]{:S(2)}) collective-permute-start(f32[128,128]{1,0:T(8,128)S(1)} %get-tuple-element.68), channel_id=1, source_target_pairs={{0,8},{8,0},{16,24},{24,16},{1,9},{9,1},{17,25},{25,17},{2,10},{10... | collective-permute-start | bytes 196616 | tf_op jit(solution)/shard_map/ppermute | solution.py:204
  49.9 2.9 %collective-permute-start.21 = (f32[128,128]{1,0:T(8,128)S(1)}, f32[128,128]{1,0:T(8,128)S(1)}, u32[]{:S(2)}, u32[]{:S(2)}) collective-permute-start(f32[128,128]{1,0:T(8,128)S(1)} %get-tuple-element.69), channel_id=1, source_target_pairs={{8,16},{16,8},{9,17},{17,9},{10,18},{18,10},{11,19},{19,11},{12,20... | collective-permute-start | bytes 196616 | tf_op jit(solution)/shard_map/ppermute | solution.py:204
  53.2 2.8 %collective-permute-start.25 = (f32[136,128]{1,0:T(8,128)S(1)}, f32[136,128]{1,0:T(8,128)S(1)}, u32[]{:S(2)}, u32[]{:S(2)}) collective-permute-start(f32[136,128]{1,0:T(8,128)S(1)} %shard_map.51), channel_id=1, source_target_pairs={{0,2},{1,3},{2,0},{3,1},{4,6},{5,7},{6,4},{7,5},{8,10},{9,11},{10,... | collective-permute-start | bytes 208904 | tf_op jit(solution)/shard_map/ppermute | solution.py:306
  56.1 6.0 %collective-permute-start.28 = (f32[136,128]{1,0:T(8,128)S(1)}, f32[136,128]{1,0:T(8,128)S(1)}, u32[]{:S(2)}, u32[]{:S(2)}) collective-permute-start(f32[136,128]{1,0:T(8,128)S(1)} %add.21), channel_id=1, source_target_pairs={{0,5},{1,4},{2,7},{3,6},{4,1},{5,0},{6,3},{7,2},{8,13},{9,12},{10,... | collective-permute-start | bytes 208904 | tf_op jit(solution)/shard_map/ppermute | solution.py:306
  57.5 5.2 %collective-permute-start.27 = (f32[136,128]{1,0:T(8,128)S(1)}, f32[136,128]{1,0:T(8,128)S(1)}, u32[]{:S(2)}, u32[]{:S(2)}) collective-permute-start(f32[136,128]{1,0:T(8,128)S(1)} %add.21), channel_id=1, source_target_pairs={{0,1},{1,0},{2,3},{3,2},{4,5},{5,4},{6,7},{7,6},{8,9},{9,8},{10,11... | collective-permute-start | bytes 208904 | tf_op jit(solution)/shard_map/ppermute | solution.py:306
  59.0 4.3 %collective-permute-start.26 = (f32[136,128]{1,0:T(8,128)S(1)}, f32[136,128]{1,0:T(8,128)S(1)}, u32[]{:S(2)}, u32[]{:S(2)}) collective-permute-start(f32[136,128]{1,0:T(8,128)S(1)} %add.21), channel_id=1, source_target_pairs={{0,4},{1,5},{2,6},{3,7},{4,0},{5,1},{6,2},{7,3},{8,12},{9,13},{10,... | collective-permute-start | bytes 208904 | tf_op jit(solution)/shard_map/ppermute | solution.py:306
  63.3 6.3 %collective-permute-start.31 = (f32[136,128]{1,0:T(8,128)S(1)}, f32[136,128]{1,0:T(8,128)S(1)}, u32[]{:S(2)}, u32[]{:S(2)}) collective-permute-start(f32[136,128]{1,0:T(8,128)S(1)} %add_add_fusion.1), channel_id=1, source_target_pairs={{0,24},{1,25},{2,26},{3,27},{4,28},{5,29},{6,30},{7,31},{8,16},{9,... | collective-permute-start | bytes 208904 | tf_op jit(solution)/shard_map/ppermute | solution.py:306
  66.0 6.2 %collective-permute-start.30 = (f32[136,128]{1,0:T(8,128)S(1)}, f32[136,128]{1,0:T(8,128)S(1)}, u32[]{:S(2)}, u32[]{:S(2)}) collective-permute-start(f32[136,128]{1,0:T(8,128)S(1)} %add_add_fusion.1), channel_id=1, source_target_pairs={{0,16},{1,17},{2,18},{3,19},{4,20},{5,21},{6,22},{7,23},{8,24},{9,... | collective-permute-start | bytes 208904 | tf_op jit(solution)/shard_map/ppermute | solution.py:306
  68.1 4.8 %collective-permute-start.29 = (f32[136,128]{1,0:T(8,128)S(1)}, f32[136,128]{1,0:T(8,128)S(1)}, u32[]{:S(2)}, u32[]{:S(2)}) collective-permute-start(f32[136,128]{1,0:T(8,128)S(1)} %add_add_fusion.1), channel_id=1, source_target_pairs={{0,8},{1,9},{2,10},{3,11},{4,12},{5,13},{6,14},{7,15},{8,0},{9,1},... | collective-permute-start | bytes 208904 | tf_op jit(solution)/shard_map/ppermute | solution.py:306
  (1 other events, 1.8 us)
